TPU v7x, 32 devices: a whole 2x2x4 slice. The times are simulated.
32 devices in a mesh: depth: 16 (over z, y, core), shot: 2 (over x).
Axes of the slice: x: 2, y: 2, z: 4, core: 2. Of those that a mesh axis runs over, the one named last changes fastest.
Arguments:
- down_state: bfloat16 [32, 4, 2, 256, 256], P('depth', 'shot'), may hold values from -6 to 6
- up_state: bfloat16 [32, 4, 2, 256, 256], P('depth', 'shot'), may hold values from -6 to 6
- source: bfloat16 [4, 2, 256, 256], P('shot'), may hold values from -6 to 6
- reflect: float32 [32, 256, 256], P('depth'), may hold values from -0.3 to 0.3
- screen_class: int32 [32, 256, 256], P('depth'), may hold values from 0 to 15
- screen_values: float32 [16], replicated, may hold values from -1 to 1
- freq_index: int32 [4], P('shot'), may hold values from 0 to 127
Outputs:
- down_out: bfloat16 [32, 4, 2, 256, 256], P('depth', 'shot')
- up_out: bfloat16 [32, 4, 2, 256, 256], P('depth', 'shot')
- gradient: float32 [32, 256, 256], P('depth', 'shot')
All inputs are finite; a program needn't handle non-finite values.
Results may differ from a plain program's by a relative error of at most 0.034.
Values may be sent and summed in bfloat16 or wider, within the bound.
No kernel may reach another device: no remote copies, remote signals or barrier semaphores. Data moves between devices by JAX's collectives and lax.ppermute only.
A program may use at most 64 MiB of HBM per device.

v0:
```python
import math

import jax
import jax.numpy as jnp
from jax import lax
from jax.sharding import PartitionSpec as P

HOPS = 3
NCLASS = 16
NFREQ = 128


def passed_along(block, axis, distance):
    devices = range(lax.axis_size(axis))
    route = [(i - distance, i) for i in devices if i - distance in devices]
    return lax.ppermute(block, axis, route)


def dft_tables(length):
    counter = jnp.arange(length, dtype=jnp.int32)
    product = counter[:, None] * counter[None, :] % length
    angles = 2.0 * math.pi / length * product.astype(jnp.float32)
    return (jnp.cos(angles).astype(jnp.bfloat16), jnp.sin(angles).astype(jnp.bfloat16))


def wavenumbers(length):
    counter = jnp.arange(length, dtype=jnp.int32)
    wrapped = jnp.where(counter >= length // 2, counter - length, counter)
    return 2.0 * math.pi / length * wrapped.astype(jnp.float32)


def propagate(planes, phase_re, phase_im, tables):
    fwd_left, fwd_right, inv_left, inv_right = tables
    first = jnp.einsum(
        "cdjk,...dkl->...cjl", fwd_left, planes, preferred_element_type=jnp.float32
    ).astype(jnp.bfloat16)
    second = jnp.einsum("...djl,dclm->...cjm", first, fwd_right, preferred_element_type=jnp.float32)
    real_part = second[..., 0, :, :]
    imag_part = second[..., 1, :, :]
    turned = jnp.stack(
        [real_part * phase_re - imag_part * phase_im, real_part * phase_im + imag_part * phase_re],
        axis=-3,
    ).astype(jnp.bfloat16)
    third = jnp.einsum(
        "cdjk,...dkl->...cjl", inv_left, turned, preferred_element_type=jnp.float32
    ).astype(jnp.bfloat16)
    return jnp.einsum(
        "...djl,dclm->...cjm", third, inv_right, preferred_element_type=jnp.float32
    ).astype(jnp.bfloat16)


def trade(down_edge, up_edge):
    got_down = passed_along(down_edge, "depth", 1)
    got_up = passed_along(up_edge, "depth", -1)
    return (got_down, got_up)


def per_device(down_state, up_state, source, reflect, screen_class, screen_values, freq_index):
    levels = down_state.shape[0]
    rows_x = down_state.shape[3]
    rows_y = down_state.shape[4]
    front_count = down_state.shape[1]
    depth_rank = lax.axis_index("depth")
    scale = 1.0 / math.sqrt(front_count * lax.axis_size("shot"))
    cos_x, sin_x = dft_tables(rows_x)
    cos_y, sin_y = dft_tables(rows_y)
    tables = (
        jnp.stack([jnp.stack([cos_x, sin_x]), jnp.stack([-sin_x, cos_x])]),
        jnp.stack([jnp.stack([cos_y, -sin_y]), jnp.stack([sin_y, cos_y])]),
        jnp.stack([jnp.stack([cos_x, -sin_x]), jnp.stack([sin_x, cos_x])]),
        jnp.stack([jnp.stack([cos_y, sin_y]), jnp.stack([-sin_y, cos_y])]),
    )
    kwave = 0.95 * math.pi * (freq_index.astype(jnp.float32) + 1.0) / NFREQ
    kx_wave = wavenumbers(rows_x)
    ky_wave = wavenumbers(rows_y)
    vertical = kwave[:, None, None] ** 2 - kx_wave[None, :, None] ** 2 - ky_wave[None, None, :] ** 2
    propag = jnp.sqrt(jnp.maximum(vertical, 0.0))
    damping = jnp.exp(-jnp.sqrt(jnp.maximum(-vertical, 0.0))) / (rows_x * rows_y)
    phase_re = damping * jnp.cos(propag)
    phase_im = damping * jnp.sin(propag)
    classes = jnp.arange(NCLASS, dtype=jnp.int32)
    onehot = (screen_class[None] == classes[:, None, None, None]).astype(jnp.float32)
    slowness = jnp.einsum("c,clxy->lxy", screen_values, onehot, precision=lax.Precision.HIGHEST)
    angle = kwave[None, :, None, None] * slowness[:, None]
    screen_re = jnp.cos(angle)
    screen_im = jnp.sin(angle)
    refl = reflect[:, None]
    top_slab = depth_rank == 0
    down = down_state
    up = up_state
    a_re = a_im = b_re = b_im = None
    for repeat in range(HOPS):
        down_edge = down[levels - 1]
        up_edge = up[0]
        got_down, got_up = trade(down_edge, up_edge)
        got_down = jnp.where(top_slab, source, got_down)
        moved = propagate(
            jnp.concatenate([got_down[None], down[: levels - 1], up[1:], got_up[None]], axis=0),
            phase_re,
            phase_im,
            tables,
        )
        from_above = moved[:levels]
        from_below = moved[levels:]
        qa_re = from_above[:, :, 0].astype(jnp.float32)
        qa_im = from_above[:, :, 1].astype(jnp.float32)
        qb_re = from_below[:, :, 0].astype(jnp.float32)
        qb_im = from_below[:, :, 1].astype(jnp.float32)
        a_re = screen_re * qa_re - screen_im * qa_im
        a_im = screen_re * qa_im + screen_im * qa_re
        b_re = screen_re * qb_re - screen_im * qb_im
        b_im = screen_re * qb_im + screen_im * qb_re
        down = jnp.stack(
            [(1.0 + refl) * a_re - refl * b_re, (1.0 + refl) * a_im - refl * b_im], axis=2
        ).astype(jnp.bfloat16)
        up = jnp.stack(
            [(1.0 - refl) * b_re + refl * a_re, (1.0 - refl) * b_im + refl * a_im], axis=2
        ).astype(jnp.bfloat16)
    terms = scale * jnp.sum(a_re * b_re + a_im * b_im, axis=1)
    gradient = lax.psum_scatter(
        terms.astype(jnp.bfloat16), "shot", scatter_dimension=1, tiled=True
    ).astype(jnp.float32)
    return (down, up, gradient)


def solution(mesh):
    return jax.shard_map(
        per_device,
        mesh=mesh,
        in_specs=(
            P("depth", "shot", None, None, None),
            P("depth", "shot", None, None, None),
            P("shot", None, None, None),
            P("depth", None, None),
            P("depth", None, None),
            P(),
            P("shot"),
        ),
        out_specs=(
            P("depth", "shot", None, None, None),
            P("depth", "shot", None, None, None),
            P("depth", "shot", None),
        ),
        check_vma=False,
    )
```

profile of v0, /device:TPU:4, one launch (start us, length us, event | category | flops | bytes accessed | tf_op | source)
XLA Modules:
  0.0 173.4 jit_solution(1771027503888791370)
XLA Ops:
  9.6 2.0 %collective-permute-start = (bf16[2,2,256,256]{2,3,1,0:T(8,128)(2,1)}, bf16[2,2,256,256]{2,3,1,0:T(8,128)(2,1)}, u32[]{:S(2)}, u32[]{:S(2)}) collective-permute-start(bf16[2,2,256,256]{2,3,1,0:T(8,128)(2,1)} %bitcast.597), channel_id=1, source_target_pairs={{0,2},{2,4},{4,6},{6,8},{8,10},{10,12},{12,14},{14,16},{16,18},{18... | collective-permute-start | bytes 1572872 | tf_op jit(solution)/shard_map/ppermute | solution.py:16
  13.6 3.6 %collective-permute-start.1 = (bf16[2,2,256,256]{2,3,1,0:T(8,128)(2,1)}, bf16[2,2,256,256]{2,3,1,0:T(8,128)(2,1)}, u32[]{:S(2)}, u32[]{:S(2)}) collective-permute-start(bf16[2,2,256,256]{2,3,1,0:T(8,128)(2,1)} %bitcast.18), channel_id=1, source_target_pairs={{2,0},{4,2},{6,4},{8,6},{10,8},{12,10},{14,12},{16,14},{18,16},{20... | collective-permute-start | bytes 1572872 | tf_op jit(solution)/shard_map/ppermute | solution.py:16
  18.6 4.6 %fusion = f32[1,2,256,256]{3,0,2,1:T(1,128)} fusion(pred[16,2,256,256]{3,2,1,0:T(32,128)(4,1)S(1)} %iota_compare_fusion, f32[16]{0:T(128)S(1)} %copy-done), kind=kOutput, calls=%fused_computation.1 | convolution fusion | flops 25165824 | bytes 2621504 | tf_op jit(solution)/shard_map/c,clxy->lxy/dot_general | solution.py:83
  31.6 2.3 %fusion.160 = (f32[2,256,256]{1,2,0:T(8,128)S(1)}, f32[2,256,256]{1,2,0:T(8,128)S(1)}) fusion(f32[256]{0:T(256)S(1)} %fusion.193, f32[2,256]{1,0:T(2,128)S(1)} %broadcast_subtract_fusion.1), kind=kLoop, calls=%fused_computation.205 | loop fusion | flops 1048576 | bytes 1051648 | tf_op jit(solution)/shard_map/mul | solution.py:79
  33.9 1.9 %select_bitcast_fusion.2 = bf16[1,2,2,256,256]{3,4,2,1,0:T(8,128)(2,1)} fusion(bf16[2,2,256,256]{2,3,1,0:T(8,128)(2,1)} %copy.155, bf16[2,2,256,256]{2,3,1,0:T(8,128)(2,1)} %collective-permute-done, pred[]{:T(512)S(6)} %eq.22), kind=kLoop, calls=%fused_computation.227 | loop fusion | flops 262144 | bytes 1572865 | tf_op jit(solution)/shard_map/broadcast_in_dim | solution.py:98
  35.8 6.1 %convolution_bitcast_fusion.2 = f32[4,2,2,256,256]{3,4,1,0,2:T(8,128)} fusion(bf16[1,2,2,256,256]{3,4,2,1,0:T(8,128)(2,1)} %bitcast.19, bf16[1,2,2,256,256]{3,4,2,1,0:T(8,128)(2,1)} %copy.249, bf16[1,2,2,256,256]{3,4,2,1,0:T(8,128)(2,1)} %copy.248, bf16[1,2,2,256,256]{3,4,2,1,0:T(8,128)(2,1)} %select_bitcast_fusion.2, ...), kind=kOutput, calls=%fused_computation.33 | convolution fusion | flops 2158231552 | bytes 7340032 | tf_op jit(solution)/shard_map/...djl,dclm->...cjm/dot_general | solution.py:37
  41.9 4.2 %subtract_convert_fusion.2 = (bf16[4,2,1,256,256]{3,4,1,0,2:T(8,128)(2,1)}, bf16[4,2,1,256,256]{3,4,1,0,2:T(8,128)(2,1)}) fusion(f32[4,2,2,256,256]{3,4,1,0,2:T(8,128)} %convolution_bitcast_fusion.2, f32[2,256,256]{1,2,0:T(8,128)S(1)} %get-tuple-element.46, f32[2,256,256]{1,2,0:T(8,128)S(1)} %get-tuple-element.45), kind=kLoop, calls=%fused_computation.76 | loop fusion | flops 4194304 | bytes 7340032 | tf_op jit(solution)/shard_map/convert.20
  46.1 5.5 %fusion.43 = bf16[4,2,2,256,256]{3,4,1,2,0:T(8,128)(2,1)} fusion(bf16[1,2,256,256]{3,2,1,0:T(8,128)(2,1)} %get-tuple-element.40, bf16[1,2,256,256]{3,2,1,0:T(8,128)(2,1)} %get-tuple-element.43, bf16[4,2,1,256,256]{3,4,1,0,2:T(8,128)(2,1)} %get-tuple-element.17, bf16[4,2,1,256,256]{3,4,1,0,2:T(8,128)(2,1)} %get-tuple-element.16, ...), kind=kOutput, calls=%fused_computation.77 | convolution fusion | flops 2151940096 | bytes 5242880 | tf_op jit(solution)/shard_map/...djl,dclm->...cjm/dot_general | solution.py:47
  51.6 7.4 %fusion.111 = (bf16[2,2,1,256,256]{3,4,1,2,0:T(8,128)(2,1)S(1)}, bf16[2,2,1,256,256]{3,4,1,2,0:T(8,128)(2,1)S(1)}, bf16[2,2,1,256,256]{3,4,1,0,2:T(8,128)(2,1)S(1)}) fusion(f32[2,256,256]{1,2,0:T(8,128)S(1)} %copy.120, f32[2,256,256]{1,2,0:T(8,128)S(1)} %bitcast.588, f32[2]{0:T(128)S(1)} %get-tuple-element.48, f32[2,256,256]{1,2,0:T(8,128)S(1)} %copy.105, ...), kind=kLoop, calls=%fused_computation.160 | loop fusion | flops 7602176 | bytes 5767176 | tf_op jit(solution)/shard_map/convert.18
  60.0 1.9 %collective-permute-start.2 = (bf16[2,2,256,256]{2,3,0,1:T(8,128)(2,1)}, bf16[2,2,256,256]{2,3,0,1:T(8,128)(2,1)}, u32[]{:S(2)}, u32[]{:S(2)}) collective-permute-start(bf16[2,2,256,256]{2,3,0,1:T(8,128)(2,1)} %fusion.170), channel_id=1, source_target_pairs={{0,2},{2,4},{4,6},{6,8},{8,10},{10,12},{12,14},{14,16},{16,18},{18... | collective-permute-start | bytes 1572872 | tf_op jit(solution)/shard_map/ppermute | solution.py:16
  61.9 4.5 %fusion.122 = bf16[2,2,1,256,256]{3,4,1,0,2:T(8,128)(2,1)S(1)} fusion(f32[2,256,256]{1,2,0:T(8,128)S(1)} %copy.134, f32[2,256,256]{1,2,0:T(8,128)S(1)} %copy.120, f32[2,256,256]{1,2,0:T(8,128)S(1)} %bitcast.589, f32[2]{0:T(128)S(1)} %get-tuple-element.48, bf16[4,2,2,256,256]{3,4,1,2,0:T(8,128)(2,1)S(1)} %copy-done.5), kind=kLoop, calls=%fused_computation.171 | loop fusion | flops 3932160 | bytes 4194312 | tf_op jit(solution)/shard_map/convert.17
  67.6 3.9 %collective-permute-start.3 = (bf16[2,2,256,256]{2,3,0,1:T(8,128)(2,1)}, bf16[2,2,256,256]{2,3,0,1:T(8,128)(2,1)}, u32[]{:S(2)}, u32[]{:S(2)}) collective-permute-start(bf16[2,2,256,256]{2,3,0,1:T(8,128)(2,1)} %get-tuple-element.32), channel_id=1, source_target_pairs={{2,0},{4,2},{6,4},{8,6},{10,8},{12,10},{14,12},{16,14},{18,16},{20... | collective-permute-start | bytes 1572872 | tf_op jit(solution)/shard_map/ppermute | solution.py:16
  71.4 2.0 %copy.133 = bf16[2,2,256,256]{2,3,0,1:T(8,128)(2,1)} copy(bf16[2,2,256,256]{3,2,1,0:T(8,128)(2,1)} %param.9) | data formatting | bytes 1048576 | tf_op args[2]
  73.5 1.9 %select_bitcast_fusion.1 = bf16[1,2,2,256,256]{3,4,1,2,0:T(8,128)(2,1)} fusion(bf16[2,2,256,256]{2,3,0,1:T(8,128)(2,1)} %copy.133, bf16[2,2,256,256]{2,3,0,1:T(8,128)(2,1)} %collective-permute-done.2, pred[]{:T(512)S(6)} %eq.22), kind=kLoop, calls=%fused_computation.226 | loop fusion | flops 262144 | bytes 1572865 | tf_op jit(solution)/shard_map/broadcast_in_dim | solution.py:98
  75.3 2.9 %collective-permute-done.3 = bf16[2,2,256,256]{2,3,0,1:T(8,128)(2,1)} collective-permute-done((bf16[2,2,256,256]{2,3,0,1:T(8,128)(2,1)}, bf16[2,2,256,256]{2,3,0,1:T(8,128)(2,1)}, u32[]{:S(2)}, u32[]{:S(2)}) %collective-permute-start.3) | collective-permute-done | bytes 524320 | tf_op jit(solution)/shard_map/ppermute | solution.py:16
  78.2 6.3 %convolution_bitcast_fusion.1 = f32[4,2,2,256,256]{3,4,1,0,2:T(8,128)} fusion(bf16[1,2,256,256]{3,2,1,0:T(8,128)(2,1)} %get-tuple-element.44, bf16[1,2,256,256]{3,2,1,0:T(8,128)(2,1)S(1)} %get-tuple-element.39, bf16[2,2,1,256,256]{3,4,1,2,0:T(8,128)(2,1)} %copy-done.12, bf16[2,2,1,256,256]{3,4,1,2,0:T(8,128)(2,1)} %copy-done.11, ...), kind=kOutput, calls=%fused_computation.32 | convolution fusion | flops 2165571584 | bytes 7864320 | tf_op jit(solution)/shard_map/...djl,dclm->...cjm/dot_general | solution.py:37
  84.4 4.2 %subtract_convert_fusion.1 = (bf16[4,2,1,256,256]{3,4,1,0,2:T(8,128)(2,1)}, bf16[4,2,1,256,256]{3,4,1,0,2:T(8,128)(2,1)}) fusion(f32[4,2,2,256,256]{3,4,1,0,2:T(8,128)} %convolution_bitcast_fusion.1, f32[2,256,256]{1,2,0:T(8,128)S(1)} %get-tuple-element.46, f32[2,256,256]{1,2,0:T(8,128)S(1)} %get-tuple-element.45), kind=kLoop, calls=%fused_computation.74 | loop fusion | flops 4194304 | bytes 7340032 | tf_op jit(solution)/shard_map/convert.14
  88.6 5.5 %fusion.46 = bf16[4,2,2,256,256]{3,4,1,0,2:T(8,128)(2,1)} fusion(bf16[1,2,256,256]{3,2,1,0:T(8,128)(2,1)} %get-tuple-element.40, bf16[1,2,256,256]{3,2,1,0:T(8,128)(2,1)} %get-tuple-element.43, bf16[4,2,1,256,256]{3,4,1,0,2:T(8,128)(2,1)} %get-tuple-element.15, bf16[4,2,1,256,256]{3,4,1,0,2:T(8,128)(2,1)} %get-tuple-element.14, ...), kind=kOutput, calls=%fused_computation.78 | convolution fusion | flops 2151940096 | bytes 5242880 | tf_op jit(solution)/shard_map/...djl,dclm->...cjm/dot_general | solution.py:47
  94.1 7.3 %fusion.124 = (bf16[2,2,1,256,256]{3,4,2,1,0:T(8,128)(2,1)S(1)}, bf16[2,2,1,256,256]{3,4,2,1,0:T(8,128)(2,1)S(1)}) fusion(f32[2,256,256]{1,2,0:T(8,128)S(1)} %copy.120, f32[2,256,256]{1,2,0:T(8,128)S(1)} %bitcast.590, f32[2]{0:T(128)S(1)} %get-tuple-element.48, f32[2,256,256]{1,2,0:T(8,128)S(1)} %copy.105, bf16[4,2,2,256,256]{3,4,1,0,2:T(8,128)(2,1)} %fusion.46), kind=kLoop, calls=%fused_computation.173 | loop fusion | flops 6553600 | bytes 4718600 | tf_op jit(solution)/shard_map/convert.12
  101.6 5.5 %collective-permute-start.4 = (bf16[2,2,256,256]{2,3,1,0:T(8,128)(2,1)S(1)}, bf16[2,2,256,256]{2,3,1,0:T(8,128)(2,1)S(1)}, u32[]{:S(2)}, u32[]{:S(2)}) collective-permute-start(bf16[2,2,256,256]{2,3,1,0:T(8,128)(2,1)S(1)} %fusion.166), channel_id=1, source_target_pairs={{0,2},{2,4},{4,6},{6,8},{8,10},{10,12},{12,14},{14,16},{16,18},{18... | collective-permute-start | bytes 1572872 | tf_op jit(solution)/shard_map/ppermute | solution.py:16
  107.1 4.9 %fusion.115 = (bf16[2,2,1,256,256]{3,4,2,1,0:T(8,128)(2,1)S(1)}, bf16[2,2,1,256,256]{3,4,2,1,0:T(8,128)(2,1)S(1)}) fusion(f32[2,256,256]{1,2,0:T(8,128)S(1)} %copy.134, f32[2,256,256]{1,2,0:T(8,128)S(1)} %copy.120, f32[2,256,256]{1,2,0:T(8,128)S(1)} %bitcast.591, f32[2]{0:T(128)S(1)} %get-tuple-element.48, bf16[4,2,2,256,256]{3,4,1,0,2:T(8,128)(2,1)S(1)} %copy-done.4), kind=kLoop, calls=%fused_computation.164 | loop fusion | flops 6553600 | bytes 4718600 | tf_op jit(solution)/shard_map/convert.10
  113.0 2.2 %collective-permute-start.5 = (bf16[2,2,256,256]{2,3,1,0:T(8,128)(2,1)S(1)}, bf16[2,2,256,256]{2,3,1,0:T(8,128)(2,1)S(1)}, u32[]{:S(2)}, u32[]{:S(2)}) collective-permute-start(bf16[2,2,256,256]{2,3,1,0:T(8,128)(2,1)S(1)} %get-tuple-element.30), channel_id=1, source_target_pairs={{2,0},{4,2},{6,4},{8,6},{10,8},{12,10},{14,12},{16,14},{18,16},{20... | collective-permute-start | bytes 1572872 | tf_op jit(solution)/shard_map/ppermute | solution.py:16
  116.0 5.5 %collective-permute-done.5 = bf16[2,2,256,256]{2,3,1,0:T(8,128)(2,1)S(1)} collective-permute-done((bf16[2,2,256,256]{2,3,1,0:T(8,128)(2,1)S(1)}, bf16[2,2,256,256]{2,3,1,0:T(8,128)(2,1)S(1)}, u32[]{:S(2)}, u32[]{:S(2)}) %collective-permute-start.5) | collective-permute-done | bytes 524320 | tf_op jit(solution)/shard_map/ppermute | solution.py:16
  122.4 5.9 %convolution_bitcast_fusion = f32[4,2,2,256,256]{3,4,1,0,2:T(8,128)} fusion(bf16[2,2,1,256,256]{3,4,2,1,0:T(8,128)(2,1)S(1)} %copy-done.10, bf16[2,2,1,256,256]{3,4,2,1,0:T(8,128)(2,1)S(1)} %copy-done.8, bf16[1,2,2,256,256]{3,4,2,1,0:T(8,128)(2,1)} %bitcast.599, bf16[1,2,2,256,256]{3,4,2,1,0:T(8,128)(2,1)} %get-tuple-element.29, ...), kind=kOutput, calls=%fused_computation.31 | convolution fusion | flops 2165571584 | bytes 7864320 | tf_op jit(solution)/shard_map/...djl,dclm->...cjm/dot_general | solution.py:37
  128.3 4.2 %subtract_convert_fusion = (bf16[4,2,1,256,256]{3,4,1,0,2:T(8,128)(2,1)}, bf16[4,2,1,256,256]{3,4,1,0,2:T(8,128)(2,1)}) fusion(f32[4,2,2,256,256]{3,4,1,0,2:T(8,128)} %convolution_bitcast_fusion, f32[2,256,256]{1,2,0:T(8,128)S(1)} %get-tuple-element.46, f32[2,256,256]{1,2,0:T(8,128)S(1)} %get-tuple-element.45), kind=kLoop, calls=%fused_computation.72 | loop fusion | flops 4194304 | bytes 7340032 | tf_op jit(solution)/shard_map/convert.8
  132.5 4.1 %fusion.49 = bf16[4,2,2,256,256]{3,4,1,0,2:T(8,128)(2,1)S(1)} fusion(bf16[1,2,256,256]{3,2,1,0:T(8,128)(2,1)} %get-tuple-element.40, bf16[1,2,256,256]{3,2,1,0:T(8,128)(2,1)} %get-tuple-element.43, bf16[4,2,1,256,256]{3,4,1,0,2:T(8,128)(2,1)} %get-tuple-element.13, bf16[4,2,1,256,256]{3,4,1,0,2:T(8,128)(2,1)} %get-tuple-element.12, ...), kind=kOutput, calls=%fused_computation.79 | convolution fusion | flops 2151940096 | bytes 5242880 | tf_op jit(solution)/shard_map/...djl,dclm->...cjm/dot_general | solution.py:47
  136.6 4.9 %fusion.99 = f32[2,256,256]{1,2,0:T(8,128)S(1)} fusion(f32[2,256,256]{1,2,0:T(8,128)S(1)} %bitcast.592, f32[2]{0:T(128)S(1)} %get-tuple-element.48, bf16[4,2,2,256,256]{3,4,1,0,2:T(8,128)(2,1)S(1)} %fusion.49), kind=kLoop, calls=%fused_computation.148 | loop fusion | flops 5373952 | bytes 3145736 | tf_op jit(solution)/shard_map/reduce_sum | solution.py:119
  141.6 6.0 %fusion.128 = (bf16[2,2,1,256,256]{3,4,2,1,0:T(8,128)(2,1)}, bf16[2,2,1,256,256]{3,4,2,1,0:T(8,128)(2,1)}) fusion(f32[2,256,256]{1,2,0:T(8,128)S(1)} %copy.120, f32[2,256,256]{1,2,0:T(8,128)S(1)} %bitcast.593, f32[2]{0:T(128)S(1)} %get-tuple-element.48, f32[2,256,256]{1,2,0:T(8,128)S(1)} %copy-done.3, bf16[4,2,2,256,256]{3,4,1,0,2:T(8,128)(2,1)S(1)} %fusion.49), kind=kLoop, calls=%fused_computation.177 | loop fusion | flops 6553600 | bytes 4718600 | tf_op jit(solution)/shard_map/convert.6
  150.2 2.3 %pad_maximum_fusion = bf16[2,2,2,256,256]{3,4,2,1,0:T(8,128)(2,1)} fusion(bf16[2,2,1,256,256]{3,4,2,1,0:T(8,128)(2,1)} %get-tuple-element.21, bf16[2,2,1,256,256]{3,4,2,1,0:T(8,128)(2,1)} %get-tuple-element.20), kind=kLoop, calls=%fused_computation.189 | loop fusion | flops 524288 | bytes 2097152 | tf_op jit(solution)/shard_map/stack | solution.py:113
  152.4 2.3 %copy.179 = bf16[2,2,2,256,256]{4,3,2,1,0:T(8,128)(2,1)} copy(bf16[2,2,2,256,256]{3,4,2,1,0:T(8,128)(2,1)} %pad_maximum_fusion) | data formatting | bytes 2097152
  154.7 5.9 %fusion.117 = (bf16[2,2,1,256,256]{3,4,2,1,0:T(8,128)(2,1)S(1)}, bf16[2,2,1,256,256]{3,4,2,1,0:T(8,128)(2,1)S(1)}) fusion(f32[2,256,256]{1,2,0:T(8,128)} %copy-done.1, f32[2,256,256]{1,2,0:T(8,128)S(1)} %copy.120, f32[2,256,256]{1,2,0:T(8,128)S(1)} %bitcast.594, f32[2]{0:T(128)S(1)} %get-tuple-element.48, bf16[4,2,2,256,256]{3,4,1,0,2:T(8,128)(2,1)S(1)} %fusion.49), kind=kLoop, calls=%fused_computation.166 | loop fusion | flops 6553600 | bytes 4718600 | tf_op jit(solution)/shard_map/convert.4
  162.0 2.6 %reduce-scatter.4.cloned.1.call-done = bf16[128,512]{1,0:T(8,128)(2,1)} async-done(((bf16[256,512]{1,0:T(8,128)(2,1)}), bf16[128,512]{1,0:T(8,128)(2,1)}) %reduce-scatter.4.cloned.1.call-update) | async-done | bytes 131088
  (78 shorter events, 24.6 us)
Async XLA Ops:
  7.2 11.5 %copy-start = (f32[16]{0:T(128)S(1)}, f32[16]{0:T(128)}, u32[]{:S(2)}) copy-start(f32[16]{0:T(128)} %param.12) | copy-start | bytes 196
  7.2 4.5 %copy-start.16 = (bf16[2,2,2,256,256]{4,3,2,1,0:T(8,128)(2,1)S(1)}, bf16[2,2,2,256,256]{4,3,2,1,0:T(8,128)(2,1)}, u32[]{:S(2)}) copy-start(bf16[2,2,2,256,256]{4,3,2,1,0:T(8,128)(2,1)} %param.8) | copy-start | bytes 3145732
  7.2 157.4 %reduce-scatter.4.cloned.1.call-start = ((), (), s32[]{:S(2)}) async-start(), calls=%async_computation.1 | async-start | bytes 393216
  8.6 8.6 %copy-start.19 = (s32[2]{0:T(128)S(1)}, s32[2]{0:T(128)}, u32[]{:S(2)}) copy-start(s32[2]{0:T(128)} %param.13) | copy-start | bytes 28
  8.6 8.6 %copy-start.13 = (f32[2,256,256]{2,1,0:T(8,128)S(1)}, f32[2,256,256]{2,1,0:T(8,128)}, u32[]{:S(2)}) copy-start(f32[2,256,256]{2,1,0:T(8,128)} %param.10) | copy-start | bytes 1572868
  9.6 7.7 %copy-start.17 = (s32[2,256,256]{2,1,0:T(8,128)S(1)}, s32[2,256,256]{2,1,0:T(8,128)}, u32[]{:S(2)}) copy-start(s32[2,256,256]{2,1,0:T(8,128)} %param.11) | copy-start | bytes 1572868
  9.6 24.3 %collective-permute-start = (bf16[2,2,256,256]{2,3,1,0:T(8,128)(2,1)}, bf16[2,2,256,256]{2,3,1,0:T(8,128)(2,1)}, u32[]{:S(2)}, u32[]{:S(2)}) collective-permute-start(bf16[2,2,256,256]{2,3,1,0:T(8,128)(2,1)} %bitcast.597), channel_id=1, source_target_pairs={{0,2},{2,4},{4,6},{6,8},{8,10},{10,12},{12,14},{14,16},{16,18},{18... | collective-permute-start | bytes 1572872 | tf_op jit(solution)/shard_map/ppermute | solution.py:16
  13.6 22.3 %collective-permute-start.1 = (bf16[2,2,256,256]{2,3,1,0:T(8,128)(2,1)}, bf16[2,2,256,256]{2,3,1,0:T(8,128)(2,1)}, u32[]{:S(2)}, u32[]{:S(2)}) collective-permute-start(bf16[2,2,256,256]{2,3,1,0:T(8,128)(2,1)} %bitcast.18), channel_id=1, source_target_pairs={{2,0},{4,2},{6,4},{8,6},{10,8},{12,10},{14,12},{16,14},{18,16},{20... | collective-permute-start | bytes 1572872 | tf_op jit(solution)/shard_map/ppermute | solution.py:16
  23.3 3.3 %copy-start.14 = (bf16[2,2,256,256]{3,2,1,0:T(8,128)(2,1)S(1)}, bf16[2,2,256,256]{3,2,1,0:T(8,128)(2,1)}, u32[]{:S(2)}) copy-start(bf16[2,2,256,256]{3,2,1,0:T(8,128)(2,1)} %param.9) | copy-start | bytes 1572868
  26.6 2.0 %copy-start.15 = (bf16[1,2,2,256,256]{4,3,2,1,0:T(8,128)(2,1)S(1)}, bf16[1,2,2,256,256]{4,3,2,1,0:T(8,128)(2,1)}, u32[]{:S(2)}) copy-start(bf16[1,2,2,256,256]{4,3,2,1,0:T(8,128)(2,1)} %get-tuple-element.35) | copy-start | bytes 1572868
  29.8 77.3 %copy-start.1 = (f32[2,256,256]{1,2,0:T(8,128)}, f32[2,256,256]{1,2,0:T(8,128)S(1)}, u32[]{:S(2)}) copy-start(f32[2,256,256]{1,2,0:T(8,128)S(1)} %copy.134) | copy-start | bytes 1572868
  30.0 64.1 %copy-start.2 = (f32[2,256,256]{1,2,0:T(8,128)}, f32[2,256,256]{1,2,0:T(8,128)S(1)}, u32[]{:S(2)}) copy-start(f32[2,256,256]{1,2,0:T(8,128)S(1)} %copy.105) | copy-start | bytes 1572868
  51.6 10.3 %copy-start.5 = (bf16[4,2,2,256,256]{3,4,1,2,0:T(8,128)(2,1)S(1)}, bf16[4,2,2,256,256]{3,4,1,2,0:T(8,128)(2,1)}, u32[]{:S(2)}) copy-start(bf16[4,2,2,256,256]{3,4,1,2,0:T(8,128)(2,1)} %fusion.43) | copy-start | bytes 6291460
  59.1 7.4 %copy-start.11 = (bf16[2,2,1,256,256]{3,4,1,2,0:T(8,128)(2,1)}, bf16[2,2,1,256,256]{3,4,1,2,0:T(8,128)(2,1)S(1)}, u32[]{:S(2)}) copy-start(bf16[2,2,1,256,256]{3,4,1,2,0:T(8,128)(2,1)S(1)} %get-tuple-element.26) | copy-start | bytes 1572868
  59.1 7.4 %copy-start.12 = (bf16[2,2,1,256,256]{3,4,1,2,0:T(8,128)(2,1)}, bf16[2,2,1,256,256]{3,4,1,2,0:T(8,128)(2,1)S(1)}, u32[]{:S(2)}) copy-start(bf16[2,2,1,256,256]{3,4,1,2,0:T(8,128)(2,1)S(1)} %get-tuple-element.27) | copy-start | bytes 1572868
  60.0 13.4 %collective-permute-start.2 = (bf16[2,2,256,256]{2,3,0,1:T(8,128)(2,1)}, bf16[2,2,256,256]{2,3,0,1:T(8,128)(2,1)}, u32[]{:S(2)}, u32[]{:S(2)}) collective-permute-start(bf16[2,2,256,256]{2,3,0,1:T(8,128)(2,1)} %fusion.170), channel_id=1, source_target_pairs={{0,2},{2,4},{4,6},{6,8},{8,10},{10,12},{12,14},{14,16},{16,18},{18... | collective-permute-start | bytes 1572872 | tf_op jit(solution)/shard_map/ppermute | solution.py:16
  67.6 10.6 %collective-permute-start.3 = (bf16[2,2,256,256]{2,3,0,1:T(8,128)(2,1)}, bf16[2,2,256,256]{2,3,0,1:T(8,128)(2,1)}, u32[]{:S(2)}, u32[]{:S(2)}) collective-permute-start(bf16[2,2,256,256]{2,3,0,1:T(8,128)(2,1)} %get-tuple-element.32), channel_id=1, source_target_pairs={{2,0},{4,2},{6,4},{8,6},{10,8},{12,10},{14,12},{16,14},{18,16},{20... | collective-permute-start | bytes 1572872 | tf_op jit(solution)/shard_map/ppermute | solution.py:16
  94.1 13.0 %copy-start.4 = (bf16[4,2,2,256,256]{3,4,1,0,2:T(8,128)(2,1)S(1)}, bf16[4,2,2,256,256]{3,4,1,0,2:T(8,128)(2,1)}, u32[]{:S(2)}) copy-start(bf16[4,2,2,256,256]{3,4,1,0,2:T(8,128)(2,1)} %fusion.46) | copy-start | bytes 6291460
  101.5 10.5 %copy-start.7 = (bf16[2,2,1,256,256]{3,4,2,1,0:T(8,128)(2,1)}, bf16[2,2,1,256,256]{3,4,2,1,0:T(8,128)(2,1)S(1)}, u32[]{:S(2)}) copy-start(bf16[2,2,1,256,256]{3,4,2,1,0:T(8,128)(2,1)S(1)} %get-tuple-element.24) | copy-start | bytes 1572868
  101.5 10.5 %copy-start.9 = (bf16[2,2,1,256,256]{3,4,2,1,0:T(8,128)(2,1)}, bf16[2,2,1,256,256]{3,4,2,1,0:T(8,128)(2,1)S(1)}, u32[]{:S(2)}) copy-start(bf16[2,2,1,256,256]{3,4,2,1,0:T(8,128)(2,1)S(1)} %get-tuple-element.25) | copy-start | bytes 1572868
  101.6 13.6 %collective-permute-start.4 = (bf16[2,2,256,256]{2,3,1,0:T(8,128)(2,1)S(1)}, bf16[2,2,256,256]{2,3,1,0:T(8,128)(2,1)S(1)}, u32[]{:S(2)}, u32[]{:S(2)}) collective-permute-start(bf16[2,2,256,256]{2,3,1,0:T(8,128)(2,1)S(1)} %fusion.166), channel_id=1, source_target_pairs={{0,2},{2,4},{4,6},{6,8},{8,10},{10,12},{12,14},{14,16},{16,18},{18... | collective-permute-start | bytes 1572872 | tf_op jit(solution)/shard_map/ppermute | solution.py:16
  112.0 3.1 %copy-start.6 = (bf16[2,2,256,256]{2,3,1,0:T(8,128)(2,1)S(1)}, bf16[2,2,256,256]{2,3,1,0:T(8,128)(2,1)}, u32[]{:S(2)}) copy-start(bf16[2,2,256,256]{2,3,1,0:T(8,128)(2,1)} %copy.155) | copy-start | bytes 1572868
  112.1 10.3 %copy-start.8 = (bf16[2,2,1,256,256]{3,4,2,1,0:T(8,128)(2,1)S(1)}, bf16[2,2,1,256,256]{3,4,2,1,0:T(8,128)(2,1)}, u32[]{:S(2)}) copy-start(bf16[2,2,1,256,256]{3,4,2,1,0:T(8,128)(2,1)} %copy-done.7) | copy-start | bytes 1572868
  112.1 10.3 %copy-start.10 = (bf16[2,2,1,256,256]{3,4,2,1,0:T(8,128)(2,1)S(1)}, bf16[2,2,1,256,256]{3,4,2,1,0:T(8,128)(2,1)}, u32[]{:S(2)}) copy-start(bf16[2,2,1,256,256]{3,4,2,1,0:T(8,128)(2,1)} %copy-done.9) | copy-start | bytes 1572868
  113.0 8.6 %collective-permute-start.5 = (bf16[2,2,256,256]{2,3,1,0:T(8,128)(2,1)S(1)}, bf16[2,2,256,256]{2,3,1,0:T(8,128)(2,1)S(1)}, u32[]{:S(2)}, u32[]{:S(2)}) collective-permute-start(bf16[2,2,256,256]{2,3,1,0:T(8,128)(2,1)S(1)} %get-tuple-element.30), channel_id=1, source_target_pairs={{2,0},{4,2},{6,4},{8,6},{10,8},{12,10},{14,12},{16,14},{18,16},{20... | collective-permute-start | bytes 1572872 | tf_op jit(solution)/shard_map/ppermute | solution.py:16
  121.6 0.8 copy-start.18
  136.6 4.9 %copy-start.3 = (f32[2,256,256]{1,2,0:T(8,128)S(1)}, f32[2,256,256]{1,2,0:T(8,128)}, u32[]{:S(2)}) copy-start(f32[2,256,256]{1,2,0:T(8,128)} %copy-done.2) | copy-start | bytes 1572868
Sparse Core Ops, SparseCore 0:
  150.3 14.3 reduce-scatter.3
where the time goes:
time: 176 us; the launch traced here: 173 us
  other arithmetic  70.3 us (40%)
  matrix products  38 us (22%)
  local copies, waits for them, and re-layouts  20.4 us (12%)
  starting transfers between devices  19.1 us (11%)
  between operations  14.5 us (8%)
  waiting for transfers between devices  11 us (6%)
    another operation x9, other arithmetic  48.7 us
    ppermute x6, starting transfers between devices, passed_along(): return lax.ppermute(block, axis, route)  19.1 us
    dot_general x3, matrix products, propagate(): jnp.einsum('...djl,dclm->...cjm', first, fwd_right, preferred_element_typ...  18.3 us
    unnamed x54, local copies, waits for them, and re-layouts  16.2 us
    dot_general x3, matrix products, propagate(): jnp.einsum('...djl,dclm->...cjm', third, inv_right, preferred_element_typ...  15.1 us
    ppermute x6, waiting for transfers between devices, passed_along(): return lax.ppermute(block, axis, route)  8.39 us
    reduce_sum x1, other arithmetic, per_device(): terms = scale * jnp.sum(a_re * b_re + a_im * b_im, axis=1)  4.91 us
    broadcast_in_dim x3, other arithmetic, per_device(): got_down[None]  4.65 us
  transfers between devices with their start and end apart: 7, of which 3 were waited for; matrix products, arithmetic and copies ran while one was open for 28% of the time, Pallas kernels for 0%

commit v1 on v0

--- a/solution.py
+++ b/solution.py
@@ -1,13 +1,23 @@
+import functools
 import math
 
 import jax
 import jax.numpy as jnp
+import numpy as np
 from jax import lax
+from jax.experimental import pallas as pl
+from jax.experimental.pallas import tpu as pltpu
 from jax.sharding import PartitionSpec as P
 
 HOPS = 3
 NCLASS = 16
 NFREQ = 128
+F32 = jnp.float32
+BF16 = jnp.bfloat16
+VMEM = pl.BlockSpec(memory_space=pltpu.VMEM)
+HBM = pl.BlockSpec(memory_space=pltpu.HBM)
+SMEM = pl.BlockSpec(memory_space=pltpu.SMEM)
+PARAMS = pltpu.CompilerParams(vmem_limit_bytes=28 * 2**20)
 
 
 def passed_along(block, axis, distance):
@@ -55,7 +65,7 @@
     return (got_down, got_up)
 
 
-def per_device(down_state, up_state, source, reflect, screen_class, screen_values, freq_index):
+def per_device_plain(down_state, up_state, source, reflect, screen_class, screen_values, freq_index):
     levels = down_state.shape[0]
     rows_x = down_state.shape[3]
     rows_y = down_state.shape[4]
@@ -123,6 +133,487 @@
     return (down, up, gradient)
 
 
+def hartley(length):
+    counter = np.arange(length)
+    angles = 2.0 * np.pi / length * (counter[:, None] * counter[None, :] % length)
+    cosine = np.cos(angles).astype(BF16).astype(np.float32)
+    sine = np.sin(angles).astype(BF16).astype(np.float32)
+    return (cosine + sine).astype(BF16)
+
+
+def odd_place():
+    return lax.rem(lax.axis_index("depth"), 2)
+
+
+def mm(left, right):
+    return jnp.dot(left, right, preferred_element_type=F32)
+
+
+def spread(real_part, imag_part, hx, hy, phase, front):
+    rows = real_part.shape[0]
+    first = mm(jnp.concatenate([real_part, imag_part], axis=0), hy).astype(BF16)
+    second_re = mm(hx, first[:rows])
+    second_im = mm(hx, first[rows:])
+    turn_re = phase[front, 0]
+    turn_im = phase[front, 1]
+    turned_re = (second_re * turn_re - second_im * turn_im).astype(BF16)
+    turned_im = (second_re * turn_im + second_im * turn_re).astype(BF16)
+    third_re = mm(hx, turned_re).astype(BF16)
+    third_im = mm(hx, turned_im).astype(BF16)
+    last = mm(jnp.concatenate([third_re, third_im], axis=0), hy).astype(BF16)
+    return last[:rows], last[rows:]
+
+
+def screened(real_part, imag_part, screen_re, screen_im):
+    return (
+        screen_re * real_part - screen_im * imag_part,
+        screen_re * imag_part + screen_im * real_part,
+    )
+
+
+def mixed(a_re, a_im, b_re, b_im, refl, screen_re, screen_im):
+    a_re, a_im, b_re, b_im = (part.astype(F32) for part in (a_re, a_im, b_re, b_im))
+    step_re = refl * (a_re - b_re)
+    step_im = refl * (a_im - b_im)
+    inward = screened(a_re + step_re, a_im + step_im, screen_re, screen_im)
+    outward = screened(b_re + step_re, b_im + step_im, screen_re, screen_im)
+    return tuple(part.astype(BF16) for part in inward + outward)
+
+
+def edges_kernel(down, up, outward_outer, inward_inner, sems):
+    levels = down.shape[0]
+
+    def fetch(first, second):
+        copies = [
+            pltpu.make_async_copy(first, outward_outer, sems.at[0]),
+            pltpu.make_async_copy(second, inward_inner, sems.at[1]),
+        ]
+        for copy in copies:
+            copy.start()
+        for copy in copies:
+            copy.wait()
+
+    odd = odd_place()
+
+    @pl.when(odd == 0)
+    def _():
+        fetch(up.at[0], down.at[levels - 1])
+
+    @pl.when(odd == 1)
+    def _():
+        fetch(down.at[levels - 1], up.at[0])
+
+
+def class_rows(slowness, kwave, shape):
+    lanes = lax.broadcasted_iota(jnp.int32, shape, 1)
+    table = jnp.zeros(shape, F32)
+    for entry in range(NCLASS):
+        table = jnp.where(lanes == entry, slowness[entry], table)
+    angle = kwave * table
+    return jnp.cos(angle), jnp.sin(angle)
+
+
+def look_up(table, classes):
+    width = 128
+    rows = classes.shape[0]
+    wide = jnp.broadcast_to(table[:1], (rows, width))
+    pieces = [
+        jnp.take_along_axis(wide, classes[:, start : start + width], axis=1, mode="promise_in_bounds")
+        for start in range(0, classes.shape[1], width)
+    ]
+    return jnp.concatenate(pieces, axis=1)
+
+
+def front_wave(freq, front):
+    return 0.95 * math.pi * (freq[front].astype(F32) + 1.0) / NFREQ
+
+
+def setup_kernel(
+    down, up, reflect, classes_in, slowness, freq, outward_outer, hx, hy,
+    q_out_inner, q_in_outer, q_out_outer, screen, phase, refl, message,
+    fields, klass, sems,
+):
+    fronts = q_out_inner.shape[0]
+    rows_x, rows_y = refl.shape[1:]
+    odd = odd_place()
+    fixed = [
+        pltpu.make_async_copy(reflect.at[odd], refl.at[0], sems.at[2]),
+        pltpu.make_async_copy(reflect.at[1 - odd], refl.at[1], sems.at[3]),
+        pltpu.make_async_copy(classes_in.at[odd], klass.at[0], sems.at[4]),
+        pltpu.make_async_copy(classes_in.at[1 - odd], klass.at[1], sems.at[5]),
+    ]
+    for copy in fixed:
+        copy.start()
+
+    @pl.when(odd == 0)
+    def _():
+        pltpu.make_async_copy(down.at[0], fields.at[0], sems.at[0]).start()
+        pltpu.make_async_copy(up.at[1], fields.at[1], sems.at[1]).start()
+
+    @pl.when(odd == 1)
+    def _():
+        pltpu.make_async_copy(up.at[1], fields.at[0], sems.at[0]).start()
+        pltpu.make_async_copy(down.at[0], fields.at[1], sems.at[1]).start()
+
+    def squares(length, axis):
+        counter = lax.broadcasted_iota(jnp.int32, (rows_x, rows_y), axis)
+        wrapped = jnp.where(counter >= length // 2, counter - length, counter)
+        wave = 2.0 * math.pi / length * wrapped.astype(F32)
+        return wave * wave
+
+    lateral = squares(rows_x, 0) + squares(rows_y, 1)
+    for front in range(fronts):
+        kwave = front_wave(freq, front)
+        vertical = kwave * kwave - lateral
+        propag = jnp.sqrt(jnp.maximum(vertical, 0.0))
+        damping = jnp.exp(-jnp.sqrt(jnp.maximum(-vertical, 0.0))) / (rows_x * rows_y)
+        phase[front, 0] = damping * jnp.cos(propag)
+        phase[front, 1] = damping * jnp.sin(propag)
+    for copy in fixed:
+        copy.wait()
+    sign = jnp.where(odd == 0, 1.0, -1.0).astype(F32)
+    for level in range(2):
+        refl[level] = sign * refl[level]
+    for front in range(fronts):
+        cos_row, sin_row = class_rows(slowness, front_wave(freq, front), (8, 128))
+        for level in range(2):
+            screen[level, front, 0] = look_up(cos_row, klass[level])
+            screen[level, front, 1] = look_up(sin_row, klass[level])
+    message[fronts, 0] = refl[0].astype(BF16)
+    message[fronts, 1] = klass[0].astype(BF16)
+    pltpu.make_async_copy(down.at[0], fields.at[0], sems.at[0]).wait()
+    pltpu.make_async_copy(down.at[0], fields.at[1], sems.at[1]).wait()
+    hx = hx[...]
+    hy = hy[...]
+    for front in range(fronts):
+        q_re, q_im = spread(fields[1, front, 0], fields[1, front, 1], hx, hy, phase, front)
+        q_out_inner[front, 0] = q_re
+        q_out_inner[front, 1] = q_im
+        b_re, b_im = screened(q_re.astype(F32), q_im.astype(F32), screen[0, front, 0], screen[0, front, 1])
+        kept = 1.0 - refl[0]
+        message[front, 0] = (kept * b_re).astype(BF16)
+        message[front, 1] = (kept * b_im).astype(BF16)
+        q_re, q_im = spread(outward_outer[front, 0], outward_outer[front, 1], hx, hy, phase, front)
+        q_out_outer[front, 0] = q_re
+        q_out_outer[front, 1] = q_im
+        q_re, q_im = spread(fields[0, front, 0], fields[0, front, 1], hx, hy, phase, front)
+        q_in_outer[front, 0] = q_re
+        q_in_outer[front, 1] = q_im
+
+
+def ahead_kernel(
+    partner, q_in_outer, screen, refl, phase, hx, hy,
+    inward_inner, q_out_inner, last_far, last_near,
+):
+    fronts = partner.shape[0]
+    half = partner.shape[2] // 2
+    far_first = lax.axis_index("shot") % 2
+    hx = hx[...]
+    hy = hy[...]
+    for front in range(fronts):
+        q_re, q_im = spread(partner[front, 0], partner[front, 1], hx, hy, phase, front)
+        in_re, in_im, out_re, out_im = mixed(
+            q_in_outer[front, 0], q_in_outer[front, 1], q_re, q_im,
+            refl[1], screen[1, front, 0], screen[1, front, 1],
+        )
+        inward_inner[front, 0] = in_re
+        inward_inner[front, 1] = in_im
+        q_re, q_im = spread(out_re, out_im, hx, hy, phase, front)
+        q_out_inner[front, 0] = q_re
+        q_out_inner[front, 1] = q_im
+        b_re, b_im = screened(q_re.astype(F32), q_im.astype(F32), screen[0, front, 0], screen[0, front, 1])
+        kept = 1.0 - refl[0]
+        parts = spread((kept * b_re).astype(BF16), (kept * b_im).astype(BF16), hx, hy, phase, front)
+        for index, part in enumerate(parts):
+            top, bottom = part[:half], part[half:]
+            flip = far_first == 0
+            last_far[front, index] = jnp.where(flip, bottom, top)
+            last_near[front, index] = jnp.where(flip, top, bottom)
+
+
+def edge_kernel(
+    arrived, source, partner, q_out_inner, screen, refl, phase, hx, hy,
+    inward_inner, q_arrived, q_out_outer, q_out_inner_next,
+):
+    fronts = partner.shape[0]
+    first = lax.axis_index("depth") == 0
+    hx = hx[...]
+    hy = hy[...]
+    for front in range(fronts):
+        entering = [jnp.where(first, source[front, part], arrived[front, part]) for part in range(2)]
+        q_re, q_im = spread(entering[0], entering[1], hx, hy, phase, front)
+        q_arrived[front, 0] = q_re
+        q_arrived[front, 1] = q_im
+        in_re, in_im, out_re, out_im = mixed(
+            q_re, q_im, q_out_inner[front, 0], q_out_inner[front, 1],
+            refl[0], screen[0, front, 0], screen[0, front, 1],
+        )
+        a_re, a_im = spread(in_re, in_im, hx, hy, phase, front)
+        b_re, b_im = spread(partner[front, 0], partner[front, 1], hx, hy, phase, front)
+        q_re, q_im = spread(out_re, out_im, hx, hy, phase, front)
+        q_out_outer[front, 0] = q_re
+        q_out_outer[front, 1] = q_im
+        in_re, in_im, out_re, out_im = mixed(
+            a_re, a_im, b_re, b_im, refl[1], screen[1, front, 0], screen[1, front, 1]
+        )
+        inward_inner[front, 0] = in_re
+        inward_inner[front, 1] = in_im
+        q_re, q_im = spread(out_re, out_im, hx, hy, phase, front)
+        q_out_inner_next[front, 0] = q_re
+        q_out_inner_next[front, 1] = q_im
+
+
+def beyond_kernel(
+    message, source, q_out_outer_0, q_out_outer_1, q_out_inner, slowness, freq, screen, refl, phase, hx, hy,
+    q_in_outer, rest,
+):
+    fronts = source.shape[0]
+    first = lax.axis_index("depth") == 0
+    hx = hx[...]
+    hy = hy[...]
+    refl_beyond = message[fronts, 0].astype(F32)
+    klass = message[fronts, 1].astype(F32).astype(jnp.int32)
+    for front in range(fronts):
+        cos_row, sin_row = class_rows(slowness, front_wave(freq, front), (8, 128))
+        back_re = refl_beyond * look_up(cos_row, klass)
+        back_im = refl_beyond * look_up(sin_row, klass)
+        part_re, part_im = screened(
+            q_out_outer_0[front, 0].astype(F32), q_out_outer_0[front, 1].astype(F32), back_re, back_im
+        )
+        entering = [
+            jnp.where(first, source[front, index], (message[front, index].astype(F32) + part).astype(BF16))
+            for index, part in enumerate((part_re, part_im))
+        ]
+        q_re, q_im = spread(entering[0], entering[1], hx, hy, phase, front)
+        in_re, in_im, _, _ = mixed(
+            q_re, q_im, q_out_inner[front, 0], q_out_inner[front, 1],
+            refl[0], screen[0, front, 0], screen[0, front, 1],
+        )
+        q_re, q_im = spread(in_re, in_im, hx, hy, phase, front)
+        q_in_outer[front, 0] = q_re
+        q_in_outer[front, 1] = q_im
+        part_re, part_im = screened(
+            q_out_outer_1[front, 0].astype(F32), q_out_outer_1[front, 1].astype(F32), back_re, back_im
+        )
+        q_re, q_im = spread(part_re.astype(BF16), part_im.astype(BF16), hx, hy, phase, front)
+        rest[front, 0] = q_re
+        rest[front, 1] = q_im
+
+
+def inner_kernel(
+    partner, q_in_outer, screen, refl, phase, hx, hy,
+    down_out, up_out, terms,
+    inward, outward, sems,
+):
+    fronts = partner.shape[0]
+    odd = odd_place()
+    hx = hx[...]
+    hy = hy[...]
+    total = None
+    for front in range(fronts):
+        q_re, q_im = spread(partner[front, 0], partner[front, 1], hx, hy, phase, front)
+        a_re, a_im = q_in_outer[front, 0], q_in_outer[front, 1]
+        in_re, in_im, out_re, out_im = mixed(
+            a_re, a_im, q_re, q_im, refl[1], screen[1, front, 0], screen[1, front, 1]
+        )
+        inward[front, 0] = in_re
+        inward[front, 1] = in_im
+        outward[front, 0] = out_re
+        outward[front, 1] = out_im
+        term = a_re.astype(F32) * q_re.astype(F32) + a_im.astype(F32) * q_im.astype(F32)
+        total = term if total is None else total + term
+
+    @pl.when(odd == 0)
+    def _():
+        pltpu.make_async_copy(inward, down_out.at[1], sems.at[0]).start()
+        pltpu.make_async_copy(outward, up_out.at[1], sems.at[1]).start()
+
+    @pl.when(odd == 1)
+    def _():
+        pltpu.make_async_copy(inward, up_out.at[0], sems.at[0]).start()
+        pltpu.make_async_copy(outward, down_out.at[0], sems.at[1]).start()
+
+    terms[...] = total
+    pltpu.make_async_copy(inward, down_out.at[0], sems.at[0]).wait()
+    pltpu.make_async_copy(outward, up_out.at[0], sems.at[1]).wait()
+
+
+def outer_rows(
+    near, last, q_arrived, rest, q_out_inner, screen, refl, down_in, up_in, down_out, up_out, inward, outward, sems
+):
+    del down_in, up_in
+    fronts, _, half, _ = last.shape
+    first = lax.axis_index("depth") == 0
+    odd = odd_place()
+    shot = lax.axis_index("shot") % 2
+    start = pl.multiple_of((shot if near else 1 - shot) * half, half)
+    rows = pl.ds(start, half)
+    total = None
+    kept = refl[0, rows, :]
+    for front in range(fronts):
+        a_re, a_im = (
+            jnp.where(
+                first,
+                q_arrived[front, part, rows, :].astype(F32),
+                last[front, part].astype(F32) + rest[front, part, rows, :].astype(F32),
+            )
+            for part in range(2)
+        )
+        b_re, b_im = (q_out_inner[front, part, rows, :].astype(F32) for part in range(2))
+        in_re, in_im, out_re, out_im = mixed(
+            a_re, a_im, b_re, b_im, kept, screen[0, front, 0, rows, :], screen[0, front, 1, rows, :]
+        )
+        inward[front, 0] = in_re
+        inward[front, 1] = in_im
+        outward[front, 0] = out_re
+        outward[front, 1] = out_im
+        term = a_re * b_re + a_im * b_im
+        total = term if total is None else total + term
+
+    def copies(level, inward_out, outward_out):
+        return [
+            pltpu.make_async_copy(inward, inward_out.at[level, :, :, rows, :], sems.at[0]),
+            pltpu.make_async_copy(outward, outward_out.at[level, :, :, rows, :], sems.at[1]),
+        ]
+
+    @pl.when(odd == 0)
+    def _():
+        for copy in copies(0, down_out, up_out):
+            copy.start()
+
+    @pl.when(odd == 1)
+    def _():
+        for copy in copies(1, up_out, down_out):
+            copy.start()
+
+    def finish():
+        for copy in copies(0, down_out, up_out):
+            copy.wait()
+
+    return rows, total, finish
+
+
+def far_rows_kernel(
+    last, q_arrived, rest, q_out_inner, screen, refl, inner_terms, down_in, up_in,
+    down_out, up_out, terms,
+    inward, outward, sems,
+):
+    rows, total, finish = outer_rows(
+        False, last, q_arrived, rest, q_out_inner, screen, refl, down_in, up_in, down_out, up_out, inward, outward, sems
+    )
+    terms[0] = total.astype(BF16)
+    terms[1] = inner_terms[rows, :].astype(BF16)
+    finish()
+
+
+def near_rows_kernel(
+    scale, last, q_arrived, rest, q_out_inner, screen, refl, inner_terms, other, down_in, up_in,
+    down_out, up_out, gradient,
+    inward, outward, sems,
+):
+    rows, total, finish = outer_rows(
+        True, last, q_arrived, rest, q_out_inner, screen, refl, down_in, up_in, down_out, up_out, inward, outward, sems
+    )
+    odd = odd_place()
+    gradient[odd] = scale * (total + other[0].astype(F32))
+    gradient[1 - odd] = scale * (inner_terms[rows, :] + other[1].astype(F32))
+    finish()
+
+
+def per_device(down_state, up_state, source, reflect, screen_class, screen_values, freq_index):
+    depth = lax.axis_size("depth")
+    shots = lax.axis_size("shot")
+    levels, fronts, parts, rows_x, rows_y = down_state.shape
+    if levels != 2 or depth % 2 or shots != 2 or HOPS != 3:
+        return per_device_plain(down_state, up_state, source, reflect, screen_class, screen_values, freq_index)
+    scale = 1.0 / math.sqrt(fronts * shots)
+    half = rows_x // 2
+    hx = jnp.asarray(hartley(rows_x))
+    hy = jnp.asarray(hartley(rows_y))
+    partners = [(i, i ^ 1) for i in range(depth)]
+    beyond = [(i, i + 1) for i in range(1, depth - 1, 2)] + [(i + 1, i) for i in range(1, depth - 1, 2)]
+    to_partner = functools.partial(lax.ppermute, axis_name="depth", perm=partners)
+    to_beyond = functools.partial(lax.ppermute, axis_name="depth", perm=beyond)
+    across = functools.partial(lax.ppermute, axis_name="shot", perm=[(0, 1), (1, 0)])
+    plane = jax.ShapeDtypeStruct((fronts, parts, rows_x, rows_y), BF16)
+    half_plane = jax.ShapeDtypeStruct((fronts, parts, half, rows_y), BF16)
+    pair = jax.ShapeDtypeStruct((2, rows_x, rows_y), F32)
+    turns = jax.ShapeDtypeStruct((fronts, parts, rows_x, rows_y), F32)
+    screens = jax.ShapeDtypeStruct((2, fronts, parts, rows_x, rows_y), F32)
+    parcel = jax.ShapeDtypeStruct((fronts + 1, parts, rows_x, rows_y), BF16)
+    state = jax.ShapeDtypeStruct(down_state.shape, BF16)
+    dma = pltpu.SemaphoreType.DMA
+
+    def call(kernel, in_specs, out_specs, out_shape, scratch=(), **more):
+        return pl.pallas_call(
+            kernel,
+            in_specs=in_specs,
+            out_specs=out_specs,
+            out_shape=out_shape,
+            scratch_shapes=list(scratch),
+            compiler_params=PARAMS,
+            **more,
+        )
+
+    out_outer, in_inner = call(edges_kernel, [HBM] * 2, [VMEM] * 2, [plane] * 2, [dma((2,))])(down_state, up_state)
+    arrived = to_beyond(out_outer)
+    partner_0 = to_partner(in_inner)
+    q_out_inner_0, q_in_outer_0, q_out_outer_0, screen, phase, refl, message = call(
+        setup_kernel,
+        [HBM] * 4 + [SMEM] * 2 + [VMEM] * 3,
+        [VMEM] * 7,
+        [plane] * 3 + [screens, turns, pair, parcel],
+        [
+            pltpu.VMEM((2, fronts, parts, rows_x, rows_y), BF16),
+            pltpu.VMEM((2, rows_x, rows_y), jnp.int32),
+            dma((6,)),
+        ],
+    )(down_state, up_state, reflect, screen_class, screen_values, freq_index, out_outer, hx, hy)
+    message = to_beyond(message)
+    in_inner_1, q_out_inner_1, last_far, last_near = call(
+        ahead_kernel, [VMEM] * 7, [VMEM] * 4, [plane] * 2 + [half_plane] * 2
+    )(partner_0, q_in_outer_0, screen, refl, phase, hx, hy)
+    partner_1 = to_partner(in_inner_1)
+    last_far = to_beyond(last_far)
+    last_near = to_beyond(last_near)
+    in_inner_2, q_arrived, q_out_outer_1, q_out_inner_2 = call(edge_kernel, [VMEM] * 9, [VMEM] * 4, [plane] * 4)(
+        arrived, source, partner_1, q_out_inner_0, screen, refl, phase, hx, hy
+    )
+    partner_2 = to_partner(in_inner_2)
+    q_in_outer_2, rest = call(
+        beyond_kernel, [VMEM] * 5 + [SMEM] * 2 + [VMEM] * 5, [VMEM] * 2, [plane] * 2
+    )(
+        message, source, q_out_outer_0, q_out_outer_1, q_out_inner_1, screen_values, freq_index,
+        screen, refl, phase, hx, hy,
+    )
+    down, up, inner_terms = call(
+        inner_kernel,
+        [VMEM] * 7,
+        [HBM] * 2 + [VMEM],
+        [state, state, jax.ShapeDtypeStruct((rows_x, rows_y), F32)],
+        [pltpu.VMEM(plane.shape, BF16)] * 2 + [dma((2,))],
+    )(partner_2, q_in_outer_2, screen, refl, phase, hx, hy)
+    halves = [pltpu.VMEM(half_plane.shape, BF16)] * 2 + [dma((2,))]
+    down, up, terms = call(
+        far_rows_kernel,
+        [VMEM] * 7 + [HBM] * 2,
+        [HBM] * 2 + [VMEM],
+        [state, state, jax.ShapeDtypeStruct((2, half, rows_y), BF16)],
+        halves,
+        input_output_aliases={7: 0, 8: 1},
+    )(last_far, q_arrived, rest, q_out_inner_2, screen, refl, inner_terms, down, up)
+    other = across(terms)
+    down, up, gradient = call(
+        functools.partial(near_rows_kernel, scale),
+        [VMEM] * 8 + [HBM] * 2,
+        [HBM] * 2 + [VMEM],
+        [state, state, jax.ShapeDtypeStruct((2, half, rows_y), F32)],
+        halves,
+        input_output_aliases={8: 0, 9: 1},
+    )(last_near, q_arrived, rest, q_out_inner_2, screen, refl, inner_terms, other, down, up)
+    return (down, up, gradient)
+
+
 def solution(mesh):
     return jax.shard_map(
         per_device,

time: 176 us -> 63.7 us (0.36); the launches traced: 173 us -> 63.5 us
  other arithmetic: 70.3 us -> 0 us
  matrix products: 38 us -> 0 us
  Pallas kernels: 0 us -> 30.3 us
  local copies, waits for them, and re-layouts: 20.4 us -> 2.51 us
  between operations: 14.5 us -> 1.01 us
  starting transfers between devices: 19.1 us -> 14.7 us
  waiting for transfers between devices: 11 us -> 14.9 us
    another operation x13 -> x0, other arithmetic: 52.9 us -> none
    dot_general x7 -> x0, matrix products: 38 us -> none  [the longest x3 18.3 us: propagate(): jnp.einsum('...djl,dclm->...cjm', first, fwd_right, preferred_element_typ...]
    pallas_call x0 -> x8, Pallas kernels: none -> 30.3 us  [the longest x1 8.29 us: per_device(): call(setup_kernel, [HBM] * 4 + [SMEM] * 2 + [VMEM] * 3, [VMEM] * 7, [plan...]
    unnamed x54 -> x16, local copies, waits for them, and re-layouts: 16.2 us -> 2.51 us
    ppermute x6 -> x8, waiting for transfers between devices: 8.39 us -> 14.9 us  [the longest x1 11.4 us: per_device(): message = to_beyond(message)]
    reduce_sum x1 -> x0, other arithmetic: 4.91 us -> none  [per_device(): terms = scale * jnp.sum(a_re * b_re + a_im * b_im, axis=1)]
    broadcast_in_dim x3 -> x0, other arithmetic: 4.65 us -> none  [per_device(): got_down[None]]
    ppermute x6 -> x8, starting transfers between devices: 19.1 us -> 14.7 us  [the longest x1 3.51 us: per_device(): last_near = to_beyond(last_near)]
  transfers between devices with their start and end apart: 7 -> 8, of which waited for: 3 -> 2; matrix products, arithmetic and copies ran while one was open for 28% -> 0% of each run, Pallas kernels for 0% -> 45%
where the time goes in v1:
time: 63.7 us; the launch traced here: 63.5 us
  Pallas kernels  30.3 us (48%)
  waiting for transfers between devices  14.9 us (23%)
  starting transfers between devices  14.7 us (23%)
  local copies, waits for them, and re-layouts  2.51 us (4%)
  between operations  1.01 us (2%)
    ppermute x1, waiting for transfers between devices, per_device(): message = to_beyond(message)  11.4 us
    pallas_call x1, Pallas kernels, per_device(): call(setup_kernel, [HBM] * 4 + [SMEM] * 2 + [VMEM] * 3, [VMEM] * 7, [plan...  8.29 us
    pallas_call x1, Pallas kernels, per_device(): call(edge_kernel, [VMEM] * 9, [VMEM] * 4, [plane] * 4)  6.56 us
    pallas_call x1, Pallas kernels, per_device(): call(beyond_kernel, [VMEM] * 5 + [SMEM] * 2 + [VMEM] * 5, [VMEM] * 2, [pl...  5.06 us
    pallas_call x1, Pallas kernels, per_device(): call(ahead_kernel, [VMEM] * 7, [VMEM] * 4, [plane] * 2 + [half_plane] * 2)  4.78 us
    ppermute x1, starting transfers between devices, per_device(): last_near = to_beyond(last_near)  3.51 us
    ppermute x1, waiting for transfers between devices, per_device(): other = across(terms)  3.47 us
    pallas_call x1, Pallas kernels, per_device(): call(inner_kernel, [VMEM] * 7, [HBM] * 2 + [VMEM], [state, state, jax.Sha...  2.68 us
  transfers between devices with their start and end apart: 8, of which 2 were waited for; matrix products, arithmetic and copies ran while one was open for 0% of the time, Pallas kernels for 45%

profile of v1, /device:TPU:4, one launch (start us, length us, event | category | flops | bytes accessed | tf_op | source)
XLA Modules:
  0.0 63.5 jit_solution(13088662050991315121)
XLA Ops:
  0.6 0.0 copy-start
  0.6 0.0 copy-start.1
  0.7 1.3 %copy-done.1 = bf16[2,2,2,256,256]{4,3,2,1,0:T(8,128)(2,1)S(1)} copy-done((bf16[2,2,2,256,256]{4,3,2,1,0:T(8,128)(2,1)S(1)}, bf16[2,2,2,256,256]{4,3,2,1,0:T(8,128)(2,1)}, u32[]{:S(2)}) %copy-start.1) | copy-done | bytes 1048600
  1.9 1.2 %copy-done.2 = bf16[2,2,2,256,256]{4,3,2,1,0:T(8,128)(2,1)S(1)} copy-done((bf16[2,2,2,256,256]{4,3,2,1,0:T(8,128)(2,1)S(1)}, bf16[2,2,2,256,256]{4,3,2,1,0:T(8,128)(2,1)}, u32[]{:S(2)}) %copy-start.2) | copy-done | bytes 1048600
  3.1 0.1 shard_map.112
  3.3 0.1 collective-permute-start
  3.3 2.1 %collective-permute-start.2 = (bf16[2,2,256,256]{3,2,1,0:T(8,128)(2,1)S(1)}, bf16[2,2,256,256]{3,2,1,0:T(8,128)(2,1)S(1)}, u32[]{:S(2)}, u32[]{:S(2)}) collective-permute-start(bf16[2,2,256,256]{3,2,1,0:T(8,128)(2,1)S(1)} %get-tuple-element.29.outward_outer), channel_id=1, source_target_pairs={{2,4},{6,8},{10,12},{14,16},{18,20},{22,24},{26,28},{4,2},{8,6},{1... | collective-permute-start | bytes 1572872 | tf_op jit(solution)/shard_map/ppermute | solution.py:559
  5.4 0.0 copy-done
  5.4 0.0 copy-done.4
  5.4 0.0 copy-done.5
  5.5 8.3 %shard_map.113 = (bf16[2,2,256,256]{3,2,1,0:T(8,128)(2,1)S(1)}, bf16[2,2,256,256]{3,2,1,0:T(8,128)(2,1)S(1)}, bf16[2,2,256,256]{3,2,1,0:T(8,128)(2,1)S(1)}, f32[...) custom-call(bf16[2,2,2,256,256]{4,3,2,1,0:T(8,128)(2,1)S(1)} %copy-d, ...), custom_call_target="tpu_custom_call" | custom-call | tf_op jit(solution)/shard_map/pallas_call | solution.py:561
  13.8 0.0 collective-permute-done.partner
  13.8 0.0 copy-start.3
  13.8 4.8 %shard_map.114 = (bf16[2,2,256,256]{3,2,1,0:T(8,128)(2,1)S(1)}, bf16[2,2,256,256]{3,2,1,0:T(8,128)(2,1)S(1)}, bf16[2,2,128,256]{3,2,1,0:T(8,128)(2,1)S(1)}, bf16[2,2,128,256]{3,2,1,0:T(8,128)(2,1)S(1)}) custom-call(bf16[2,2,256,256]{3,2,1,0:T(8,128)(2,1)S(1)} %collective-permute-done.partner, bf16[2,2,256,256]{3,2,1,0:T(8,128)(2,1)S(1)} %get-tuple-element.30.q_in_outer, ...), custom_call_target="tpu_custom_call" | custom-call | tf_op jit(solution)/shard_map/pallas_call | solution.py:573
  18.6 1.7 %collective-permute-start.3 = (bf16[2,2,256,256]{3,2,1,0:T(8,128)(2,1)S(1)}, bf16[2,2,256,256]{3,2,1,0:T(8,128)(2,1)S(1)}, u32[]{:S(2)}, u32[]{:S(2)}) collective-permute-start(bf16[2,2,256,256]{3,2,1,0:T(8,128)(2,1)S(1)} %get-tuple-element.35), channel_id=1, source_target_pairs={{0,2},{2,0},{4,6},{6,4},{8,10},{10,8},{12,14},{14,12},{16,18},{18,... | collective-permute-start | bytes 1572872 | tf_op jit(solution)/shard_map/ppermute | solution.py:576
  20.3 2.2 %collective-permute-start.4 = (bf16[3,2,256,256]{3,2,1,0:T(8,128)(2,1)S(1)}, bf16[3,2,256,256]{3,2,1,0:T(8,128)(2,1)S(1)}, u32[]{:S(2)}, u32[]{:S(2)}) collective-permute-start(bf16[3,2,256,256]{3,2,1,0:T(8,128)(2,1)S(1)} %get-tuple-element.38), channel_id=1, source_target_pairs={{2,4},{6,8},{10,12},{14,16},{18,20},{22,24},{26,28},{4,2},{8,6},{1... | collective-permute-start | bytes 2359304 | tf_op jit(solution)/shard_map/ppermute | solution.py:572
  22.5 0.0 collective-permute-done.2.arrived
  22.5 0.0 collective-permute-done.3.partner
  22.5 6.6 %shard_map.115 = (bf16[2,2,256,256]{3,2,1,0:T(8,128)(2,1)S(1)}, bf16[2,2,256,256]{3,2,1,0:T(8,128)(2,1)S(1)}, bf16[2,2,256,256]{3,2,1,0:T(8,128)(2,1)S(1)}, bf16[2,2,256,256]{3,2,1,0:T(8,128)(2,1)S(1)}) custom-call(bf16[2,2,256,256]{3,2,1,0:T(8,128)(2,1)S(1)} %collective-permute-done.2.arrived, bf16[2,2,256,256]{3,2,1,0:T(8,128)(2,1)S(1)} %copy-done.3, ...), custom_call_target="tpu_custom_call" | custom-call | tf_op jit(solution)/shard_map/pallas_call | solution.py:579
  29.1 1.6 %collective-permute-start.5 = (bf16[2,2,256,256]{3,2,1,0:T(8,128)(2,1)S(1)}, bf16[2,2,256,256]{3,2,1,0:T(8,128)(2,1)S(1)}, u32[]{:S(2)}, u32[]{:S(2)}) collective-permute-start(bf16[2,2,256,256]{3,2,1,0:T(8,128)(2,1)S(1)} %get-tuple-element.44), channel_id=1, source_target_pairs={{0,2},{2,0},{4,6},{6,4},{8,10},{10,8},{12,14},{14,12},{16,18},{18,... | collective-permute-start | bytes 1572872 | tf_op jit(solution)/shard_map/ppermute | solution.py:582
  30.6 2.0 %collective-permute-start.6 = (bf16[2,2,128,256]{3,2,1,0:T(8,128)(2,1)S(1)}, bf16[2,2,128,256]{3,2,1,0:T(8,128)(2,1)S(1)}, u32[]{:S(2)}, u32[]{:S(2)}) collective-permute-start(bf16[2,2,128,256]{3,2,1,0:T(8,128)(2,1)S(1)} %get-tuple-element.47), channel_id=1, source_target_pairs={{2,4},{6,8},{10,12},{14,16},{18,20},{22,24},{26,28},{4,2},{8,6},{1... | collective-permute-start | bytes 786440 | tf_op jit(solution)/shard_map/ppermute | solution.py:577
  32.7 3.5 %collective-permute-start.1 = (bf16[2,2,128,256]{3,2,1,0:T(8,128)(2,1)S(1)}, bf16[2,2,128,256]{3,2,1,0:T(8,128)(2,1)S(1)}, u32[]{:S(2)}, u32[]{:S(2)}) collective-permute-start(bf16[2,2,128,256]{3,2,1,0:T(8,128)(2,1)S(1)} %get-tuple-element.34), channel_id=1, source_target_pairs={{2,4},{6,8},{10,12},{14,16},{18,20},{22,24},{26,28},{4,2},{8,6},{1... | collective-permute-start | bytes 786440 | tf_op jit(solution)/shard_map/ppermute | solution.py:578
  36.2 11.4 %collective-permute-done.4.message = bf16[3,2,256,256]{3,2,1,0:T(8,128)(2,1)S(1)} collective-permute-done((bf16[3,2,256,256]{3,2,1,0:T(8,128)(2,1)S(1)}, bf16[3,2,256,256]{3,2,1,0:T(8,128)(2,1)S(1)}, u32[]{:S(2)}, u32[]{:S(2)}) %collective-permute-start.4) | collective-permute-done | bytes 786464 | tf_op jit(solution)/shard_map/ppermute | solution.py:572
  47.6 5.1 %shard_map.116 = (bf16[2,2,256,256]{3,2,1,0:T(8,128)(2,1)S(1)}, bf16[2,2,256,256]{3,2,1,0:T(8,128)(2,1)S(1)}) custom-call(bf16[3,2,256,256]{3,2,1,0:T(8,128)(2,1)S(1)} %collective-permute-done.4.message, bf16[2,2,256,256]{3,2,1,0:T(8,128)(2,1)S(1)} %copy-done.3, bf16[2,2,256,256]{3,2,1,0:T(8,128)(2,1)S(1)} %get-tuple-element.39.q_out_outer_0, ...), custom_call_target="tpu_custom_call" | custom-call | tf_op jit(solution)/shard_map/pallas_call | solution.py:583
  52.7 0.0 collective-permute-done.5.partner
  52.7 2.7 %shard_map.117 = (bf16[2,2,2,256,256]{4,3,2,1,0:T(8,128)(2,1)}, bf16[2,2,2,256,256]{4,3,2,1,0:T(8,128)(2,1)}, f32[256,256]{1,0:T(8,128)S(1)}) custom-call(bf16[2,2,256,256]{3,2,1,0:T(8,128)(2,1)S(1)} %collective-permute-done.5.partner, bf16[2,2,256,256]{3,2,1,0:T(8,128)(2,1)S(1)} %get-tuple-element.45.q_in_outer, ...), custom_call_target="tpu_custom_call" | custom-call | tf_op jit(solution)/shard_map/pallas_call | solution.py:589
  55.4 0.0 collective-permute-done.6.last
  55.4 1.1 %shard_map.118 = (bf16[2,2,2,256,256]{4,3,2,1,0:T(8,128)(2,1)}, bf16[2,2,2,256,256]{4,3,2,1,0:T(8,128)(2,1)}, bf16[2,128,256]{2,1,0:T(8,128)(2,1)S(1)}) custom-call(bf16[2,2,128,256]{3,2,1,0:T(8,128)(2,1)S(1)} %collective-permute-done.6.last, bf16[2,2,256,256]{3,2,1,0:T(8,128)(2,1)S(1)} %get-tuple-element.37.q_arrived, ...), custom_call_target="tpu_custom_call", output_to_operand_aliasing={{0}: (7, {}), {1}: (8, {})} | custom-call | tf_op jit(solution)/shard_map/pallas_call | solution.py:597
  56.5 1.6 %collective-permute-start.7 = (bf16[2,128,256]{2,1,0:T(8,128)(2,1)S(1)}, bf16[2,128,256]{2,1,0:T(8,128)(2,1)S(1)}, u32[]{:S(2)}, u32[]{:S(2)}) collective-permute-start(bf16[2,128,256]{2,1,0:T(8,128)(2,1)S(1)} %get-tuple-element.50), channel_id=1, source_target_pairs={{0,1},{1,0},{2,3},{3,2},{4,5},{5,4},{6,7},{7,6},{8,9},{9,8},{10,11... | collective-permute-start | bytes 393224 | tf_op jit(solution)/shard_map/ppermute | solution.py:605
  58.0 0.0 collective-permute-done.1.last
  58.0 3.5 %collective-permute-done.7.other = bf16[2,128,256]{2,1,0:T(8,128)(2,1)S(1)} collective-permute-done((bf16[2,128,256]{2,1,0:T(8,128)(2,1)S(1)}, bf16[2,128,256]{2,1,0:T(8,128)(2,1)S(1)}, u32[]{:S(2)}, u32[]{:S(2)}) %collective-permute-start.7) | collective-permute-done | bytes 131104 | tf_op jit(solution)/shard_map/ppermute | solution.py:605
  61.5 1.8 %shard_map.119 = (bf16[2,2,2,256,256]{4,3,2,1,0:T(8,128)(2,1)}, bf16[2,2,2,256,256]{4,3,2,1,0:T(8,128)(2,1)}, f32[2,128,256]{2,1,0:T(8,128)}) custom-call(bf16[2,2,128,256]{3,2,1,0:T(8,128)(2,1)S(1)} %collective-permute-done.1.last, bf16[2,2,256,256]{3,2,1,0:T(8,128)(2,1)S(1)} %get-tuple-element.37.q_arrived, ...), custom_call_target="tpu_custom_call", output_to_operand_aliasing={{0}: (8, {}), {1}: (9, {})} | custom-call | tf_op jit(solution)/shard_map/pallas_call | solution.py:606
  (8 shorter events, 0.0 us)
Async XLA Ops:
  0.6 4.8 %copy-start = (bf16[256,256]{1,0:T(8,128)(2,1)S(1)}, bf16[256,256]{1,0:T(8,128)(2,1)}, u32[]{:S(2)}) copy-start(bf16[256,256]{1,0:T(8,128)(2,1)} %constant.2.clone.hx.hy) | copy-start | bytes 393220
  0.6 1.3 %copy-start.1 = (bf16[2,2,2,256,256]{4,3,2,1,0:T(8,128)(2,1)S(1)}, bf16[2,2,2,256,256]{4,3,2,1,0:T(8,128)(2,1)}, u32[]{:S(2)}) copy-start(bf16[2,2,2,256,256]{4,3,2,1,0:T(8,128)(2,1)} %down.3) | copy-start | bytes 3145732
  1.9 1.2 %copy-start.2 = (bf16[2,2,2,256,256]{4,3,2,1,0:T(8,128)(2,1)S(1)}, bf16[2,2,2,256,256]{4,3,2,1,0:T(8,128)(2,1)}, u32[]{:S(2)}) copy-start(bf16[2,2,2,256,256]{4,3,2,1,0:T(8,128)(2,1)} %up.3) | copy-start | bytes 3145732
  3.1 2.3 %copy-start.4 = (f32[2,256,256]{2,1,0:T(8,128)S(1)}, f32[2,256,256]{2,1,0:T(8,128)}, u32[]{:S(2)}) copy-start(f32[2,256,256]{2,1,0:T(8,128)} %reflect.1) | copy-start | bytes 1572868
  3.1 2.3 %copy-start.5 = (s32[2,256,256]{2,1,0:T(8,128)S(1)}, s32[2,256,256]{2,1,0:T(8,128)}, u32[]{:S(2)}) copy-start(s32[2,256,256]{2,1,0:T(8,128)} %classes_in.1) | copy-start | bytes 1572868
  3.1 2.3 %copy-start.6 = (f32[16]{0:T(128)S(1)}, f32[16]{0:T(128)}, u32[]{:S(2)}) copy-start(f32[16]{0:T(128)} %slowness.3) | copy-start | bytes 196
  3.1 2.3 %copy-start.7 = (s32[2]{0:T(128)S(1)}, s32[2]{0:T(128)}, u32[]{:S(2)}) copy-start(s32[2]{0:T(128)} %freq.3) | copy-start | bytes 28
  3.3 10.5 %collective-permute-start = (bf16[2,2,256,256]{3,2,1,0:T(8,128)(2,1)S(1)}, bf16[2,2,256,256]{3,2,1,0:T(8,128)(2,1)S(1)}, u32[]{:S(2)}, u32[]{:S(2)}) collective-permute-start(bf16[2,2,256,256]{3,2,1,0:T(8,128)(2,1)S(1)} %get-tuple-element.28), channel_id=1, source_target_pairs={{0,2},{2,0},{4,6},{6,4},{8,10},{10,8},{12,14},{14,12},{16,18},{18,... | collective-permute-start | bytes 1572872 | tf_op jit(solution)/shard_map/ppermute | solution.py:560
  3.3 19.1 %collective-permute-start.2 = (bf16[2,2,256,256]{3,2,1,0:T(8,128)(2,1)S(1)}, bf16[2,2,256,256]{3,2,1,0:T(8,128)(2,1)S(1)}, u32[]{:S(2)}, u32[]{:S(2)}) collective-permute-start(bf16[2,2,256,256]{3,2,1,0:T(8,128)(2,1)S(1)} %get-tuple-element.29.outward_outer), channel_id=1, source_target_pairs={{2,4},{6,8},{10,12},{14,16},{18,20},{22,24},{26,28},{4,2},{8,6},{1... | collective-permute-start | bytes 1572872 | tf_op jit(solution)/shard_map/ppermute | solution.py:559
  13.8 8.7 %copy-start.3 = (bf16[2,2,256,256]{3,2,1,0:T(8,128)(2,1)S(1)}, bf16[2,2,256,256]{3,2,1,0:T(8,128)(2,1)}, u32[]{:S(2)}) copy-start(bf16[2,2,256,256]{3,2,1,0:T(8,128)(2,1)} %source.3) | copy-start | bytes 1572868
  18.6 3.9 %collective-permute-start.3 = (bf16[2,2,256,256]{3,2,1,0:T(8,128)(2,1)S(1)}, bf16[2,2,256,256]{3,2,1,0:T(8,128)(2,1)S(1)}, u32[]{:S(2)}, u32[]{:S(2)}) collective-permute-start(bf16[2,2,256,256]{3,2,1,0:T(8,128)(2,1)S(1)} %get-tuple-element.35), channel_id=1, source_target_pairs={{0,2},{2,0},{4,6},{6,4},{8,10},{10,8},{12,14},{14,12},{16,18},{18,... | collective-permute-start | bytes 1572872 | tf_op jit(solution)/shard_map/ppermute | solution.py:576
  20.3 27.3 %collective-permute-start.4 = (bf16[3,2,256,256]{3,2,1,0:T(8,128)(2,1)S(1)}, bf16[3,2,256,256]{3,2,1,0:T(8,128)(2,1)S(1)}, u32[]{:S(2)}, u32[]{:S(2)}) collective-permute-start(bf16[3,2,256,256]{3,2,1,0:T(8,128)(2,1)S(1)} %get-tuple-element.38), channel_id=1, source_target_pairs={{2,4},{6,8},{10,12},{14,16},{18,20},{22,24},{26,28},{4,2},{8,6},{1... | collective-permute-start | bytes 2359304 | tf_op jit(solution)/shard_map/ppermute | solution.py:572
  29.1 23.6 %collective-permute-start.5 = (bf16[2,2,256,256]{3,2,1,0:T(8,128)(2,1)S(1)}, bf16[2,2,256,256]{3,2,1,0:T(8,128)(2,1)S(1)}, u32[]{:S(2)}, u32[]{:S(2)}) collective-permute-start(bf16[2,2,256,256]{3,2,1,0:T(8,128)(2,1)S(1)} %get-tuple-element.44), channel_id=1, source_target_pairs={{0,2},{2,0},{4,6},{6,4},{8,10},{10,8},{12,14},{14,12},{16,18},{18,... | collective-permute-start | bytes 1572872 | tf_op jit(solution)/shard_map/ppermute | solution.py:582
  30.6 24.7 %collective-permute-start.6 = (bf16[2,2,128,256]{3,2,1,0:T(8,128)(2,1)S(1)}, bf16[2,2,128,256]{3,2,1,0:T(8,128)(2,1)S(1)}, u32[]{:S(2)}, u32[]{:S(2)}) collective-permute-start(bf16[2,2,128,256]{3,2,1,0:T(8,128)(2,1)S(1)} %get-tuple-element.47), channel_id=1, source_target_pairs={{2,4},{6,8},{10,12},{14,16},{18,20},{22,24},{26,28},{4,2},{8,6},{1... | collective-permute-start | bytes 786440 | tf_op jit(solution)/shard_map/ppermute | solution.py:577
  32.7 25.4 %collective-permute-start.1 = (bf16[2,2,128,256]{3,2,1,0:T(8,128)(2,1)S(1)}, bf16[2,2,128,256]{3,2,1,0:T(8,128)(2,1)S(1)}, u32[]{:S(2)}, u32[]{:S(2)}) collective-permute-start(bf16[2,2,128,256]{3,2,1,0:T(8,128)(2,1)S(1)} %get-tuple-element.34), channel_id=1, source_target_pairs={{2,4},{6,8},{10,12},{14,16},{18,20},{22,24},{26,28},{4,2},{8,6},{1... | collective-permute-start | bytes 786440 | tf_op jit(solution)/shard_map/ppermute | solution.py:578
  56.5 5.0 %collective-permute-start.7 = (bf16[2,128,256]{2,1,0:T(8,128)(2,1)S(1)}, bf16[2,128,256]{2,1,0:T(8,128)(2,1)S(1)}, u32[]{:S(2)}, u32[]{:S(2)}) collective-permute-start(bf16[2,128,256]{2,1,0:T(8,128)(2,1)S(1)} %get-tuple-element.50), channel_id=1, source_target_pairs={{0,1},{1,0},{2,3},{3,2},{4,5},{5,4},{6,7},{7,6},{8,9},{9,8},{10,11... | collective-permute-start | bytes 393224 | tf_op jit(solution)/shard_map/ppermute | solution.py:605

commit v2 on v1

v2 whole, which is shorter than its diff:
```python
import functools
import math

import jax
import jax.numpy as jnp
import numpy as np
from jax import lax
from jax.experimental import pallas as pl
from jax.experimental.pallas import tpu as pltpu
from jax.sharding import PartitionSpec as P

HOPS = 3
NCLASS = 16
NFREQ = 128
F32 = jnp.float32
BF16 = jnp.bfloat16
VMEM = pl.BlockSpec(memory_space=pltpu.VMEM)
HBM = pl.BlockSpec(memory_space=pltpu.HBM)
SMEM = pl.BlockSpec(memory_space=pltpu.SMEM)
PARAMS = pltpu.CompilerParams(vmem_limit_bytes=28 * 2**20)


def passed_along(block, axis, distance):
    devices = range(lax.axis_size(axis))
    route = [(i - distance, i) for i in devices if i - distance in devices]
    return lax.ppermute(block, axis, route)


def dft_tables(length):
    counter = jnp.arange(length, dtype=jnp.int32)
    product = counter[:, None] * counter[None, :] % length
    angles = 2.0 * math.pi / length * product.astype(jnp.float32)
    return (jnp.cos(angles).astype(jnp.bfloat16), jnp.sin(angles).astype(jnp.bfloat16))


def wavenumbers(length):
    counter = jnp.arange(length, dtype=jnp.int32)
    wrapped = jnp.where(counter >= length // 2, counter - length, counter)
    return 2.0 * math.pi / length * wrapped.astype(jnp.float32)


def propagate(planes, phase_re, phase_im, tables):
    fwd_left, fwd_right, inv_left, inv_right = tables
    first = jnp.einsum(
        "cdjk,...dkl->...cjl", fwd_left, planes, preferred_element_type=jnp.float32
    ).astype(jnp.bfloat16)
    second = jnp.einsum("...djl,dclm->...cjm", first, fwd_right, preferred_element_type=jnp.float32)
    real_part = second[..., 0, :, :]
    imag_part = second[..., 1, :, :]
    turned = jnp.stack(
        [real_part * phase_re - imag_part * phase_im, real_part * phase_im + imag_part * phase_re],
        axis=-3,
    ).astype(jnp.bfloat16)
    third = jnp.einsum(
        "cdjk,...dkl->...cjl", inv_left, turned, preferred_element_type=jnp.float32
    ).astype(jnp.bfloat16)
    return jnp.einsum(
        "...djl,dclm->...cjm", third, inv_right, preferred_element_type=jnp.float32
    ).astype(jnp.bfloat16)


def trade(down_edge, up_edge):
    got_down = passed_along(down_edge, "depth", 1)
    got_up = passed_along(up_edge, "depth", -1)
    return (got_down, got_up)


def per_device_plain(down_state, up_state, source, reflect, screen_class, screen_values, freq_index):
    levels = down_state.shape[0]
    rows_x = down_state.shape[3]
    rows_y = down_state.shape[4]
    front_count = down_state.shape[1]
    depth_rank = lax.axis_index("depth")
    scale = 1.0 / math.sqrt(front_count * lax.axis_size("shot"))
    cos_x, sin_x = dft_tables(rows_x)
    cos_y, sin_y = dft_tables(rows_y)
    tables = (
        jnp.stack([jnp.stack([cos_x, sin_x]), jnp.stack([-sin_x, cos_x])]),
        jnp.stack([jnp.stack([cos_y, -sin_y]), jnp.stack([sin_y, cos_y])]),
        jnp.stack([jnp.stack([cos_x, -sin_x]), jnp.stack([sin_x, cos_x])]),
        jnp.stack([jnp.stack([cos_y, sin_y]), jnp.stack([-sin_y, cos_y])]),
    )
    kwave = 0.95 * math.pi * (freq_index.astype(jnp.float32) + 1.0) / NFREQ
    kx_wave = wavenumbers(rows_x)
    ky_wave = wavenumbers(rows_y)
    vertical = kwave[:, None, None] ** 2 - kx_wave[None, :, None] ** 2 - ky_wave[None, None, :] ** 2
    propag = jnp.sqrt(jnp.maximum(vertical, 0.0))
    damping = jnp.exp(-jnp.sqrt(jnp.maximum(-vertical, 0.0))) / (rows_x * rows_y)
    phase_re = damping * jnp.cos(propag)
    phase_im = damping * jnp.sin(propag)
    classes = jnp.arange(NCLASS, dtype=jnp.int32)
    onehot = (screen_class[None] == classes[:, None, None, None]).astype(jnp.float32)
    slowness = jnp.einsum("c,clxy->lxy", screen_values, onehot, precision=lax.Precision.HIGHEST)
    angle = kwave[None, :, None, None] * slowness[:, None]
    screen_re = jnp.cos(angle)
    screen_im = jnp.sin(angle)
    refl = reflect[:, None]
    top_slab = depth_rank == 0
    down = down_state
    up = up_state
    a_re = a_im = b_re = b_im = None
    for repeat in range(HOPS):
        down_edge = down[levels - 1]
        up_edge = up[0]
        got_down, got_up = trade(down_edge, up_edge)
        got_down = jnp.where(top_slab, source, got_down)
        moved = propagate(
            jnp.concatenate([got_down[None], down[: levels - 1], up[1:], got_up[None]], axis=0),
            phase_re,
            phase_im,
            tables,
        )
        from_above = moved[:levels]
        from_below = moved[levels:]
        qa_re = from_above[:, :, 0].astype(jnp.float32)
        qa_im = from_above[:, :, 1].astype(jnp.float32)
        qb_re = from_below[:, :, 0].astype(jnp.float32)
        qb_im = from_below[:, :, 1].astype(jnp.float32)
        a_re = screen_re * qa_re - screen_im * qa_im
        a_im = screen_re * qa_im + screen_im * qa_re
        b_re = screen_re * qb_re - screen_im * qb_im
        b_im = screen_re * qb_im + screen_im * qb_re
        down = jnp.stack(
            [(1.0 + refl) * a_re - refl * b_re, (1.0 + refl) * a_im - refl * b_im], axis=2
        ).astype(jnp.bfloat16)
        up = jnp.stack(
            [(1.0 - refl) * b_re + refl * a_re, (1.0 - refl) * b_im + refl * a_im], axis=2
        ).astype(jnp.bfloat16)
    terms = scale * jnp.sum(a_re * b_re + a_im * b_im, axis=1)
    gradient = lax.psum_scatter(
        terms.astype(jnp.bfloat16), "shot", scatter_dimension=1, tiled=True
    ).astype(jnp.float32)
    return (down, up, gradient)


def hartley(length):
    counter = np.arange(length)
    angles = 2.0 * np.pi / length * (counter[:, None] * counter[None, :] % length)
    cosine = np.cos(angles).astype(BF16).astype(np.float32)
    sine = np.sin(angles).astype(BF16).astype(np.float32)
    return (cosine + sine).astype(BF16)


def odd_place():
    return lax.rem(lax.axis_index("depth"), 2)


def mm(left, right):
    return jnp.dot(left, right, preferred_element_type=F32)


def spread(jobs, work, hx, hy, phase):
    jobs = list(enumerate(jobs))
    for slot, (plane, _, _) in jobs:
        for part in range(2):
            work[slot, part] = mm(plane[part], hy[...]).astype(BF16)
    for slot, (_, front, _) in jobs:
        turn_re, turn_im = phase[front, 0], phase[front, 1]
        part_re = mm(hx[...], work[slot, 0])
        part_im = mm(hx[...], work[slot, 1])
        work[slot, 0] = (part_re * turn_re - part_im * turn_im).astype(BF16)
        work[slot, 1] = (part_re * turn_im + part_im * turn_re).astype(BF16)
    for slot, _ in jobs:
        for part in range(2):
            work[slot, part] = mm(hx[...], work[slot, part]).astype(BF16)
    for slot, (_, _, target) in jobs:
        for part in range(2):
            target[part] = mm(work[slot, part], hy[...]).astype(BF16)


def screened(real_part, imag_part, screen_re, screen_im):
    return (
        screen_re * real_part - screen_im * imag_part,
        screen_re * imag_part + screen_im * real_part,
    )


def mixed(a_re, a_im, b_re, b_im, refl, screen_re, screen_im):
    a_re, a_im, b_re, b_im = (part.astype(F32) for part in (a_re, a_im, b_re, b_im))
    step_re = refl * (a_re - b_re)
    step_im = refl * (a_im - b_im)
    inward = screened(a_re + step_re, a_im + step_im, screen_re, screen_im)
    outward = screened(b_re + step_re, b_im + step_im, screen_re, screen_im)
    return tuple(part.astype(BF16) for part in inward + outward)


def put(target, real_part, imag_part):
    target[0] = real_part.astype(BF16)
    target[1] = imag_part.astype(BF16)


def edges_kernel(down, up, reflect, classes_in, parcel, inward_inner, refl, klass, sems):
    levels = down.shape[0]
    fronts = inward_inner.shape[0]
    odd = odd_place()
    outward_outer = parcel.at[pl.ds(0, fronts)]

    def fetch(first, second):
        pltpu.make_async_copy(first, outward_outer, sems.at[0]).start()
        pltpu.make_async_copy(second, inward_inner, sems.at[1]).start()

    fixed = [
        pltpu.make_async_copy(reflect.at[odd], refl, sems.at[2]),
        pltpu.make_async_copy(classes_in.at[odd], klass, sems.at[3]),
    ]
    for copy in fixed:
        copy.start()

    @pl.when(odd == 0)
    def _():
        fetch(up.at[0], down.at[levels - 1])

    @pl.when(odd == 1)
    def _():
        fetch(down.at[levels - 1], up.at[0])

    for copy in fixed:
        copy.wait()
    put(parcel.at[fronts], jnp.where(odd == 0, 1.0, -1.0).astype(F32) * refl[...], klass[...])
    pltpu.make_async_copy(up.at[0], outward_outer, sems.at[0]).wait()
    pltpu.make_async_copy(up.at[0], inward_inner, sems.at[1]).wait()


def class_rows(slowness, kwave, shape):
    lanes = lax.broadcasted_iota(jnp.int32, shape, 1)
    table = jnp.zeros(shape, F32)
    for entry in range(NCLASS):
        table = jnp.where(lanes == entry, slowness[entry], table)
    angle = kwave * table
    return jnp.cos(angle), jnp.sin(angle)


def look_up(table, classes):
    width = 128
    rows = classes.shape[0]
    wide = jnp.broadcast_to(table[:1], (rows, width))
    pieces = [
        jnp.take_along_axis(wide, classes[:, start : start + width], axis=1, mode="promise_in_bounds")
        for start in range(0, classes.shape[1], width)
    ]
    return jnp.concatenate(pieces, axis=1)


def front_wave(freq, front):
    return 0.95 * math.pi * (freq[front].astype(F32) + 1.0) / NFREQ


def series(square, shift):
    total = jnp.full_like(square, 1.0 / math.factorial(18 + shift))
    for order in range(16, -1, -2):
        total = 1.0 / math.factorial(order + shift) - square * total
    return total


def setup_kernel(
    down, up, reflect, classes_in, slowness, freq, parcel, hx, hy,
    q_out_inner, q_in_outer, q_out_outer, screen, phase, refl, second,
    fields, klass, work, sems,
):
    fronts = q_out_inner.shape[0]
    rows_x, rows_y = refl.shape[1:]
    odd = odd_place()
    fixed = [
        pltpu.make_async_copy(reflect.at[odd], refl.at[0], sems.at[2]),
        pltpu.make_async_copy(reflect.at[1 - odd], refl.at[1], sems.at[3]),
        pltpu.make_async_copy(classes_in.at[odd], klass.at[0], sems.at[4]),
        pltpu.make_async_copy(classes_in.at[1 - odd], klass.at[1], sems.at[5]),
    ]
    for copy in fixed:
        copy.start()

    @pl.when(odd == 0)
    def _():
        pltpu.make_async_copy(down.at[0], fields.at[0], sems.at[0]).start()
        pltpu.make_async_copy(up.at[1], fields.at[1], sems.at[1]).start()

    @pl.when(odd == 1)
    def _():
        pltpu.make_async_copy(up.at[1], fields.at[0], sems.at[0]).start()
        pltpu.make_async_copy(down.at[0], fields.at[1], sems.at[1]).start()

    def squares(length, axis):
        counter = lax.broadcasted_iota(jnp.int32, (rows_x, rows_y), axis)
        wrapped = jnp.where(counter >= length // 2, counter - length, counter)
        wave = 2.0 * math.pi / length * wrapped.astype(F32)
        return wave * wave

    lateral = squares(rows_x, 0) + squares(rows_y, 1)
    level_out = 1.0 / (rows_x * rows_y)
    for front in range(fronts):
        kwave = front_wave(freq, front)
        vertical = kwave * kwave - lateral
        travels = vertical > 0.0
        square = jnp.maximum(vertical, 0.0)
        root = jnp.sqrt(jnp.abs(vertical))
        phase[front, 0] = jnp.where(travels, series(square, 0), jnp.exp(-root)) * level_out
        phase[front, 1] = jnp.where(travels, root * series(square, 1), 0.0) * level_out
    for copy in fixed:
        copy.wait()
    sign = jnp.where(odd == 0, 1.0, -1.0).astype(F32)
    for level in range(2):
        refl[level] = sign * refl[level]
    for front in range(fronts):
        cos_row, sin_row = class_rows(slowness, front_wave(freq, front), (8, 128))
        for level in range(2):
            screen[level, front, 0] = look_up(cos_row, klass[level])
            screen[level, front, 1] = look_up(sin_row, klass[level])
    pltpu.make_async_copy(down.at[0], fields.at[0], sems.at[0]).wait()
    pltpu.make_async_copy(down.at[0], fields.at[1], sems.at[1]).wait()
    jobs = [(fields.at[1, front], front, q_out_inner.at[front]) for front in range(fronts)]
    jobs += [(fields.at[0, front], front, q_in_outer.at[front]) for front in range(fronts)]
    spread(jobs, work, hx, hy, phase)
    jobs = leaving(q_out_inner, refl, screen, fields.at[0], second)
    jobs += [(parcel.at[front], front, q_out_outer.at[front]) for front in range(fronts)]
    spread(jobs, work, hx, hy, phase)


def leaving(q_out_inner, refl, screen, field, target):
    fronts = q_out_inner.shape[0]
    kept = 1.0 - refl[0]
    for front in range(fronts):
        b_re, b_im = (q_out_inner[front, part].astype(F32) for part in range(2))
        b_re, b_im = screened(b_re, b_im, screen[0, front, 0], screen[0, front, 1])
        put(field.at[front], kept * b_re, kept * b_im)
    return [(field.at[front], front, target.at[front]) for front in range(fronts)]


def ahead_kernel(
    partner, q_in_outer, screen, refl, phase, hx, hy,
    inward_inner, q_out_inner, last_far, last_near,
    field, third, work,
):
    fronts = partner.shape[0]
    half = partner.shape[2] // 2
    far_bottom = lax.axis_index("shot") % 2 == 0
    spread([(partner.at[front], front, third.at[front]) for front in range(fronts)], work, hx, hy, phase)
    for front in range(fronts):
        in_re, in_im, out_re, out_im = mixed(
            q_in_outer[front, 0], q_in_outer[front, 1], third[front, 0], third[front, 1],
            refl[1], screen[1, front, 0], screen[1, front, 1],
        )
        put(inward_inner.at[front], in_re, in_im)
        put(field.at[front], out_re, out_im)
    spread([(field.at[front], front, q_out_inner.at[front]) for front in range(fronts)], work, hx, hy, phase)
    spread(leaving(q_out_inner, refl, screen, field, third), work, hx, hy, phase)
    for front in range(fronts):
        for part in range(2):
            top, bottom = third[front, part, :half], third[front, part, half:]
            last_far[front, part] = jnp.where(far_bottom, bottom, top)
            last_near[front, part] = jnp.where(far_bottom, top, bottom)


def edge_kernel(
    arrived, source, partner, q_out_inner, q_out_outer, slowness, freq, screen, refl, phase, hx, hy,
    inward_inner, q_arrived, q_out_inner_next, rest_2, rest_3,
    inward, outward, q_partner, q_inward, q_outward, work,
):
    fronts = partner.shape[0]
    everyone = range(fronts)
    first = lax.axis_index("depth") == 0
    for front in everyone:
        put(inward.at[front], *(jnp.where(first, source[front, part], arrived[front, part]) for part in range(2)))
    jobs = [(inward.at[front], front, q_arrived.at[front]) for front in everyone]
    jobs += [(partner.at[front], front, q_partner.at[front]) for front in everyone]
    spread(jobs, work, hx, hy, phase)
    for front in everyone:
        in_re, in_im, out_re, out_im = mixed(
            q_arrived[front, 0], q_arrived[front, 1], q_out_inner[front, 0], q_out_inner[front, 1],
            refl[0], screen[0, front, 0], screen[0, front, 1],
        )
        put(inward.at[front], in_re, in_im)
        put(outward.at[front], out_re, out_im)
    jobs = [(inward.at[front], front, q_inward.at[front]) for front in everyone]
    jobs += [(outward.at[front], front, q_outward.at[front]) for front in everyone]
    spread(jobs, work, hx, hy, phase)
    refl_beyond = arrived[fronts, 0].astype(F32)
    klass = arrived[fronts, 1].astype(F32).astype(jnp.int32)
    for front in everyone:
        in_re, in_im, out_re, out_im = mixed(
            q_inward[front, 0], q_inward[front, 1], q_partner[front, 0], q_partner[front, 1],
            refl[1], screen[1, front, 0], screen[1, front, 1],
        )
        put(inward_inner.at[front], in_re, in_im)
        put(inward.at[front], out_re, out_im)
        cos_row, sin_row = class_rows(slowness, front_wave(freq, front), (8, 128))
        back_re = refl_beyond * look_up(cos_row, klass)
        back_im = refl_beyond * look_up(sin_row, klass)
        for known, target in ((q_out_outer, q_inward), (q_outward, q_partner)):
            known_re, known_im = (known[front, part].astype(F32) for part in range(2))
            put(target.at[front], *screened(known_re, known_im, back_re, back_im))
    jobs = [(inward.at[front], front, q_out_inner_next.at[front]) for front in everyone]
    jobs += [(q_inward.at[front], front, rest_2.at[front]) for front in everyone]
    jobs += [(q_partner.at[front], front, rest_3.at[front]) for front in everyone]
    spread(jobs, work, hx, hy, phase)


def inner_kernel(
    second, rest_2, q_arrived, q_out_inner, partner, screen, refl, phase, hx, hy,
    inward, outward, terms,
    field, q_partner, q_inward, work,
):
    fronts = partner.shape[0]
    everyone = range(fronts)
    first = lax.axis_index("depth") == 0
    for front in everyone:
        a_re, a_im = (
            jnp.where(
                first,
                q_arrived[front, part].astype(F32),
                second[front, part].astype(F32) + rest_2[front, part].astype(F32),
            )
            for part in range(2)
        )
        in_re, in_im, _, _ = mixed(
            a_re, a_im, q_out_inner[front, 0], q_out_inner[front, 1],
            refl[0], screen[0, front, 0], screen[0, front, 1],
        )
        put(field.at[front], in_re, in_im)
    jobs = [(field.at[front], front, q_inward.at[front]) for front in everyone]
    jobs += [(partner.at[front], front, q_partner.at[front]) for front in everyone]
    spread(jobs, work, hx, hy, phase)
    total = None
    for front in everyone:
        a_re, a_im = (q_inward[front, part].astype(F32) for part in range(2))
        b_re, b_im = (q_partner[front, part].astype(F32) for part in range(2))
        in_re, in_im, out_re, out_im = mixed(
            a_re, a_im, b_re, b_im, refl[1], screen[1, front, 0], screen[1, front, 1]
        )
        put(inward.at[front], in_re, in_im)
        put(outward.at[front], out_re, out_im)
        term = a_re * b_re + a_im * b_im
        total = term if total is None else total + term
    terms[...] = total


def outer_rows(near, last, q_arrived, rest, q_out_inner, screen, refl, inward, outward):
    fronts, _, half, _ = last.shape
    first = lax.axis_index("depth") == 0
    shot = lax.axis_index("shot") % 2
    rows = pl.ds(pl.multiple_of((shot if near else 1 - shot) * half, half), half)
    total = None
    for front in range(fronts):
        a_re, a_im = (
            jnp.where(
                first,
                q_arrived[front, part, rows, :].astype(F32),
                last[front, part].astype(F32) + rest[front, part, rows, :].astype(F32),
            )
            for part in range(2)
        )
        b_re, b_im = (q_out_inner[front, part, rows, :].astype(F32) for part in range(2))
        in_re, in_im, out_re, out_im = mixed(
            a_re, a_im, b_re, b_im, refl[0, rows, :], screen[0, front, 0, rows, :], screen[0, front, 1, rows, :]
        )
        put(inward.at[front], in_re, in_im)
        put(outward.at[front], out_re, out_im)
        term = a_re * b_re + a_im * b_im
        total = term if total is None else total + term
    return rows, total


def send_home(level, rows, inward, outward, down_out, up_out, sems):
    odd = odd_place()

    def copies(place, inward_out, outward_out):
        return [
            pltpu.make_async_copy(inward, inward_out.at[place, :, :, rows, :], sems.at[0]),
            pltpu.make_async_copy(outward, outward_out.at[place, :, :, rows, :], sems.at[1]),
        ]

    @pl.when(odd == 0)
    def _():
        for copy in copies(level, down_out, up_out):
            copy.start()

    @pl.when(odd == 1)
    def _():
        for copy in copies(1 - level, up_out, down_out):
            copy.start()

    return copies(0, down_out, up_out)


def far_rows_kernel(
    last, q_arrived, rest, q_out_inner, screen, refl, inner_terms, inner_in, inner_out,
    down_out, up_out, terms,
    inward, outward, sems,
):
    every_row = pl.ds(0, inner_in.shape[2])
    waits = send_home(1, every_row, inner_in, inner_out, down_out, up_out, sems.at[1])
    rows, total = outer_rows(False, last, q_arrived, rest, q_out_inner, screen, refl, inward, outward)
    waits += send_home(0, rows, inward, outward, down_out, up_out, sems.at[0])
    terms[0] = total.astype(BF16)
    terms[1] = inner_terms[rows, :].astype(BF16)
    for copy in waits:
        copy.wait()


def near_rows_kernel(
    scale, last, q_arrived, rest, q_out_inner, screen, refl, inner_terms, other, down_in, up_in,
    down_out, up_out, gradient,
    inward, outward, sums, sems,
):
    del down_in, up_in
    rows, total = outer_rows(True, last, q_arrived, rest, q_out_inner, screen, refl, inward, outward)
    waits = send_home(0, rows, inward, outward, down_out, up_out, sems.at[0])
    odd = odd_place()
    sums[odd] = scale * (total + other[0].astype(F32))
    sums[1 - odd] = scale * (inner_terms[rows, :] + other[1].astype(F32))
    done = pltpu.make_async_copy(sums, gradient, sems.at[1, 0])
    done.start()
    for copy in waits + [done]:
        copy.wait()


def per_device(down_state, up_state, source, reflect, screen_class, screen_values, freq_index):
    depth = lax.axis_size("depth")
    shots = lax.axis_size("shot")
    levels, fronts, parts, rows_x, rows_y = down_state.shape
    if levels != 2 or depth % 2 or shots != 2 or HOPS != 3:
        return per_device_plain(down_state, up_state, source, reflect, screen_class, screen_values, freq_index)
    scale = 1.0 / math.sqrt(fronts * shots)
    half = rows_x // 2
    hx = jnp.asarray(hartley(rows_x))
    hy = jnp.asarray(hartley(rows_y))
    partners = [(i, i ^ 1) for i in range(depth)]
    beyond = [(i, i + 1) for i in range(1, depth - 1, 2)] + [(i + 1, i) for i in range(1, depth - 1, 2)]
    to_partner = functools.partial(lax.ppermute, axis_name="depth", perm=partners)
    to_beyond = functools.partial(lax.ppermute, axis_name="depth", perm=beyond)
    across = functools.partial(lax.ppermute, axis_name="shot", perm=[(0, 1), (1, 0)])
    plane = jax.ShapeDtypeStruct((fronts, parts, rows_x, rows_y), BF16)
    half_plane = jax.ShapeDtypeStruct((fronts, parts, half, rows_y), BF16)
    pair = jax.ShapeDtypeStruct((2, rows_x, rows_y), F32)
    turns = jax.ShapeDtypeStruct((fronts, parts, rows_x, rows_y), F32)
    screens = jax.ShapeDtypeStruct((2, fronts, parts, rows_x, rows_y), F32)
    state = jax.ShapeDtypeStruct(down_state.shape, BF16)
    dma = pltpu.SemaphoreType.DMA

    def call(kernel, in_specs, out_specs, out_shape, scratch=(), **more):
        return pl.pallas_call(
            kernel,
            in_specs=in_specs,
            out_specs=out_specs,
            out_shape=out_shape,
            scratch_shapes=list(scratch),
            compiler_params=PARAMS,
            **more,
        )

    def kept_in_hbm(*arrays):
        return [pltpu.with_memory_space_constraint(array, pltpu.HBM) for array in arrays]

    def buffers(count, shape=plane):
        return [pltpu.VMEM(shape.shape, shape.dtype)] * count

    def work(slots):
        return pltpu.VMEM((slots, *plane.shape[1:]), BF16)

    parcel, in_inner = call(
        edges_kernel,
        [HBM] * 4,
        [VMEM] * 2,
        [jax.ShapeDtypeStruct((fronts + 1, parts, rows_x, rows_y), BF16), plane],
        [pltpu.VMEM((rows_x, rows_y), F32), pltpu.VMEM((rows_x, rows_y), jnp.int32), dma((4,))],
    )(*kept_in_hbm(down_state, up_state, reflect, screen_class))
    arrived = to_beyond(parcel)
    partner_0 = to_partner(in_inner)
    q_out_inner_0, q_in_outer_0, q_out_outer_0, screen, phase, refl, second = call(
        setup_kernel,
        [HBM] * 4 + [SMEM] * 2 + [VMEM] * 3,
        [VMEM] * 7,
        [plane] * 3 + [screens, turns, pair, plane],
        [
            pltpu.VMEM((2, *plane.shape), BF16),
            pltpu.VMEM((2, rows_x, rows_y), jnp.int32),
            work(2 * fronts),
            dma((6,)),
        ],
    )(*kept_in_hbm(down_state, up_state, reflect, screen_class), screen_values, freq_index, parcel, hx, hy)
    second = to_beyond(second)
    in_inner_1, q_out_inner_1, last_far, last_near = call(
        ahead_kernel, [VMEM] * 7, [VMEM] * 4, [plane] * 2 + [half_plane] * 2, buffers(2) + [work(fronts)]
    )(partner_0, q_in_outer_0, screen, refl, phase, hx, hy)
    partner_1 = to_partner(in_inner_1)
    last_far = to_beyond(last_far)
    last_near = to_beyond(last_near)
    in_inner_2, q_arrived, q_out_inner_2, rest_2, rest_3 = call(
        edge_kernel,
        [VMEM] * 5 + [SMEM] * 2 + [VMEM] * 5,
        [VMEM] * 5,
        [plane] * 5,
        buffers(5) + [work(3 * fronts)],
    )(
        arrived, source, partner_1, q_out_inner_0, q_out_outer_0, screen_values, freq_index,
        screen, refl, phase, hx, hy,
    )
    partner_2 = to_partner(in_inner_2)
    inner_in, inner_out, inner_terms = call(
        inner_kernel,
        [VMEM] * 10,
        [VMEM] * 3,
        [plane, plane, jax.ShapeDtypeStruct((rows_x, rows_y), F32)],
        buffers(3) + [work(2 * fronts)],
    )(second, rest_2, q_arrived, q_out_inner_1, partner_2, screen, refl, phase, hx, hy)
    down, up, terms = call(
        far_rows_kernel,
        [VMEM] * 9,
        [HBM] * 2 + [VMEM],
        [state, state, jax.ShapeDtypeStruct((2, half, rows_y), BF16)],
        buffers(2, half_plane) + [dma((2, 2))],
    )(last_far, q_arrived, rest_3, q_out_inner_2, screen, refl, inner_terms, inner_in, inner_out)
    other = across(terms)
    down, up, gradient = call(
        functools.partial(near_rows_kernel, scale),
        [VMEM] * 8 + [HBM] * 2,
        [HBM] * 3,
        [state, state, jax.ShapeDtypeStruct((2, half, rows_y), F32)],
        buffers(2, half_plane) + [pltpu.VMEM((2, half, rows_y), F32), dma((2, 2))],
        input_output_aliases={8: 0, 9: 1},
    )(last_near, q_arrived, rest_3, q_out_inner_2, screen, refl, inner_terms, other, down, up)
    return (down, up, gradient)


def solution(mesh):
    return jax.shard_map(
        per_device,
        mesh=mesh,
        in_specs=(
            P("depth", "shot", None, None, None),
            P("depth", "shot", None, None, None),
            P("shot", None, None, None),
            P("depth", None, None),
            P("depth", None, None),
            P(),
            P("shot"),
        ),
        out_specs=(
            P("depth", "shot", None, None, None),
            P("depth", "shot", None, None, None),
            P("depth", "shot", None),
        ),
        check_vma=False,
    )
```

time: 63.7 us -> 57 us (0.89)
  Pallas kernels: 30.3 us -> 21 us
  waiting for transfers between devices: 14.9 us -> 21.6 us
  local copies, waits for them, and re-layouts: 2.51 us -> 0.02 us
  starting transfers between devices: 14.7 us -> 13.1 us
    pallas_call x6 -> x5, Pallas kernels: 20.3 us -> 13.7 us  [the longest x1 6.23 us: per_device(): call(edge_kernel, [VMEM] * 5 + [SMEM] * 2 + [VMEM] * 5, [VMEM] * 5, [plan...]
    ppermute x1, waiting for transfers between devices: 0.01 us -> 5.64 us  [per_device(): last_far = to_beyond(last_far)]
    unnamed x16 -> x8, local copies, waits for them, and re-layouts: 2.51 us -> 0.02 us
    pallas_call x1, Pallas kernels: 8.29 us -> 6.13 us  [per_device(): call(setup_kernel, [HBM] * 4 + [SMEM] * 2 + [VMEM] * 3, [VMEM] * 7, [plan...]
    ppermute x1, starting transfers between devices: 1.58 us -> 0.07 us  [per_device(): partner_2 = to_partner(in_inner_2)]
    ppermute x2, waiting for transfers between devices: 11.4 us -> 12.5 us  [the longest x1 12.5 us: per_device(): arrived = to_beyond(parcel)]
  transfers between devices with their start and end apart: 8 -> 8, of which waited for: 2 -> 4; matrix products, arithmetic and copies ran while one was open for 0% -> 0% of each run, Pallas kernels for 45% -> 32%
where the time goes in v2:
time: 57 us; the launch traced here: 56.7 us
  waiting for transfers between devices  21.6 us (38%)
  Pallas kernels  21 us (37%)
  starting transfers between devices  13.1 us (23%)
  between operations  0.97 us (2%)
    ppermute x1, waiting for transfers between devices, per_device(): arrived = to_beyond(parcel)  12.5 us
    pallas_call x1, Pallas kernels, per_device(): call(edge_kernel, [VMEM] * 5 + [SMEM] * 2 + [VMEM] * 5, [VMEM] * 5, [plan...  6.23 us
    pallas_call x1, Pallas kernels, per_device(): call(setup_kernel, [HBM] * 4 + [SMEM] * 2 + [VMEM] * 3, [VMEM] * 7, [plan...  6.13 us
    ppermute x1, waiting for transfers between devices, per_device(): last_far = to_beyond(last_far)  5.64 us
    ppermute x1, starting transfers between devices, per_device(): last_near = to_beyond(last_near)  3.64 us
    ppermute x1, waiting for transfers between devices, per_device(): other = across(terms)  3.4 us
    pallas_call x1, Pallas kernels, per_device(): call(ahead_kernel, [VMEM] * 7, [VMEM] * 4, [plane] * 2 + [half_plane] * 2...  2.82 us
    ppermute x1, starting transfers between devices, per_device(): second = to_beyond(second)  2.2 us
  transfers between devices with their start and end apart: 8, of which 4 were waited for; matrix products, arithmetic and copies ran while one was open for 0% of the time, Pallas kernels for 32%

profile of v2, /device:TPU:4, one launch (start us, length us, event | category | flops | bytes accessed | tf_op | source)
XLA Modules:
  0.0 56.7 jit_solution(8906106379784927490)
XLA Ops:
  0.6 0.0 copy-start
  0.6 0.0 copy-start.3
  0.7 0.0 copy-start.2
  0.7 1.5 %shard_map.112 = (bf16[3,2,256,256]{3,2,1,0:T(8,128)(2,1)S(1)}, bf16[2,2,256,256]{3,2,1,0:T(8,128)(2,1)S(1)}) custom-call(bf16[2,2,2,256,256]{4,3,2,1,0:T(8,128)(2,1)} %down.3, bf16[2,2,2,256,256]{4,3,2,1,0:T(8,128)(2,1)} %up.3, f32[2,256,256]{2,1,0:T(8,128)} %reflect.3, s32[2,256,256]{2,1,0:T(8,128)} %classes_in.3), custom_call_target="tpu_custom_call" | custom-call | tf_op jit(solution)/shard_map/pallas_call | solution.py:559
  2.1 0.1 collective-permute-start
  2.2 1.9 %collective-permute-start.2 = (bf16[3,2,256,256]{3,2,1,0:T(8,128)(2,1)S(1)}, bf16[3,2,256,256]{3,2,1,0:T(8,128)(2,1)S(1)}, u32[]{:S(2)}, u32[]{:S(2)}) collective-permute-start(bf16[3,2,256,256]{3,2,1,0:T(8,128)(2,1)S(1)} %get-tuple-element.28.parcel), channel_id=1, source_target_pairs={{2,4},{6,8},{10,12},{14,16},{18,20},{22,24},{26,28},{4,2},{8,6},{1... | collective-permute-start | bytes 2359304 | tf_op jit(solution)/shard_map/ppermute | solution.py:566
  4.1 0.0 copy-done
  4.1 0.0 copy-done.3
  4.2 0.0 copy-done.2
  4.2 6.1 %shard_map.113 = (bf16[2,2,256,256]{3,2,1,0:T(8,128)(2,1)S(1)}, bf16[2,2,256,256]{3,2,1,0:T(8,128)(2,1)S(1)}, bf16[2,2,256,256]{3,2,1,0:T(8,128)(2,1)S(1)}, f32[...) custom-call(bf16[2,2,2,256,256]{4,3,2,1,0:T(8,128)(2,1)} %down.3, ...), custom_call_target="tpu_custom_call" | custom-call | tf_op jit(solution)/shard_map/pallas_call | solution.py:568
  10.3 0.0 collective-permute-done.partner
  10.3 0.0 copy-start.1
  10.3 2.8 %shard_map.114 = (bf16[2,2,256,256]{3,2,1,0:T(8,128)(2,1)S(1)}, bf16[2,2,256,256]{3,2,1,0:T(8,128)(2,1)S(1)}, bf16[2,2,128,256]{3,2,1,0:T(8,128)(2,1)S(1)}, bf16[2,2,128,256]{3,2,1,0:T(8,128)(2,1)S(1)}) custom-call(bf16[2,2,256,256]{3,2,1,0:T(8,128)(2,1)S(1)} %collective-permute-done.partner, bf16[2,2,256,256]{3,2,1,0:T(8,128)(2,1)S(1)} %get-tuple-element.29.q_in_outer, ...), custom_call_target="tpu_custom_call" | custom-call | tf_op jit(solution)/shard_map/pallas_call | solution.py:581
  13.1 1.7 %collective-permute-start.3 = (bf16[2,2,256,256]{3,2,1,0:T(8,128)(2,1)S(1)}, bf16[2,2,256,256]{3,2,1,0:T(8,128)(2,1)S(1)}, u32[]{:S(2)}, u32[]{:S(2)}) collective-permute-start(bf16[2,2,256,256]{3,2,1,0:T(8,128)(2,1)S(1)} %get-tuple-element.34), channel_id=1, source_target_pairs={{0,2},{2,0},{4,6},{6,4},{8,10},{10,8},{12,14},{14,12},{16,18},{18,... | collective-permute-start | bytes 1572872 | tf_op jit(solution)/shard_map/ppermute | solution.py:584
  14.9 2.2 %collective-permute-start.4 = (bf16[2,2,256,256]{3,2,1,0:T(8,128)(2,1)S(1)}, bf16[2,2,256,256]{3,2,1,0:T(8,128)(2,1)S(1)}, u32[]{:S(2)}, u32[]{:S(2)}) collective-permute-start(bf16[2,2,256,256]{3,2,1,0:T(8,128)(2,1)S(1)} %get-tuple-element.40), channel_id=1, source_target_pairs={{2,4},{6,8},{10,12},{14,16},{18,20},{22,24},{26,28},{4,2},{8,6},{1... | collective-permute-start | bytes 1572872 | tf_op jit(solution)/shard_map/ppermute | solution.py:580
  17.1 12.5 %collective-permute-done.2.arrived = bf16[3,2,256,256]{3,2,1,0:T(8,128)(2,1)S(1)} collective-permute-done((bf16[3,2,256,256]{3,2,1,0:T(8,128)(2,1)S(1)}, bf16[3,2,256,256]{3,2,1,0:T(8,128)(2,1)S(1)}, u32[]{:S(2)}, u32[]{:S(2)}) %collective-permute-start.2) | collective-permute-done | bytes 786464 | tf_op jit(solution)/shard_map/ppermute | solution.py:566
  29.6 0.0 collective-permute-done.3.partner
  29.6 0.0 copy-done.1
  29.6 6.2 %shard_map.115 = (bf16[2,2,256,256]{3,2,1,0:T(8,128)(2,1)S(1)}, bf16[2,2,256,256]{3,2,1,0:T(8,128)(2,1)S(1)}, bf16[2,2,256,256]{3,2,1,0:T(8,128)(2,1)S(1)}, bf16...) custom-call(bf16[3,2,256,256]{3,2,1,0:T(8,128)(2,1)S(1)} %collective-permute-done.2.arrived, ...), custom_call_target="tpu_custom_call" | custom-call | tf_op jit(solution)/shard_map/pallas_call | solution.py:587
  35.8 0.1 collective-permute-start.5
  35.9 1.9 %collective-permute-start.6 = (bf16[2,2,128,256]{3,2,1,0:T(8,128)(2,1)S(1)}, bf16[2,2,128,256]{3,2,1,0:T(8,128)(2,1)S(1)}, u32[]{:S(2)}, u32[]{:S(2)}) collective-permute-start(bf16[2,2,128,256]{3,2,1,0:T(8,128)(2,1)S(1)} %get-tuple-element.45), channel_id=1, source_target_pairs={{2,4},{6,8},{10,12},{14,16},{18,20},{22,24},{26,28},{4,2},{8,6},{1... | collective-permute-start | bytes 786440 | tf_op jit(solution)/shard_map/ppermute | solution.py:585
  37.8 3.6 %collective-permute-start.1 = (bf16[2,2,128,256]{3,2,1,0:T(8,128)(2,1)S(1)}, bf16[2,2,128,256]{3,2,1,0:T(8,128)(2,1)S(1)}, u32[]{:S(2)}, u32[]{:S(2)}) collective-permute-start(bf16[2,2,128,256]{3,2,1,0:T(8,128)(2,1)S(1)} %get-tuple-element.33), channel_id=1, source_target_pairs={{2,4},{6,8},{10,12},{14,16},{18,20},{22,24},{26,28},{4,2},{8,6},{1... | collective-permute-start | bytes 786440 | tf_op jit(solution)/shard_map/ppermute | solution.py:586
  41.5 0.0 collective-permute-done.4.second
  41.5 0.0 collective-permute-done.5.partner
  41.5 2.1 %shard_map.116 = (bf16[2,2,256,256]{3,2,1,0:T(8,128)(2,1)S(1)}, bf16[2,2,256,256]{3,2,1,0:T(8,128)(2,1)S(1)}, f32[256,256]{1,0:T(8,128)S(1)}) custom-call(bf16[2,2,256,256]{3,2,1,0:T(8,128)(2,1)S(1)} %collective-permute-done.4.second, bf16[2,2,256,256]{3,2,1,0:T(8,128)(2,1)S(1)} %get-tuple-element.41.rest_2, ...), custom_call_target="tpu_custom_call" | custom-call | tf_op jit(solution)/shard_map/pallas_call | solution.py:598
  43.5 5.6 %collective-permute-done.6.last = bf16[2,2,128,256]{3,2,1,0:T(8,128)(2,1)S(1)} collective-permute-done((bf16[2,2,128,256]{3,2,1,0:T(8,128)(2,1)S(1)}, bf16[2,2,128,256]{3,2,1,0:T(8,128)(2,1)S(1)}, u32[]{:S(2)}, u32[]{:S(2)}) %collective-permute-start.6) | collective-permute-done | bytes 262176 | tf_op jit(solution)/shard_map/ppermute | solution.py:585
  49.2 1.2 %shard_map.117 = (bf16[2,2,2,256,256]{4,3,2,1,0:T(8,128)(2,1)}, bf16[2,2,2,256,256]{4,3,2,1,0:T(8,128)(2,1)}, bf16[2,128,256]{2,1,0:T(8,128)(2,1)S(1)}) custom-call(bf16[2,2,128,256]{3,2,1,0:T(8,128)(2,1)S(1)} %collective-permute-done.6.last, bf16[2,2,256,256]{3,2,1,0:T(8,128)(2,1)S(1)} %get-tuple-element.37.q_arrived, ...), custom_call_target="tpu_custom_call" | custom-call | tf_op jit(solution)/shard_map/pallas_call | solution.py:605
  50.4 1.6 %collective-permute-start.7 = (bf16[2,128,256]{2,1,0:T(8,128)(2,1)S(1)}, bf16[2,128,256]{2,1,0:T(8,128)(2,1)S(1)}, u32[]{:S(2)}, u32[]{:S(2)}) collective-permute-start(bf16[2,128,256]{2,1,0:T(8,128)(2,1)S(1)} %get-tuple-element.48), channel_id=1, source_target_pairs={{0,1},{1,0},{2,3},{3,2},{4,5},{5,4},{6,7},{7,6},{8,9},{9,8},{10,11... | collective-permute-start | bytes 393224 | tf_op jit(solution)/shard_map/ppermute | solution.py:612
  51.9 0.1 collective-permute-done.1.last
  52.0 3.4 %collective-permute-done.7.other = bf16[2,128,256]{2,1,0:T(8,128)(2,1)S(1)} collective-permute-done((bf16[2,128,256]{2,1,0:T(8,128)(2,1)S(1)}, bf16[2,128,256]{2,1,0:T(8,128)(2,1)S(1)}, u32[]{:S(2)}, u32[]{:S(2)}) %collective-permute-start.7) | collective-permute-done | bytes 131104 | tf_op jit(solution)/shard_map/ppermute | solution.py:612
  55.4 1.2 %shard_map.118 = (bf16[2,2,2,256,256]{4,3,2,1,0:T(8,128)(2,1)}, bf16[2,2,2,256,256]{4,3,2,1,0:T(8,128)(2,1)}, f32[2,128,256]{2,1,0:T(8,128)}) custom-call(bf16[2,2,128,256]{3,2,1,0:T(8,128)(2,1)S(1)} %collective-permute-done.1.last, bf16[2,2,256,256]{3,2,1,0:T(8,128)(2,1)S(1)} %get-tuple-element.37.q_arrived, ...), custom_call_target="tpu_custom_call", output_to_operand_aliasing={{0}: (8, {}), {1}: (9, {})} | custom-call | tf_op jit(solution)/shard_map/pallas_call | solution.py:613
Async XLA Ops:
  0.6 3.5 %copy-start = (bf16[256,256]{1,0:T(8,128)(2,1)S(1)}, bf16[256,256]{1,0:T(8,128)(2,1)}, u32[]{:S(2)}) copy-start(bf16[256,256]{1,0:T(8,128)(2,1)} %constant.2.clone.hx.hy) | copy-start | bytes 393220
  0.6 3.5 %copy-start.3 = (s32[2]{0:T(128)S(1)}, s32[2]{0:T(128)}, u32[]{:S(2)}) copy-start(s32[2]{0:T(128)} %freq.3) | copy-start | bytes 28
  0.7 3.5 %copy-start.2 = (f32[16]{0:T(128)S(1)}, f32[16]{0:T(128)}, u32[]{:S(2)}) copy-start(f32[16]{0:T(128)} %slowness.3) | copy-start | bytes 196
  2.1 8.2 %collective-permute-start = (bf16[2,2,256,256]{3,2,1,0:T(8,128)(2,1)S(1)}, bf16[2,2,256,256]{3,2,1,0:T(8,128)(2,1)S(1)}, u32[]{:S(2)}, u32[]{:S(2)}) collective-permute-start(bf16[2,2,256,256]{3,2,1,0:T(8,128)(2,1)S(1)} %get-tuple-element.27), channel_id=1, source_target_pairs={{0,2},{2,0},{4,6},{6,4},{8,10},{10,8},{12,14},{14,12},{16,18},{18,... | collective-permute-start | bytes 1572872 | tf_op jit(solution)/shard_map/ppermute | solution.py:567
  2.2 27.4 %collective-permute-start.2 = (bf16[3,2,256,256]{3,2,1,0:T(8,128)(2,1)S(1)}, bf16[3,2,256,256]{3,2,1,0:T(8,128)(2,1)S(1)}, u32[]{:S(2)}, u32[]{:S(2)}) collective-permute-start(bf16[3,2,256,256]{3,2,1,0:T(8,128)(2,1)S(1)} %get-tuple-element.28.parcel), channel_id=1, source_target_pairs={{2,4},{6,8},{10,12},{14,16},{18,20},{22,24},{26,28},{4,2},{8,6},{1... | collective-permute-start | bytes 2359304 | tf_op jit(solution)/shard_map/ppermute | solution.py:566
  10.3 19.3 %copy-start.1 = (bf16[2,2,256,256]{3,2,1,0:T(8,128)(2,1)S(1)}, bf16[2,2,256,256]{3,2,1,0:T(8,128)(2,1)}, u32[]{:S(2)}) copy-start(bf16[2,2,256,256]{3,2,1,0:T(8,128)(2,1)} %source.1) | copy-start | bytes 1572868
  13.1 16.4 %collective-permute-start.3 = (bf16[2,2,256,256]{3,2,1,0:T(8,128)(2,1)S(1)}, bf16[2,2,256,256]{3,2,1,0:T(8,128)(2,1)S(1)}, u32[]{:S(2)}, u32[]{:S(2)}) collective-permute-start(bf16[2,2,256,256]{3,2,1,0:T(8,128)(2,1)S(1)} %get-tuple-element.34), channel_id=1, source_target_pairs={{0,2},{2,0},{4,6},{6,4},{8,10},{10,8},{12,14},{14,12},{16,18},{18,... | collective-permute-start | bytes 1572872 | tf_op jit(solution)/shard_map/ppermute | solution.py:584
  14.9 26.6 %collective-permute-start.4 = (bf16[2,2,256,256]{3,2,1,0:T(8,128)(2,1)S(1)}, bf16[2,2,256,256]{3,2,1,0:T(8,128)(2,1)S(1)}, u32[]{:S(2)}, u32[]{:S(2)}) collective-permute-start(bf16[2,2,256,256]{3,2,1,0:T(8,128)(2,1)S(1)} %get-tuple-element.40), channel_id=1, source_target_pairs={{2,4},{6,8},{10,12},{14,16},{18,20},{22,24},{26,28},{4,2},{8,6},{1... | collective-permute-start | bytes 1572872 | tf_op jit(solution)/shard_map/ppermute | solution.py:580
  35.8 5.7 %collective-permute-start.5 = (bf16[2,2,256,256]{3,2,1,0:T(8,128)(2,1)S(1)}, bf16[2,2,256,256]{3,2,1,0:T(8,128)(2,1)S(1)}, u32[]{:S(2)}, u32[]{:S(2)}) collective-permute-start(bf16[2,2,256,256]{3,2,1,0:T(8,128)(2,1)S(1)} %get-tuple-element.43), channel_id=1, source_target_pairs={{0,2},{2,0},{4,6},{6,4},{8,10},{10,8},{12,14},{14,12},{16,18},{18,... | collective-permute-start | bytes 1572872 | tf_op jit(solution)/shard_map/ppermute | solution.py:597
  35.9 13.3 %collective-permute-start.6 = (bf16[2,2,128,256]{3,2,1,0:T(8,128)(2,1)S(1)}, bf16[2,2,128,256]{3,2,1,0:T(8,128)(2,1)S(1)}, u32[]{:S(2)}, u32[]{:S(2)}) collective-permute-start(bf16[2,2,128,256]{3,2,1,0:T(8,128)(2,1)S(1)} %get-tuple-element.45), channel_id=1, source_target_pairs={{2,4},{6,8},{10,12},{14,16},{18,20},{22,24},{26,28},{4,2},{8,6},{1... | collective-permute-start | bytes 786440 | tf_op jit(solution)/shard_map/ppermute | solution.py:585
  37.8 14.2 %collective-permute-start.1 = (bf16[2,2,128,256]{3,2,1,0:T(8,128)(2,1)S(1)}, bf16[2,2,128,256]{3,2,1,0:T(8,128)(2,1)S(1)}, u32[]{:S(2)}, u32[]{:S(2)}) collective-permute-start(bf16[2,2,128,256]{3,2,1,0:T(8,128)(2,1)S(1)} %get-tuple-element.33), channel_id=1, source_target_pairs={{2,4},{6,8},{10,12},{14,16},{18,20},{22,24},{26,28},{4,2},{8,6},{1... | collective-permute-start | bytes 786440 | tf_op jit(solution)/shard_map/ppermute | solution.py:586
  50.4 5.0 %collective-permute-start.7 = (bf16[2,128,256]{2,1,0:T(8,128)(2,1)S(1)}, bf16[2,128,256]{2,1,0:T(8,128)(2,1)S(1)}, u32[]{:S(2)}, u32[]{:S(2)}) collective-permute-start(bf16[2,128,256]{2,1,0:T(8,128)(2,1)S(1)} %get-tuple-element.48), channel_id=1, source_target_pairs={{0,1},{1,0},{2,3},{3,2},{4,5},{5,4},{6,7},{7,6},{8,9},{9,8},{10,11... | collective-permute-start | bytes 393224 | tf_op jit(solution)/shard_map/ppermute | solution.py:612

commit v3 on v2

--- a/solution.py
+++ b/solution.py
@@ -189,19 +189,31 @@
     target[1] = imag_part.astype(BF16)
 
 
+def half_rows(of, half):
+    shot = lax.rem(lax.axis_index("shot"), 2)
+    return pl.ds(pl.multiple_of((shot if of == 0 else 1 - shot) * half, half), half)
+
+
+def joined(mine, other):
+    shot = lax.rem(lax.axis_index("shot"), 2)
+    return jnp.concatenate([jnp.where(shot == 0, mine, other), jnp.where(shot == 0, other, mine)], axis=0)
+
+
 def edges_kernel(down, up, reflect, classes_in, parcel, inward_inner, refl, klass, sems):
     levels = down.shape[0]
     fronts = inward_inner.shape[0]
+    half = refl.shape[0]
     odd = odd_place()
-    outward_outer = parcel.at[pl.ds(0, fronts)]
+    rows = half_rows(0, half)
 
     def fetch(first, second):
-        pltpu.make_async_copy(first, outward_outer, sems.at[0]).start()
+        for front in range(fronts):
+            pltpu.make_async_copy(first.at[front], parcel.at[pl.ds(2 * front, 2)], sems.at[0]).start()
         pltpu.make_async_copy(second, inward_inner, sems.at[1]).start()
 
     fixed = [
-        pltpu.make_async_copy(reflect.at[odd], refl, sems.at[2]),
-        pltpu.make_async_copy(classes_in.at[odd], klass, sems.at[3]),
+        pltpu.make_async_copy(reflect.at[odd, rows], refl, sems.at[2]),
+        pltpu.make_async_copy(classes_in.at[odd, rows], klass, sems.at[3]),
     ]
     for copy in fixed:
         copy.start()
@@ -216,8 +228,10 @@
 
     for copy in fixed:
         copy.wait()
-    put(parcel.at[fronts], jnp.where(odd == 0, 1.0, -1.0).astype(F32) * refl[...], klass[...])
-    pltpu.make_async_copy(up.at[0], outward_outer, sems.at[0]).wait()
+    parcel[2 * fronts, :half] = (jnp.where(odd == 0, 1.0, -1.0).astype(F32) * refl[...]).astype(BF16)
+    parcel[2 * fronts, half:] = klass[...].astype(BF16)
+    for front in range(fronts):
+        pltpu.make_async_copy(up.at[0, front], parcel.at[pl.ds(2 * front, 2)], sems.at[0]).wait()
     pltpu.make_async_copy(up.at[0], inward_inner, sems.at[1]).wait()
 
 
@@ -253,8 +267,8 @@
 
 
 def setup_kernel(
-    down, up, reflect, classes_in, slowness, freq, parcel, hx, hy,
-    q_out_inner, q_in_outer, q_out_outer, screen, phase, refl, second,
+    down, up, reflect, classes_in, slowness, freq, hx, hy,
+    q_out_inner, q_in_outer, screen, phase, refl,
     fields, klass, work, sems,
 ):
     fronts = q_out_inner.shape[0]
@@ -310,9 +324,6 @@
     jobs = [(fields.at[1, front], front, q_out_inner.at[front]) for front in range(fronts)]
     jobs += [(fields.at[0, front], front, q_in_outer.at[front]) for front in range(fronts)]
     spread(jobs, work, hx, hy, phase)
-    jobs = leaving(q_out_inner, refl, screen, fields.at[0], second)
-    jobs += [(parcel.at[front], front, q_out_outer.at[front]) for front in range(fronts)]
-    spread(jobs, work, hx, hy, phase)
 
 
 def leaving(q_out_inner, refl, screen, field, target):
@@ -326,40 +337,45 @@
 
 
 def ahead_kernel(
-    partner, q_in_outer, screen, refl, phase, hx, hy,
-    inward_inner, q_out_inner, last_far, last_near,
-    field, third, work,
+    partner, parcel, q_in_outer, q_out_inner, screen, refl, phase, hx, hy,
+    inward_inner, q_out_inner_next, q_out_outer, second, last,
+    field, other_field, q_field, work,
 ):
-    fronts = partner.shape[0]
-    half = partner.shape[2] // 2
-    far_bottom = lax.axis_index("shot") % 2 == 0
-    spread([(partner.at[front], front, third.at[front]) for front in range(fronts)], work, hx, hy, phase)
-    for front in range(fronts):
+    fronts, _, rows_x, _ = partner.shape
+    everyone = range(fronts)
+    half = rows_x // 2
+    far_bottom = lax.rem(lax.axis_index("shot"), 2) == 0
+    jobs = leaving(q_out_inner, refl, screen, field, second.at[:, :, pl.ds(0, rows_x)])
+    jobs += [(partner.at[front], front, q_field.at[front]) for front in everyone]
+    spread(jobs, work, hx, hy, phase)
+    for front in everyone:
         in_re, in_im, out_re, out_im = mixed(
-            q_in_outer[front, 0], q_in_outer[front, 1], third[front, 0], third[front, 1],
+            q_in_outer[front, 0], q_in_outer[front, 1], q_field[front, 0], q_field[front, 1],
             refl[1], screen[1, front, 0], screen[1, front, 1],
         )
         put(inward_inner.at[front], in_re, in_im)
-        put(field.at[front], out_re, out_im)
-    spread([(field.at[front], front, q_out_inner.at[front]) for front in range(fronts)], work, hx, hy, phase)
-    spread(leaving(q_out_inner, refl, screen, field, third), work, hx, hy, phase)
-    for front in range(fronts):
+        put(other_field.at[front], out_re, out_im)
+    jobs = [(other_field.at[front], front, q_out_inner_next.at[front]) for front in everyone]
+    jobs += [(parcel.at[pl.ds(2 * front, 2)], front, q_out_outer.at[front]) for front in everyone]
+    spread(jobs, work, hx, hy, phase)
+    spread(leaving(q_out_inner_next, refl, screen, field, q_field), work, hx, hy, phase)
+    for front in everyone:
         for part in range(2):
-            top, bottom = third[front, part, :half], third[front, part, half:]
-            last_far[front, part] = jnp.where(far_bottom, bottom, top)
-            last_near[front, part] = jnp.where(far_bottom, top, bottom)
+            top, bottom = q_field[front, part, :half], q_field[front, part, half:]
+            second[front, part, rows_x:] = jnp.where(far_bottom, bottom, top)
+            last[front, part] = jnp.where(far_bottom, top, bottom)
 
 
 def edge_kernel(
-    arrived, source, partner, q_out_inner, q_out_outer, slowness, freq, screen, refl, phase, hx, hy,
-    inward_inner, q_arrived, q_out_inner_next, rest_2, rest_3,
-    inward, outward, q_partner, q_inward, q_outward, work,
+    arrived, source, partner, q_out_inner, screen, refl, phase, hx, hy,
+    inward_inner, out_inner, q_arrived, q_out_outer,
+    inward, outward, q_partner, q_inward, work,
 ):
     fronts = partner.shape[0]
     everyone = range(fronts)
     first = lax.axis_index("depth") == 0
     for front in everyone:
-        put(inward.at[front], *(jnp.where(first, source[front, part], arrived[front, part]) for part in range(2)))
+        put(inward.at[front], *(jnp.where(first, source[front, part], arrived[2 * front + part]) for part in range(2)))
     jobs = [(inward.at[front], front, q_arrived.at[front]) for front in everyone]
     jobs += [(partner.at[front], front, q_partner.at[front]) for front in everyone]
     spread(jobs, work, hx, hy, phase)
@@ -371,35 +387,51 @@
         put(inward.at[front], in_re, in_im)
         put(outward.at[front], out_re, out_im)
     jobs = [(inward.at[front], front, q_inward.at[front]) for front in everyone]
-    jobs += [(outward.at[front], front, q_outward.at[front]) for front in everyone]
+    jobs += [(outward.at[front], front, q_out_outer.at[front]) for front in everyone]
     spread(jobs, work, hx, hy, phase)
-    refl_beyond = arrived[fronts, 0].astype(F32)
-    klass = arrived[fronts, 1].astype(F32).astype(jnp.int32)
     for front in everyone:
         in_re, in_im, out_re, out_im = mixed(
             q_inward[front, 0], q_inward[front, 1], q_partner[front, 0], q_partner[front, 1],
             refl[1], screen[1, front, 0], screen[1, front, 1],
         )
         put(inward_inner.at[front], in_re, in_im)
-        put(inward.at[front], out_re, out_im)
+        put(out_inner.at[front], out_re, out_im)
+
+
+def beyond_kernel(
+    mine, other, out_inner, q_out_outer_0, q_out_outer_1, slowness, freq, phase, hx, hy,
+    q_out_inner, rest_2, rest_3,
+    field_2, field_3, work,
+):
+    fronts = out_inner.shape[0]
+    everyone = range(fronts)
+    half = mine.shape[0] // 2
+    refl_beyond = joined(mine[:half], other[:half]).astype(F32)
+    klass = joined(mine[half:], other[half:]).astype(F32).astype(jnp.int32)
+    for front in everyone:
         cos_row, sin_row = class_rows(slowness, front_wave(freq, front), (8, 128))
         back_re = refl_beyond * look_up(cos_row, klass)
         back_im = refl_beyond * look_up(sin_row, klass)
-        for known, target in ((q_out_outer, q_inward), (q_outward, q_partner)):
+        for known, target in ((q_out_outer_0, field_2), (q_out_outer_1, field_3)):
             known_re, known_im = (known[front, part].astype(F32) for part in range(2))
             put(target.at[front], *screened(known_re, known_im, back_re, back_im))
-    jobs = [(inward.at[front], front, q_out_inner_next.at[front]) for front in everyone]
-    jobs += [(q_inward.at[front], front, rest_2.at[front]) for front in everyone]
-    jobs += [(q_partner.at[front], front, rest_3.at[front]) for front in everyone]
+    jobs = [(out_inner.at[front], front, q_out_inner.at[front]) for front in everyone]
+    jobs += [(field_2.at[front], front, rest_2.at[front]) for front in everyone]
+    jobs += [(field_3.at[front], front, rest_3.at[front]) for front in everyone]
     spread(jobs, work, hx, hy, phase)
 
 
+def partner_kernel(partner, phase, hx, hy, q_partner, work):
+    fronts = partner.shape[0]
+    spread([(partner.at[front], front, q_partner.at[front]) for front in range(fronts)], work, hx, hy, phase)
+
+
 def inner_kernel(
-    second, rest_2, q_arrived, q_out_inner, partner, screen, refl, phase, hx, hy,
-    inward, outward, terms,
-    field, q_partner, q_inward, work,
+    second, rest_2, rest_3, q_arrived, q_out_inner_1, q_out_inner_2, q_partner, screen, refl, phase, hx, hy,
+    inward, outward, far_inward, far_outward, terms, inner_terms,
+    field, q_inward, work,
 ):
-    fronts = partner.shape[0]
+    fronts, _, rows_x, _ = q_partner.shape
     everyone = range(fronts)
     first = lax.axis_index("depth") == 0
     for front in everyone:
@@ -407,18 +439,21 @@
             jnp.where(
                 first,
                 q_arrived[front, part].astype(F32),
-                second[front, part].astype(F32) + rest_2[front, part].astype(F32),
+                second[front, part, :rows_x].astype(F32) + rest_2[front, part].astype(F32),
             )
             for part in range(2)
         )
         in_re, in_im, _, _ = mixed(
-            a_re, a_im, q_out_inner[front, 0], q_out_inner[front, 1],
+            a_re, a_im, q_out_inner_1[front, 0], q_out_inner_1[front, 1],
             refl[0], screen[0, front, 0], screen[0, front, 1],
         )
         put(field.at[front], in_re, in_im)
-    jobs = [(field.at[front], front, q_inward.at[front]) for front in everyone]
-    jobs += [(partner.at[front], front, q_partner.at[front]) for front in everyone]
-    spread(jobs, work, hx, hy, phase)
+    spread([(field.at[front], front, q_inward.at[front]) for front in everyone], work, hx, hy, phase)
+    rows, total = outer_rows(
+        1, second.at[:, :, pl.ds(rows_x, rows_x // 2)], q_arrived, rest_3, q_out_inner_2, screen, refl,
+        far_inward, far_outward,
+    )
+    terms[0] = total.astype(BF16)
     total = None
     for front in everyone:
         a_re, a_im = (q_inward[front, part].astype(F32) for part in range(2))
@@ -430,14 +465,14 @@
         put(outward.at[front], out_re, out_im)
         term = a_re * b_re + a_im * b_im
         total = term if total is None else total + term
-    terms[...] = total
-
-
-def outer_rows(near, last, q_arrived, rest, q_out_inner, screen, refl, inward, outward):
+    inner_terms[...] = total
+    terms[1] = inner_terms[rows, :].astype(BF16)
+
+
+def outer_rows(of, last, q_arrived, rest, q_out_inner, screen, refl, inward, outward, ready=None):
     fronts, _, half, _ = last.shape
     first = lax.axis_index("depth") == 0
-    shot = lax.axis_index("shot") % 2
-    rows = pl.ds(pl.multiple_of((shot if near else 1 - shot) * half, half), half)
+    rows = half_rows(of, half)
     total = None
     for front in range(fronts):
         a_re, a_im = (
@@ -481,17 +516,10 @@
     return copies(0, down_out, up_out)
 
 
-def far_rows_kernel(
-    last, q_arrived, rest, q_out_inner, screen, refl, inner_terms, inner_in, inner_out,
-    down_out, up_out, terms,
-    inward, outward, sems,
-):
-    every_row = pl.ds(0, inner_in.shape[2])
-    waits = send_home(1, every_row, inner_in, inner_out, down_out, up_out, sems.at[1])
-    rows, total = outer_rows(False, last, q_arrived, rest, q_out_inner, screen, refl, inward, outward)
-    waits += send_home(0, rows, inward, outward, down_out, up_out, sems.at[0])
-    terms[0] = total.astype(BF16)
-    terms[1] = inner_terms[rows, :].astype(BF16)
+def home_kernel(inward, outward, far_inward, far_outward, down_out, up_out, sems):
+    rows_x, half = inward.shape[2], far_inward.shape[2]
+    waits = send_home(1, pl.ds(0, rows_x), inward, outward, down_out, up_out, sems.at[0])
+    waits += send_home(0, half_rows(1, half), far_inward, far_outward, down_out, up_out, sems.at[1])
     for copy in waits:
         copy.wait()
 
@@ -502,7 +530,7 @@
     inward, outward, sums, sems,
 ):
     del down_in, up_in
-    rows, total = outer_rows(True, last, q_arrived, rest, q_out_inner, screen, refl, inward, outward)
+    rows, total = outer_rows(0, last, q_arrived, rest, q_out_inner, screen, refl, inward, outward)
     waits = send_home(0, rows, inward, outward, down_out, up_out, sems.at[0])
     odd = odd_place()
     sums[odd] = scale * (total + other[0].astype(F32))
@@ -517,7 +545,7 @@
     depth = lax.axis_size("depth")
     shots = lax.axis_size("shot")
     levels, fronts, parts, rows_x, rows_y = down_state.shape
-    if levels != 2 or depth % 2 or shots != 2 or HOPS != 3:
+    if levels != 2 or depth % 2 or shots % 2 or HOPS != 3:
         return per_device_plain(down_state, up_state, source, reflect, screen_class, screen_values, freq_index)
     scale = 1.0 / math.sqrt(fronts * shots)
     half = rows_x // 2
@@ -527,7 +555,7 @@
     beyond = [(i, i + 1) for i in range(1, depth - 1, 2)] + [(i + 1, i) for i in range(1, depth - 1, 2)]
     to_partner = functools.partial(lax.ppermute, axis_name="depth", perm=partners)
     to_beyond = functools.partial(lax.ppermute, axis_name="depth", perm=beyond)
-    across = functools.partial(lax.ppermute, axis_name="shot", perm=[(0, 1), (1, 0)])
+    across = functools.partial(lax.ppermute, axis_name="shot", perm=[(i, i ^ 1) for i in range(shots)])
     plane = jax.ShapeDtypeStruct((fronts, parts, rows_x, rows_y), BF16)
     half_plane = jax.ShapeDtypeStruct((fronts, parts, half, rows_y), BF16)
     pair = jax.ShapeDtypeStruct((2, rows_x, rows_y), F32)
@@ -560,56 +588,62 @@
         edges_kernel,
         [HBM] * 4,
         [VMEM] * 2,
-        [jax.ShapeDtypeStruct((fronts + 1, parts, rows_x, rows_y), BF16), plane],
-        [pltpu.VMEM((rows_x, rows_y), F32), pltpu.VMEM((rows_x, rows_y), jnp.int32), dma((4,))],
+        [jax.ShapeDtypeStruct((fronts * parts + 1, rows_x, rows_y), BF16), plane],
+        [pltpu.VMEM((half, rows_y), F32), pltpu.VMEM((half, rows_y), jnp.int32), dma((4,))],
     )(*kept_in_hbm(down_state, up_state, reflect, screen_class))
     arrived = to_beyond(parcel)
     partner_0 = to_partner(in_inner)
-    q_out_inner_0, q_in_outer_0, q_out_outer_0, screen, phase, refl, second = call(
+    q_out_inner_0, q_in_outer_0, screen, phase, refl = call(
         setup_kernel,
-        [HBM] * 4 + [SMEM] * 2 + [VMEM] * 3,
-        [VMEM] * 7,
-        [plane] * 3 + [screens, turns, pair, plane],
+        [HBM] * 4 + [SMEM] * 2 + [VMEM] * 2,
+        [VMEM] * 5,
+        [plane] * 2 + [screens, turns, pair],
         [
             pltpu.VMEM((2, *plane.shape), BF16),
             pltpu.VMEM((2, rows_x, rows_y), jnp.int32),
             work(2 * fronts),
             dma((6,)),
         ],
-    )(*kept_in_hbm(down_state, up_state, reflect, screen_class), screen_values, freq_index, parcel, hx, hy)
+    )(*kept_in_hbm(down_state, up_state, reflect, screen_class), screen_values, freq_index, hx, hy)
+    in_inner_1, q_out_inner_1, q_out_outer_0, second, last = call(
+        ahead_kernel,
+        [VMEM] * 9,
+        [VMEM] * 5,
+        [plane] * 3 + [jax.ShapeDtypeStruct((fronts, parts, rows_x + half, rows_y), BF16), half_plane],
+        buffers(3) + [work(2 * fronts)],
+    )(partner_0, parcel, q_in_outer_0, q_out_inner_0, screen, refl, phase, hx, hy)
+    partner_1 = to_partner(in_inner_1)
     second = to_beyond(second)
-    in_inner_1, q_out_inner_1, last_far, last_near = call(
-        ahead_kernel, [VMEM] * 7, [VMEM] * 4, [plane] * 2 + [half_plane] * 2, buffers(2) + [work(fronts)]
-    )(partner_0, q_in_outer_0, screen, refl, phase, hx, hy)
-    partner_1 = to_partner(in_inner_1)
-    last_far = to_beyond(last_far)
-    last_near = to_beyond(last_near)
-    in_inner_2, q_arrived, q_out_inner_2, rest_2, rest_3 = call(
-        edge_kernel,
-        [VMEM] * 5 + [SMEM] * 2 + [VMEM] * 5,
-        [VMEM] * 5,
-        [plane] * 5,
-        buffers(5) + [work(3 * fronts)],
+    last = to_beyond(last)
+    mine = arrived[fronts * parts]
+    swapped = across(mine)
+    in_inner_2, out_inner_2, q_arrived, q_out_outer_1 = call(
+        edge_kernel, [VMEM] * 9, [VMEM] * 4, [plane] * 4, buffers(4) + [work(2 * fronts)]
+    )(arrived, source, partner_1, q_out_inner_0, screen, refl, phase, hx, hy)
+    partner_2 = to_partner(in_inner_2)
+    q_out_inner_2, rest_2, rest_3 = call(
+        beyond_kernel,
+        [VMEM] * 5 + [SMEM] * 2 + [VMEM] * 3,
+        [VMEM] * 3,
+        [plane] * 3,
+        buffers(2) + [work(3 * fronts)],
+    )(mine, swapped, out_inner_2, q_out_outer_0, q_out_outer_1, screen_values, freq_index, phase, hx, hy)
+    q_partner = call(partner_kernel, [VMEM] * 4, VMEM, plane, [work(fronts)])(partner_2, phase, hx, hy)
+    inner_in, inner_out, far_in, far_out, terms, inner_terms = call(
+        inner_kernel,
+        [VMEM] * 12,
+        [VMEM] * 6,
+        [plane] * 2
+        + [half_plane] * 2
+        + [jax.ShapeDtypeStruct((2, half, rows_y), BF16), jax.ShapeDtypeStruct((rows_x, rows_y), F32)],
+        buffers(2) + [work(fronts)],
     )(
-        arrived, source, partner_1, q_out_inner_0, q_out_outer_0, screen_values, freq_index,
-        screen, refl, phase, hx, hy,
+        second, rest_2, rest_3, q_arrived, q_out_inner_1, q_out_inner_2, q_partner, screen, refl, phase, hx, hy
     )
-    partner_2 = to_partner(in_inner_2)
-    inner_in, inner_out, inner_terms = call(
-        inner_kernel,
-        [VMEM] * 10,
-        [VMEM] * 3,
-        [plane, plane, jax.ShapeDtypeStruct((rows_x, rows_y), F32)],
-        buffers(3) + [work(2 * fronts)],
-    )(second, rest_2, q_arrived, q_out_inner_1, partner_2, screen, refl, phase, hx, hy)
-    down, up, terms = call(
-        far_rows_kernel,
-        [VMEM] * 9,
-        [HBM] * 2 + [VMEM],
-        [state, state, jax.ShapeDtypeStruct((2, half, rows_y), BF16)],
-        buffers(2, half_plane) + [dma((2, 2))],
-    )(last_far, q_arrived, rest_3, q_out_inner_2, screen, refl, inner_terms, inner_in, inner_out)
-    other = across(terms)
+    other = across(terms) if shots == 2 else jnp.zeros_like(terms)
+    down, up = call(home_kernel, [VMEM] * 4, [HBM] * 2, [state] * 2, [dma((2, 2))])(
+        inner_in, inner_out, far_in, far_out
+    )
     down, up, gradient = call(
         functools.partial(near_rows_kernel, scale),
         [VMEM] * 8 + [HBM] * 2,
@@ -617,7 +651,13 @@
         [state, state, jax.ShapeDtypeStruct((2, half, rows_y), F32)],
         buffers(2, half_plane) + [pltpu.VMEM((2, half, rows_y), F32), dma((2, 2))],
         input_output_aliases={8: 0, 9: 1},
-    )(last_near, q_arrived, rest_3, q_out_inner_2, screen, refl, inner_terms, other, down, up)
+    )(last, q_arrived, rest_3, q_out_inner_2, screen, refl, inner_terms, other, down, up)
+    if shots != 2:
+        terms = scale * terms.astype(F32)
+        far = jnp.where(odd_place() == 0, terms, terms[::-1])
+        top = lax.rem(lax.axis_index("shot"), 2) == 0
+        whole = jnp.concatenate([jnp.where(top, gradient, far), jnp.where(top, far, gradient)], axis=1)
+        gradient = lax.psum_scatter(whole.astype(BF16), "shot", scatter_dimension=1, tiled=True).astype(F32)
     return (down, up, gradient)
 
 

time: 57 us -> 52.4 us (0.919)
  the two profiles are of different devices: /device:TPU:4 before, /device:TPU:0 now
where the time goes in v3:
time: 52.4 us; the launch traced here: 52.2 us
  starting transfers between devices  22.9 us (44%)
  Pallas kernels  20.9 us (40%)
  waiting for transfers between devices  7.34 us (14%)
  between operations  0.98 us (2%)
    ppermute x1, starting transfers between devices, per_device(): partner_2 = to_partner(in_inner_2)  13.2 us
    pallas_call x1, Pallas kernels, per_device(): call(setup_kernel, [HBM] * 4 + [SMEM] * 2 + [VMEM] * 2, [VMEM] * 5, [plan...  4.65 us
    ppermute x1, starting transfers between devices, per_device(): partner_1 = to_partner(in_inner_1)  3.93 us
    pallas_call x1, Pallas kernels, per_device(): call(ahead_kernel, [VMEM] * 9, [VMEM] * 5, [plane] * 3 + [jax.ShapeDtypeS...  3.54 us
    ppermute x1, waiting for transfers between devices, per_device(): other = across(terms) if shots == 2 else jnp.zeros_like(terms)  3.43 us
    ppermute x1, waiting for transfers between devices, per_device(): swapped = across(mine)  3.08 us
    pallas_call x1, Pallas kernels, per_device(): call(beyond_kernel, [VMEM] * 5 + [SMEM] * 2 + [VMEM] * 3, [VMEM] * 3, [pl...  2.96 us
    pallas_call x1, Pallas kernels, per_device(): call(edge_kernel, [VMEM] * 9, [VMEM] * 4, [plane] * 4, buffers(4) + [work...  2.95 us
  transfers between devices with their start and end apart: 8, of which 3 were waited for; matrix products, arithmetic and copies ran while one was open for 0% of the time, Pallas kernels for 35%

profile of v3, /device:TPU:0, one launch (start us, length us, event | category | flops | bytes accessed | tf_op | source)
XLA Modules:
  0.0 52.2 jit_solution(10227714836606863084)
XLA Ops:
  0.6 0.0 copy-start
  0.6 0.0 copy-start.3
  0.7 0.0 copy-start.2
  0.7 1.4 %shard_map.112 = (bf16[5,256,256]{2,1,0:T(8,128)(2,1)S(1)}, bf16[2,2,256,256]{3,2,1,0:T(8,128)(2,1)S(1)}) custom-call(bf16[2,2,2,256,256]{4,3,2,1,0:T(8,128)(2,1)} %down.3, bf16[2,2,2,256,256]{4,3,2,1,0:T(8,128)(2,1)} %up.3, f32[2,256,256]{2,1,0:T(8,128)} %reflect.3, s32[2,256,256]{2,1,0:T(8,128)} %classes_in.3), custom_call_target="tpu_custom_call" | custom-call | tf_op jit(solution)/shard_map/pallas_call | solution.py:587
  2.1 0.5 collective-permute-start
  2.6 0.7 %collective-permute-start.2 = (bf16[5,256,256]{2,1,0:T(8,128)(2,1)S(1)}, bf16[5,256,256]{2,1,0:T(8,128)(2,1)S(1)}, u32[]{:S(2)}, u32[]{:S(2)}) collective-permute-start(bf16[5,256,256]{2,1,0:T(8,128)(2,1)S(1)} %get-tuple-element.31.parcel), channel_id=1, source_target_pairs={{2,4},{6,8},{10,12},{14,16},{18,20},{22,24},{26,28},{4,2},{8,6},{1... | collective-permute-start | bytes 1966088 | tf_op jit(solution)/shard_map/ppermute | solution.py:594
  3.3 0.0 copy-done
  3.3 0.0 copy-done.3
  3.3 4.7 %shard_map.113 = (bf16[2,2,256,256]{3,2,1,0:T(8,128)(2,1)S(1)}, bf16[2,2,256,256]{3,2,1,0:T(8,128)(2,1)S(1)}, f32[2,2,2,256,256]{4,3,2,1,0:T(8,128)S(1)}, f32[2,...) custom-call(bf16[2,2,2,256,256]{4,3,2,1,0:T(8,128)(2,1)} %down.3, bf16[2,2,2,256,256]{4,3,2,1,0:T(8,128)(2,1)} %up.3, ...), custom_call_target="tpu_custom_call" | custom-call | tf_op jit(solution)/shard_map/pallas_call | solution.py:596
  8.0 0.0 collective-permute-done.partner
  8.0 0.0 copy-start.1
  8.0 3.5 %shard_map.114 = (bf16[2,2,256,256]{3,2,1,0:T(8,128)(2,1)S(1)}, bf16[2,2,256,256]{3,2,1,0:T(8,128)(2,1)S(1)}, bf16[2,2,256,256]{3,2,1,0:T(8,128)(2,1)S(1)}, bf16...) custom-call(bf16[2,2,256,256]{3,2,1,0:T(8,128)(2,1)S(1)} %collective-permute-done.partner, ...), custom_call_target="tpu_custom_call" | custom-call | tf_op jit(solution)/shard_map/pallas_call | solution.py:608
  11.6 3.9 %collective-permute-start.3 = (bf16[2,2,256,256]{3,2,1,0:T(8,128)(2,1)S(1)}, bf16[2,2,256,256]{3,2,1,0:T(8,128)(2,1)S(1)}, u32[]{:S(2)}, u32[]{:S(2)}) collective-permute-start(bf16[2,2,256,256]{3,2,1,0:T(8,128)(2,1)S(1)} %get-tuple-element.38), channel_id=1, source_target_pairs={{0,2},{2,0},{4,6},{6,4},{8,10},{10,8},{12,14},{14,12},{16,18},{18,... | collective-permute-start | bytes 1572872 | tf_op jit(solution)/shard_map/ppermute | solution.py:615
  15.5 0.7 %collective-permute-start.5 = (bf16[2,2,384,256]{3,2,1,0:T(8,128)(2,1)S(1)}, bf16[2,2,384,256]{3,2,1,0:T(8,128)(2,1)S(1)}, u32[]{:S(2)}, u32[]{:S(2)}) collective-permute-start(bf16[2,2,384,256]{3,2,1,0:T(8,128)(2,1)S(1)} %get-tuple-element.45), channel_id=1, source_target_pairs={{2,4},{6,8},{10,12},{14,16},{18,20},{22,24},{26,28},{4,2},{8,6},{1... | collective-permute-start | bytes 2359304 | tf_op jit(solution)/shard_map/ppermute | solution.py:616
  16.2 0.0 collective-permute-done.2.arrived
  16.2 0.8 %collective-permute-done.3.partner = bf16[2,2,256,256]{3,2,1,0:T(8,128)(2,1)S(1)} collective-permute-done((bf16[2,2,256,256]{3,2,1,0:T(8,128)(2,1)S(1)}, bf16[2,2,256,256]{3,2,1,0:T(8,128)(2,1)S(1)}, u32[]{:S(2)}, u32[]{:S(2)}) %collective-permute-start.3) | collective-permute-done | bytes 524320 | tf_op jit(solution)/shard_map/ppermute | solution.py:615
  17.0 0.0 copy-done.1
  17.0 3.0 %shard_map.115 = (bf16[2,2,256,256]{3,2,1,0:T(8,128)(2,1)S(1)}, bf16[2,2,256,256]{3,2,1,0:T(8,128)(2,1)S(1)}, bf16[2,2,256,256]{3,2,1,0:T(8,128)(2,1)S(1)}, bf16[2,2,256,256]{3,2,1,0:T(8,128)(2,1)S(1)}) custom-call(bf16[5,256,256]{2,1,0:T(8,128)(2,1)S(1)} %collective-permute-done.2.arrived, bf16[2,2,256,256]{3,2,1,0:T(8,128)(2,1)S(1)} %copy-done.1, ...), custom_call_target="tpu_custom_call" | custom-call | tf_op jit(solution)/shard_map/pallas_call | solution.py:620
  20.0 13.2 %collective-permute-start.6 = (bf16[2,2,256,256]{3,2,1,0:T(8,128)(2,1)S(1)}, bf16[2,2,256,256]{3,2,1,0:T(8,128)(2,1)S(1)}, u32[]{:S(2)}, u32[]{:S(2)}) collective-permute-start(bf16[2,2,256,256]{3,2,1,0:T(8,128)(2,1)S(1)} %get-tuple-element.48), channel_id=1, source_target_pairs={{0,2},{2,0},{4,6},{6,4},{8,10},{10,8},{12,14},{14,12},{16,18},{18,... | collective-permute-start | bytes 1572872 | tf_op jit(solution)/shard_map/ppermute | solution.py:623
  33.2 1.6 %collective-permute-start.4 = (bf16[256,256]{1,0:T(8,128)(2,1)S(1)}, bf16[256,256]{1,0:T(8,128)(2,1)S(1)}, u32[]{:S(2)}, u32[]{:S(2)}) collective-permute-start(bf16[256,256]{1,0:T(8,128)(2,1)S(1)} %slice_bitcast_fusion.mine), channel_id=1, source_target_pairs={{0,1},{1,0},{2,3},{3,2},{4,5},{5,4},{6,7},{7,6},{8,9},{9,8},{10,11... | collective-permute-start | bytes 393224 | tf_op jit(solution)/shard_map/ppermute | solution.py:619
  34.7 0.8 %collective-permute-start.1 = (bf16[2,2,128,256]{3,2,1,0:T(8,128)(2,1)S(1)}, bf16[2,2,128,256]{3,2,1,0:T(8,128)(2,1)S(1)}, u32[]{:S(2)}, u32[]{:S(2)}) collective-permute-start(bf16[2,2,128,256]{3,2,1,0:T(8,128)(2,1)S(1)} %get-tuple-element.37), channel_id=1, source_target_pairs={{2,4},{6,8},{10,12},{14,16},{18,20},{22,24},{26,28},{4,2},{8,6},{1... | collective-permute-start | bytes 786440 | tf_op jit(solution)/shard_map/ppermute | solution.py:617
  35.6 3.1 %collective-permute-done.4.other = bf16[256,256]{1,0:T(8,128)(2,1)S(1)} collective-permute-done((bf16[256,256]{1,0:T(8,128)(2,1)S(1)}, bf16[256,256]{1,0:T(8,128)(2,1)S(1)}, u32[]{:S(2)}, u32[]{:S(2)}) %collective-permute-start.4) | collective-permute-done | bytes 131104 | tf_op jit(solution)/shard_map/ppermute | solution.py:619
  38.7 3.0 %shard_map.116 = (bf16[2,2,256,256]{3,2,1,0:T(8,128)(2,1)S(1)}, bf16[2,2,256,256]{3,2,1,0:T(8,128)(2,1)S(1)}, bf16[2,2,256,256]{3,2,1,0:T(8,128)(2,1)S(1)}) custom-call(bf16[256,256]{1,0:T(8,128)(2,1)S(1)} %slice_bitcast_fusion.mine, bf16[256,256]{1,0:T(8,128)(2,1)S(1)} %collective-permute-done.4.other, ...), custom_call_target="tpu_custom_call" | custom-call | tf_op jit(solution)/shard_map/pallas_call | solution.py:624
  41.6 0.0 collective-permute-done.6.partner
  41.6 0.9 %shard_map.117.q_partner = bf16[2,2,256,256]{3,2,1,0:T(8,128)(2,1)S(1)} custom-call(bf16[2,2,256,256]{3,2,1,0:T(8,128)(2,1)S(1)} %collective-permute-done.6.partner, f32[2,2,256,256]{3,2,1,0:T(8,128)S(1)} %get-tuple-element.36.phase, bf16[256,256]{1,0:T(8,128)(2,1)S(1)} %copy-done, bf16[256,256]{1,0:T(8,128)(2,1)S(1)} %copy-done), custom_call_target="tpu_custom_call" | custom-call | tf_op jit(solution)/shard_map/pallas_call | solution.py:631
  42.5 0.0 collective-permute-done.5.second
  42.5 2.2 %shard_map.118 = (bf16[2,2,256,256]{3,2,1,0:T(8,128)(2,1)S(1)}, bf16[2,2,256,256]{3,2,1,0:T(8,128)(2,1)S(1)}, bf16[2,2,128,256]{3,2,1,0:T(8,128)(2,1)S(1)}, bf16...) custom-call(bf16[2,2,384,256]{3,2,1,0:T(8,128)(2,1)S(1)} %collective-permute-done.5.second, ...), custom_call_target="tpu_custom_call" | custom-call | tf_op jit(solution)/shard_map/pallas_call | solution.py:632
  44.7 1.5 %collective-permute-start.7 = (bf16[2,128,256]{2,1,0:T(8,128)(2,1)S(1)}, bf16[2,128,256]{2,1,0:T(8,128)(2,1)S(1)}, u32[]{:S(2)}, u32[]{:S(2)}) collective-permute-start(bf16[2,128,256]{2,1,0:T(8,128)(2,1)S(1)} %get-tuple-element.50), channel_id=1, source_target_pairs={{0,1},{1,0},{2,3},{3,2},{4,5},{5,4},{6,7},{7,6},{8,9},{9,8},{10,11... | collective-permute-start | bytes 393224 | tf_op jit(solution)/shard_map/ppermute | solution.py:643
  46.2 1.2 %shard_map.119 = (bf16[2,2,2,256,256]{4,3,2,1,0:T(8,128)(2,1)}, bf16[2,2,2,256,256]{4,3,2,1,0:T(8,128)(2,1)}) custom-call(bf16[2,2,256,256]{3,2,1,0:T(8,128)(2,1)S(1)} %get-tuple-element.51.inward, bf16[2,2,256,256]{3,2,1,0:T(8,128)(2,1)S(1)} %get-tuple-element.52.outward, bf16[2,2,128,256]{3,2,1,0:T(8,128)(2,1)S(1)} %get-tuple-element.53.far_inward, ...), custom_call_target="tpu_custom_call" | custom-call | tf_op jit(solution)/shard_map/pallas_call | solution.py:644
  47.4 0.0 collective-permute-done.1.last
  47.4 3.4 %collective-permute-done.7.other = bf16[2,128,256]{2,1,0:T(8,128)(2,1)S(1)} collective-permute-done((bf16[2,128,256]{2,1,0:T(8,128)(2,1)S(1)}, bf16[2,128,256]{2,1,0:T(8,128)(2,1)S(1)}, u32[]{:S(2)}, u32[]{:S(2)}) %collective-permute-start.7) | collective-permute-done | bytes 131104 | tf_op jit(solution)/shard_map/ppermute | solution.py:643
  50.9 1.2 %shard_map.120 = (bf16[2,2,2,256,256]{4,3,2,1,0:T(8,128)(2,1)}, bf16[2,2,2,256,256]{4,3,2,1,0:T(8,128)(2,1)}, f32[2,128,256]{2,1,0:T(8,128)}) custom-call(bf16[2,2,128,256]{3,2,1,0:T(8,128)(2,1)S(1)} %collective-permute-done.1.last, bf16[2,2,256,256]{3,2,1,0:T(8,128)(2,1)S(1)} %get-tuple-element.39.q_arrived, ...), custom_call_target="tpu_custom_call", output_to_operand_aliasing={{0}: (8, {}), {1}: (9, {})} | custom-call | tf_op jit(solution)/shard_map/pallas_call | solution.py:647
  (2 shorter events, 0.0 us)
Async XLA Ops:
  0.6 2.7 %copy-start = (bf16[256,256]{1,0:T(8,128)(2,1)S(1)}, bf16[256,256]{1,0:T(8,128)(2,1)}, u32[]{:S(2)}) copy-start(bf16[256,256]{1,0:T(8,128)(2,1)} %constant.2.clone.hx.hy) | copy-start | bytes 393220
  0.6 2.7 %copy-start.3 = (s32[2]{0:T(128)S(1)}, s32[2]{0:T(128)}, u32[]{:S(2)}) copy-start(s32[2]{0:T(128)} %freq.3) | copy-start | bytes 28
  0.7 2.7 %copy-start.2 = (f32[16]{0:T(128)S(1)}, f32[16]{0:T(128)}, u32[]{:S(2)}) copy-start(f32[16]{0:T(128)} %slowness.3) | copy-start | bytes 196
  2.1 5.9 %collective-permute-start = (bf16[2,2,256,256]{3,2,1,0:T(8,128)(2,1)S(1)}, bf16[2,2,256,256]{3,2,1,0:T(8,128)(2,1)S(1)}, u32[]{:S(2)}, u32[]{:S(2)}) collective-permute-start(bf16[2,2,256,256]{3,2,1,0:T(8,128)(2,1)S(1)} %get-tuple-element.30), channel_id=1, source_target_pairs={{0,2},{2,0},{4,6},{6,4},{8,10},{10,8},{12,14},{14,12},{16,18},{18,... | collective-permute-start | bytes 1572872 | tf_op jit(solution)/shard_map/ppermute | solution.py:595
  2.6 13.6 %collective-permute-start.2 = (bf16[5,256,256]{2,1,0:T(8,128)(2,1)S(1)}, bf16[5,256,256]{2,1,0:T(8,128)(2,1)S(1)}, u32[]{:S(2)}, u32[]{:S(2)}) collective-permute-start(bf16[5,256,256]{2,1,0:T(8,128)(2,1)S(1)} %get-tuple-element.31.parcel), channel_id=1, source_target_pairs={{2,4},{6,8},{10,12},{14,16},{18,20},{22,24},{26,28},{4,2},{8,6},{1... | collective-permute-start | bytes 1966088 | tf_op jit(solution)/shard_map/ppermute | solution.py:594
  8.0 9.0 %copy-start.1 = (bf16[2,2,256,256]{3,2,1,0:T(8,128)(2,1)S(1)}, bf16[2,2,256,256]{3,2,1,0:T(8,128)(2,1)}, u32[]{:S(2)}) copy-start(bf16[2,2,256,256]{3,2,1,0:T(8,128)(2,1)} %source.1) | copy-start | bytes 1572868
  11.6 5.5 %collective-permute-start.3 = (bf16[2,2,256,256]{3,2,1,0:T(8,128)(2,1)S(1)}, bf16[2,2,256,256]{3,2,1,0:T(8,128)(2,1)S(1)}, u32[]{:S(2)}, u32[]{:S(2)}) collective-permute-start(bf16[2,2,256,256]{3,2,1,0:T(8,128)(2,1)S(1)} %get-tuple-element.38), channel_id=1, source_target_pairs={{0,2},{2,0},{4,6},{6,4},{8,10},{10,8},{12,14},{14,12},{16,18},{18,... | collective-permute-start | bytes 1572872 | tf_op jit(solution)/shard_map/ppermute | solution.py:615
  15.5 27.0 %collective-permute-start.5 = (bf16[2,2,384,256]{3,2,1,0:T(8,128)(2,1)S(1)}, bf16[2,2,384,256]{3,2,1,0:T(8,128)(2,1)S(1)}, u32[]{:S(2)}, u32[]{:S(2)}) collective-permute-start(bf16[2,2,384,256]{3,2,1,0:T(8,128)(2,1)S(1)} %get-tuple-element.45), channel_id=1, source_target_pairs={{2,4},{6,8},{10,12},{14,16},{18,20},{22,24},{26,28},{4,2},{8,6},{1... | collective-permute-start | bytes 2359304 | tf_op jit(solution)/shard_map/ppermute | solution.py:616
  20.0 21.6 %collective-permute-start.6 = (bf16[2,2,256,256]{3,2,1,0:T(8,128)(2,1)S(1)}, bf16[2,2,256,256]{3,2,1,0:T(8,128)(2,1)S(1)}, u32[]{:S(2)}, u32[]{:S(2)}) collective-permute-start(bf16[2,2,256,256]{3,2,1,0:T(8,128)(2,1)S(1)} %get-tuple-element.48), channel_id=1, source_target_pairs={{0,2},{2,0},{4,6},{6,4},{8,10},{10,8},{12,14},{14,12},{16,18},{18,... | collective-permute-start | bytes 1572872 | tf_op jit(solution)/shard_map/ppermute | solution.py:623
  33.2 5.5 %collective-permute-start.4 = (bf16[256,256]{1,0:T(8,128)(2,1)S(1)}, bf16[256,256]{1,0:T(8,128)(2,1)S(1)}, u32[]{:S(2)}, u32[]{:S(2)}) collective-permute-start(bf16[256,256]{1,0:T(8,128)(2,1)S(1)} %slice_bitcast_fusion.mine), channel_id=1, source_target_pairs={{0,1},{1,0},{2,3},{3,2},{4,5},{5,4},{6,7},{7,6},{8,9},{9,8},{10,11... | collective-permute-start | bytes 393224 | tf_op jit(solution)/shard_map/ppermute | solution.py:619
  34.7 12.7 %collective-permute-start.1 = (bf16[2,2,128,256]{3,2,1,0:T(8,128)(2,1)S(1)}, bf16[2,2,128,256]{3,2,1,0:T(8,128)(2,1)S(1)}, u32[]{:S(2)}, u32[]{:S(2)}) collective-permute-start(bf16[2,2,128,256]{3,2,1,0:T(8,128)(2,1)S(1)} %get-tuple-element.37), channel_id=1, source_target_pairs={{2,4},{6,8},{10,12},{14,16},{18,20},{22,24},{26,28},{4,2},{8,6},{1... | collective-permute-start | bytes 786440 | tf_op jit(solution)/shard_map/ppermute | solution.py:617
  44.7 6.2 %collective-permute-start.7 = (bf16[2,128,256]{2,1,0:T(8,128)(2,1)S(1)}, bf16[2,128,256]{2,1,0:T(8,128)(2,1)S(1)}, u32[]{:S(2)}, u32[]{:S(2)}) collective-permute-start(bf16[2,128,256]{2,1,0:T(8,128)(2,1)S(1)} %get-tuple-element.50), channel_id=1, source_target_pairs={{0,1},{1,0},{2,3},{3,2},{4,5},{5,4},{6,7},{7,6},{8,9},{9,8},{10,11... | collective-permute-start | bytes 393224 | tf_op jit(solution)/shard_map/ppermute | solution.py:643

commit v4 on v3

--- a/solution.py
+++ b/solution.py
@@ -367,10 +367,11 @@
 
 
 def edge_kernel(
-    arrived, source, partner, q_out_inner, screen, refl, phase, hx, hy,
-    inward_inner, out_inner, q_arrived, q_out_outer,
+    arrived, source, partner, q_out_inner, screen, refl, phase, hx, hy, held_in,
+    inward_inner, out_inner, q_arrived, q_out_outer, held_out,
     inward, outward, q_partner, q_inward, work,
 ):
+    del held_in, held_out
     fronts = partner.shape[0]
     everyone = range(fronts)
     first = lax.axis_index("depth") == 0
@@ -399,10 +400,11 @@
 
 
 def beyond_kernel(
-    mine, other, out_inner, q_out_outer_0, q_out_outer_1, slowness, freq, phase, hx, hy,
-    q_out_inner, rest_2, rest_3,
+    mine, other, out_inner, q_out_outer_0, q_out_outer_1, slowness, freq, phase, hx, hy, last_in, inner_in,
+    q_out_inner, rest_2, rest_3, last_out, inner_out,
     field_2, field_3, work,
 ):
+    del last_in, inner_in, last_out, inner_out
     fronts = out_inner.shape[0]
     everyone = range(fronts)
     half = mine.shape[0] // 2
@@ -613,21 +615,30 @@
         buffers(3) + [work(2 * fronts)],
     )(partner_0, parcel, q_in_outer_0, q_out_inner_0, screen, refl, phase, hx, hy)
     partner_1 = to_partner(in_inner_1)
-    second = to_beyond(second)
-    last = to_beyond(last)
     mine = arrived[fronts * parts]
     swapped = across(mine)
-    in_inner_2, out_inner_2, q_arrived, q_out_outer_1 = call(
-        edge_kernel, [VMEM] * 9, [VMEM] * 4, [plane] * 4, buffers(4) + [work(2 * fronts)]
-    )(arrived, source, partner_1, q_out_inner_0, screen, refl, phase, hx, hy)
+    in_inner_2, out_inner_2, q_arrived, q_out_outer_1, second = call(
+        edge_kernel,
+        [VMEM] * 10,
+        [VMEM] * 5,
+        [plane] * 4 + [jax.ShapeDtypeStruct(second.shape, BF16)],
+        buffers(4) + [work(2 * fronts)],
+        input_output_aliases={9: 4},
+    )(arrived, source, partner_1, q_out_inner_0, screen, refl, phase, hx, hy, second)
+    second = to_beyond(second)
+    q_out_inner_2, rest_2, rest_3, last, in_inner_2 = call(
+        beyond_kernel,
+        [VMEM] * 5 + [SMEM] * 2 + [VMEM] * 5,
+        [VMEM] * 5,
+        [plane] * 3 + [half_plane, plane],
+        buffers(2) + [work(3 * fronts)],
+        input_output_aliases={10: 3, 11: 4},
+    )(
+        mine, swapped, out_inner_2, q_out_outer_0, q_out_outer_1, screen_values, freq_index,
+        phase, hx, hy, last, in_inner_2,
+    )
+    last = to_beyond(last)
     partner_2 = to_partner(in_inner_2)
-    q_out_inner_2, rest_2, rest_3 = call(
-        beyond_kernel,
-        [VMEM] * 5 + [SMEM] * 2 + [VMEM] * 3,
-        [VMEM] * 3,
-        [plane] * 3,
-        buffers(2) + [work(3 * fronts)],
-    )(mine, swapped, out_inner_2, q_out_outer_0, q_out_outer_1, screen_values, freq_index, phase, hx, hy)
     q_partner = call(partner_kernel, [VMEM] * 4, VMEM, plane, [work(fronts)])(partner_2, phase, hx, hy)
     inner_in, inner_out, far_in, far_out, terms, inner_terms = call(
         inner_kernel,

time: 52.4 us -> 53.3 us (1.017)
  the two profiles are of different devices: /device:TPU:0 before, /device:TPU:4 now
where the time goes in v4:
time: 53.3 us; the launch traced here: 53.1 us
  Pallas kernels  20.9 us (39%)
  waiting for transfers between devices  19.8 us (37%)
  starting transfers between devices  11.4 us (21%)
  between operations  0.98 us (2%)
    ppermute x1, waiting for transfers between devices, per_device(): arrived = to_beyond(parcel)  7.07 us
    ppermute x1, waiting for transfers between devices, per_device(): second = to_beyond(second)  6.89 us
    pallas_call x1, Pallas kernels, per_device(): call(setup_kernel, [HBM] * 4 + [SMEM] * 2 + [VMEM] * 2, [VMEM] * 5, [plan...  4.65 us
    pallas_call x1, Pallas kernels, per_device(): call(ahead_kernel, [VMEM] * 9, [VMEM] * 5, [plane] * 3 + [jax.ShapeDtypeS...  3.52 us
    ppermute x1, waiting for transfers between devices, per_device(): swapped = across(mine)  3.48 us
    pallas_call x1, Pallas kernels, per_device(): call(edge_kernel, [VMEM] * 10, [VMEM] * 5, [plane] * 4 + [jax.ShapeDtypeS...  2.96 us
    pallas_call x1, Pallas kernels, per_device(): call(beyond_kernel, [VMEM] * 5 + [SMEM] * 2 + [VMEM] * 5, [VMEM] * 5, [pl...  2.95 us
    ppermute x1, starting transfers between devices, per_device(): last = to_beyond(last)  2.49 us
  transfers between devices with their start and end apart: 8, of which 4 were waited for; matrix products, arithmetic and copies ran while one was open for 0% of the time, Pallas kernels for 29%

profile of v4, /device:TPU:4, one launch (start us, length us, event | category | flops | bytes accessed | tf_op | source)
XLA Modules:
  0.0 53.1 jit_solution(3320631775421895310)
XLA Ops:
  0.6 0.0 copy-start
  0.6 0.0 copy-start.2
  0.7 0.0 copy-start.3
  0.7 1.4 %shard_map.112 = (bf16[5,256,256]{2,1,0:T(8,128)(2,1)S(1)}, bf16[2,2,256,256]{3,2,1,0:T(8,128)(2,1)S(1)}) custom-call(bf16[2,2,2,256,256]{4,3,2,1,0:T(8,128)(2,1)} %down.3, bf16[2,2,2,256,256]{4,3,2,1,0:T(8,128)(2,1)} %up.3, f32[2,256,256]{2,1,0:T(8,128)} %reflect.3, s32[2,256,256]{2,1,0:T(8,128)} %classes_in.3), custom_call_target="tpu_custom_call" | custom-call | tf_op jit(solution)/shard_map/pallas_call | solution.py:589
  2.1 0.1 collective-permute-start.2
  2.2 1.9 %collective-permute-start = (bf16[5,256,256]{2,1,0:T(8,128)(2,1)S(1)}, bf16[5,256,256]{2,1,0:T(8,128)(2,1)S(1)}, u32[]{:S(2)}, u32[]{:S(2)}) collective-permute-start(bf16[5,256,256]{2,1,0:T(8,128)(2,1)S(1)} %get-tuple-element.33.parcel), channel_id=1, source_target_pairs={{2,4},{6,8},{10,12},{14,16},{18,20},{22,24},{26,28},{4,2},{8,6},{1... | collective-permute-start | bytes 1966088 | tf_op jit(solution)/shard_map/ppermute | solution.py:596
  4.1 0.0 copy-done
  4.1 0.0 copy-done.2
  4.1 4.7 %shard_map.113 = (bf16[2,2,256,256]{3,2,1,0:T(8,128)(2,1)S(1)}, bf16[2,2,256,256]{3,2,1,0:T(8,128)(2,1)S(1)}, f32[2,2,2,256,256]{4,3,2,1,0:T(8,128)S(1)}, f32[2,...) custom-call(bf16[2,2,2,256,256]{4,3,2,1,0:T(8,128)(2,1)} %down.3, bf16[2,2,2,256,256]{4,3,2,1,0:T(8,128)(2,1)} %up.3, ...), custom_call_target="tpu_custom_call" | custom-call | tf_op jit(solution)/shard_map/pallas_call | solution.py:598
  8.8 0.0 collective-permute-done.2.partner
  8.8 0.0 copy-start.1
  8.8 3.5 %shard_map.114 = (bf16[2,2,256,256]{3,2,1,0:T(8,128)(2,1)S(1)}, bf16[2,2,256,256]{3,2,1,0:T(8,128)(2,1)S(1)}, bf16[2,2,256,256]{3,2,1,0:T(8,128)(2,1)S(1)}, bf16...) custom-call(bf16[2,2,256,256]{3,2,1,0:T(8,128)(2,1)S(1)} %collective-permute-done.2.partner, ...), custom_call_target="tpu_custom_call" | custom-call | tf_op jit(solution)/shard_map/pallas_call | solution.py:610
  12.3 1.7 %collective-permute-start.3 = (bf16[2,2,256,256]{3,2,1,0:T(8,128)(2,1)S(1)}, bf16[2,2,256,256]{3,2,1,0:T(8,128)(2,1)S(1)}, u32[]{:S(2)}, u32[]{:S(2)}) collective-permute-start(bf16[2,2,256,256]{3,2,1,0:T(8,128)(2,1)S(1)} %get-tuple-element.40), channel_id=1, source_target_pairs={{0,2},{2,0},{4,6},{6,4},{8,10},{10,8},{12,14},{14,12},{16,18},{18,... | collective-permute-start | bytes 1572872 | tf_op jit(solution)/shard_map/ppermute | solution.py:617
  14.0 7.1 %collective-permute-done.arrived = bf16[5,256,256]{2,1,0:T(8,128)(2,1)S(1)} collective-permute-done((bf16[5,256,256]{2,1,0:T(8,128)(2,1)S(1)}, bf16[5,256,256]{2,1,0:T(8,128)(2,1)S(1)}, u32[]{:S(2)}, u32[]{:S(2)}) %collective-permute-start) | collective-permute-done | bytes 655392 | tf_op jit(solution)/shard_map/ppermute | solution.py:596
  21.1 0.0 collective-permute-done.3.partner
  21.1 0.0 copy-done.1
  21.1 3.0 %shard_map.115 = (bf16[2,2,256,256]{3,2,1,0:T(8,128)(2,1)S(1)}, bf16[2,2,256,256]{3,2,1,0:T(8,128)(2,1)S(1)}, bf16[2,2,256,256]{3,2,1,0:T(8,128)(2,1)S(1)}, bf16...) custom-call(bf16[5,256,256]{2,1,0:T(8,128)(2,1)S(1)} %collective-permute-done.arrived,, ...), custom_call_target="tpu_custom_call", output_to_operand_aliasing={{4}: (9, {})} | custom-call | tf_op jit(solution)/shard_map/pallas_call | solution.py:620
  24.1 2.1 %collective-permute-start.5 = (bf16[2,2,384,256]{3,2,1,0:T(8,128)(2,1)S(1)}, bf16[2,2,384,256]{3,2,1,0:T(8,128)(2,1)S(1)}, u32[]{:S(2)}, u32[]{:S(2)}) collective-permute-start(bf16[2,2,384,256]{3,2,1,0:T(8,128)(2,1)S(1)} %get-tuple-element.51), channel_id=1, source_target_pairs={{2,4},{6,8},{10,12},{14,16},{18,20},{22,24},{26,28},{4,2},{8,6},{1... | collective-permute-start | bytes 2359304 | tf_op jit(solution)/shard_map/ppermute | solution.py:628
  26.2 1.6 %collective-permute-start.1 = (bf16[256,256]{1,0:T(8,128)(2,1)S(1)}, bf16[256,256]{1,0:T(8,128)(2,1)S(1)}, u32[]{:S(2)}, u32[]{:S(2)}) collective-permute-start(bf16[256,256]{1,0:T(8,128)(2,1)S(1)} %slice_bitcast_fusion.mine), channel_id=1, source_target_pairs={{0,1},{1,0},{2,3},{3,2},{4,5},{5,4},{6,7},{7,6},{8,9},{9,8},{10,11... | collective-permute-start | bytes 393224 | tf_op jit(solution)/shard_map/ppermute | solution.py:619
  27.8 3.5 %collective-permute-done.1.other = bf16[256,256]{1,0:T(8,128)(2,1)S(1)} collective-permute-done((bf16[256,256]{1,0:T(8,128)(2,1)S(1)}, bf16[256,256]{1,0:T(8,128)(2,1)S(1)}, u32[]{:S(2)}, u32[]{:S(2)}) %collective-permute-start.1) | collective-permute-done | bytes 131104 | tf_op jit(solution)/shard_map/ppermute | solution.py:619
  31.2 3.0 %shard_map.116 = (bf16[2,2,256,256]{3,2,1,0:T(8,128)(2,1)S(1)}, bf16[2,2,256,256]{3,2,1,0:T(8,128)(2,1)S(1)}, bf16[2,2,256,256]{3,2,1,0:T(8,128)(2,1)S(1)}, bf16...) custom-call(bf16[256,256]{1,0:T(8,128)(2,1)S(1)} %slice_bitcast_fusion, ...), custom_call_target="tpu_custom_call", output_to_operand_aliasing={{3}: (10, {}), {4}: (11, {})} | custom-call | tf_op jit(solution)/shard_map/pallas_call | solution.py:629
  34.2 0.1 collective-permute-start.6
  34.3 2.5 %collective-permute-start.4 = (bf16[2,2,128,256]{3,2,1,0:T(8,128)(2,1)S(1)}, bf16[2,2,128,256]{3,2,1,0:T(8,128)(2,1)S(1)}, u32[]{:S(2)}, u32[]{:S(2)}) collective-permute-start(bf16[2,2,128,256]{3,2,1,0:T(8,128)(2,1)S(1)} %get-tuple-element.47), channel_id=1, source_target_pairs={{2,4},{6,8},{10,12},{14,16},{18,20},{22,24},{26,28},{4,2},{8,6},{1... | collective-permute-start | bytes 786440 | tf_op jit(solution)/shard_map/ppermute | solution.py:640
  36.8 0.0 collective-permute-done.6.partner
  36.8 0.9 %shard_map.117.q_partner = bf16[2,2,256,256]{3,2,1,0:T(8,128)(2,1)S(1)} custom-call(bf16[2,2,256,256]{3,2,1,0:T(8,128)(2,1)S(1)} %collective-permute-done.6.partner, f32[2,2,256,256]{3,2,1,0:T(8,128)S(1)} %get-tuple-element.39.phase, bf16[256,256]{1,0:T(8,128)(2,1)S(1)} %copy-done, bf16[256,256]{1,0:T(8,128)(2,1)S(1)} %copy-done), custom_call_target="tpu_custom_call" | custom-call | tf_op jit(solution)/shard_map/pallas_call | solution.py:642
  37.6 6.9 %collective-permute-done.5.second = bf16[2,2,384,256]{3,2,1,0:T(8,128)(2,1)S(1)} collective-permute-done((bf16[2,2,384,256]{3,2,1,0:T(8,128)(2,1)S(1)}, bf16[2,2,384,256]{3,2,1,0:T(8,128)(2,1)S(1)}, u32[]{:S(2)}, u32[]{:S(2)}) %collective-permute-start.5) | collective-permute-done | bytes 786464 | tf_op jit(solution)/shard_map/ppermute | solution.py:628
  44.5 2.2 %shard_map.118 = (bf16[2,2,256,256]{3,2,1,0:T(8,128)(2,1)S(1)}, bf16[2,2,256,256]{3,2,1,0:T(8,128)(2,1)S(1)}, bf16[2,2,128,256]{3,2,1,0:T(8,128)(2,1)S(1)}, bf16...) custom-call(bf16[2,2,384,256]{3,2,1,0:T(8,128)(2,1)S(1)} %collective-permute-done.5.second, ...), custom_call_target="tpu_custom_call" | custom-call | tf_op jit(solution)/shard_map/pallas_call | solution.py:643
  46.7 1.5 %collective-permute-start.7 = (bf16[2,128,256]{2,1,0:T(8,128)(2,1)S(1)}, bf16[2,128,256]{2,1,0:T(8,128)(2,1)S(1)}, u32[]{:S(2)}, u32[]{:S(2)}) collective-permute-start(bf16[2,128,256]{2,1,0:T(8,128)(2,1)S(1)} %get-tuple-element.56), channel_id=1, source_target_pairs={{0,1},{1,0},{2,3},{3,2},{4,5},{5,4},{6,7},{7,6},{8,9},{9,8},{10,11... | collective-permute-start | bytes 393224 | tf_op jit(solution)/shard_map/ppermute | solution.py:654
  48.2 1.2 %shard_map.119 = (bf16[2,2,2,256,256]{4,3,2,1,0:T(8,128)(2,1)}, bf16[2,2,2,256,256]{4,3,2,1,0:T(8,128)(2,1)}) custom-call(bf16[2,2,256,256]{3,2,1,0:T(8,128)(2,1)S(1)} %get-tuple-element.57.inward, bf16[2,2,256,256]{3,2,1,0:T(8,128)(2,1)S(1)} %get-tuple-element.58.outward, bf16[2,2,128,256]{3,2,1,0:T(8,128)(2,1)S(1)} %get-tuple-element.59.far_inward, ...), custom_call_target="tpu_custom_call" | custom-call | tf_op jit(solution)/shard_map/pallas_call | solution.py:655
  49.4 0.0 collective-permute-done.4.last
  49.4 2.3 %collective-permute-done.7.other = bf16[2,128,256]{2,1,0:T(8,128)(2,1)S(1)} collective-permute-done((bf16[2,128,256]{2,1,0:T(8,128)(2,1)S(1)}, bf16[2,128,256]{2,1,0:T(8,128)(2,1)S(1)}, u32[]{:S(2)}, u32[]{:S(2)}) %collective-permute-start.7) | collective-permute-done | bytes 131104 | tf_op jit(solution)/shard_map/ppermute | solution.py:654
  51.7 1.2 %shard_map.120 = (bf16[2,2,2,256,256]{4,3,2,1,0:T(8,128)(2,1)}, bf16[2,2,2,256,256]{4,3,2,1,0:T(8,128)(2,1)}, f32[2,128,256]{2,1,0:T(8,128)}) custom-call(bf16[2,2,128,256]{3,2,1,0:T(8,128)(2,1)S(1)} %collective-permute-done.4.last, bf16[2,2,256,256]{3,2,1,0:T(8,128)(2,1)S(1)} %get-tuple-element.48.q_arrived, ...), custom_call_target="tpu_custom_call", output_to_operand_aliasing={{0}: (8, {}), {1}: (9, {})} | custom-call | tf_op jit(solution)/shard_map/pallas_call | solution.py:658
  (2 shorter events, 0.0 us)
Async XLA Ops:
  0.6 3.5 %copy-start = (bf16[256,256]{1,0:T(8,128)(2,1)S(1)}, bf16[256,256]{1,0:T(8,128)(2,1)}, u32[]{:S(2)}) copy-start(bf16[256,256]{1,0:T(8,128)(2,1)} %constant.2.clone.hx.hy) | copy-start | bytes 393220
  0.6 3.5 %copy-start.2 = (f32[16]{0:T(128)S(1)}, f32[16]{0:T(128)}, u32[]{:S(2)}) copy-start(f32[16]{0:T(128)} %slowness.3) | copy-start | bytes 196
  0.7 3.5 %copy-start.3 = (s32[2]{0:T(128)S(1)}, s32[2]{0:T(128)}, u32[]{:S(2)}) copy-start(s32[2]{0:T(128)} %freq.3) | copy-start | bytes 28
  2.1 6.7 %collective-permute-start.2 = (bf16[2,2,256,256]{3,2,1,0:T(8,128)(2,1)S(1)}, bf16[2,2,256,256]{3,2,1,0:T(8,128)(2,1)S(1)}, u32[]{:S(2)}, u32[]{:S(2)}) collective-permute-start(bf16[2,2,256,256]{3,2,1,0:T(8,128)(2,1)S(1)} %get-tuple-element.34), channel_id=1, source_target_pairs={{0,2},{2,0},{4,6},{6,4},{8,10},{10,8},{12,14},{14,12},{16,18},{18,... | collective-permute-start | bytes 1572872 | tf_op jit(solution)/shard_map/ppermute | solution.py:597
  2.2 18.9 %collective-permute-start = (bf16[5,256,256]{2,1,0:T(8,128)(2,1)S(1)}, bf16[5,256,256]{2,1,0:T(8,128)(2,1)S(1)}, u32[]{:S(2)}, u32[]{:S(2)}) collective-permute-start(bf16[5,256,256]{2,1,0:T(8,128)(2,1)S(1)} %get-tuple-element.33.parcel), channel_id=1, source_target_pairs={{2,4},{6,8},{10,12},{14,16},{18,20},{22,24},{26,28},{4,2},{8,6},{1... | collective-permute-start | bytes 1966088 | tf_op jit(solution)/shard_map/ppermute | solution.py:596
  8.8 12.3 %copy-start.1 = (bf16[2,2,256,256]{3,2,1,0:T(8,128)(2,1)S(1)}, bf16[2,2,256,256]{3,2,1,0:T(8,128)(2,1)}, u32[]{:S(2)}) copy-start(bf16[2,2,256,256]{3,2,1,0:T(8,128)(2,1)} %source.1) | copy-start | bytes 1572868
  12.3 8.8 %collective-permute-start.3 = (bf16[2,2,256,256]{3,2,1,0:T(8,128)(2,1)S(1)}, bf16[2,2,256,256]{3,2,1,0:T(8,128)(2,1)S(1)}, u32[]{:S(2)}, u32[]{:S(2)}) collective-permute-start(bf16[2,2,256,256]{3,2,1,0:T(8,128)(2,1)S(1)} %get-tuple-element.40), channel_id=1, source_target_pairs={{0,2},{2,0},{4,6},{6,4},{8,10},{10,8},{12,14},{14,12},{16,18},{18,... | collective-permute-start | bytes 1572872 | tf_op jit(solution)/shard_map/ppermute | solution.py:617
  24.1 20.5 %collective-permute-start.5 = (bf16[2,2,384,256]{3,2,1,0:T(8,128)(2,1)S(1)}, bf16[2,2,384,256]{3,2,1,0:T(8,128)(2,1)S(1)}, u32[]{:S(2)}, u32[]{:S(2)}) collective-permute-start(bf16[2,2,384,256]{3,2,1,0:T(8,128)(2,1)S(1)} %get-tuple-element.51), channel_id=1, source_target_pairs={{2,4},{6,8},{10,12},{14,16},{18,20},{22,24},{26,28},{4,2},{8,6},{1... | collective-permute-start | bytes 2359304 | tf_op jit(solution)/shard_map/ppermute | solution.py:628
  26.2 5.0 %collective-permute-start.1 = (bf16[256,256]{1,0:T(8,128)(2,1)S(1)}, bf16[256,256]{1,0:T(8,128)(2,1)S(1)}, u32[]{:S(2)}, u32[]{:S(2)}) collective-permute-start(bf16[256,256]{1,0:T(8,128)(2,1)S(1)} %slice_bitcast_fusion.mine), channel_id=1, source_target_pairs={{0,1},{1,0},{2,3},{3,2},{4,5},{5,4},{6,7},{7,6},{8,9},{9,8},{10,11... | collective-permute-start | bytes 393224 | tf_op jit(solution)/shard_map/ppermute | solution.py:619
  34.2 2.6 %collective-permute-start.6 = (bf16[2,2,256,256]{3,2,1,0:T(8,128)(2,1)S(1)}, bf16[2,2,256,256]{3,2,1,0:T(8,128)(2,1)S(1)}, u32[]{:S(2)}, u32[]{:S(2)}) collective-permute-start(bf16[2,2,256,256]{3,2,1,0:T(8,128)(2,1)S(1)} %get-tuple-element.54), channel_id=1, source_target_pairs={{0,2},{2,0},{4,6},{6,4},{8,10},{10,8},{12,14},{14,12},{16,18},{18,... | collective-permute-start | bytes 1572872 | tf_op jit(solution)/shard_map/ppermute | solution.py:641
  34.3 15.2 %collective-permute-start.4 = (bf16[2,2,128,256]{3,2,1,0:T(8,128)(2,1)S(1)}, bf16[2,2,128,256]{3,2,1,0:T(8,128)(2,1)S(1)}, u32[]{:S(2)}, u32[]{:S(2)}) collective-permute-start(bf16[2,2,128,256]{3,2,1,0:T(8,128)(2,1)S(1)} %get-tuple-element.47), channel_id=1, source_target_pairs={{2,4},{6,8},{10,12},{14,16},{18,20},{22,24},{26,28},{4,2},{8,6},{1... | collective-permute-start | bytes 786440 | tf_op jit(solution)/shard_map/ppermute | solution.py:640
  46.7 5.0 %collective-permute-start.7 = (bf16[2,128,256]{2,1,0:T(8,128)(2,1)S(1)}, bf16[2,128,256]{2,1,0:T(8,128)(2,1)S(1)}, u32[]{:S(2)}, u32[]{:S(2)}) collective-permute-start(bf16[2,128,256]{2,1,0:T(8,128)(2,1)S(1)} %get-tuple-element.56), channel_id=1, source_target_pairs={{0,1},{1,0},{2,3},{3,2},{4,5},{5,4},{6,7},{7,6},{8,9},{9,8},{10,11... | collective-permute-start | bytes 393224 | tf_op jit(solution)/shard_map/ppermute | solution.py:654

commit v5 on v3

--- a/solution.py
+++ b/solution.py
@@ -194,29 +194,13 @@
     return pl.ds(pl.multiple_of((shot if of == 0 else 1 - shot) * half, half), half)
 
 
-def joined(mine, other):
-    shot = lax.rem(lax.axis_index("shot"), 2)
-    return jnp.concatenate([jnp.where(shot == 0, mine, other), jnp.where(shot == 0, other, mine)], axis=0)
-
-
-def edges_kernel(down, up, reflect, classes_in, parcel, inward_inner, refl, klass, sems):
+def edges_kernel(down, up, outward_outer, inward_inner, sems):
     levels = down.shape[0]
-    fronts = inward_inner.shape[0]
-    half = refl.shape[0]
     odd = odd_place()
-    rows = half_rows(0, half)
 
     def fetch(first, second):
-        for front in range(fronts):
-            pltpu.make_async_copy(first.at[front], parcel.at[pl.ds(2 * front, 2)], sems.at[0]).start()
+        pltpu.make_async_copy(first, outward_outer, sems.at[0]).start()
         pltpu.make_async_copy(second, inward_inner, sems.at[1]).start()
-
-    fixed = [
-        pltpu.make_async_copy(reflect.at[odd, rows], refl, sems.at[2]),
-        pltpu.make_async_copy(classes_in.at[odd, rows], klass, sems.at[3]),
-    ]
-    for copy in fixed:
-        copy.start()
 
     @pl.when(odd == 0)
     def _():
@@ -226,12 +210,7 @@
     def _():
         fetch(down.at[levels - 1], up.at[0])
 
-    for copy in fixed:
-        copy.wait()
-    parcel[2 * fronts, :half] = (jnp.where(odd == 0, 1.0, -1.0).astype(F32) * refl[...]).astype(BF16)
-    parcel[2 * fronts, half:] = klass[...].astype(BF16)
-    for front in range(fronts):
-        pltpu.make_async_copy(up.at[0, front], parcel.at[pl.ds(2 * front, 2)], sems.at[0]).wait()
+    pltpu.make_async_copy(up.at[0], outward_outer, sems.at[0]).wait()
     pltpu.make_async_copy(up.at[0], inward_inner, sems.at[1]).wait()
 
 
@@ -326,59 +305,29 @@
     spread(jobs, work, hx, hy, phase)
 
 
-def leaving(q_out_inner, refl, screen, field, target):
-    fronts = q_out_inner.shape[0]
-    kept = 1.0 - refl[0]
-    for front in range(fronts):
-        b_re, b_im = (q_out_inner[front, part].astype(F32) for part in range(2))
-        b_re, b_im = screened(b_re, b_im, screen[0, front, 0], screen[0, front, 1])
-        put(field.at[front], kept * b_re, kept * b_im)
-    return [(field.at[front], front, target.at[front]) for front in range(fronts)]
-
-
 def ahead_kernel(
-    partner, parcel, q_in_outer, q_out_inner, screen, refl, phase, hx, hy,
-    inward_inner, q_out_inner_next, q_out_outer, second, last,
-    field, other_field, q_field, work,
-):
-    fronts, _, rows_x, _ = partner.shape
-    everyone = range(fronts)
-    half = rows_x // 2
-    far_bottom = lax.rem(lax.axis_index("shot"), 2) == 0
-    jobs = leaving(q_out_inner, refl, screen, field, second.at[:, :, pl.ds(0, rows_x)])
-    jobs += [(partner.at[front], front, q_field.at[front]) for front in everyone]
-    spread(jobs, work, hx, hy, phase)
+    partner, q_in_outer, screen, refl, phase, hx, hy,
+    inward_inner, q_out_inner,
+    q_field, field, work,
+):
+    everyone = range(partner.shape[0])
+    spread([(partner.at[front], front, q_field.at[front]) for front in everyone], work, hx, hy, phase)
     for front in everyone:
         in_re, in_im, out_re, out_im = mixed(
             q_in_outer[front, 0], q_in_outer[front, 1], q_field[front, 0], q_field[front, 1],
             refl[1], screen[1, front, 0], screen[1, front, 1],
         )
         put(inward_inner.at[front], in_re, in_im)
-        put(other_field.at[front], out_re, out_im)
-    jobs = [(other_field.at[front], front, q_out_inner_next.at[front]) for front in everyone]
-    jobs += [(parcel.at[pl.ds(2 * front, 2)], front, q_out_outer.at[front]) for front in everyone]
-    spread(jobs, work, hx, hy, phase)
-    spread(leaving(q_out_inner_next, refl, screen, field, q_field), work, hx, hy, phase)
-    for front in everyone:
-        for part in range(2):
-            top, bottom = q_field[front, part, :half], q_field[front, part, half:]
-            second[front, part, rows_x:] = jnp.where(far_bottom, bottom, top)
-            last[front, part] = jnp.where(far_bottom, top, bottom)
-
-
-def edge_kernel(
-    arrived, source, partner, q_out_inner, screen, refl, phase, hx, hy,
-    inward_inner, out_inner, q_arrived, q_out_outer,
-    inward, outward, q_partner, q_inward, work,
-):
-    fronts = partner.shape[0]
-    everyone = range(fronts)
+        put(field.at[front], out_re, out_im)
+    spread([(field.at[front], front, q_out_inner.at[front]) for front in everyone], work, hx, hy, phase)
+
+
+def outer_step(arrived, source, q_out_inner, screen, refl, phase, hx, hy, inward, outward, q_arrived, work):
+    everyone = range(arrived.shape[0])
     first = lax.axis_index("depth") == 0
     for front in everyone:
-        put(inward.at[front], *(jnp.where(first, source[front, part], arrived[2 * front + part]) for part in range(2)))
-    jobs = [(inward.at[front], front, q_arrived.at[front]) for front in everyone]
-    jobs += [(partner.at[front], front, q_partner.at[front]) for front in everyone]
-    spread(jobs, work, hx, hy, phase)
+        put(inward.at[front], *(jnp.where(first, source[front, part], arrived[front, part]) for part in range(2)))
+    spread([(inward.at[front], front, q_arrived.at[front]) for front in everyone], work, hx, hy, phase)
     for front in everyone:
         in_re, in_im, out_re, out_im = mixed(
             q_arrived[front, 0], q_arrived[front, 1], q_out_inner[front, 0], q_out_inner[front, 1],
@@ -386,74 +335,61 @@
         )
         put(inward.at[front], in_re, in_im)
         put(outward.at[front], out_re, out_im)
-    jobs = [(inward.at[front], front, q_inward.at[front]) for front in everyone]
-    jobs += [(outward.at[front], front, q_out_outer.at[front]) for front in everyone]
+
+
+def edge_kernel(
+    arrived, source, q_out_inner, screen, refl, phase, hx, hy,
+    inward, outward, q_arrived,
+    work,
+):
+    outer_step(arrived, source, q_out_inner, screen, refl, phase, hx, hy, inward, outward, q_arrived, work)
+
+
+def last_edge_kernel(
+    arrived, source, q_out_inner, screen, refl, phase, hx, hy,
+    inward, last_far, last_near,
+    outward, q_field, work,
+):
+    everyone = range(arrived.shape[0])
+    half = arrived.shape[2] // 2
+    far_bottom = lax.rem(lax.axis_index("shot"), 2) == 0
+    outer_step(arrived, source, q_out_inner, screen, refl, phase, hx, hy, inward, outward, q_field, work)
+    spread([(outward.at[front], front, q_field.at[front]) for front in everyone], work, hx, hy, phase)
+    for front in everyone:
+        for part in range(2):
+            top, bottom = q_field[front, part, :half], q_field[front, part, half:]
+            last_far[front, part] = jnp.where(far_bottom, bottom, top)
+            last_near[front, part] = jnp.where(far_bottom, top, bottom)
+
+
+def inner_kernel(
+    inward_outer, partner, screen, refl, phase, hx, hy,
+    inward, outward,
+    q_inward, q_partner, work,
+):
+    everyone = range(partner.shape[0])
+    jobs = [(inward_outer.at[front], front, q_inward.at[front]) for front in everyone]
+    jobs += [(partner.at[front], front, q_partner.at[front]) for front in everyone]
     spread(jobs, work, hx, hy, phase)
     for front in everyone:
         in_re, in_im, out_re, out_im = mixed(
             q_inward[front, 0], q_inward[front, 1], q_partner[front, 0], q_partner[front, 1],
             refl[1], screen[1, front, 0], screen[1, front, 1],
         )
-        put(inward_inner.at[front], in_re, in_im)
-        put(out_inner.at[front], out_re, out_im)
-
-
-def beyond_kernel(
-    mine, other, out_inner, q_out_outer_0, q_out_outer_1, slowness, freq, phase, hx, hy,
-    q_out_inner, rest_2, rest_3,
-    field_2, field_3, work,
-):
-    fronts = out_inner.shape[0]
-    everyone = range(fronts)
-    half = mine.shape[0] // 2
-    refl_beyond = joined(mine[:half], other[:half]).astype(F32)
-    klass = joined(mine[half:], other[half:]).astype(F32).astype(jnp.int32)
-    for front in everyone:
-        cos_row, sin_row = class_rows(slowness, front_wave(freq, front), (8, 128))
-        back_re = refl_beyond * look_up(cos_row, klass)
-        back_im = refl_beyond * look_up(sin_row, klass)
-        for known, target in ((q_out_outer_0, field_2), (q_out_outer_1, field_3)):
-            known_re, known_im = (known[front, part].astype(F32) for part in range(2))
-            put(target.at[front], *screened(known_re, known_im, back_re, back_im))
-    jobs = [(out_inner.at[front], front, q_out_inner.at[front]) for front in everyone]
-    jobs += [(field_2.at[front], front, rest_2.at[front]) for front in everyone]
-    jobs += [(field_3.at[front], front, rest_3.at[front]) for front in everyone]
+        put(inward.at[front], in_re, in_im)
+        put(outward.at[front], out_re, out_im)
+
+
+def last_inner_kernel(
+    inward_outer, partner, out_inner, screen, refl, phase, hx, hy,
+    inward, outward, terms, q_out_inner,
+    q_inward, q_partner, work,
+):
+    everyone = range(partner.shape[0])
+    jobs = [(inward_outer.at[front], front, q_inward.at[front]) for front in everyone]
+    jobs += [(partner.at[front], front, q_partner.at[front]) for front in everyone]
+    jobs += [(out_inner.at[front], front, q_out_inner.at[front]) for front in everyone]
     spread(jobs, work, hx, hy, phase)
-
-
-def partner_kernel(partner, phase, hx, hy, q_partner, work):
-    fronts = partner.shape[0]
-    spread([(partner.at[front], front, q_partner.at[front]) for front in range(fronts)], work, hx, hy, phase)
-
-
-def inner_kernel(
-    second, rest_2, rest_3, q_arrived, q_out_inner_1, q_out_inner_2, q_partner, screen, refl, phase, hx, hy,
-    inward, outward, far_inward, far_outward, terms, inner_terms,
-    field, q_inward, work,
-):
-    fronts, _, rows_x, _ = q_partner.shape
-    everyone = range(fronts)
-    first = lax.axis_index("depth") == 0
-    for front in everyone:
-        a_re, a_im = (
-            jnp.where(
-                first,
-                q_arrived[front, part].astype(F32),
-                second[front, part, :rows_x].astype(F32) + rest_2[front, part].astype(F32),
-            )
-            for part in range(2)
-        )
-        in_re, in_im, _, _ = mixed(
-            a_re, a_im, q_out_inner_1[front, 0], q_out_inner_1[front, 1],
-            refl[0], screen[0, front, 0], screen[0, front, 1],
-        )
-        put(field.at[front], in_re, in_im)
-    spread([(field.at[front], front, q_inward.at[front]) for front in everyone], work, hx, hy, phase)
-    rows, total = outer_rows(
-        1, second.at[:, :, pl.ds(rows_x, rows_x // 2)], q_arrived, rest_3, q_out_inner_2, screen, refl,
-        far_inward, far_outward,
-    )
-    terms[0] = total.astype(BF16)
     total = None
     for front in everyone:
         a_re, a_im = (q_inward[front, part].astype(F32) for part in range(2))
@@ -465,22 +401,26 @@
         put(outward.at[front], out_re, out_im)
         term = a_re * b_re + a_im * b_im
         total = term if total is None else total + term
-    inner_terms[...] = total
+    terms[...] = total
+
+
+def far_rows_kernel(
+    last, q_arrived, q_out_inner, screen, refl, inner_terms,
+    inward, outward, terms,
+):
+    rows, total = outer_rows(1, last, q_arrived, q_out_inner, screen, refl, inward, outward)
+    terms[0] = total.astype(BF16)
     terms[1] = inner_terms[rows, :].astype(BF16)
 
 
-def outer_rows(of, last, q_arrived, rest, q_out_inner, screen, refl, inward, outward, ready=None):
+def outer_rows(of, last, q_arrived, q_out_inner, screen, refl, inward, outward):
     fronts, _, half, _ = last.shape
     first = lax.axis_index("depth") == 0
     rows = half_rows(of, half)
     total = None
     for front in range(fronts):
         a_re, a_im = (
-            jnp.where(
-                first,
-                q_arrived[front, part, rows, :].astype(F32),
-                last[front, part].astype(F32) + rest[front, part, rows, :].astype(F32),
-            )
+            jnp.where(first, q_arrived[front, part, rows, :], last[front, part]).astype(F32)
             for part in range(2)
         )
         b_re, b_im = (q_out_inner[front, part, rows, :].astype(F32) for part in range(2))
@@ -525,12 +465,12 @@
 
 
 def near_rows_kernel(
-    scale, last, q_arrived, rest, q_out_inner, screen, refl, inner_terms, other, down_in, up_in,
+    scale, last, q_arrived, q_out_inner, screen, refl, inner_terms, other, down_in, up_in,
     down_out, up_out, gradient,
     inward, outward, sums, sems,
 ):
     del down_in, up_in
-    rows, total = outer_rows(0, last, q_arrived, rest, q_out_inner, screen, refl, inward, outward)
+    rows, total = outer_rows(0, last, q_arrived, q_out_inner, screen, refl, inward, outward)
     waits = send_home(0, rows, inward, outward, down_out, up_out, sems.at[0])
     odd = odd_place()
     sums[odd] = scale * (total + other[0].astype(F32))
@@ -584,14 +524,10 @@
     def work(slots):
         return pltpu.VMEM((slots, *plane.shape[1:]), BF16)
 
-    parcel, in_inner = call(
-        edges_kernel,
-        [HBM] * 4,
-        [VMEM] * 2,
-        [jax.ShapeDtypeStruct((fronts * parts + 1, rows_x, rows_y), BF16), plane],
-        [pltpu.VMEM((half, rows_y), F32), pltpu.VMEM((half, rows_y), jnp.int32), dma((4,))],
-    )(*kept_in_hbm(down_state, up_state, reflect, screen_class))
-    arrived = to_beyond(parcel)
+    out_outer, in_inner = call(edges_kernel, [HBM] * 2, [VMEM] * 2, [plane] * 2, [dma((2,))])(
+        *kept_in_hbm(down_state, up_state)
+    )
+    arrived_0 = to_beyond(out_outer)
     partner_0 = to_partner(in_inner)
     q_out_inner_0, q_in_outer_0, screen, phase, refl = call(
         setup_kernel,
@@ -605,53 +541,49 @@
             dma((6,)),
         ],
     )(*kept_in_hbm(down_state, up_state, reflect, screen_class), screen_values, freq_index, hx, hy)
-    in_inner_1, q_out_inner_1, q_out_outer_0, second, last = call(
-        ahead_kernel,
-        [VMEM] * 9,
-        [VMEM] * 5,
-        [plane] * 3 + [jax.ShapeDtypeStruct((fronts, parts, rows_x + half, rows_y), BF16), half_plane],
-        buffers(3) + [work(2 * fronts)],
-    )(partner_0, parcel, q_in_outer_0, q_out_inner_0, screen, refl, phase, hx, hy)
+    fixed = (screen, refl, phase, hx, hy)
+    in_inner_1, q_out_inner_1 = call(ahead_kernel, [VMEM] * 7, [VMEM] * 2, [plane] * 2, buffers(2) + [work(fronts)])(
+        partner_0, q_in_outer_0, *fixed
+    )
     partner_1 = to_partner(in_inner_1)
-    second = to_beyond(second)
-    last = to_beyond(last)
-    mine = arrived[fronts * parts]
-    swapped = across(mine)
-    in_inner_2, out_inner_2, q_arrived, q_out_outer_1 = call(
-        edge_kernel, [VMEM] * 9, [VMEM] * 4, [plane] * 4, buffers(4) + [work(2 * fronts)]
-    )(arrived, source, partner_1, q_out_inner_0, screen, refl, phase, hx, hy)
+    in_outer_1, out_outer_1, q_arrived = call(edge_kernel, [VMEM] * 8, [VMEM] * 3, [plane] * 3, [work(fronts)])(
+        arrived_0, source, q_out_inner_0, *fixed
+    )
+    arrived_1 = to_beyond(out_outer_1)
+    in_inner_2, out_inner_2 = call(
+        inner_kernel, [VMEM] * 7, [VMEM] * 2, [plane] * 2, buffers(2) + [work(2 * fronts)]
+    )(in_outer_1, partner_1, *fixed)
     partner_2 = to_partner(in_inner_2)
-    q_out_inner_2, rest_2, rest_3 = call(
-        beyond_kernel,
-        [VMEM] * 5 + [SMEM] * 2 + [VMEM] * 3,
+    in_outer_2, last_far, last_near = call(
+        last_edge_kernel, [VMEM] * 8, [VMEM] * 3, [plane] + [half_plane] * 2, buffers(2) + [work(fronts)]
+    )(arrived_1, source, q_out_inner_1, *fixed)
+    last_far = to_beyond(last_far)
+    last_near = to_beyond(last_near)
+    inner_in, inner_out, inner_terms, q_out_inner_2 = call(
+        last_inner_kernel,
+        [VMEM] * 8,
+        [VMEM] * 4,
+        [plane] * 2 + [jax.ShapeDtypeStruct((rows_x, rows_y), F32), plane],
+        buffers(2) + [work(3 * fronts)],
+    )(in_outer_2, partner_2, out_inner_2, *fixed)
+    far_in, far_out, terms = call(
+        far_rows_kernel,
+        [VMEM] * 6,
         [VMEM] * 3,
-        [plane] * 3,
-        buffers(2) + [work(3 * fronts)],
-    )(mine, swapped, out_inner_2, q_out_outer_0, q_out_outer_1, screen_values, freq_index, phase, hx, hy)
-    q_partner = call(partner_kernel, [VMEM] * 4, VMEM, plane, [work(fronts)])(partner_2, phase, hx, hy)
-    inner_in, inner_out, far_in, far_out, terms, inner_terms = call(
-        inner_kernel,
-        [VMEM] * 12,
-        [VMEM] * 6,
-        [plane] * 2
-        + [half_plane] * 2
-        + [jax.ShapeDtypeStruct((2, half, rows_y), BF16), jax.ShapeDtypeStruct((rows_x, rows_y), F32)],
-        buffers(2) + [work(fronts)],
-    )(
-        second, rest_2, rest_3, q_arrived, q_out_inner_1, q_out_inner_2, q_partner, screen, refl, phase, hx, hy
-    )
+        [half_plane] * 2 + [jax.ShapeDtypeStruct((2, half, rows_y), BF16)],
+    )(last_far, q_arrived, q_out_inner_2, screen, refl, inner_terms)
     other = across(terms) if shots == 2 else jnp.zeros_like(terms)
     down, up = call(home_kernel, [VMEM] * 4, [HBM] * 2, [state] * 2, [dma((2, 2))])(
         inner_in, inner_out, far_in, far_out
     )
     down, up, gradient = call(
         functools.partial(near_rows_kernel, scale),
-        [VMEM] * 8 + [HBM] * 2,
+        [VMEM] * 7 + [HBM] * 2,
         [HBM] * 3,
         [state, state, jax.ShapeDtypeStruct((2, half, rows_y), F32)],
         buffers(2, half_plane) + [pltpu.VMEM((2, half, rows_y), F32), dma((2, 2))],
-        input_output_aliases={8: 0, 9: 1},
-    )(last, q_arrived, rest_3, q_out_inner_2, screen, refl, inner_terms, other, down, up)
+        input_output_aliases={7: 0, 8: 1},
+    )(last_near, q_arrived, q_out_inner_2, screen, refl, inner_terms, other, down, up)
     if shots != 2:
         terms = scale * terms.astype(F32)
         far = jnp.where(odd_place() == 0, terms, terms[::-1])

time: 52.4 us -> 50.3 us (0.960)
  the two profiles are of different devices: /device:TPU:0 before, /device:TPU:4 now
where the time goes in v5:
time: 50.3 us; the launch traced here: 50.1 us
  waiting for transfers between devices  18.3 us (36%)
  Pallas kernels  17.7 us (35%)
  starting transfers between devices  13 us (26%)
  between operations  0.99 us (2%)
    ppermute x1, waiting for transfers between devices, per_device(): arrived_1 = to_beyond(out_outer_1)  9.36 us
    ppermute x1, waiting for transfers between devices, per_device(): arrived_0 = to_beyond(out_outer)  5.8 us
    pallas_call x1, Pallas kernels, per_device(): call(setup_kernel, [HBM] * 4 + [SMEM] * 2 + [VMEM] * 2, [VMEM] * 5, [plan...  4.69 us
    ppermute x1, starting transfers between devices, per_device(): last_near = to_beyond(last_near)  3.82 us
    ppermute x1, waiting for transfers between devices, per_device(): other = across(terms) if shots == 2 else jnp.zeros_like(terms)  2.29 us
    pallas_call x1, Pallas kernels, per_device(): call(last_inner_kernel, [VMEM] * 8, [VMEM] * 4, [plane] * 2 + [jax.ShapeD...  2.28 us
    pallas_call x1, Pallas kernels, per_device(): call(last_edge_kernel, [VMEM] * 8, [VMEM] * 3, [plane] + [half_plane] * 2...  2 us
    pallas_call x1, Pallas kernels, per_device(): call(ahead_kernel, [VMEM] * 7, [VMEM] * 2, [plane] * 2, buffers(2) + [wor...  1.95 us
  transfers between devices with their start and end apart: 8, of which 4 were waited for; matrix products, arithmetic and copies ran while one was open for 0% of the time, Pallas kernels for 31%

profile of v5, /device:TPU:4, one launch (start us, length us, event | category | flops | bytes accessed | tf_op | source)
XLA Modules:
  0.0 50.1 jit_solution(16547721518692897933)
XLA Ops:
  0.6 0.0 copy-start
  0.6 0.0 copy-start.3
  0.7 0.0 copy-start.2
  0.7 1.3 %shard_map.112 = (bf16[2,2,256,256]{3,2,1,0:T(8,128)(2,1)S(1)}, bf16[2,2,256,256]{3,2,1,0:T(8,128)(2,1)S(1)}) custom-call(bf16[2,2,2,256,256]{4,3,2,1,0:T(8,128)(2,1)} %down.3, bf16[2,2,2,256,256]{4,3,2,1,0:T(8,128)(2,1)} %up.3), custom_call_target="tpu_custom_call" | custom-call | tf_op jit(solution)/shard_map/pallas_call | solution.py:527
  2.0 0.1 collective-permute-start.2
  2.0 1.9 %collective-permute-start = (bf16[2,2,256,256]{3,2,1,0:T(8,128)(2,1)S(1)}, bf16[2,2,256,256]{3,2,1,0:T(8,128)(2,1)S(1)}, u32[]{:S(2)}, u32[]{:S(2)}) collective-permute-start(bf16[2,2,256,256]{3,2,1,0:T(8,128)(2,1)S(1)} %get-tuple-element.29), channel_id=1, source_target_pairs={{2,4},{6,8},{10,12},{14,16},{18,20},{22,24},{26,28},{4,2},{8,6},{1... | collective-permute-start | bytes 1572872 | tf_op jit(solution)/shard_map/ppermute | solution.py:530
  4.0 0.0 copy-done
  4.0 0.0 copy-done.3
  4.0 4.7 %shard_map.113 = (bf16[2,2,256,256]{3,2,1,0:T(8,128)(2,1)S(1)}, bf16[2,2,256,256]{3,2,1,0:T(8,128)(2,1)S(1)}, f32[2,2,2,256,256]{4,3,2,1,0:T(8,128)S(1)}, f32[2,...) custom-call(bf16[2,2,2,256,256]{4,3,2,1,0:T(8,128)(2,1)} %down.3, bf16[2,2,2,256,256]{4,3,2,1,0:T(8,128)(2,1)} %up.3, ...), custom_call_target="tpu_custom_call" | custom-call | tf_op jit(solution)/shard_map/pallas_call | solution.py:532
  8.7 0.0 collective-permute-done.2.partner
  8.7 0.0 copy-start.1
  8.7 1.9 %shard_map.115 = (bf16[2,2,256,256]{3,2,1,0:T(8,128)(2,1)S(1)}, bf16[2,2,256,256]{3,2,1,0:T(8,128)(2,1)S(1)}) custom-call(bf16[2,2,256,256]{3,2,1,0:T(8,128)(2,1)S(1)} %collective-permute-done.2.partner, bf16[2,2,256,256]{3,2,1,0:T(8,128)(2,1)S(1)} %get-tuple-element.36.q_in_outer, f32[2,2,2,256,256]{4,3,2,1,0:T(8,128)S(1)} %get-tuple-element.31.screen, ...), custom_call_target="tpu_custom_call" | custom-call | tf_op jit(solution)/shard_map/pallas_call | solution.py:545
  10.7 1.7 %collective-permute-start.4 = (bf16[2,2,256,256]{3,2,1,0:T(8,128)(2,1)S(1)}, bf16[2,2,256,256]{3,2,1,0:T(8,128)(2,1)S(1)}, u32[]{:S(2)}, u32[]{:S(2)}) collective-permute-start(bf16[2,2,256,256]{3,2,1,0:T(8,128)(2,1)S(1)} %get-tuple-element.42), channel_id=1, source_target_pairs={{0,2},{2,0},{4,6},{6,4},{8,10},{10,8},{12,14},{14,12},{16,18},{18,... | collective-permute-start | bytes 1572872 | tf_op jit(solution)/shard_map/ppermute | solution.py:548
  12.4 5.8 %collective-permute-done.arrived = bf16[2,2,256,256]{3,2,1,0:T(8,128)(2,1)S(1)} collective-permute-done((bf16[2,2,256,256]{3,2,1,0:T(8,128)(2,1)S(1)}, bf16[2,2,256,256]{3,2,1,0:T(8,128)(2,1)S(1)}, u32[]{:S(2)}, u32[]{:S(2)}) %collective-permute-start) | collective-permute-done | bytes 524320 | tf_op jit(solution)/shard_map/ppermute | solution.py:530
  18.2 1.2 %shard_map.114 = (bf16[2,2,256,256]{3,2,1,0:T(8,128)(2,1)S(1)}, bf16[2,2,256,256]{3,2,1,0:T(8,128)(2,1)S(1)}, bf16[2,2,256,256]{3,2,1,0:T(8,128)(2,1)S(1)}) custom-call(bf16[2,2,256,256]{3,2,1,0:T(8,128)(2,1)S(1)} %collective-permute-done.arrived, bf16[2,2,256,256]{3,2,1,0:T(8,128)(2,1)S(1)} %copy-done.1, ...), custom_call_target="tpu_custom_call" | custom-call | tf_op jit(solution)/shard_map/pallas_call | solution.py:549
  19.4 1.9 %collective-permute-start.1 = (bf16[2,2,256,256]{3,2,1,0:T(8,128)(2,1)S(1)}, bf16[2,2,256,256]{3,2,1,0:T(8,128)(2,1)S(1)}, u32[]{:S(2)}, u32[]{:S(2)}) collective-permute-start(bf16[2,2,256,256]{3,2,1,0:T(8,128)(2,1)S(1)} %get-tuple-element.34), channel_id=1, source_target_pairs={{2,4},{6,8},{10,12},{14,16},{18,20},{22,24},{26,28},{4,2},{8,6},{1... | collective-permute-start | bytes 1572872 | tf_op jit(solution)/shard_map/ppermute | solution.py:552
  21.3 0.0 collective-permute-done.4.partner
  21.3 1.7 %shard_map.117 = (bf16[2,2,256,256]{3,2,1,0:T(8,128)(2,1)S(1)}, bf16[2,2,256,256]{3,2,1,0:T(8,128)(2,1)S(1)}) custom-call(bf16[2,2,256,256]{3,2,1,0:T(8,128)(2,1)S(1)} %get-tuple-element.41.inward_outer, bf16[2,2,256,256]{3,2,1,0:T(8,128)(2,1)S(1)} %collective-permute-done.4.partner, f32[2,2,2,256,256]{4,3,2,1,0:T(8,128)S(1)} %get-tuple-element.31.screen, ...), custom_call_target="tpu_custom_call" | custom-call | tf_op jit(solution)/shard_map/pallas_call | solution.py:553
  23.0 0.1 collective-permute-start.5
  23.1 9.4 %collective-permute-done.1.arrived = bf16[2,2,256,256]{3,2,1,0:T(8,128)(2,1)S(1)} collective-permute-done((bf16[2,2,256,256]{3,2,1,0:T(8,128)(2,1)S(1)}, bf16[2,2,256,256]{3,2,1,0:T(8,128)(2,1)S(1)}, u32[]{:S(2)}, u32[]{:S(2)}) %collective-permute-start.1) | collective-permute-done | bytes 524320 | tf_op jit(solution)/shard_map/ppermute | solution.py:552
  32.5 2.0 %shard_map.116 = (bf16[2,2,256,256]{3,2,1,0:T(8,128)(2,1)S(1)}, bf16[2,2,128,256]{3,2,1,0:T(8,128)(2,1)S(1)}, bf16[2,2,128,256]{3,2,1,0:T(8,128)(2,1)S(1)}) custom-call(bf16[2,2,256,256]{3,2,1,0:T(8,128)(2,1)S(1)} %collective-permute-done.1.arrived, bf16[2,2,256,256]{3,2,1,0:T(8,128)(2,1)S(1)} %copy-done.1, ...), custom_call_target="tpu_custom_call" | custom-call | tf_op jit(solution)/shard_map/pallas_call | solution.py:557
  34.5 1.9 %collective-permute-start.6 = (bf16[2,2,128,256]{3,2,1,0:T(8,128)(2,1)S(1)}, bf16[2,2,128,256]{3,2,1,0:T(8,128)(2,1)S(1)}, u32[]{:S(2)}, u32[]{:S(2)}) collective-permute-start(bf16[2,2,128,256]{3,2,1,0:T(8,128)(2,1)S(1)} %get-tuple-element.47), channel_id=1, source_target_pairs={{2,4},{6,8},{10,12},{14,16},{18,20},{22,24},{26,28},{4,2},{8,6},{1... | collective-permute-start | bytes 786440 | tf_op jit(solution)/shard_map/ppermute | solution.py:560
  36.4 3.8 %collective-permute-start.3 = (bf16[2,2,128,256]{3,2,1,0:T(8,128)(2,1)S(1)}, bf16[2,2,128,256]{3,2,1,0:T(8,128)(2,1)S(1)}, u32[]{:S(2)}, u32[]{:S(2)}) collective-permute-start(bf16[2,2,128,256]{3,2,1,0:T(8,128)(2,1)S(1)} %get-tuple-element.38), channel_id=1, source_target_pairs={{2,4},{6,8},{10,12},{14,16},{18,20},{22,24},{26,28},{4,2},{8,6},{1... | collective-permute-start | bytes 786440 | tf_op jit(solution)/shard_map/ppermute | solution.py:561
  40.2 0.0 collective-permute-done.5.partner
  40.2 2.3 %shard_map.118 = (bf16[2,2,256,256]{3,2,1,0:T(8,128)(2,1)S(1)}, bf16[2,2,256,256]{3,2,1,0:T(8,128)(2,1)S(1)}, f32[256,256]{1,0:T(8,128)S(1)}, bf16[2,2,256,256]{3,2,1,0:T(8,128)(2,1)S(1)}) custom-call(bf16[2,2,256,256]{3,2,1,0:T(8,128)(2,1)S(1)} %get-tuple-element.40.inward_outer, bf16[2,2,256,256]{3,2,1,0:T(8,128)(2,1)S(1)} %collective-permute-done.5.partner, ...), custom_call_target="tpu_custom_call" | custom-call | tf_op jit(solution)/shard_map/pallas_call | solution.py:562
  42.5 0.9 %collective-permute-done.6.last = bf16[2,2,128,256]{3,2,1,0:T(8,128)(2,1)S(1)} collective-permute-done((bf16[2,2,128,256]{3,2,1,0:T(8,128)(2,1)S(1)}, bf16[2,2,128,256]{3,2,1,0:T(8,128)(2,1)S(1)}, u32[]{:S(2)}, u32[]{:S(2)}) %collective-permute-start.6) | collective-permute-done | bytes 262176 | tf_op jit(solution)/shard_map/ppermute | solution.py:560
  43.4 0.3 shard_map.119
  43.8 1.6 %collective-permute-start.7 = (bf16[2,128,256]{2,1,0:T(8,128)(2,1)S(1)}, bf16[2,128,256]{2,1,0:T(8,128)(2,1)S(1)}, u32[]{:S(2)}, u32[]{:S(2)}) collective-permute-start(bf16[2,128,256]{2,1,0:T(8,128)(2,1)S(1)} %get-tuple-element.48), channel_id=1, source_target_pairs={{0,1},{1,0},{2,3},{3,2},{4,5},{5,4},{6,7},{7,6},{8,9},{9,8},{10,11... | collective-permute-start | bytes 393224 | tf_op jit(solution)/shard_map/ppermute | solution.py:575
  45.3 1.2 %shard_map.120 = (bf16[2,2,2,256,256]{4,3,2,1,0:T(8,128)(2,1)}, bf16[2,2,2,256,256]{4,3,2,1,0:T(8,128)(2,1)}) custom-call(bf16[2,2,256,256]{3,2,1,0:T(8,128)(2,1)S(1)} %get-tuple-element.49.inward, bf16[2,2,256,256]{3,2,1,0:T(8,128)(2,1)S(1)} %get-tuple-element.50.outward, bf16[2,2,128,256]{3,2,1,0:T(8,128)(2,1)S(1)} %get-tuple-element.51.far_inward, ...), custom_call_target="tpu_custom_call" | custom-call | tf_op jit(solution)/shard_map/pallas_call | solution.py:576
  46.5 0.0 collective-permute-done.3.last
  46.5 2.3 %collective-permute-done.7.other = bf16[2,128,256]{2,1,0:T(8,128)(2,1)S(1)} collective-permute-done((bf16[2,128,256]{2,1,0:T(8,128)(2,1)S(1)}, bf16[2,128,256]{2,1,0:T(8,128)(2,1)S(1)}, u32[]{:S(2)}, u32[]{:S(2)}) %collective-permute-start.7) | collective-permute-done | bytes 131104 | tf_op jit(solution)/shard_map/ppermute | solution.py:575
  48.8 1.1 %shard_map.121 = (bf16[2,2,2,256,256]{4,3,2,1,0:T(8,128)(2,1)}, bf16[2,2,2,256,256]{4,3,2,1,0:T(8,128)(2,1)}, f32[2,128,256]{2,1,0:T(8,128)}) custom-call(bf16[2,2,128,256]{3,2,1,0:T(8,128)(2,1)S(1)} %collective-permute-done.3.last, bf16[2,2,256,256]{3,2,1,0:T(8,128)(2,1)S(1)} %get-tuple-element.39.q_arrived, ...), custom_call_target="tpu_custom_call", output_to_operand_aliasing={{0}: (7, {}), {1}: (8, {})} | custom-call | tf_op jit(solution)/shard_map/pallas_call | solution.py:579
  (2 shorter events, 0.0 us)
Async XLA Ops:
  0.6 3.3 %copy-start = (bf16[256,256]{1,0:T(8,128)(2,1)S(1)}, bf16[256,256]{1,0:T(8,128)(2,1)}, u32[]{:S(2)}) copy-start(bf16[256,256]{1,0:T(8,128)(2,1)} %constant.2.clone.hx.hy) | copy-start | bytes 393220
  0.6 3.3 %copy-start.3 = (s32[2]{0:T(128)S(1)}, s32[2]{0:T(128)}, u32[]{:S(2)}) copy-start(s32[2]{0:T(128)} %freq.1) | copy-start | bytes 28
  0.7 3.3 %copy-start.2 = (f32[16]{0:T(128)S(1)}, f32[16]{0:T(128)}, u32[]{:S(2)}) copy-start(f32[16]{0:T(128)} %slowness.1) | copy-start | bytes 196
  2.0 6.7 %collective-permute-start.2 = (bf16[2,2,256,256]{3,2,1,0:T(8,128)(2,1)S(1)}, bf16[2,2,256,256]{3,2,1,0:T(8,128)(2,1)S(1)}, u32[]{:S(2)}, u32[]{:S(2)}) collective-permute-start(bf16[2,2,256,256]{3,2,1,0:T(8,128)(2,1)S(1)} %get-tuple-element.35), channel_id=1, source_target_pairs={{0,2},{2,0},{4,6},{6,4},{8,10},{10,8},{12,14},{14,12},{16,18},{18,... | collective-permute-start | bytes 1572872 | tf_op jit(solution)/shard_map/ppermute | solution.py:531
  2.0 16.1 %collective-permute-start = (bf16[2,2,256,256]{3,2,1,0:T(8,128)(2,1)S(1)}, bf16[2,2,256,256]{3,2,1,0:T(8,128)(2,1)S(1)}, u32[]{:S(2)}, u32[]{:S(2)}) collective-permute-start(bf16[2,2,256,256]{3,2,1,0:T(8,128)(2,1)S(1)} %get-tuple-element.29), channel_id=1, source_target_pairs={{2,4},{6,8},{10,12},{14,16},{18,20},{22,24},{26,28},{4,2},{8,6},{1... | collective-permute-start | bytes 1572872 | tf_op jit(solution)/shard_map/ppermute | solution.py:530
  8.7 9.5 %copy-start.1 = (bf16[2,2,256,256]{3,2,1,0:T(8,128)(2,1)S(1)}, bf16[2,2,256,256]{3,2,1,0:T(8,128)(2,1)}, u32[]{:S(2)}) copy-start(bf16[2,2,256,256]{3,2,1,0:T(8,128)(2,1)} %source.3) | copy-start | bytes 1572868
  10.7 10.7 %collective-permute-start.4 = (bf16[2,2,256,256]{3,2,1,0:T(8,128)(2,1)S(1)}, bf16[2,2,256,256]{3,2,1,0:T(8,128)(2,1)S(1)}, u32[]{:S(2)}, u32[]{:S(2)}) collective-permute-start(bf16[2,2,256,256]{3,2,1,0:T(8,128)(2,1)S(1)} %get-tuple-element.42), channel_id=1, source_target_pairs={{0,2},{2,0},{4,6},{6,4},{8,10},{10,8},{12,14},{14,12},{16,18},{18,... | collective-permute-start | bytes 1572872 | tf_op jit(solution)/shard_map/ppermute | solution.py:548
  19.4 13.1 %collective-permute-start.1 = (bf16[2,2,256,256]{3,2,1,0:T(8,128)(2,1)S(1)}, bf16[2,2,256,256]{3,2,1,0:T(8,128)(2,1)S(1)}, u32[]{:S(2)}, u32[]{:S(2)}) collective-permute-start(bf16[2,2,256,256]{3,2,1,0:T(8,128)(2,1)S(1)} %get-tuple-element.34), channel_id=1, source_target_pairs={{2,4},{6,8},{10,12},{14,16},{18,20},{22,24},{26,28},{4,2},{8,6},{1... | collective-permute-start | bytes 1572872 | tf_op jit(solution)/shard_map/ppermute | solution.py:552
  23.0 17.2 %collective-permute-start.5 = (bf16[2,2,256,256]{3,2,1,0:T(8,128)(2,1)S(1)}, bf16[2,2,256,256]{3,2,1,0:T(8,128)(2,1)S(1)}, u32[]{:S(2)}, u32[]{:S(2)}) collective-permute-start(bf16[2,2,256,256]{3,2,1,0:T(8,128)(2,1)S(1)} %get-tuple-element.43), channel_id=1, source_target_pairs={{0,2},{2,0},{4,6},{6,4},{8,10},{10,8},{12,14},{14,12},{16,18},{18,... | collective-permute-start | bytes 1572872 | tf_op jit(solution)/shard_map/ppermute | solution.py:556
  34.5 8.9 %collective-permute-start.6 = (bf16[2,2,128,256]{3,2,1,0:T(8,128)(2,1)S(1)}, bf16[2,2,128,256]{3,2,1,0:T(8,128)(2,1)S(1)}, u32[]{:S(2)}, u32[]{:S(2)}) collective-permute-start(bf16[2,2,128,256]{3,2,1,0:T(8,128)(2,1)S(1)} %get-tuple-element.47), channel_id=1, source_target_pairs={{2,4},{6,8},{10,12},{14,16},{18,20},{22,24},{26,28},{4,2},{8,6},{1... | collective-permute-start | bytes 786440 | tf_op jit(solution)/shard_map/ppermute | solution.py:560
  36.4 10.1 %collective-permute-start.3 = (bf16[2,2,128,256]{3,2,1,0:T(8,128)(2,1)S(1)}, bf16[2,2,128,256]{3,2,1,0:T(8,128)(2,1)S(1)}, u32[]{:S(2)}, u32[]{:S(2)}) collective-permute-start(bf16[2,2,128,256]{3,2,1,0:T(8,128)(2,1)S(1)} %get-tuple-element.38), channel_id=1, source_target_pairs={{2,4},{6,8},{10,12},{14,16},{18,20},{22,24},{26,28},{4,2},{8,6},{1... | collective-permute-start | bytes 786440 | tf_op jit(solution)/shard_map/ppermute | solution.py:561
  43.8 5.0 %collective-permute-start.7 = (bf16[2,128,256]{2,1,0:T(8,128)(2,1)S(1)}, bf16[2,128,256]{2,1,0:T(8,128)(2,1)S(1)}, u32[]{:S(2)}, u32[]{:S(2)}) collective-permute-start(bf16[2,128,256]{2,1,0:T(8,128)(2,1)S(1)} %get-tuple-element.48), channel_id=1, source_target_pairs={{0,1},{1,0},{2,3},{3,2},{4,5},{5,4},{6,7},{7,6},{8,9},{9,8},{10,11... | collective-permute-start | bytes 393224 | tf_op jit(solution)/shard_map/ppermute | solution.py:575

commit v6 on v5

--- a/solution.py
+++ b/solution.py
@@ -346,10 +346,11 @@
 
 
 def last_edge_kernel(
-    arrived, source, q_out_inner, screen, refl, phase, hx, hy,
+    arrived, source, q_out_inner, screen, refl, phase, hx, hy, after,
     inward, last_far, last_near,
     outward, q_field, work,
 ):
+    del after
     everyone = range(arrived.shape[0])
     half = arrived.shape[2] // 2
     far_bottom = lax.rem(lax.axis_index("shot"), 2) == 0
@@ -380,15 +381,19 @@
         put(outward.at[front], out_re, out_im)
 
 
+def spread_kernel(fields, phase, hx, hy, q_fields, work):
+    everyone = range(fields.shape[0])
+    spread([(fields.at[front], front, q_fields.at[front]) for front in everyone], work, hx, hy, phase)
+
+
 def last_inner_kernel(
-    inward_outer, partner, out_inner, screen, refl, phase, hx, hy,
-    inward, outward, terms, q_out_inner,
+    inward_outer, partner, screen, refl, phase, hx, hy,
+    inward, outward, terms, far_terms,
     q_inward, q_partner, work,
 ):
-    everyone = range(partner.shape[0])
+    everyone = range(inward_outer.shape[0])
     jobs = [(inward_outer.at[front], front, q_inward.at[front]) for front in everyone]
     jobs += [(partner.at[front], front, q_partner.at[front]) for front in everyone]
-    jobs += [(out_inner.at[front], front, q_out_inner.at[front]) for front in everyone]
     spread(jobs, work, hx, hy, phase)
     total = None
     for front in everyone:
@@ -402,15 +407,13 @@
         term = a_re * b_re + a_im * b_im
         total = term if total is None else total + term
     terms[...] = total
-
-
-def far_rows_kernel(
-    last, q_arrived, q_out_inner, screen, refl, inner_terms,
-    inward, outward, terms,
-):
-    rows, total = outer_rows(1, last, q_arrived, q_out_inner, screen, refl, inward, outward)
-    terms[0] = total.astype(BF16)
-    terms[1] = inner_terms[rows, :].astype(BF16)
+    far_terms[...] = terms[half_rows(1, far_terms.shape[0]), :].astype(BF16)
+
+
+def far_rows_kernel(last, q_arrived, q_out_inner, screen, refl, after, inward, outward, terms):
+    del after
+    _, total = outer_rows(1, last, q_arrived, q_out_inner, screen, refl, inward, outward)
+    terms[...] = total.astype(BF16)
 
 
 def outer_rows(of, last, q_arrived, q_out_inner, screen, refl, inward, outward):
@@ -456,29 +459,28 @@
     return copies(0, down_out, up_out)
 
 
-def home_kernel(inward, outward, far_inward, far_outward, down_out, up_out, sems):
-    rows_x, half = inward.shape[2], far_inward.shape[2]
-    waits = send_home(1, pl.ds(0, rows_x), inward, outward, down_out, up_out, sems.at[0])
-    waits += send_home(0, half_rows(1, half), far_inward, far_outward, down_out, up_out, sems.at[1])
+def near_rows_kernel(
+    last, q_arrived, q_out_inner, screen, refl, inner_in, inner_out, far_in, far_out,
+    down_out, up_out, terms,
+    inward, outward, sems,
+):
+    rows_x, half = inner_in.shape[2], far_in.shape[2]
+    waits = send_home(1, pl.ds(0, rows_x), inner_in, inner_out, down_out, up_out, sems.at[0])
+    waits += send_home(0, half_rows(1, half), far_in, far_out, down_out, up_out, sems.at[1])
+    rows, total = outer_rows(0, last, q_arrived, q_out_inner, screen, refl, inward, outward)
+    waits += send_home(0, rows, inward, outward, down_out, up_out, sems.at[2])
+    terms[...] = total
     for copy in waits:
         copy.wait()
 
 
-def near_rows_kernel(
-    scale, last, q_arrived, q_out_inner, screen, refl, inner_terms, other, down_in, up_in,
-    down_out, up_out, gradient,
-    inward, outward, sums, sems,
-):
-    del down_in, up_in
-    rows, total = outer_rows(0, last, q_arrived, q_out_inner, screen, refl, inward, outward)
-    waits = send_home(0, rows, inward, outward, down_out, up_out, sems.at[0])
+def gradient_kernel(scale, outer_terms, inner_terms, outer_other, inner_other, gradient, sums, sems):
     odd = odd_place()
-    sums[odd] = scale * (total + other[0].astype(F32))
-    sums[1 - odd] = scale * (inner_terms[rows, :] + other[1].astype(F32))
-    done = pltpu.make_async_copy(sums, gradient, sems.at[1, 0])
+    sums[odd] = scale * (outer_terms[...] + outer_other[...].astype(F32))
+    sums[1 - odd] = scale * (inner_terms[half_rows(0, sums.shape[1]), :] + inner_other[...].astype(F32))
+    done = pltpu.make_async_copy(sums, gradient, sems.at[0])
     done.start()
-    for copy in waits + [done]:
-        copy.wait()
+    done.wait()
 
 
 def per_device(down_state, up_state, source, reflect, screen_class, screen_values, freq_index):
@@ -554,38 +556,48 @@
         inner_kernel, [VMEM] * 7, [VMEM] * 2, [plane] * 2, buffers(2) + [work(2 * fronts)]
     )(in_outer_1, partner_1, *fixed)
     partner_2 = to_partner(in_inner_2)
+    q_out_inner_2 = call(spread_kernel, [VMEM] * 4, VMEM, plane, [work(fronts)])(out_inner_2, phase, hx, hy)
     in_outer_2, last_far, last_near = call(
-        last_edge_kernel, [VMEM] * 8, [VMEM] * 3, [plane] + [half_plane] * 2, buffers(2) + [work(fronts)]
-    )(arrived_1, source, q_out_inner_1, *fixed)
+        last_edge_kernel,
+        [VMEM] * 8 + [pl.BlockSpec(memory_space=pl.ANY)],
+        [VMEM] * 3,
+        [plane] + [half_plane] * 2,
+        buffers(2) + [work(fronts)],
+    )(arrived_1, source, q_out_inner_1, *fixed, q_out_inner_2)
     last_far = to_beyond(last_far)
     last_near = to_beyond(last_near)
-    inner_in, inner_out, inner_terms, q_out_inner_2 = call(
+    half_sum = jax.ShapeDtypeStruct((half, rows_y), BF16)
+    inner_in, inner_out, inner_terms, inner_far = call(
         last_inner_kernel,
-        [VMEM] * 8,
+        [VMEM] * 7,
         [VMEM] * 4,
-        [plane] * 2 + [jax.ShapeDtypeStruct((rows_x, rows_y), F32), plane],
-        buffers(2) + [work(3 * fronts)],
-    )(in_outer_2, partner_2, out_inner_2, *fixed)
-    far_in, far_out, terms = call(
+        [plane] * 2 + [jax.ShapeDtypeStruct((rows_x, rows_y), F32), half_sum],
+        buffers(2) + [work(2 * fronts)],
+    )(in_outer_2, partner_2, *fixed)
+    inner_other = across(inner_far) if shots == 2 else jnp.zeros_like(inner_far)
+    far_in, far_out, outer_far = call(
         far_rows_kernel,
-        [VMEM] * 6,
+        [VMEM] * 5 + [pl.BlockSpec(memory_space=pl.ANY)],
         [VMEM] * 3,
-        [half_plane] * 2 + [jax.ShapeDtypeStruct((2, half, rows_y), BF16)],
+        [half_plane] * 2 + [half_sum],
     )(last_far, q_arrived, q_out_inner_2, screen, refl, inner_terms)
-    other = across(terms) if shots == 2 else jnp.zeros_like(terms)
-    down, up = call(home_kernel, [VMEM] * 4, [HBM] * 2, [state] * 2, [dma((2, 2))])(
-        inner_in, inner_out, far_in, far_out
-    )
-    down, up, gradient = call(
-        functools.partial(near_rows_kernel, scale),
-        [VMEM] * 7 + [HBM] * 2,
-        [HBM] * 3,
-        [state, state, jax.ShapeDtypeStruct((2, half, rows_y), F32)],
-        buffers(2, half_plane) + [pltpu.VMEM((2, half, rows_y), F32), dma((2, 2))],
-        input_output_aliases={7: 0, 8: 1},
-    )(last_near, q_arrived, q_out_inner_2, screen, refl, inner_terms, other, down, up)
+    outer_other = across(outer_far) if shots == 2 else jnp.zeros_like(outer_far)
+    down, up, outer_near = call(
+        near_rows_kernel,
+        [VMEM] * 9,
+        [HBM] * 2 + [VMEM],
+        [state, state, jax.ShapeDtypeStruct((half, rows_y), F32)],
+        buffers(2, half_plane) + [dma((3, 2))],
+    )(last_near, q_arrived, q_out_inner_2, screen, refl, inner_in, inner_out, far_in, far_out)
+    gradient = call(
+        functools.partial(gradient_kernel, scale),
+        [VMEM] * 4,
+        HBM,
+        jax.ShapeDtypeStruct((2, half, rows_y), F32),
+        [pltpu.VMEM((2, half, rows_y), F32), dma((1,))],
+    )(outer_near, inner_terms, outer_other, inner_other)
     if shots != 2:
-        terms = scale * terms.astype(F32)
+        terms = scale * jnp.stack([outer_far, inner_far]).astype(F32)
         far = jnp.where(odd_place() == 0, terms, terms[::-1])
         top = lax.rem(lax.axis_index("shot"), 2) == 0
         whole = jnp.concatenate([jnp.where(top, gradient, far), jnp.where(top, far, gradient)], axis=1)

time: 50.3 us -> 49.2 us (0.978)
  waiting for transfers between devices: 18.3 us -> 15.8 us
  starting transfers between devices: 13 us -> 14.5 us
    ppermute x1 -> x2, waiting for transfers between devices: 2.29 us -> 0.55 us  [the longest x1 0.55 us: per_device(): outer_other = across(outer_far) if shots == 2 else jnp.zeros_like(outer_far)]
    ppermute x1 -> x2, starting transfers between devices: 1.56 us -> 3.04 us  [the longest x1 1.54 us: per_device(): inner_other = across(inner_far) if shots == 2 else jnp.zeros_like(inner_far)]
    ppermute x1, waiting for transfers between devices: 0.01 us -> 0.91 us  [per_device(): last_near = to_beyond(last_near)]
    ppermute x1, waiting for transfers between devices: 0.89 us -> 0.01 us  [per_device(): last_far = to_beyond(last_far)]
    ppermute x1, waiting for transfers between devices: 9.36 us -> 8.53 us  [per_device(): arrived_1 = to_beyond(out_outer_1)]
    pallas_call x5 -> x6, Pallas kernels: 6.9 us -> 6.96 us  [the longest x1 1.97 us: per_device(): call(last_edge_kernel, [VMEM] * 8 + [pl.BlockSpec(memory_space=pl.ANY)],...]
  transfers between devices with their start and end apart: 8 -> 9, of which waited for: 4 -> 4; matrix products, arithmetic and copies ran while one was open for 0% -> 0% of each run, Pallas kernels for 31% -> 32%
where the time goes in v6:
time: 49.2 us; the launch traced here: 49 us
  Pallas kernels  17.7 us (36%)
  waiting for transfers between devices  15.8 us (32%)
  starting transfers between devices  14.5 us (29%)
  between operations  1 us (2%)
    ppermute x1, waiting for transfers between devices, per_device(): arrived_1 = to_beyond(out_outer_1)  8.53 us
    ppermute x1, waiting for transfers between devices, per_device(): arrived_0 = to_beyond(out_outer)  5.84 us
    pallas_call x1, Pallas kernels, per_device(): call(setup_kernel, [HBM] * 4 + [SMEM] * 2 + [VMEM] * 2, [VMEM] * 5, [plan...  4.65 us
    ppermute x1, starting transfers between devices, per_device(): last_near = to_beyond(last_near)  3.82 us
    pallas_call x1, Pallas kernels, per_device(): call(last_edge_kernel, [VMEM] * 8 + [pl.BlockSpec(memory_space=pl.ANY)],...  1.97 us
    pallas_call x1, Pallas kernels, per_device(): call(ahead_kernel, [VMEM] * 7, [VMEM] * 2, [plane] * 2, buffers(2) + [wor...  1.94 us
    ppermute x1, starting transfers between devices, per_device(): arrived_0 = to_beyond(out_outer)  1.92 us
    ppermute x1, starting transfers between devices, per_device(): arrived_1 = to_beyond(out_outer_1)  1.92 us
  transfers between devices with their start and end apart: 9, of which 4 were waited for; matrix products, arithmetic and copies ran while one was open for 0% of the time, Pallas kernels for 32%

profile of v6, /device:TPU:4, one launch (start us, length us, event | category | flops | bytes accessed | tf_op | source)
XLA Modules:
  0.0 49.0 jit_solution(12434647542201592879)
XLA Ops:
  0.6 0.0 copy-start
  0.6 0.0 copy-start.3
  0.7 1.3 %shard_map.112 = (bf16[2,2,256,256]{3,2,1,0:T(8,128)(2,1)S(1)}, bf16[2,2,256,256]{3,2,1,0:T(8,128)(2,1)S(1)}) custom-call(bf16[2,2,2,256,256]{4,3,2,1,0:T(8,128)(2,1)} %down.3, bf16[2,2,2,256,256]{4,3,2,1,0:T(8,128)(2,1)} %up.3), custom_call_target="tpu_custom_call" | custom-call | tf_op jit(solution)/shard_map/pallas_call | solution.py:529
  2.0 0.1 collective-permute-start.2
  2.0 1.9 %collective-permute-start = (bf16[2,2,256,256]{3,2,1,0:T(8,128)(2,1)S(1)}, bf16[2,2,256,256]{3,2,1,0:T(8,128)(2,1)S(1)}, u32[]{:S(2)}, u32[]{:S(2)}) collective-permute-start(bf16[2,2,256,256]{3,2,1,0:T(8,128)(2,1)S(1)} %get-tuple-element.30), channel_id=1, source_target_pairs={{2,4},{6,8},{10,12},{14,16},{18,20},{22,24},{26,28},{4,2},{8,6},{1... | collective-permute-start | bytes 1572872 | tf_op jit(solution)/shard_map/ppermute | solution.py:532
  4.0 4.7 %shard_map.113 = (bf16[2,2,256,256]{3,2,1,0:T(8,128)(2,1)S(1)}, bf16[2,2,256,256]{3,2,1,0:T(8,128)(2,1)S(1)}, f32[2,2,2,256,256]{4,3,2,1,0:T(8,128)S(1)}, f32[2,...) custom-call(bf16[2,2,2,256,256]{4,3,2,1,0:T(8,128)(2,1)} %down.3, bf16[2,2,2,256,256]{4,3,2,1,0:T(8,128)(2,1)} %up.3, ...), custom_call_target="tpu_custom_call" | custom-call | tf_op jit(solution)/shard_map/pallas_call | solution.py:534
  8.6 0.0 collective-permute-done.2.partner
  8.7 0.0 copy-start.1
  8.7 1.9 %shard_map.115 = (bf16[2,2,256,256]{3,2,1,0:T(8,128)(2,1)S(1)}, bf16[2,2,256,256]{3,2,1,0:T(8,128)(2,1)S(1)}) custom-call(bf16[2,2,256,256]{3,2,1,0:T(8,128)(2,1)S(1)} %collective-permute-done.2.partner, bf16[2,2,256,256]{3,2,1,0:T(8,128)(2,1)S(1)} %get-tuple-element.37.q_in_outer, f32[2,2,2,256,256]{4,3,2,1,0:T(8,128)S(1)} %get-tuple-element.32.screen, ...), custom_call_target="tpu_custom_call" | custom-call | tf_op jit(solution)/shard_map/pallas_call | solution.py:547
  10.6 1.7 %collective-permute-start.3 = (bf16[2,2,256,256]{3,2,1,0:T(8,128)(2,1)S(1)}, bf16[2,2,256,256]{3,2,1,0:T(8,128)(2,1)S(1)}, u32[]{:S(2)}, u32[]{:S(2)}) collective-permute-start(bf16[2,2,256,256]{3,2,1,0:T(8,128)(2,1)S(1)} %get-tuple-element.40), channel_id=1, source_target_pairs={{0,2},{2,0},{4,6},{6,4},{8,10},{10,8},{12,14},{14,12},{16,18},{18,... | collective-permute-start | bytes 1572872 | tf_op jit(solution)/shard_map/ppermute | solution.py:550
  12.3 5.8 %collective-permute-done.arrived = bf16[2,2,256,256]{3,2,1,0:T(8,128)(2,1)S(1)} collective-permute-done((bf16[2,2,256,256]{3,2,1,0:T(8,128)(2,1)S(1)}, bf16[2,2,256,256]{3,2,1,0:T(8,128)(2,1)S(1)}, u32[]{:S(2)}, u32[]{:S(2)}) %collective-permute-start) | collective-permute-done | bytes 524320 | tf_op jit(solution)/shard_map/ppermute | solution.py:532
  18.2 1.2 %shard_map.114 = (bf16[2,2,256,256]{3,2,1,0:T(8,128)(2,1)S(1)}, bf16[2,2,256,256]{3,2,1,0:T(8,128)(2,1)S(1)}, bf16[2,2,256,256]{3,2,1,0:T(8,128)(2,1)S(1)}) custom-call(bf16[2,2,256,256]{3,2,1,0:T(8,128)(2,1)S(1)} %collective-permute-done.arrived, bf16[2,2,256,256]{3,2,1,0:T(8,128)(2,1)S(1)} %copy-done.1, ...), custom_call_target="tpu_custom_call" | custom-call | tf_op jit(solution)/shard_map/pallas_call | solution.py:551
  19.4 1.9 %collective-permute-start.1 = (bf16[2,2,256,256]{3,2,1,0:T(8,128)(2,1)S(1)}, bf16[2,2,256,256]{3,2,1,0:T(8,128)(2,1)S(1)}, u32[]{:S(2)}, u32[]{:S(2)}) collective-permute-start(bf16[2,2,256,256]{3,2,1,0:T(8,128)(2,1)S(1)} %get-tuple-element.35), channel_id=1, source_target_pairs={{2,4},{6,8},{10,12},{14,16},{18,20},{22,24},{26,28},{4,2},{8,6},{1... | collective-permute-start | bytes 1572872 | tf_op jit(solution)/shard_map/ppermute | solution.py:554
  21.3 0.0 collective-permute-done.3.partner
  21.3 1.6 %shard_map.116 = (bf16[2,2,256,256]{3,2,1,0:T(8,128)(2,1)S(1)}, bf16[2,2,256,256]{3,2,1,0:T(8,128)(2,1)S(1)}) custom-call(bf16[2,2,256,256]{3,2,1,0:T(8,128)(2,1)S(1)} %get-tuple-element.39.inward_outer, bf16[2,2,256,256]{3,2,1,0:T(8,128)(2,1)S(1)} %collective-permute-done.3.partner, f32[2,2,2,256,256]{4,3,2,1,0:T(8,128)S(1)} %get-tuple-element.32.screen, ...), custom_call_target="tpu_custom_call" | custom-call | tf_op jit(solution)/shard_map/pallas_call | solution.py:555
  23.0 0.1 collective-permute-start.5
  23.1 0.9 %shard_map.117.after.q_out_inner = bf16[2,2,256,256]{3,2,1,0:T(8,128)(2,1)S(1)} custom-call(bf16[2,2,256,256]{3,2,1,0:T(8,128)(2,1)S(1)} %get-tuple-element.41.fields, f32[2,2,256,256]{3,2,1,0:T(8,128)S(1)} %get-tuple-element.34.phase, bf16[256,256]{1,0:T(8,128)(2,1)S(1)} %copy-done, bf16[256,256]{1,0:T(8,128)(2,1)S(1)} %copy-done), custom_call_target="tpu_custom_call" | custom-call | tf_op jit(solution)/shard_map/pallas_call | solution.py:559
  23.9 8.5 %collective-permute-done.1.arrived = bf16[2,2,256,256]{3,2,1,0:T(8,128)(2,1)S(1)} collective-permute-done((bf16[2,2,256,256]{3,2,1,0:T(8,128)(2,1)S(1)}, bf16[2,2,256,256]{3,2,1,0:T(8,128)(2,1)S(1)}, u32[]{:S(2)}, u32[]{:S(2)}) %collective-permute-start.1) | collective-permute-done | bytes 524320 | tf_op jit(solution)/shard_map/ppermute | solution.py:554
  32.5 2.0 %shard_map.118 = (bf16[2,2,256,256]{3,2,1,0:T(8,128)(2,1)S(1)}, bf16[2,2,128,256]{3,2,1,0:T(8,128)(2,1)S(1)}, bf16[2,2,128,256]{3,2,1,0:T(8,128)(2,1)S(1)}) custom-call(bf16[2,2,256,256]{3,2,1,0:T(8,128)(2,1)S(1)} %collective-permute-done.1.arrived, bf16[2,2,256,256]{3,2,1,0:T(8,128)(2,1)S(1)} %copy-done.1, ...), custom_call_target="tpu_custom_call" | custom-call | tf_op jit(solution)/shard_map/pallas_call | solution.py:560
  34.4 1.9 %collective-permute-start.6 = (bf16[2,2,128,256]{3,2,1,0:T(8,128)(2,1)S(1)}, bf16[2,2,128,256]{3,2,1,0:T(8,128)(2,1)S(1)}, u32[]{:S(2)}, u32[]{:S(2)}) collective-permute-start(bf16[2,2,128,256]{3,2,1,0:T(8,128)(2,1)S(1)} %get-tuple-element.48), channel_id=1, source_target_pairs={{2,4},{6,8},{10,12},{14,16},{18,20},{22,24},{26,28},{4,2},{8,6},{1... | collective-permute-start | bytes 786440 | tf_op jit(solution)/shard_map/ppermute | solution.py:567
  36.4 3.8 %collective-permute-start.4 = (bf16[2,2,128,256]{3,2,1,0:T(8,128)(2,1)S(1)}, bf16[2,2,128,256]{3,2,1,0:T(8,128)(2,1)S(1)}, u32[]{:S(2)}, u32[]{:S(2)}) collective-permute-start(bf16[2,2,128,256]{3,2,1,0:T(8,128)(2,1)S(1)} %get-tuple-element.42), channel_id=1, source_target_pairs={{2,4},{6,8},{10,12},{14,16},{18,20},{22,24},{26,28},{4,2},{8,6},{1... | collective-permute-start | bytes 786440 | tf_op jit(solution)/shard_map/ppermute | solution.py:568
  40.2 0.0 collective-permute-done.5.partner
  40.2 1.7 %shard_map.119 = (bf16[2,2,256,256]{3,2,1,0:T(8,128)(2,1)S(1)}, bf16[2,2,256,256]{3,2,1,0:T(8,128)(2,1)S(1)}, f32[256,256]{1,0:T(8,128)S(1)}, bf16[128,256]{1,0:T(8,128)(2,1)S(1)}) custom-call(bf16[2,2,256,256]{3,2,1,0:T(8,128)(2,1)S(1)} %get-tuple-element.44.inward_outer, bf16[2,2,256,256]{3,2,1,0:T(8,128)(2,1)S(1)} %collective-permute-done.5.partner, ...), custom_call_target="tpu_custom_call" | custom-call | tf_op jit(solution)/shard_map/pallas_call | solution.py:570
  41.9 1.5 %collective-permute-start.8 = (bf16[128,256]{1,0:T(8,128)(2,1)S(1)}, bf16[128,256]{1,0:T(8,128)(2,1)S(1)}, u32[]{:S(2)}, u32[]{:S(2)}) collective-permute-start(bf16[128,256]{1,0:T(8,128)(2,1)S(1)} %get-tuple-element.56), channel_id=1, source_target_pairs={{0,1},{1,0},{2,3},{3,2},{4,5},{5,4},{6,7},{7,6},{8,9},{9,8},{10,11... | collective-permute-start | bytes 196616 | tf_op jit(solution)/shard_map/ppermute | solution.py:577
  43.4 0.0 collective-permute-done.6.last
  43.4 0.3 shard_map.120
  43.8 1.5 %collective-permute-start.7 = (bf16[128,256]{1,0:T(8,128)(2,1)S(1)}, bf16[128,256]{1,0:T(8,128)(2,1)S(1)}, u32[]{:S(2)}, u32[]{:S(2)}) collective-permute-start(bf16[128,256]{1,0:T(8,128)(2,1)S(1)} %get-tuple-element.55), channel_id=1, source_target_pairs={{0,1},{1,0},{2,3},{3,2},{4,5},{5,4},{6,7},{7,6},{8,9},{9,8},{10,11... | collective-permute-start | bytes 196616 | tf_op jit(solution)/shard_map/ppermute | solution.py:584
  45.3 0.9 %collective-permute-done.4.last = bf16[2,2,128,256]{3,2,1,0:T(8,128)(2,1)S(1)} collective-permute-done((bf16[2,2,128,256]{3,2,1,0:T(8,128)(2,1)S(1)}, bf16[2,2,128,256]{3,2,1,0:T(8,128)(2,1)S(1)}, u32[]{:S(2)}, u32[]{:S(2)}) %collective-permute-start.4) | collective-permute-done | bytes 262176 | tf_op jit(solution)/shard_map/ppermute | solution.py:568
  46.2 1.4 %shard_map.121 = (bf16[2,2,2,256,256]{4,3,2,1,0:T(8,128)(2,1)}, bf16[2,2,2,256,256]{4,3,2,1,0:T(8,128)(2,1)}, f32[128,256]{1,0:T(8,128)S(1)}) custom-call(bf16[2,2,128,256]{3,2,1,0:T(8,128)(2,1)S(1)} %collective-permute-done.4.last, bf16[2,2,256,256]{3,2,1,0:T(8,128)(2,1)S(1)} %get-tuple-element.43.q_arrived, ...), custom_call_target="tpu_custom_call" | custom-call | tf_op jit(solution)/shard_map/pallas_call | solution.py:585
  47.6 0.0 collective-permute-done.8.inner_other
  47.6 0.5 %collective-permute-done.7.outer_other = bf16[128,256]{1,0:T(8,128)(2,1)S(1)} collective-permute-done((bf16[128,256]{1,0:T(8,128)(2,1)S(1)}, bf16[128,256]{1,0:T(8,128)(2,1)S(1)}, u32[]{:S(2)}, u32[]{:S(2)}) %collective-permute-start.7) | collective-permute-done | bytes 65568 | tf_op jit(solution)/shard_map/ppermute | solution.py:584
  48.1 0.7 %shard_map.122 = f32[2,128,256]{2,1,0:T(8,128)} custom-call(f32[128,256]{1,0:T(8,128)S(1)} %get-tuple-element.54.outer_terms, f32[256,256]{1,0:T(8,128)S(1)} %get-tuple-element.49.after.inner_terms, bf16[128,256]{1,0:T(8,128)(2,1)S(1)} %collective-permute-done.7.outer_other, bf16[128,256]{1,0:T(8,128)(2,1)S(1)} %collective-permute-done.8.inner_other), custom_call_target="tpu_custom_call" | custom-call | tf_op jit(solution)/shard_map/pallas_call | solution.py:592
  (5 shorter events, 0.0 us)
Async XLA Ops:
  0.6 3.3 %copy-start = (bf16[256,256]{1,0:T(8,128)(2,1)S(1)}, bf16[256,256]{1,0:T(8,128)(2,1)}, u32[]{:S(2)}) copy-start(bf16[256,256]{1,0:T(8,128)(2,1)} %constant.2.clone.hx.hy) | copy-start | bytes 393220
  0.6 3.3 %copy-start.3 = (s32[2]{0:T(128)S(1)}, s32[2]{0:T(128)}, u32[]{:S(2)}) copy-start(s32[2]{0:T(128)} %freq.1) | copy-start | bytes 28
  0.7 3.3 %copy-start.2 = (f32[16]{0:T(128)S(1)}, f32[16]{0:T(128)}, u32[]{:S(2)}) copy-start(f32[16]{0:T(128)} %slowness.1) | copy-start | bytes 196
  2.0 6.7 %collective-permute-start.2 = (bf16[2,2,256,256]{3,2,1,0:T(8,128)(2,1)S(1)}, bf16[2,2,256,256]{3,2,1,0:T(8,128)(2,1)S(1)}, u32[]{:S(2)}, u32[]{:S(2)}) collective-permute-start(bf16[2,2,256,256]{3,2,1,0:T(8,128)(2,1)S(1)} %get-tuple-element.36), channel_id=1, source_target_pairs={{0,2},{2,0},{4,6},{6,4},{8,10},{10,8},{12,14},{14,12},{16,18},{18,... | collective-permute-start | bytes 1572872 | tf_op jit(solution)/shard_map/ppermute | solution.py:533
  2.0 16.1 %collective-permute-start = (bf16[2,2,256,256]{3,2,1,0:T(8,128)(2,1)S(1)}, bf16[2,2,256,256]{3,2,1,0:T(8,128)(2,1)S(1)}, u32[]{:S(2)}, u32[]{:S(2)}) collective-permute-start(bf16[2,2,256,256]{3,2,1,0:T(8,128)(2,1)S(1)} %get-tuple-element.30), channel_id=1, source_target_pairs={{2,4},{6,8},{10,12},{14,16},{18,20},{22,24},{26,28},{4,2},{8,6},{1... | collective-permute-start | bytes 1572872 | tf_op jit(solution)/shard_map/ppermute | solution.py:532
  8.7 9.5 %copy-start.1 = (bf16[2,2,256,256]{3,2,1,0:T(8,128)(2,1)S(1)}, bf16[2,2,256,256]{3,2,1,0:T(8,128)(2,1)}, u32[]{:S(2)}) copy-start(bf16[2,2,256,256]{3,2,1,0:T(8,128)(2,1)} %source.3) | copy-start | bytes 1572868
  10.6 10.7 %collective-permute-start.3 = (bf16[2,2,256,256]{3,2,1,0:T(8,128)(2,1)S(1)}, bf16[2,2,256,256]{3,2,1,0:T(8,128)(2,1)S(1)}, u32[]{:S(2)}, u32[]{:S(2)}) collective-permute-start(bf16[2,2,256,256]{3,2,1,0:T(8,128)(2,1)S(1)} %get-tuple-element.40), channel_id=1, source_target_pairs={{0,2},{2,0},{4,6},{6,4},{8,10},{10,8},{12,14},{14,12},{16,18},{18,... | collective-permute-start | bytes 1572872 | tf_op jit(solution)/shard_map/ppermute | solution.py:550
  19.4 13.1 %collective-permute-start.1 = (bf16[2,2,256,256]{3,2,1,0:T(8,128)(2,1)S(1)}, bf16[2,2,256,256]{3,2,1,0:T(8,128)(2,1)S(1)}, u32[]{:S(2)}, u32[]{:S(2)}) collective-permute-start(bf16[2,2,256,256]{3,2,1,0:T(8,128)(2,1)S(1)} %get-tuple-element.35), channel_id=1, source_target_pairs={{2,4},{6,8},{10,12},{14,16},{18,20},{22,24},{26,28},{4,2},{8,6},{1... | collective-permute-start | bytes 1572872 | tf_op jit(solution)/shard_map/ppermute | solution.py:554
  23.0 17.2 %collective-permute-start.5 = (bf16[2,2,256,256]{3,2,1,0:T(8,128)(2,1)S(1)}, bf16[2,2,256,256]{3,2,1,0:T(8,128)(2,1)S(1)}, u32[]{:S(2)}, u32[]{:S(2)}) collective-permute-start(bf16[2,2,256,256]{3,2,1,0:T(8,128)(2,1)S(1)} %get-tuple-element.45), channel_id=1, source_target_pairs={{0,2},{2,0},{4,6},{6,4},{8,10},{10,8},{12,14},{14,12},{16,18},{18,... | collective-permute-start | bytes 1572872 | tf_op jit(solution)/shard_map/ppermute | solution.py:558
  34.4 9.0 %collective-permute-start.6 = (bf16[2,2,128,256]{3,2,1,0:T(8,128)(2,1)S(1)}, bf16[2,2,128,256]{3,2,1,0:T(8,128)(2,1)S(1)}, u32[]{:S(2)}, u32[]{:S(2)}) collective-permute-start(bf16[2,2,128,256]{3,2,1,0:T(8,128)(2,1)S(1)} %get-tuple-element.48), channel_id=1, source_target_pairs={{2,4},{6,8},{10,12},{14,16},{18,20},{22,24},{26,28},{4,2},{8,6},{1... | collective-permute-start | bytes 786440 | tf_op jit(solution)/shard_map/ppermute | solution.py:567
  36.4 9.8 %collective-permute-start.4 = (bf16[2,2,128,256]{3,2,1,0:T(8,128)(2,1)S(1)}, bf16[2,2,128,256]{3,2,1,0:T(8,128)(2,1)S(1)}, u32[]{:S(2)}, u32[]{:S(2)}) collective-permute-start(bf16[2,2,128,256]{3,2,1,0:T(8,128)(2,1)S(1)} %get-tuple-element.42), channel_id=1, source_target_pairs={{2,4},{6,8},{10,12},{14,16},{18,20},{22,24},{26,28},{4,2},{8,6},{1... | collective-permute-start | bytes 786440 | tf_op jit(solution)/shard_map/ppermute | solution.py:568
  41.9 5.7 %collective-permute-start.8 = (bf16[128,256]{1,0:T(8,128)(2,1)S(1)}, bf16[128,256]{1,0:T(8,128)(2,1)S(1)}, u32[]{:S(2)}, u32[]{:S(2)}) collective-permute-start(bf16[128,256]{1,0:T(8,128)(2,1)S(1)} %get-tuple-element.56), channel_id=1, source_target_pairs={{0,1},{1,0},{2,3},{3,2},{4,5},{5,4},{6,7},{7,6},{8,9},{9,8},{10,11... | collective-permute-start | bytes 196616 | tf_op jit(solution)/shard_map/ppermute | solution.py:577
  43.8 4.3 %collective-permute-start.7 = (bf16[128,256]{1,0:T(8,128)(2,1)S(1)}, bf16[128,256]{1,0:T(8,128)(2,1)S(1)}, u32[]{:S(2)}, u32[]{:S(2)}) collective-permute-start(bf16[128,256]{1,0:T(8,128)(2,1)S(1)} %get-tuple-element.55), channel_id=1, source_target_pairs={{0,1},{1,0},{2,3},{3,2},{4,5},{5,4},{6,7},{7,6},{8,9},{9,8},{10,11... | collective-permute-start | bytes 196616 | tf_op jit(solution)/shard_map/ppermute | solution.py:584

commit v7 on v5

--- a/solution.py
+++ b/solution.py
@@ -153,7 +153,7 @@
     jobs = list(enumerate(jobs))
     for slot, (plane, _, _) in jobs:
         for part in range(2):
-            work[slot, part] = mm(plane[part], hy[...]).astype(BF16)
+            work[slot, part] = mm(plane(part) if callable(plane) else plane[part], hy[...]).astype(BF16)
     for slot, (_, front, _) in jobs:
         turn_re, turn_im = phase[front, 0], phase[front, 1]
         part_re = mm(hx[...], work[slot, 0])
@@ -165,7 +165,11 @@
             work[slot, part] = mm(hx[...], work[slot, part]).astype(BF16)
     for slot, (_, _, target) in jobs:
         for part in range(2):
-            target[part] = mm(work[slot, part], hy[...]).astype(BF16)
+            if isinstance(target, list):
+                for rows, piece in target:
+                    piece[part] = mm(work[slot, part, rows, :], hy[...]).astype(BF16)
+            else:
+                target[part] = mm(work[slot, part], hy[...]).astype(BF16)
 
 
 def screened(real_part, imag_part, screen_re, screen_im):
@@ -175,13 +179,16 @@
     )
 
 
-def mixed(a_re, a_im, b_re, b_im, refl, screen_re, screen_im):
+def mixed(a_re, a_im, b_re, b_im, refl, screen_re, screen_im, waves="both"):
     a_re, a_im, b_re, b_im = (part.astype(F32) for part in (a_re, a_im, b_re, b_im))
     step_re = refl * (a_re - b_re)
     step_im = refl * (a_im - b_im)
-    inward = screened(a_re + step_re, a_im + step_im, screen_re, screen_im)
-    outward = screened(b_re + step_re, b_im + step_im, screen_re, screen_im)
-    return tuple(part.astype(BF16) for part in inward + outward)
+    fields = ()
+    if waves != "outward":
+        fields += screened(a_re + step_re, a_im + step_im, screen_re, screen_im)
+    if waves != "inward":
+        fields += screened(b_re + step_re, b_im + step_im, screen_re, screen_im)
+    return fields
 
 
 def put(target, real_part, imag_part):
@@ -322,54 +329,54 @@
     spread([(field.at[front], front, q_out_inner.at[front]) for front in everyone], work, hx, hy, phase)
 
 
-def outer_step(arrived, source, q_out_inner, screen, refl, phase, hx, hy, inward, outward, q_arrived, work):
+def entering(arrived, source, front):
+    first = lax.axis_index("depth") == 0
+    return lambda part: jnp.where(first, source[front, part], arrived[front, part])
+
+
+def outer_step(q_arrived, q_out_inner, screen, refl, waves, field):
+    for front in range(field.shape[0]):
+        put(
+            field.at[front],
+            *mixed(
+                q_arrived[front, 0], q_arrived[front, 1], q_out_inner[front, 0], q_out_inner[front, 1],
+                refl[0], screen[0, front, 0], screen[0, front, 1], waves,
+            ),
+        )
+
+
+def edge_kernel(arrived, source, q_out_inner, screen, refl, phase, hx, hy, outward, q_arrived, work):
     everyone = range(arrived.shape[0])
-    first = lax.axis_index("depth") == 0
-    for front in everyone:
-        put(inward.at[front], *(jnp.where(first, source[front, part], arrived[front, part]) for part in range(2)))
-    spread([(inward.at[front], front, q_arrived.at[front]) for front in everyone], work, hx, hy, phase)
-    for front in everyone:
-        in_re, in_im, out_re, out_im = mixed(
-            q_arrived[front, 0], q_arrived[front, 1], q_out_inner[front, 0], q_out_inner[front, 1],
-            refl[0], screen[0, front, 0], screen[0, front, 1],
-        )
-        put(inward.at[front], in_re, in_im)
-        put(outward.at[front], out_re, out_im)
-
-
-def edge_kernel(
-    arrived, source, q_out_inner, screen, refl, phase, hx, hy,
-    inward, outward, q_arrived,
-    work,
+    spread([(entering(arrived, source, front), front, q_arrived.at[front]) for front in everyone], work, hx, hy, phase)
+    outer_step(q_arrived, q_out_inner, screen, refl, "outward", outward)
+
+
+def last_edge_kernel(
+    arrived, source, q_out_inner, screen, refl, phase, hx, hy, after,
+    q_arrived, last_far, last_near,
+    outward, work,
 ):
-    outer_step(arrived, source, q_out_inner, screen, refl, phase, hx, hy, inward, outward, q_arrived, work)
-
-
-def last_edge_kernel(
-    arrived, source, q_out_inner, screen, refl, phase, hx, hy,
-    inward, last_far, last_near,
-    outward, q_field, work,
-):
+    del after
     everyone = range(arrived.shape[0])
     half = arrived.shape[2] // 2
-    far_bottom = lax.rem(lax.axis_index("shot"), 2) == 0
-    outer_step(arrived, source, q_out_inner, screen, refl, phase, hx, hy, inward, outward, q_field, work)
-    spread([(outward.at[front], front, q_field.at[front]) for front in everyone], work, hx, hy, phase)
-    for front in everyone:
-        for part in range(2):
-            top, bottom = q_field[front, part, :half], q_field[front, part, half:]
-            last_far[front, part] = jnp.where(far_bottom, bottom, top)
-            last_near[front, part] = jnp.where(far_bottom, top, bottom)
+    spread([(entering(arrived, source, front), front, q_arrived.at[front]) for front in everyone], work, hx, hy, phase)
+    outer_step(q_arrived, q_out_inner, screen, refl, "outward", outward)
+    jobs = [
+        (outward.at[front], front, [(half_rows(1, half), last_far.at[front]), (half_rows(0, half), last_near.at[front])])
+        for front in everyone
+    ]
+    spread(jobs, work, hx, hy, phase)
 
 
 def inner_kernel(
-    inward_outer, partner, screen, refl, phase, hx, hy,
+    q_arrived, q_out_inner, partner, screen, refl, phase, hx, hy,
     inward, outward,
-    q_inward, q_partner, work,
+    field, q_inward, q_partner, work,
 ):
     everyone = range(partner.shape[0])
-    jobs = [(inward_outer.at[front], front, q_inward.at[front]) for front in everyone]
-    jobs += [(partner.at[front], front, q_partner.at[front]) for front in everyone]
+    outer_step(q_arrived, q_out_inner, screen, refl, "inward", field)
+    jobs = [(partner.at[front], front, q_partner.at[front]) for front in everyone]
+    jobs += [(field.at[front], front, q_inward.at[front]) for front in everyone]
     spread(jobs, work, hx, hy, phase)
     for front in everyone:
         in_re, in_im, out_re, out_im = mixed(
@@ -380,15 +387,20 @@
         put(outward.at[front], out_re, out_im)
 
 
+def spread_kernel(fields, phase, hx, hy, q_fields, work):
+    everyone = range(fields.shape[0])
+    spread([(fields.at[front], front, q_fields.at[front]) for front in everyone], work, hx, hy, phase)
+
+
 def last_inner_kernel(
-    inward_outer, partner, out_inner, screen, refl, phase, hx, hy,
-    inward, outward, terms, q_out_inner,
-    q_inward, q_partner, work,
+    q_arrived, q_out_inner, partner, screen, refl, phase, hx, hy,
+    inward, outward, terms,
+    field, q_inward, q_partner, work,
 ):
     everyone = range(partner.shape[0])
-    jobs = [(inward_outer.at[front], front, q_inward.at[front]) for front in everyone]
-    jobs += [(partner.at[front], front, q_partner.at[front]) for front in everyone]
-    jobs += [(out_inner.at[front], front, q_out_inner.at[front]) for front in everyone]
+    outer_step(q_arrived, q_out_inner, screen, refl, "inward", field)
+    jobs = [(partner.at[front], front, q_partner.at[front]) for front in everyone]
+    jobs += [(field.at[front], front, q_inward.at[front]) for front in everyone]
     spread(jobs, work, hx, hy, phase)
     total = None
     for front in everyone:
@@ -404,10 +416,7 @@
     terms[...] = total
 
 
-def far_rows_kernel(
-    last, q_arrived, q_out_inner, screen, refl, inner_terms,
-    inward, outward, terms,
-):
+def far_rows_kernel(last, q_arrived, q_out_inner, screen, refl, inner_terms, inward, outward, terms):
     rows, total = outer_rows(1, last, q_arrived, q_out_inner, screen, refl, inward, outward)
     terms[0] = total.astype(BF16)
     terms[1] = inner_terms[rows, :].astype(BF16)
@@ -456,26 +465,20 @@
     return copies(0, down_out, up_out)
 
 
-def home_kernel(inward, outward, far_inward, far_outward, down_out, up_out, sems):
-    rows_x, half = inward.shape[2], far_inward.shape[2]
-    waits = send_home(1, pl.ds(0, rows_x), inward, outward, down_out, up_out, sems.at[0])
-    waits += send_home(0, half_rows(1, half), far_inward, far_outward, down_out, up_out, sems.at[1])
-    for copy in waits:
-        copy.wait()
-
-
 def near_rows_kernel(
-    scale, last, q_arrived, q_out_inner, screen, refl, inner_terms, other, down_in, up_in,
+    scale, last, q_arrived, q_out_inner, screen, refl, inner_in, inner_out, far_in, far_out, inner_terms, other,
     down_out, up_out, gradient,
     inward, outward, sums, sems,
 ):
-    del down_in, up_in
+    rows_x, half = inner_in.shape[2], far_in.shape[2]
+    waits = send_home(1, pl.ds(0, rows_x), inner_in, inner_out, down_out, up_out, sems.at[0])
+    waits += send_home(0, half_rows(1, half), far_in, far_out, down_out, up_out, sems.at[1])
     rows, total = outer_rows(0, last, q_arrived, q_out_inner, screen, refl, inward, outward)
-    waits = send_home(0, rows, inward, outward, down_out, up_out, sems.at[0])
+    waits += send_home(0, rows, inward, outward, down_out, up_out, sems.at[2])
     odd = odd_place()
     sums[odd] = scale * (total + other[0].astype(F32))
     sums[1 - odd] = scale * (inner_terms[rows, :] + other[1].astype(F32))
-    done = pltpu.make_async_copy(sums, gradient, sems.at[1, 0])
+    done = pltpu.make_async_copy(sums, gradient, sems.at[3, 0])
     done.start()
     for copy in waits + [done]:
         copy.wait()
@@ -546,26 +549,31 @@
         partner_0, q_in_outer_0, *fixed
     )
     partner_1 = to_partner(in_inner_1)
-    in_outer_1, out_outer_1, q_arrived = call(edge_kernel, [VMEM] * 8, [VMEM] * 3, [plane] * 3, [work(fronts)])(
+    out_outer_1, q_arrived = call(edge_kernel, [VMEM] * 8, [VMEM] * 2, [plane] * 2, [work(fronts)])(
         arrived_0, source, q_out_inner_0, *fixed
     )
     arrived_1 = to_beyond(out_outer_1)
     in_inner_2, out_inner_2 = call(
-        inner_kernel, [VMEM] * 7, [VMEM] * 2, [plane] * 2, buffers(2) + [work(2 * fronts)]
-    )(in_outer_1, partner_1, *fixed)
+        inner_kernel, [VMEM] * 8, [VMEM] * 2, [plane] * 2, buffers(3) + [work(2 * fronts)]
+    )(q_arrived, q_out_inner_0, partner_1, *fixed)
     partner_2 = to_partner(in_inner_2)
-    in_outer_2, last_far, last_near = call(
-        last_edge_kernel, [VMEM] * 8, [VMEM] * 3, [plane] + [half_plane] * 2, buffers(2) + [work(fronts)]
-    )(arrived_1, source, q_out_inner_1, *fixed)
+    q_out_inner_2 = call(spread_kernel, [VMEM] * 4, VMEM, plane, [work(fronts)])(out_inner_2, phase, hx, hy)
+    q_arrived_1, last_far, last_near = call(
+        last_edge_kernel,
+        [VMEM] * 8 + [pl.BlockSpec(memory_space=pl.ANY)],
+        [VMEM] * 3,
+        [plane] + [half_plane] * 2,
+        buffers(1) + [work(fronts)],
+    )(arrived_1, source, q_out_inner_1, *fixed, q_out_inner_2)
     last_far = to_beyond(last_far)
     last_near = to_beyond(last_near)
-    inner_in, inner_out, inner_terms, q_out_inner_2 = call(
+    inner_in, inner_out, inner_terms = call(
         last_inner_kernel,
         [VMEM] * 8,
-        [VMEM] * 4,
-        [plane] * 2 + [jax.ShapeDtypeStruct((rows_x, rows_y), F32), plane],
-        buffers(2) + [work(3 * fronts)],
-    )(in_outer_2, partner_2, out_inner_2, *fixed)
+        [VMEM] * 3,
+        [plane] * 2 + [jax.ShapeDtypeStruct((rows_x, rows_y), F32)],
+        buffers(3) + [work(2 * fronts)],
+    )(q_arrived_1, q_out_inner_1, partner_2, *fixed)
     far_in, far_out, terms = call(
         far_rows_kernel,
         [VMEM] * 6,
@@ -573,17 +581,13 @@
         [half_plane] * 2 + [jax.ShapeDtypeStruct((2, half, rows_y), BF16)],
     )(last_far, q_arrived, q_out_inner_2, screen, refl, inner_terms)
     other = across(terms) if shots == 2 else jnp.zeros_like(terms)
-    down, up = call(home_kernel, [VMEM] * 4, [HBM] * 2, [state] * 2, [dma((2, 2))])(
-        inner_in, inner_out, far_in, far_out
-    )
     down, up, gradient = call(
         functools.partial(near_rows_kernel, scale),
-        [VMEM] * 7 + [HBM] * 2,
+        [VMEM] * 11,
         [HBM] * 3,
         [state, state, jax.ShapeDtypeStruct((2, half, rows_y), F32)],
-        buffers(2, half_plane) + [pltpu.VMEM((2, half, rows_y), F32), dma((2, 2))],
-        input_output_aliases={7: 0, 8: 1},
-    )(last_near, q_arrived, q_out_inner_2, screen, refl, inner_terms, other, down, up)
+        buffers(2, half_plane) + [pltpu.VMEM((2, half, rows_y), F32), dma((4, 2))],
+    )(last_near, q_arrived, q_out_inner_2, screen, refl, inner_in, inner_out, far_in, far_out, inner_terms, other)
     if shots != 2:
         terms = scale * terms.astype(F32)
         far = jnp.where(odd_place() == 0, terms, terms[::-1])

time: 50.3 us -> 50.3 us (level)
  waiting for transfers between devices: 18.3 us -> 19.1 us
  Pallas kernels: 17.7 us -> 17 us
    ppermute x1, waiting for transfers between devices: 9.36 us -> 8.38 us  [per_device(): arrived_1 = to_beyond(out_outer_1)]
    ppermute x1, waiting for transfers between devices: 0.01 us -> 0.9 us  [per_device(): last_near = to_beyond(last_near)]
    pallas_call x6, Pallas kernels: 9.48 us -> 8.78 us  [the longest x1 1.82 us: per_device(): call(last_edge_kernel, [VMEM] * 8 + [pl.BlockSpec(memory_space=pl.ANY)],...]
  transfers between devices with their start and end apart: 8 -> 8, of which waited for: 4 -> 5; matrix products, arithmetic and copies ran while one was open for 0% -> 0% of each run, Pallas kernels for 31% -> 28%
where the time goes in v7:
time: 50.3 us; the launch traced here: 50.1 us
  waiting for transfers between devices  19.1 us (38%)
  Pallas kernels  17 us (34%)
  starting transfers between devices  13 us (26%)
  between operations  0.99 us (2%)
    ppermute x1, waiting for transfers between devices, per_device(): arrived_1 = to_beyond(out_outer_1)  8.38 us
    ppermute x1, waiting for transfers between devices, per_device(): arrived_0 = to_beyond(out_outer)  5.84 us
    pallas_call x1, Pallas kernels, per_device(): call(setup_kernel, [HBM] * 4 + [SMEM] * 2 + [VMEM] * 2, [VMEM] * 5, [plan...  4.65 us
    ppermute x1, starting transfers between devices, per_device(): last_near = to_beyond(last_near)  3.82 us
    ppermute x1, waiting for transfers between devices, per_device(): other = across(terms) if shots == 2 else jnp.zeros_like(terms)  2.57 us
    pallas_call x1, Pallas kernels, per_device(): call(ahead_kernel, [VMEM] * 7, [VMEM] * 2, [plane] * 2, buffers(2) + [wor...  1.94 us
    ppermute x1, starting transfers between devices, per_device(): arrived_0 = to_beyond(out_outer)  1.92 us
    ppermute x1, starting transfers between devices, per_device(): arrived_1 = to_beyond(out_outer_1)  1.92 us
  transfers between devices with their start and end apart: 8, of which 5 were waited for; matrix products, arithmetic and copies ran while one was open for 0% of the time, Pallas kernels for 28%

profile of v7, /device:TPU:4, one launch (start us, length us, event | category | flops | bytes accessed | tf_op | source)
XLA Modules:
  0.0 50.1 jit_solution(362482790213386441)
XLA Ops:
  0.6 0.0 copy-start
  0.6 0.0 copy-start.3
  0.7 0.0 copy-start.2
  0.7 1.3 %shard_map.112 = (bf16[2,2,256,256]{3,2,1,0:T(8,128)(2,1)S(1)}, bf16[2,2,256,256]{3,2,1,0:T(8,128)(2,1)S(1)}) custom-call(bf16[2,2,2,256,256]{4,3,2,1,0:T(8,128)(2,1)} %down.3, bf16[2,2,2,256,256]{4,3,2,1,0:T(8,128)(2,1)} %up.3), custom_call_target="tpu_custom_call" | custom-call | tf_op jit(solution)/shard_map/pallas_call | solution.py:530
  2.0 0.1 collective-permute-start.2
  2.0 1.9 %collective-permute-start = (bf16[2,2,256,256]{3,2,1,0:T(8,128)(2,1)S(1)}, bf16[2,2,256,256]{3,2,1,0:T(8,128)(2,1)S(1)}, u32[]{:S(2)}, u32[]{:S(2)}) collective-permute-start(bf16[2,2,256,256]{3,2,1,0:T(8,128)(2,1)S(1)} %get-tuple-element.25), channel_id=1, source_target_pairs={{2,4},{6,8},{10,12},{14,16},{18,20},{22,24},{26,28},{4,2},{8,6},{1... | collective-permute-start | bytes 1572872 | tf_op jit(solution)/shard_map/ppermute | solution.py:533
  4.0 0.0 copy-done
  4.0 0.0 copy-done.3
  4.0 4.7 %shard_map.113 = (bf16[2,2,256,256]{3,2,1,0:T(8,128)(2,1)S(1)}, bf16[2,2,256,256]{3,2,1,0:T(8,128)(2,1)S(1)}, f32[2,2,2,256,256]{4,3,2,1,0:T(8,128)S(1)}, f32[2,...) custom-call(bf16[2,2,2,256,256]{4,3,2,1,0:T(8,128)(2,1)} %down.3, bf16[2,2,2,256,256]{4,3,2,1,0:T(8,128)(2,1)} %up.3, ...), custom_call_target="tpu_custom_call" | custom-call | tf_op jit(solution)/shard_map/pallas_call | solution.py:535
  8.6 0.0 collective-permute-done.2.partner
  8.7 0.0 copy-start.1
  8.7 1.9 %shard_map.115 = (bf16[2,2,256,256]{3,2,1,0:T(8,128)(2,1)S(1)}, bf16[2,2,256,256]{3,2,1,0:T(8,128)(2,1)S(1)}) custom-call(bf16[2,2,256,256]{3,2,1,0:T(8,128)(2,1)S(1)} %collective-permute-done.2.partner, bf16[2,2,256,256]{3,2,1,0:T(8,128)(2,1)S(1)} %get-tuple-element.32.q_in_outer, f32[2,2,2,256,256]{4,3,2,1,0:T(8,128)S(1)} %get-tuple-element.27.screen, ...), custom_call_target="tpu_custom_call" | custom-call | tf_op jit(solution)/shard_map/pallas_call | solution.py:548
  10.6 1.7 %collective-permute-start.3 = (bf16[2,2,256,256]{3,2,1,0:T(8,128)(2,1)S(1)}, bf16[2,2,256,256]{3,2,1,0:T(8,128)(2,1)S(1)}, u32[]{:S(2)}, u32[]{:S(2)}) collective-permute-start(bf16[2,2,256,256]{3,2,1,0:T(8,128)(2,1)S(1)} %get-tuple-element.35), channel_id=1, source_target_pairs={{0,2},{2,0},{4,6},{6,4},{8,10},{10,8},{12,14},{14,12},{16,18},{18,... | collective-permute-start | bytes 1572872 | tf_op jit(solution)/shard_map/ppermute | solution.py:551
  12.3 5.8 %collective-permute-done.arrived = bf16[2,2,256,256]{3,2,1,0:T(8,128)(2,1)S(1)} collective-permute-done((bf16[2,2,256,256]{3,2,1,0:T(8,128)(2,1)S(1)}, bf16[2,2,256,256]{3,2,1,0:T(8,128)(2,1)S(1)}, u32[]{:S(2)}, u32[]{:S(2)}) %collective-permute-start) | collective-permute-done | bytes 524320 | tf_op jit(solution)/shard_map/ppermute | solution.py:533
  18.2 1.1 %shard_map.114 = (bf16[2,2,256,256]{3,2,1,0:T(8,128)(2,1)S(1)}, bf16[2,2,256,256]{3,2,1,0:T(8,128)(2,1)S(1)}) custom-call(bf16[2,2,256,256]{3,2,1,0:T(8,128)(2,1)S(1)} %collective-permute-done.arrived, bf16[2,2,256,256]{3,2,1,0:T(8,128)(2,1)S(1)} %copy-done.1, bf16[2,2,256,256]{3,2,1,0:T(8,128)(2,1)S(1)} %get-tuple-element.26.q_out_inner, ...), custom_call_target="tpu_custom_call" | custom-call | tf_op jit(solution)/shard_map/pallas_call | solution.py:552
  19.2 1.9 %collective-permute-start.1 = (bf16[2,2,256,256]{3,2,1,0:T(8,128)(2,1)S(1)}, bf16[2,2,256,256]{3,2,1,0:T(8,128)(2,1)S(1)}, u32[]{:S(2)}, u32[]{:S(2)}) collective-permute-start(bf16[2,2,256,256]{3,2,1,0:T(8,128)(2,1)S(1)} %get-tuple-element.30), channel_id=1, source_target_pairs={{2,4},{6,8},{10,12},{14,16},{18,20},{22,24},{26,28},{4,2},{8,6},{1... | collective-permute-start | bytes 1572872 | tf_op jit(solution)/shard_map/ppermute | solution.py:555
  21.1 0.0 collective-permute-done.3.partner
  21.1 1.8 %shard_map.116 = (bf16[2,2,256,256]{3,2,1,0:T(8,128)(2,1)S(1)}, bf16[2,2,256,256]{3,2,1,0:T(8,128)(2,1)S(1)}) custom-call(bf16[2,2,256,256]{3,2,1,0:T(8,128)(2,1)S(1)} %get-tuple-element.34.q_arrived, bf16[2,2,256,256]{3,2,1,0:T(8,128)(2,1)S(1)} %get-tuple-element.26.q_out_inner, bf16[2,2,256,256]{3,2,1,0:T(8,128)(2,1)S(1)} %collective-permute-done.3.partner, ...), custom_call_target="tpu_custom_call" | custom-call | tf_op jit(solution)/shard_map/pallas_call | solution.py:556
  22.9 0.1 collective-permute-start.5
  23.0 0.9 %shard_map.117.after.q_out_inner = bf16[2,2,256,256]{3,2,1,0:T(8,128)(2,1)S(1)} custom-call(bf16[2,2,256,256]{3,2,1,0:T(8,128)(2,1)S(1)} %get-tuple-element.36.fields, f32[2,2,256,256]{3,2,1,0:T(8,128)S(1)} %get-tuple-element.29.phase, bf16[256,256]{1,0:T(8,128)(2,1)S(1)} %copy-done, bf16[256,256]{1,0:T(8,128)(2,1)S(1)} %copy-done), custom_call_target="tpu_custom_call" | custom-call | tf_op jit(solution)/shard_map/pallas_call | solution.py:560
  23.9 8.4 %collective-permute-done.1.arrived = bf16[2,2,256,256]{3,2,1,0:T(8,128)(2,1)S(1)} collective-permute-done((bf16[2,2,256,256]{3,2,1,0:T(8,128)(2,1)S(1)}, bf16[2,2,256,256]{3,2,1,0:T(8,128)(2,1)S(1)}, u32[]{:S(2)}, u32[]{:S(2)}) %collective-permute-start.1) | collective-permute-done | bytes 524320 | tf_op jit(solution)/shard_map/ppermute | solution.py:555
  32.3 1.8 %shard_map.118 = (bf16[2,2,256,256]{3,2,1,0:T(8,128)(2,1)S(1)}, bf16[2,2,128,256]{3,2,1,0:T(8,128)(2,1)S(1)}, bf16[2,2,128,256]{3,2,1,0:T(8,128)(2,1)S(1)}) custom-call(bf16[2,2,256,256]{3,2,1,0:T(8,128)(2,1)S(1)} %collective-permute-done.1.arrived, bf16[2,2,256,256]{3,2,1,0:T(8,128)(2,1)S(1)} %copy-done.1, ...), custom_call_target="tpu_custom_call" | custom-call | tf_op jit(solution)/shard_map/pallas_call | solution.py:561
  34.1 1.9 %collective-permute-start.6 = (bf16[2,2,128,256]{3,2,1,0:T(8,128)(2,1)S(1)}, bf16[2,2,128,256]{3,2,1,0:T(8,128)(2,1)S(1)}, u32[]{:S(2)}, u32[]{:S(2)}) collective-permute-start(bf16[2,2,128,256]{3,2,1,0:T(8,128)(2,1)S(1)} %get-tuple-element.42), channel_id=1, source_target_pairs={{2,4},{6,8},{10,12},{14,16},{18,20},{22,24},{26,28},{4,2},{8,6},{1... | collective-permute-start | bytes 786440 | tf_op jit(solution)/shard_map/ppermute | solution.py:568
  36.0 3.8 %collective-permute-start.4 = (bf16[2,2,128,256]{3,2,1,0:T(8,128)(2,1)S(1)}, bf16[2,2,128,256]{3,2,1,0:T(8,128)(2,1)S(1)}, u32[]{:S(2)}, u32[]{:S(2)}) collective-permute-start(bf16[2,2,128,256]{3,2,1,0:T(8,128)(2,1)S(1)} %get-tuple-element.37), channel_id=1, source_target_pairs={{2,4},{6,8},{10,12},{14,16},{18,20},{22,24},{26,28},{4,2},{8,6},{1... | collective-permute-start | bytes 786440 | tf_op jit(solution)/shard_map/ppermute | solution.py:569
  39.9 0.0 collective-permute-done.5.partner
  39.9 1.8 %shard_map.119 = (bf16[2,2,256,256]{3,2,1,0:T(8,128)(2,1)S(1)}, bf16[2,2,256,256]{3,2,1,0:T(8,128)(2,1)S(1)}, f32[256,256]{1,0:T(8,128)S(1)}) custom-call(bf16[2,2,256,256]{3,2,1,0:T(8,128)(2,1)S(1)} %get-tuple-element.38.q_arrived, bf16[2,2,256,256]{3,2,1,0:T(8,128)(2,1)S(1)} %get-tuple-element.33.q_out_inner, ...), custom_call_target="tpu_custom_call" | custom-call | tf_op jit(solution)/shard_map/pallas_call | solution.py:570
  41.7 1.4 %collective-permute-done.6.last = bf16[2,2,128,256]{3,2,1,0:T(8,128)(2,1)S(1)} collective-permute-done((bf16[2,2,128,256]{3,2,1,0:T(8,128)(2,1)S(1)}, bf16[2,2,128,256]{3,2,1,0:T(8,128)(2,1)S(1)}, u32[]{:S(2)}, u32[]{:S(2)}) %collective-permute-start.6) | collective-permute-done | bytes 262176 | tf_op jit(solution)/shard_map/ppermute | solution.py:568
  43.1 0.3 shard_map.120
  43.4 1.6 %collective-permute-start.7 = (bf16[2,128,256]{2,1,0:T(8,128)(2,1)S(1)}, bf16[2,128,256]{2,1,0:T(8,128)(2,1)S(1)}, u32[]{:S(2)}, u32[]{:S(2)}) collective-permute-start(bf16[2,128,256]{2,1,0:T(8,128)(2,1)S(1)} %get-tuple-element.46), channel_id=1, source_target_pairs={{0,1},{1,0},{2,3},{3,2},{4,5},{5,4},{6,7},{7,6},{8,9},{9,8},{10,11... | collective-permute-start | bytes 393224 | tf_op jit(solution)/shard_map/ppermute | solution.py:583
  45.0 0.9 %collective-permute-done.4.last = bf16[2,2,128,256]{3,2,1,0:T(8,128)(2,1)S(1)} collective-permute-done((bf16[2,2,128,256]{3,2,1,0:T(8,128)(2,1)S(1)}, bf16[2,2,128,256]{3,2,1,0:T(8,128)(2,1)S(1)}, u32[]{:S(2)}, u32[]{:S(2)}) %collective-permute-start.4) | collective-permute-done | bytes 262176 | tf_op jit(solution)/shard_map/ppermute | solution.py:569
  45.9 2.6 %collective-permute-done.7.other = bf16[2,128,256]{2,1,0:T(8,128)(2,1)S(1)} collective-permute-done((bf16[2,128,256]{2,1,0:T(8,128)(2,1)S(1)}, bf16[2,128,256]{2,1,0:T(8,128)(2,1)S(1)}, u32[]{:S(2)}, u32[]{:S(2)}) %collective-permute-start.7) | collective-permute-done | bytes 131104 | tf_op jit(solution)/shard_map/ppermute | solution.py:583
  48.4 1.5 %shard_map.121 = (bf16[2,2,2,256,256]{4,3,2,1,0:T(8,128)(2,1)}, bf16[2,2,2,256,256]{4,3,2,1,0:T(8,128)(2,1)}, f32[2,128,256]{2,1,0:T(8,128)}) custom-call(bf16[2,2,128,256]{3,2,1,0:T(8,128)(2,1)S(1)} %collective-permute-done.4.last, bf16[2,2,256,256]{3,2,1,0:T(8,128)(2,1)S(1)} %get-tuple-element.34.q_arrived, ...), custom_call_target="tpu_custom_call" | custom-call | tf_op jit(solution)/shard_map/pallas_call | solution.py:584
  (2 shorter events, 0.0 us)
Async XLA Ops:
  0.6 3.3 %copy-start = (bf16[256,256]{1,0:T(8,128)(2,1)S(1)}, bf16[256,256]{1,0:T(8,128)(2,1)}, u32[]{:S(2)}) copy-start(bf16[256,256]{1,0:T(8,128)(2,1)} %constant.2.clone.hx.hy) | copy-start | bytes 393220
  0.6 3.3 %copy-start.3 = (s32[2]{0:T(128)S(1)}, s32[2]{0:T(128)}, u32[]{:S(2)}) copy-start(s32[2]{0:T(128)} %freq.1) | copy-start | bytes 28
  0.7 3.3 %copy-start.2 = (f32[16]{0:T(128)S(1)}, f32[16]{0:T(128)}, u32[]{:S(2)}) copy-start(f32[16]{0:T(128)} %slowness.1) | copy-start | bytes 196
  2.0 6.7 %collective-permute-start.2 = (bf16[2,2,256,256]{3,2,1,0:T(8,128)(2,1)S(1)}, bf16[2,2,256,256]{3,2,1,0:T(8,128)(2,1)S(1)}, u32[]{:S(2)}, u32[]{:S(2)}) collective-permute-start(bf16[2,2,256,256]{3,2,1,0:T(8,128)(2,1)S(1)} %get-tuple-element.31), channel_id=1, source_target_pairs={{0,2},{2,0},{4,6},{6,4},{8,10},{10,8},{12,14},{14,12},{16,18},{18,... | collective-permute-start | bytes 1572872 | tf_op jit(solution)/shard_map/ppermute | solution.py:534
  2.0 16.1 %collective-permute-start = (bf16[2,2,256,256]{3,2,1,0:T(8,128)(2,1)S(1)}, bf16[2,2,256,256]{3,2,1,0:T(8,128)(2,1)S(1)}, u32[]{:S(2)}, u32[]{:S(2)}) collective-permute-start(bf16[2,2,256,256]{3,2,1,0:T(8,128)(2,1)S(1)} %get-tuple-element.25), channel_id=1, source_target_pairs={{2,4},{6,8},{10,12},{14,16},{18,20},{22,24},{26,28},{4,2},{8,6},{1... | collective-permute-start | bytes 1572872 | tf_op jit(solution)/shard_map/ppermute | solution.py:533
  8.7 9.5 %copy-start.1 = (bf16[2,2,256,256]{3,2,1,0:T(8,128)(2,1)S(1)}, bf16[2,2,256,256]{3,2,1,0:T(8,128)(2,1)}, u32[]{:S(2)}) copy-start(bf16[2,2,256,256]{3,2,1,0:T(8,128)(2,1)} %source.3) | copy-start | bytes 1572868
  10.6 10.5 %collective-permute-start.3 = (bf16[2,2,256,256]{3,2,1,0:T(8,128)(2,1)S(1)}, bf16[2,2,256,256]{3,2,1,0:T(8,128)(2,1)S(1)}, u32[]{:S(2)}, u32[]{:S(2)}) collective-permute-start(bf16[2,2,256,256]{3,2,1,0:T(8,128)(2,1)S(1)} %get-tuple-element.35), channel_id=1, source_target_pairs={{0,2},{2,0},{4,6},{6,4},{8,10},{10,8},{12,14},{14,12},{16,18},{18,... | collective-permute-start | bytes 1572872 | tf_op jit(solution)/shard_map/ppermute | solution.py:551
  19.2 13.1 %collective-permute-start.1 = (bf16[2,2,256,256]{3,2,1,0:T(8,128)(2,1)S(1)}, bf16[2,2,256,256]{3,2,1,0:T(8,128)(2,1)S(1)}, u32[]{:S(2)}, u32[]{:S(2)}) collective-permute-start(bf16[2,2,256,256]{3,2,1,0:T(8,128)(2,1)S(1)} %get-tuple-element.30), channel_id=1, source_target_pairs={{2,4},{6,8},{10,12},{14,16},{18,20},{22,24},{26,28},{4,2},{8,6},{1... | collective-permute-start | bytes 1572872 | tf_op jit(solution)/shard_map/ppermute | solution.py:555
  22.9 16.9 %collective-permute-start.5 = (bf16[2,2,256,256]{3,2,1,0:T(8,128)(2,1)S(1)}, bf16[2,2,256,256]{3,2,1,0:T(8,128)(2,1)S(1)}, u32[]{:S(2)}, u32[]{:S(2)}) collective-permute-start(bf16[2,2,256,256]{3,2,1,0:T(8,128)(2,1)S(1)} %get-tuple-element.39), channel_id=1, source_target_pairs={{0,2},{2,0},{4,6},{6,4},{8,10},{10,8},{12,14},{14,12},{16,18},{18,... | collective-permute-start | bytes 1572872 | tf_op jit(solution)/shard_map/ppermute | solution.py:559
  34.1 8.9 %collective-permute-start.6 = (bf16[2,2,128,256]{3,2,1,0:T(8,128)(2,1)S(1)}, bf16[2,2,128,256]{3,2,1,0:T(8,128)(2,1)S(1)}, u32[]{:S(2)}, u32[]{:S(2)}) collective-permute-start(bf16[2,2,128,256]{3,2,1,0:T(8,128)(2,1)S(1)} %get-tuple-element.42), channel_id=1, source_target_pairs={{2,4},{6,8},{10,12},{14,16},{18,20},{22,24},{26,28},{4,2},{8,6},{1... | collective-permute-start | bytes 786440 | tf_op jit(solution)/shard_map/ppermute | solution.py:568
  36.0 9.8 %collective-permute-start.4 = (bf16[2,2,128,256]{3,2,1,0:T(8,128)(2,1)S(1)}, bf16[2,2,128,256]{3,2,1,0:T(8,128)(2,1)S(1)}, u32[]{:S(2)}, u32[]{:S(2)}) collective-permute-start(bf16[2,2,128,256]{3,2,1,0:T(8,128)(2,1)S(1)} %get-tuple-element.37), channel_id=1, source_target_pairs={{2,4},{6,8},{10,12},{14,16},{18,20},{22,24},{26,28},{4,2},{8,6},{1... | collective-permute-start | bytes 786440 | tf_op jit(solution)/shard_map/ppermute | solution.py:569
  43.4 5.0 %collective-permute-start.7 = (bf16[2,128,256]{2,1,0:T(8,128)(2,1)S(1)}, bf16[2,128,256]{2,1,0:T(8,128)(2,1)S(1)}, u32[]{:S(2)}, u32[]{:S(2)}) collective-permute-start(bf16[2,128,256]{2,1,0:T(8,128)(2,1)S(1)} %get-tuple-element.46), channel_id=1, source_target_pairs={{0,1},{1,0},{2,3},{3,2},{4,5},{5,4},{6,7},{7,6},{8,9},{9,8},{10,11... | collective-permute-start | bytes 393224 | tf_op jit(solution)/shard_map/ppermute | solution.py:583

commit v8 on v7

--- a/solution.py
+++ b/solution.py
@@ -254,7 +254,7 @@
 
 def setup_kernel(
     down, up, reflect, classes_in, slowness, freq, hx, hy,
-    q_out_inner, q_in_outer, screen, phase, refl,
+    q_out_inner, q_in_outer, screen, phase, refl, outward_outer,
     fields, klass, work, sems,
 ):
     fronts = q_out_inner.shape[0]
@@ -273,11 +273,13 @@
     def _():
         pltpu.make_async_copy(down.at[0], fields.at[0], sems.at[0]).start()
         pltpu.make_async_copy(up.at[1], fields.at[1], sems.at[1]).start()
+        pltpu.make_async_copy(up.at[0], outward_outer, sems.at[6]).start()
 
     @pl.when(odd == 1)
     def _():
         pltpu.make_async_copy(up.at[1], fields.at[0], sems.at[0]).start()
         pltpu.make_async_copy(down.at[0], fields.at[1], sems.at[1]).start()
+        pltpu.make_async_copy(down.at[1], outward_outer, sems.at[6]).start()
 
     def squares(length, axis):
         counter = lax.broadcasted_iota(jnp.int32, (rows_x, rows_y), axis)
@@ -307,6 +309,7 @@
             screen[level, front, 1] = look_up(sin_row, klass[level])
     pltpu.make_async_copy(down.at[0], fields.at[0], sems.at[0]).wait()
     pltpu.make_async_copy(down.at[0], fields.at[1], sems.at[1]).wait()
+    pltpu.make_async_copy(down.at[0], outward_outer, sems.at[6]).wait()
     jobs = [(fields.at[1, front], front, q_out_inner.at[front]) for front in range(fronts)]
     jobs += [(fields.at[0, front], front, q_in_outer.at[front]) for front in range(fronts)]
     spread(jobs, work, hx, hy, phase)
@@ -331,7 +334,7 @@
 
 def entering(arrived, source, front):
     first = lax.axis_index("depth") == 0
-    return lambda part: jnp.where(first, source[front, part], arrived[front, part])
+    return lambda part: jnp.where(first, source[front, part], arrived(front, part))
 
 
 def outer_step(q_arrived, q_out_inner, screen, refl, waves, field):
@@ -345,8 +348,17 @@
         )
 
 
-def edge_kernel(arrived, source, q_out_inner, screen, refl, phase, hx, hy, outward, q_arrived, work):
-    everyone = range(arrived.shape[0])
+def late_pair():
+    return lax.rem(lax.div(lax.axis_index("depth") + 1, 2), 2) == 1
+
+
+def edge_kernel(early, late, source, q_out_inner, screen, refl, phase, hx, hy, outward, q_arrived, work):
+    everyone = range(early.shape[0])
+    is_late = late_pair()
+
+    def arrived(front, part):
+        return jnp.where(is_late, late[front, part], early[front, part])
+
     spread([(entering(arrived, source, front), front, q_arrived.at[front]) for front in everyone], work, hx, hy, phase)
     outer_step(q_arrived, q_out_inner, screen, refl, "outward", outward)
 
@@ -359,7 +371,11 @@
     del after
     everyone = range(arrived.shape[0])
     half = arrived.shape[2] // 2
-    spread([(entering(arrived, source, front), front, q_arrived.at[front]) for front in everyone], work, hx, hy, phase)
+
+    def received(front, part):
+        return arrived[front, part]
+
+    spread([(entering(received, source, front), front, q_arrived.at[front]) for front in everyone], work, hx, hy, phase)
     outer_step(q_arrived, q_out_inner, screen, refl, "outward", outward)
     jobs = [
         (outward.at[front], front, [(half_rows(1, half), last_far.at[front]), (half_rows(0, half), last_near.at[front])])
@@ -394,7 +410,7 @@
 
 def last_inner_kernel(
     q_arrived, q_out_inner, partner, screen, refl, phase, hx, hy,
-    inward, outward, terms,
+    inward, outward, terms, far_terms,
     field, q_inward, q_partner, work,
 ):
     everyone = range(partner.shape[0])
@@ -414,12 +430,13 @@
         term = a_re * b_re + a_im * b_im
         total = term if total is None else total + term
     terms[...] = total
-
-
-def far_rows_kernel(last, q_arrived, q_out_inner, screen, refl, inner_terms, inward, outward, terms):
-    rows, total = outer_rows(1, last, q_arrived, q_out_inner, screen, refl, inward, outward)
-    terms[0] = total.astype(BF16)
-    terms[1] = inner_terms[rows, :].astype(BF16)
+    far_terms[...] = terms[half_rows(1, far_terms.shape[0]), :].astype(BF16)
+
+
+def far_rows_kernel(last, q_arrived, q_out_inner, screen, refl, after, inward, outward, terms):
+    del after
+    _, total = outer_rows(1, last, q_arrived, q_out_inner, screen, refl, inward, outward)
+    terms[...] = total.astype(BF16)
 
 
 def outer_rows(of, last, q_arrived, q_out_inner, screen, refl, inward, outward):
@@ -466,22 +483,27 @@
 
 
 def near_rows_kernel(
-    scale, last, q_arrived, q_out_inner, screen, refl, inner_in, inner_out, far_in, far_out, inner_terms, other,
-    down_out, up_out, gradient,
-    inward, outward, sums, sems,
+    last, q_arrived, q_out_inner, screen, refl, inner_in, inner_out, far_in, far_out,
+    down_out, up_out, terms,
+    inward, outward, sems,
 ):
     rows_x, half = inner_in.shape[2], far_in.shape[2]
     waits = send_home(1, pl.ds(0, rows_x), inner_in, inner_out, down_out, up_out, sems.at[0])
     waits += send_home(0, half_rows(1, half), far_in, far_out, down_out, up_out, sems.at[1])
     rows, total = outer_rows(0, last, q_arrived, q_out_inner, screen, refl, inward, outward)
     waits += send_home(0, rows, inward, outward, down_out, up_out, sems.at[2])
+    terms[...] = total
+    for copy in waits:
+        copy.wait()
+
+
+def gradient_kernel(scale, outer_terms, inner_terms, outer_other, inner_other, gradient, sums, sems):
     odd = odd_place()
-    sums[odd] = scale * (total + other[0].astype(F32))
-    sums[1 - odd] = scale * (inner_terms[rows, :] + other[1].astype(F32))
-    done = pltpu.make_async_copy(sums, gradient, sems.at[3, 0])
+    sums[odd] = scale * (outer_terms[...] + outer_other[...].astype(F32))
+    sums[1 - odd] = scale * (inner_terms[half_rows(0, sums.shape[1]), :] + inner_other[...].astype(F32))
+    done = pltpu.make_async_copy(sums, gradient, sems.at[0])
     done.start()
-    for copy in waits + [done]:
-        copy.wait()
+    done.wait()
 
 
 def per_device(down_state, up_state, source, reflect, screen_class, screen_values, freq_index):
@@ -495,7 +517,11 @@
     hx = jnp.asarray(hartley(rows_x))
     hy = jnp.asarray(hartley(rows_y))
     partners = [(i, i ^ 1) for i in range(depth)]
-    beyond = [(i, i + 1) for i in range(1, depth - 1, 2)] + [(i + 1, i) for i in range(1, depth - 1, 2)]
+    early_pairs, late_pairs = (
+        [(i, i + 1) for i in range(start, depth - 1, 4)] + [(i + 1, i) for i in range(start, depth - 1, 4)]
+        for start in (3, 1)
+    )
+    beyond = early_pairs + late_pairs
     to_partner = functools.partial(lax.ppermute, axis_name="depth", perm=partners)
     to_beyond = functools.partial(lax.ppermute, axis_name="depth", perm=beyond)
     across = functools.partial(lax.ppermute, axis_name="shot", perm=[(i, i ^ 1) for i in range(shots)])
@@ -530,27 +556,28 @@
     out_outer, in_inner = call(edges_kernel, [HBM] * 2, [VMEM] * 2, [plane] * 2, [dma((2,))])(
         *kept_in_hbm(down_state, up_state)
     )
-    arrived_0 = to_beyond(out_outer)
+    arrived_early = to_beyond(out_outer, perm=early_pairs)
     partner_0 = to_partner(in_inner)
-    q_out_inner_0, q_in_outer_0, screen, phase, refl = call(
+    q_out_inner_0, q_in_outer_0, screen, phase, refl, out_outer_again = call(
         setup_kernel,
         [HBM] * 4 + [SMEM] * 2 + [VMEM] * 2,
-        [VMEM] * 5,
-        [plane] * 2 + [screens, turns, pair],
+        [VMEM] * 6,
+        [plane] * 2 + [screens, turns, pair, plane],
         [
             pltpu.VMEM((2, *plane.shape), BF16),
             pltpu.VMEM((2, rows_x, rows_y), jnp.int32),
             work(2 * fronts),
-            dma((6,)),
+            dma((7,)),
         ],
     )(*kept_in_hbm(down_state, up_state, reflect, screen_class), screen_values, freq_index, hx, hy)
+    arrived_late = to_beyond(out_outer_again, perm=late_pairs)
     fixed = (screen, refl, phase, hx, hy)
     in_inner_1, q_out_inner_1 = call(ahead_kernel, [VMEM] * 7, [VMEM] * 2, [plane] * 2, buffers(2) + [work(fronts)])(
         partner_0, q_in_outer_0, *fixed
     )
     partner_1 = to_partner(in_inner_1)
-    out_outer_1, q_arrived = call(edge_kernel, [VMEM] * 8, [VMEM] * 2, [plane] * 2, [work(fronts)])(
-        arrived_0, source, q_out_inner_0, *fixed
+    out_outer_1, q_arrived = call(edge_kernel, [VMEM] * 9, [VMEM] * 2, [plane] * 2, [work(fronts)])(
+        arrived_early, arrived_late, source, q_out_inner_0, *fixed
     )
     arrived_1 = to_beyond(out_outer_1)
     in_inner_2, out_inner_2 = call(
@@ -567,29 +594,38 @@
     )(arrived_1, source, q_out_inner_1, *fixed, q_out_inner_2)
     last_far = to_beyond(last_far)
     last_near = to_beyond(last_near)
-    inner_in, inner_out, inner_terms = call(
+    half_sum = jax.ShapeDtypeStruct((half, rows_y), BF16)
+    inner_in, inner_out, inner_terms, inner_far = call(
         last_inner_kernel,
         [VMEM] * 8,
-        [VMEM] * 3,
-        [plane] * 2 + [jax.ShapeDtypeStruct((rows_x, rows_y), F32)],
+        [VMEM] * 4,
+        [plane] * 2 + [jax.ShapeDtypeStruct((rows_x, rows_y), F32), half_sum],
         buffers(3) + [work(2 * fronts)],
     )(q_arrived_1, q_out_inner_1, partner_2, *fixed)
-    far_in, far_out, terms = call(
+    inner_other = across(inner_far) if shots == 2 else jnp.zeros_like(inner_far)
+    far_in, far_out, outer_far = call(
         far_rows_kernel,
-        [VMEM] * 6,
+        [VMEM] * 5 + [pl.BlockSpec(memory_space=pl.ANY)],
         [VMEM] * 3,
-        [half_plane] * 2 + [jax.ShapeDtypeStruct((2, half, rows_y), BF16)],
+        [half_plane] * 2 + [half_sum],
     )(last_far, q_arrived, q_out_inner_2, screen, refl, inner_terms)
-    other = across(terms) if shots == 2 else jnp.zeros_like(terms)
-    down, up, gradient = call(
-        functools.partial(near_rows_kernel, scale),
-        [VMEM] * 11,
-        [HBM] * 3,
-        [state, state, jax.ShapeDtypeStruct((2, half, rows_y), F32)],
-        buffers(2, half_plane) + [pltpu.VMEM((2, half, rows_y), F32), dma((4, 2))],
-    )(last_near, q_arrived, q_out_inner_2, screen, refl, inner_in, inner_out, far_in, far_out, inner_terms, other)
+    outer_other = across(outer_far) if shots == 2 else jnp.zeros_like(outer_far)
+    down, up, outer_near = call(
+        near_rows_kernel,
+        [VMEM] * 9,
+        [HBM] * 2 + [VMEM],
+        [state, state, jax.ShapeDtypeStruct((half, rows_y), F32)],
+        buffers(2, half_plane) + [dma((3, 2))],
+    )(last_near, q_arrived, q_out_inner_2, screen, refl, inner_in, inner_out, far_in, far_out)
+    gradient = call(
+        functools.partial(gradient_kernel, scale),
+        [VMEM] * 4,
+        HBM,
+        jax.ShapeDtypeStruct((2, half, rows_y), F32),
+        [pltpu.VMEM((2, half, rows_y), F32), dma((1,))],
+    )(outer_near, inner_terms, outer_other, inner_other)
     if shots != 2:
-        terms = scale * terms.astype(F32)
+        terms = scale * jnp.stack([outer_far, inner_far]).astype(F32)
         far = jnp.where(odd_place() == 0, terms, terms[::-1])
         top = lax.rem(lax.axis_index("shot"), 2) == 0
         whole = jnp.concatenate([jnp.where(top, gradient, far), jnp.where(top, far, gradient)], axis=1)

time: 50.3 us -> 49.9 us (level)
  waiting for transfers between devices: 19.1 us -> 15.7 us
  starting transfers between devices: 13 us -> 15.2 us
  Pallas kernels: 17 us -> 17.7 us
    ppermute x2 -> x4, starting transfers between devices: 3.49 us -> 5.67 us  [the longest x1 1.92 us: per_device(): arrived_late = to_beyond(out_outer_again, perm=late_pairs)]
    ppermute x1, waiting for transfers between devices: 8.38 us -> 6.82 us  [per_device(): arrived_1 = to_beyond(out_outer_1)]
    ppermute x2 -> x4, waiting for transfers between devices: 8.4 us -> 7.18 us  [the longest x1 6.69 us: per_device(): arrived_late = to_beyond(out_outer_again, perm=late_pairs)]
    pallas_call x5 -> x6, Pallas kernels: 9.3 us -> 9.98 us  [the longest x1 4.66 us: per_device(): call(setup_kernel, [HBM] * 4 + [SMEM] * 2 + [VMEM] * 2, [VMEM] * 6, [plan...]
    ppermute x1, waiting for transfers between devices: 1.37 us -> 0.8 us  [per_device(): last_far = to_beyond(last_far)]
  transfers between devices with their start and end apart: 8 -> 10, of which waited for: 5 -> 5; matrix products, arithmetic and copies ran while one was open for 0% -> 0% of each run, Pallas kernels for 28% -> 32%
where the time goes in v8:
time: 49.9 us; the launch traced here: 49.6 us
  Pallas kernels  17.7 us (35%)
  waiting for transfers between devices  15.7 us (31%)
  starting transfers between devices  15.2 us (30%)
  between operations  1.01 us (2%)
    ppermute x1, waiting for transfers between devices, per_device(): arrived_1 = to_beyond(out_outer_1)  6.82 us
    ppermute x1, waiting for transfers between devices, per_device(): arrived_late = to_beyond(out_outer_again, perm=late_pairs)  6.69 us
    pallas_call x1, Pallas kernels, per_device(): call(setup_kernel, [HBM] * 4 + [SMEM] * 2 + [VMEM] * 2, [VMEM] * 6, [plan...  4.66 us
    ppermute x1, starting transfers between devices, per_device(): last_near = to_beyond(last_near)  3.82 us
    pallas_call x1, Pallas kernels, per_device(): call(ahead_kernel, [VMEM] * 7, [VMEM] * 2, [plane] * 2, buffers(2) + [wor...  1.94 us
    ppermute x1, starting transfers between devices, per_device(): last_far = to_beyond(last_far)  1.92 us
    ppermute x1, starting transfers between devices, per_device(): arrived_late = to_beyond(out_outer_again, perm=late_pairs)  1.92 us
    ppermute x1, starting transfers between devices, per_device(): arrived_1 = to_beyond(out_outer_1)  1.92 us
  transfers between devices with their start and end apart: 10, of which 5 were waited for; matrix products, arithmetic and copies ran while one was open for 0% of the time, Pallas kernels for 32%

profile of v8, /device:TPU:4, one launch (start us, length us, event | category | flops | bytes accessed | tf_op | source)
XLA Modules:
  0.0 49.6 jit_solution(13750885468401212784)
XLA Ops:
  0.6 0.0 copy-start
  0.7 1.3 %shard_map.112 = (bf16[2,2,256,256]{3,2,1,0:T(8,128)(2,1)S(1)}, bf16[2,2,256,256]{3,2,1,0:T(8,128)(2,1)S(1)}) custom-call(bf16[2,2,2,256,256]{4,3,2,1,0:T(8,128)(2,1)} %down.3, bf16[2,2,2,256,256]{4,3,2,1,0:T(8,128)(2,1)} %up.3), custom_call_target="tpu_custom_call" | custom-call | tf_op jit(solution)/shard_map/pallas_call | solution.py:556
  2.0 0.1 collective-permute-start.3
  2.0 0.7 %collective-permute-start = (bf16[2,2,256,256]{3,2,1,0:T(8,128)(2,1)S(1)}, bf16[2,2,256,256]{3,2,1,0:T(8,128)(2,1)S(1)}, u32[]{:S(2)}, u32[]{:S(2)}) collective-permute-start(bf16[2,2,256,256]{3,2,1,0:T(8,128)(2,1)S(1)} %get-tuple-element.30), channel_id=1, source_target_pairs={{6,8},{14,16},{22,24},{8,6},{16,14},{24,22},{7,9},{15,17},{23,25},... | collective-permute-start | bytes 1572872 | tf_op jit(solution)/shard_map/ppermute | solution.py:559
  2.8 4.7 %shard_map.113 = (bf16[2,2,256,256]{3,2,1,0:T(8,128)(2,1)S(1)}, bf16[2,2,256,256]{3,2,1,0:T(8,128)(2,1)S(1)}, f32[2,2,2,256,256]{4,3,2,1,0:T(8,128)S(1)}, f32[2,...) custom-call(bf16[2,2,2,256,256]{4,3,2,1,0:T(8,128)(2,1)} %down.3, ...), custom_call_target="tpu_custom_call" | custom-call | tf_op jit(solution)/shard_map/pallas_call | solution.py:561
  7.4 1.9 %collective-permute-start.1 = (bf16[2,2,256,256]{3,2,1,0:T(8,128)(2,1)S(1)}, bf16[2,2,256,256]{3,2,1,0:T(8,128)(2,1)S(1)}, u32[]{:S(2)}, u32[]{:S(2)}) collective-permute-start(bf16[2,2,256,256]{3,2,1,0:T(8,128)(2,1)S(1)} %get-tuple-element.31), channel_id=1, source_target_pairs={{2,4},{10,12},{18,20},{26,28},{4,2},{12,10},{20,18},{28,26},{3,5},... | collective-permute-start | bytes 1572872 | tf_op jit(solution)/shard_map/ppermute | solution.py:573
  9.4 0.0 collective-permute-done.3.partner
  9.4 0.0 copy-start.1
  9.4 1.9 %shard_map.115 = (bf16[2,2,256,256]{3,2,1,0:T(8,128)(2,1)S(1)}, bf16[2,2,256,256]{3,2,1,0:T(8,128)(2,1)S(1)}) custom-call(bf16[2,2,256,256]{3,2,1,0:T(8,128)(2,1)S(1)} %collective-permute-done.3.partner, bf16[2,2,256,256]{3,2,1,0:T(8,128)(2,1)S(1)} %get-tuple-element.38.q_in_outer, f32[2,2,2,256,256]{4,3,2,1,0:T(8,128)S(1)} %get-tuple-element.33.screen, ...), custom_call_target="tpu_custom_call" | custom-call | tf_op jit(solution)/shard_map/pallas_call | solution.py:575
  11.3 1.7 %collective-permute-start.4 = (bf16[2,2,256,256]{3,2,1,0:T(8,128)(2,1)S(1)}, bf16[2,2,256,256]{3,2,1,0:T(8,128)(2,1)S(1)}, u32[]{:S(2)}, u32[]{:S(2)}) collective-permute-start(bf16[2,2,256,256]{3,2,1,0:T(8,128)(2,1)S(1)} %get-tuple-element.41), channel_id=1, source_target_pairs={{0,2},{2,0},{4,6},{6,4},{8,10},{10,8},{12,14},{14,12},{16,18},{18,... | collective-permute-start | bytes 1572872 | tf_op jit(solution)/shard_map/ppermute | solution.py:578
  13.0 0.0 collective-permute-done.early
  13.0 6.7 %collective-permute-done.1.late = bf16[2,2,256,256]{3,2,1,0:T(8,128)(2,1)S(1)} collective-permute-done((bf16[2,2,256,256]{3,2,1,0:T(8,128)(2,1)S(1)}, bf16[2,2,256,256]{3,2,1,0:T(8,128)(2,1)S(1)}, u32[]{:S(2)}, u32[]{:S(2)}) %collective-permute-start.1) | collective-permute-done | bytes 524320 | tf_op jit(solution)/shard_map/ppermute | solution.py:573
  19.7 1.1 %shard_map.114 = (bf16[2,2,256,256]{3,2,1,0:T(8,128)(2,1)S(1)}, bf16[2,2,256,256]{3,2,1,0:T(8,128)(2,1)S(1)}) custom-call(bf16[2,2,256,256]{3,2,1,0:T(8,128)(2,1)S(1)} %collective-permute-done.early, bf16[2,2,256,256]{3,2,1,0:T(8,128)(2,1)S(1)} %collective-permute-done.1.late, bf16[2,2,256,256]{3,2,1,0:T(8,128)(2,1)S(1)} %copy-done.1, ...), custom_call_target="tpu_custom_call" | custom-call | tf_op jit(solution)/shard_map/pallas_call | solution.py:579
  20.8 1.9 %collective-permute-start.2 = (bf16[2,2,256,256]{3,2,1,0:T(8,128)(2,1)S(1)}, bf16[2,2,256,256]{3,2,1,0:T(8,128)(2,1)S(1)}, u32[]{:S(2)}, u32[]{:S(2)}) collective-permute-start(bf16[2,2,256,256]{3,2,1,0:T(8,128)(2,1)S(1)} %get-tuple-element.36), channel_id=1, source_target_pairs={{6,8},{14,16},{22,24},{8,6},{16,14},{24,22},{2,4},{10,12},{18,20},... | collective-permute-start | bytes 1572872 | tf_op jit(solution)/shard_map/ppermute | solution.py:582
  22.7 0.0 collective-permute-done.4.partner
  22.7 1.8 %shard_map.116 = (bf16[2,2,256,256]{3,2,1,0:T(8,128)(2,1)S(1)}, bf16[2,2,256,256]{3,2,1,0:T(8,128)(2,1)S(1)}) custom-call(bf16[2,2,256,256]{3,2,1,0:T(8,128)(2,1)S(1)} %get-tuple-element.40.q_arrived, bf16[2,2,256,256]{3,2,1,0:T(8,128)(2,1)S(1)} %get-tuple-element.32.q_out_inner, bf16[2,2,256,256]{3,2,1,0:T(8,128)(2,1)S(1)} %collective-permute-done.4.partner, ...), custom_call_target="tpu_custom_call" | custom-call | tf_op jit(solution)/shard_map/pallas_call | solution.py:583
  24.5 0.1 collective-permute-start.6
  24.6 0.9 %shard_map.117.after.q_out_inner = bf16[2,2,256,256]{3,2,1,0:T(8,128)(2,1)S(1)} custom-call(bf16[2,2,256,256]{3,2,1,0:T(8,128)(2,1)S(1)} %get-tuple-element.42.fields, f32[2,2,256,256]{3,2,1,0:T(8,128)S(1)} %get-tuple-element.35.phase, bf16[256,256]{1,0:T(8,128)(2,1)S(1)} %copy-done, bf16[256,256]{1,0:T(8,128)(2,1)S(1)} %copy-done), custom_call_target="tpu_custom_call" | custom-call | tf_op jit(solution)/shard_map/pallas_call | solution.py:587
  25.5 6.8 %collective-permute-done.2.arrived = bf16[2,2,256,256]{3,2,1,0:T(8,128)(2,1)S(1)} collective-permute-done((bf16[2,2,256,256]{3,2,1,0:T(8,128)(2,1)S(1)}, bf16[2,2,256,256]{3,2,1,0:T(8,128)(2,1)S(1)}, u32[]{:S(2)}, u32[]{:S(2)}) %collective-permute-start.2) | collective-permute-done | bytes 524320 | tf_op jit(solution)/shard_map/ppermute | solution.py:582
  32.3 1.8 %shard_map.118 = (bf16[2,2,256,256]{3,2,1,0:T(8,128)(2,1)S(1)}, bf16[2,2,128,256]{3,2,1,0:T(8,128)(2,1)S(1)}, bf16[2,2,128,256]{3,2,1,0:T(8,128)(2,1)S(1)}) custom-call(bf16[2,2,256,256]{3,2,1,0:T(8,128)(2,1)S(1)} %collective-permute-done.2.arrived, bf16[2,2,256,256]{3,2,1,0:T(8,128)(2,1)S(1)} %copy-done.1, ...), custom_call_target="tpu_custom_call" | custom-call | tf_op jit(solution)/shard_map/pallas_call | solution.py:588
  34.1 1.9 %collective-permute-start.7 = (bf16[2,2,128,256]{3,2,1,0:T(8,128)(2,1)S(1)}, bf16[2,2,128,256]{3,2,1,0:T(8,128)(2,1)S(1)}, u32[]{:S(2)}, u32[]{:S(2)}) collective-permute-start(bf16[2,2,128,256]{3,2,1,0:T(8,128)(2,1)S(1)} %get-tuple-element.48), channel_id=1, source_target_pairs={{6,8},{14,16},{22,24},{8,6},{16,14},{24,22},{2,4},{10,12},{18,20},... | collective-permute-start | bytes 786440 | tf_op jit(solution)/shard_map/ppermute | solution.py:595
  36.1 3.8 %collective-permute-start.5 = (bf16[2,2,128,256]{3,2,1,0:T(8,128)(2,1)S(1)}, bf16[2,2,128,256]{3,2,1,0:T(8,128)(2,1)S(1)}, u32[]{:S(2)}, u32[]{:S(2)}) collective-permute-start(bf16[2,2,128,256]{3,2,1,0:T(8,128)(2,1)S(1)} %get-tuple-element.43), channel_id=1, source_target_pairs={{6,8},{14,16},{22,24},{8,6},{16,14},{24,22},{2,4},{10,12},{18,20},... | collective-permute-start | bytes 786440 | tf_op jit(solution)/shard_map/ppermute | solution.py:596
  39.9 1.8 %shard_map.119 = (bf16[2,2,256,256]{3,2,1,0:T(8,128)(2,1)S(1)}, bf16[2,2,256,256]{3,2,1,0:T(8,128)(2,1)S(1)}, f32[256,256]{1,0:T(8,128)S(1)}, bf16[128,256]{1,0:T(8,128)(2,1)S(1)}) custom-call(bf16[2,2,256,256]{3,2,1,0:T(8,128)(2,1)S(1)} %get-tuple-element.44.q_arrived, bf16[2,2,256,256]{3,2,1,0:T(8,128)(2,1)S(1)} %get-tuple-element.39.q_out_inner, ...), custom_call_target="tpu_custom_call" | custom-call | tf_op jit(solution)/shard_map/pallas_call | solution.py:598
  41.7 1.5 %collective-permute-start.9 = (bf16[128,256]{1,0:T(8,128)(2,1)S(1)}, bf16[128,256]{1,0:T(8,128)(2,1)S(1)}, u32[]{:S(2)}, u32[]{:S(2)}) collective-permute-start(bf16[128,256]{1,0:T(8,128)(2,1)S(1)} %get-tuple-element.56), channel_id=1, source_target_pairs={{0,1},{1,0},{2,3},{3,2},{4,5},{5,4},{6,7},{7,6},{8,9},{9,8},{10,11... | collective-permute-start | bytes 196616 | tf_op jit(solution)/shard_map/ppermute | solution.py:605
  43.2 0.8 %collective-permute-done.7.last = bf16[2,2,128,256]{3,2,1,0:T(8,128)(2,1)S(1)} collective-permute-done((bf16[2,2,128,256]{3,2,1,0:T(8,128)(2,1)S(1)}, bf16[2,2,128,256]{3,2,1,0:T(8,128)(2,1)S(1)}, u32[]{:S(2)}, u32[]{:S(2)}) %collective-permute-start.7) | collective-permute-done | bytes 262176 | tf_op jit(solution)/shard_map/ppermute | solution.py:595
  44.0 0.3 shard_map.120
  44.4 1.5 %collective-permute-start.8 = (bf16[128,256]{1,0:T(8,128)(2,1)S(1)}, bf16[128,256]{1,0:T(8,128)(2,1)S(1)}, u32[]{:S(2)}, u32[]{:S(2)}) collective-permute-start(bf16[128,256]{1,0:T(8,128)(2,1)S(1)} %get-tuple-element.55), channel_id=1, source_target_pairs={{0,1},{1,0},{2,3},{3,2},{4,5},{5,4},{6,7},{7,6},{8,9},{9,8},{10,11... | collective-permute-start | bytes 196616 | tf_op jit(solution)/shard_map/ppermute | solution.py:612
  45.9 0.9 %collective-permute-done.5.last = bf16[2,2,128,256]{3,2,1,0:T(8,128)(2,1)S(1)} collective-permute-done((bf16[2,2,128,256]{3,2,1,0:T(8,128)(2,1)S(1)}, bf16[2,2,128,256]{3,2,1,0:T(8,128)(2,1)S(1)}, u32[]{:S(2)}, u32[]{:S(2)}) %collective-permute-start.5) | collective-permute-done | bytes 262176 | tf_op jit(solution)/shard_map/ppermute | solution.py:596
  46.9 1.4 %shard_map.121 = (bf16[2,2,2,256,256]{4,3,2,1,0:T(8,128)(2,1)}, bf16[2,2,2,256,256]{4,3,2,1,0:T(8,128)(2,1)}, f32[128,256]{1,0:T(8,128)S(1)}) custom-call(bf16[2,2,128,256]{3,2,1,0:T(8,128)(2,1)S(1)} %collective-permute-done.5.last, bf16[2,2,256,256]{3,2,1,0:T(8,128)(2,1)S(1)} %get-tuple-element.40.q_arrived, ...), custom_call_target="tpu_custom_call" | custom-call | tf_op jit(solution)/shard_map/pallas_call | solution.py:613
  48.2 0.0 collective-permute-done.9.inner_other
  48.2 0.5 collective-permute-done.8.outer_other
  48.7 0.7 %shard_map.122 = f32[2,128,256]{2,1,0:T(8,128)} custom-call(f32[128,256]{1,0:T(8,128)S(1)} %get-tuple-element.54.outer_terms, f32[256,256]{1,0:T(8,128)S(1)} %get-tuple-element.49.after.inner_terms, bf16[128,256]{1,0:T(8,128)(2,1)S(1)} %collective-permute-done.8.outer_other, bf16[128,256]{1,0:T(8,128)(2,1)S(1)} %collective-permute-done.9.inner_other), custom_call_target="tpu_custom_call" | custom-call | tf_op jit(solution)/shard_map/pallas_call | solution.py:620
  (7 shorter events, 0.0 us)
Async XLA Ops:
  0.6 2.1 %copy-start = (bf16[256,256]{1,0:T(8,128)(2,1)S(1)}, bf16[256,256]{1,0:T(8,128)(2,1)}, u32[]{:S(2)}) copy-start(bf16[256,256]{1,0:T(8,128)(2,1)} %constant.2.clone.hx.hy) | copy-start | bytes 393220
  0.6 2.1 %copy-start.3 = (s32[2]{0:T(128)S(1)}, s32[2]{0:T(128)}, u32[]{:S(2)}) copy-start(s32[2]{0:T(128)} %freq.1) | copy-start | bytes 28
  0.7 2.1 %copy-start.2 = (f32[16]{0:T(128)S(1)}, f32[16]{0:T(128)}, u32[]{:S(2)}) copy-start(f32[16]{0:T(128)} %slowness.1) | copy-start | bytes 196
  2.0 7.4 %collective-permute-start.3 = (bf16[2,2,256,256]{3,2,1,0:T(8,128)(2,1)S(1)}, bf16[2,2,256,256]{3,2,1,0:T(8,128)(2,1)S(1)}, u32[]{:S(2)}, u32[]{:S(2)}) collective-permute-start(bf16[2,2,256,256]{3,2,1,0:T(8,128)(2,1)S(1)} %get-tuple-element.37), channel_id=1, source_target_pairs={{0,2},{2,0},{4,6},{6,4},{8,10},{10,8},{12,14},{14,12},{16,18},{18,... | collective-permute-start | bytes 1572872 | tf_op jit(solution)/shard_map/ppermute | solution.py:560
  2.0 11.0 %collective-permute-start = (bf16[2,2,256,256]{3,2,1,0:T(8,128)(2,1)S(1)}, bf16[2,2,256,256]{3,2,1,0:T(8,128)(2,1)S(1)}, u32[]{:S(2)}, u32[]{:S(2)}) collective-permute-start(bf16[2,2,256,256]{3,2,1,0:T(8,128)(2,1)S(1)} %get-tuple-element.30), channel_id=1, source_target_pairs={{6,8},{14,16},{22,24},{8,6},{16,14},{24,22},{7,9},{15,17},{23,25},... | collective-permute-start | bytes 1572872 | tf_op jit(solution)/shard_map/ppermute | solution.py:559
  7.4 12.3 %collective-permute-start.1 = (bf16[2,2,256,256]{3,2,1,0:T(8,128)(2,1)S(1)}, bf16[2,2,256,256]{3,2,1,0:T(8,128)(2,1)S(1)}, u32[]{:S(2)}, u32[]{:S(2)}) collective-permute-start(bf16[2,2,256,256]{3,2,1,0:T(8,128)(2,1)S(1)} %get-tuple-element.31), channel_id=1, source_target_pairs={{2,4},{10,12},{18,20},{26,28},{4,2},{12,10},{20,18},{28,26},{3,5},... | collective-permute-start | bytes 1572872 | tf_op jit(solution)/shard_map/ppermute | solution.py:573
  9.4 10.3 %copy-start.1 = (bf16[2,2,256,256]{3,2,1,0:T(8,128)(2,1)S(1)}, bf16[2,2,256,256]{3,2,1,0:T(8,128)(2,1)}, u32[]{:S(2)}) copy-start(bf16[2,2,256,256]{3,2,1,0:T(8,128)(2,1)} %source.3) | copy-start | bytes 1572868
  11.3 11.4 %collective-permute-start.4 = (bf16[2,2,256,256]{3,2,1,0:T(8,128)(2,1)S(1)}, bf16[2,2,256,256]{3,2,1,0:T(8,128)(2,1)S(1)}, u32[]{:S(2)}, u32[]{:S(2)}) collective-permute-start(bf16[2,2,256,256]{3,2,1,0:T(8,128)(2,1)S(1)} %get-tuple-element.41), channel_id=1, source_target_pairs={{0,2},{2,0},{4,6},{6,4},{8,10},{10,8},{12,14},{14,12},{16,18},{18,... | collective-permute-start | bytes 1572872 | tf_op jit(solution)/shard_map/ppermute | solution.py:578
  20.8 11.5 %collective-permute-start.2 = (bf16[2,2,256,256]{3,2,1,0:T(8,128)(2,1)S(1)}, bf16[2,2,256,256]{3,2,1,0:T(8,128)(2,1)S(1)}, u32[]{:S(2)}, u32[]{:S(2)}) collective-permute-start(bf16[2,2,256,256]{3,2,1,0:T(8,128)(2,1)S(1)} %get-tuple-element.36), channel_id=1, source_target_pairs={{6,8},{14,16},{22,24},{8,6},{16,14},{24,22},{2,4},{10,12},{18,20},... | collective-permute-start | bytes 1572872 | tf_op jit(solution)/shard_map/ppermute | solution.py:582
  24.5 15.4 %collective-permute-start.6 = (bf16[2,2,256,256]{3,2,1,0:T(8,128)(2,1)S(1)}, bf16[2,2,256,256]{3,2,1,0:T(8,128)(2,1)S(1)}, u32[]{:S(2)}, u32[]{:S(2)}) collective-permute-start(bf16[2,2,256,256]{3,2,1,0:T(8,128)(2,1)S(1)} %get-tuple-element.45), channel_id=1, source_target_pairs={{0,2},{2,0},{4,6},{6,4},{8,10},{10,8},{12,14},{14,12},{16,18},{18,... | collective-permute-start | bytes 1572872 | tf_op jit(solution)/shard_map/ppermute | solution.py:586
  34.1 9.9 %collective-permute-start.7 = (bf16[2,2,128,256]{3,2,1,0:T(8,128)(2,1)S(1)}, bf16[2,2,128,256]{3,2,1,0:T(8,128)(2,1)S(1)}, u32[]{:S(2)}, u32[]{:S(2)}) collective-permute-start(bf16[2,2,128,256]{3,2,1,0:T(8,128)(2,1)S(1)} %get-tuple-element.48), channel_id=1, source_target_pairs={{6,8},{14,16},{22,24},{8,6},{16,14},{24,22},{2,4},{10,12},{18,20},... | collective-permute-start | bytes 786440 | tf_op jit(solution)/shard_map/ppermute | solution.py:595
  36.1 10.8 %collective-permute-start.5 = (bf16[2,2,128,256]{3,2,1,0:T(8,128)(2,1)S(1)}, bf16[2,2,128,256]{3,2,1,0:T(8,128)(2,1)S(1)}, u32[]{:S(2)}, u32[]{:S(2)}) collective-permute-start(bf16[2,2,128,256]{3,2,1,0:T(8,128)(2,1)S(1)} %get-tuple-element.43), channel_id=1, source_target_pairs={{6,8},{14,16},{22,24},{8,6},{16,14},{24,22},{2,4},{10,12},{18,20},... | collective-permute-start | bytes 786440 | tf_op jit(solution)/shard_map/ppermute | solution.py:596
  41.7 6.5 %collective-permute-start.9 = (bf16[128,256]{1,0:T(8,128)(2,1)S(1)}, bf16[128,256]{1,0:T(8,128)(2,1)S(1)}, u32[]{:S(2)}, u32[]{:S(2)}) collective-permute-start(bf16[128,256]{1,0:T(8,128)(2,1)S(1)} %get-tuple-element.56), channel_id=1, source_target_pairs={{0,1},{1,0},{2,3},{3,2},{4,5},{5,4},{6,7},{7,6},{8,9},{9,8},{10,11... | collective-permute-start | bytes 196616 | tf_op jit(solution)/shard_map/ppermute | solution.py:605
  44.4 4.3 %collective-permute-start.8 = (bf16[128,256]{1,0:T(8,128)(2,1)S(1)}, bf16[128,256]{1,0:T(8,128)(2,1)S(1)}, u32[]{:S(2)}, u32[]{:S(2)}) collective-permute-start(bf16[128,256]{1,0:T(8,128)(2,1)S(1)} %get-tuple-element.55), channel_id=1, source_target_pairs={{0,1},{1,0},{2,3},{3,2},{4,5},{5,4},{6,7},{7,6},{8,9},{9,8},{10,11... | collective-permute-start | bytes 196616 | tf_op jit(solution)/shard_map/ppermute | solution.py:612

commit v9 on v8

--- a/solution.py
+++ b/solution.py
@@ -254,7 +254,7 @@
 
 def setup_kernel(
     down, up, reflect, classes_in, slowness, freq, hx, hy,
-    q_out_inner, q_in_outer, screen, phase, refl, outward_outer,
+    q_out_inner, q_in_outer, screen, phase, refl,
     fields, klass, work, sems,
 ):
     fronts = q_out_inner.shape[0]
@@ -273,13 +273,11 @@
     def _():
         pltpu.make_async_copy(down.at[0], fields.at[0], sems.at[0]).start()
         pltpu.make_async_copy(up.at[1], fields.at[1], sems.at[1]).start()
-        pltpu.make_async_copy(up.at[0], outward_outer, sems.at[6]).start()
 
     @pl.when(odd == 1)
     def _():
         pltpu.make_async_copy(up.at[1], fields.at[0], sems.at[0]).start()
         pltpu.make_async_copy(down.at[0], fields.at[1], sems.at[1]).start()
-        pltpu.make_async_copy(down.at[1], outward_outer, sems.at[6]).start()
 
     def squares(length, axis):
         counter = lax.broadcasted_iota(jnp.int32, (rows_x, rows_y), axis)
@@ -309,7 +307,6 @@
             screen[level, front, 1] = look_up(sin_row, klass[level])
     pltpu.make_async_copy(down.at[0], fields.at[0], sems.at[0]).wait()
     pltpu.make_async_copy(down.at[0], fields.at[1], sems.at[1]).wait()
-    pltpu.make_async_copy(down.at[0], outward_outer, sems.at[6]).wait()
     jobs = [(fields.at[1, front], front, q_out_inner.at[front]) for front in range(fronts)]
     jobs += [(fields.at[0, front], front, q_in_outer.at[front]) for front in range(fronts)]
     spread(jobs, work, hx, hy, phase)
@@ -334,7 +331,7 @@
 
 def entering(arrived, source, front):
     first = lax.axis_index("depth") == 0
-    return lambda part: jnp.where(first, source[front, part], arrived(front, part))
+    return lambda part: jnp.where(first, source[front, part], arrived[front, part])
 
 
 def outer_step(q_arrived, q_out_inner, screen, refl, waves, field):
@@ -348,17 +345,8 @@
         )
 
 
-def late_pair():
-    return lax.rem(lax.div(lax.axis_index("depth") + 1, 2), 2) == 1
-
-
-def edge_kernel(early, late, source, q_out_inner, screen, refl, phase, hx, hy, outward, q_arrived, work):
-    everyone = range(early.shape[0])
-    is_late = late_pair()
-
-    def arrived(front, part):
-        return jnp.where(is_late, late[front, part], early[front, part])
-
+def edge_kernel(arrived, source, q_out_inner, screen, refl, phase, hx, hy, outward, q_arrived, work):
+    everyone = range(arrived.shape[0])
     spread([(entering(arrived, source, front), front, q_arrived.at[front]) for front in everyone], work, hx, hy, phase)
     outer_step(q_arrived, q_out_inner, screen, refl, "outward", outward)
 
@@ -371,11 +359,7 @@
     del after
     everyone = range(arrived.shape[0])
     half = arrived.shape[2] // 2
-
-    def received(front, part):
-        return arrived[front, part]
-
-    spread([(entering(received, source, front), front, q_arrived.at[front]) for front in everyone], work, hx, hy, phase)
+    spread([(entering(arrived, source, front), front, q_arrived.at[front]) for front in everyone], work, hx, hy, phase)
     outer_step(q_arrived, q_out_inner, screen, refl, "outward", outward)
     jobs = [
         (outward.at[front], front, [(half_rows(1, half), last_far.at[front]), (half_rows(0, half), last_near.at[front])])
@@ -517,11 +501,7 @@
     hx = jnp.asarray(hartley(rows_x))
     hy = jnp.asarray(hartley(rows_y))
     partners = [(i, i ^ 1) for i in range(depth)]
-    early_pairs, late_pairs = (
-        [(i, i + 1) for i in range(start, depth - 1, 4)] + [(i + 1, i) for i in range(start, depth - 1, 4)]
-        for start in (3, 1)
-    )
-    beyond = early_pairs + late_pairs
+    beyond = [(i, i + 1) for i in range(1, depth - 1, 2)] + [(i + 1, i) for i in range(1, depth - 1, 2)]
     to_partner = functools.partial(lax.ppermute, axis_name="depth", perm=partners)
     to_beyond = functools.partial(lax.ppermute, axis_name="depth", perm=beyond)
     across = functools.partial(lax.ppermute, axis_name="shot", perm=[(i, i ^ 1) for i in range(shots)])
@@ -556,28 +536,27 @@
     out_outer, in_inner = call(edges_kernel, [HBM] * 2, [VMEM] * 2, [plane] * 2, [dma((2,))])(
         *kept_in_hbm(down_state, up_state)
     )
-    arrived_early = to_beyond(out_outer, perm=early_pairs)
+    arrived_0 = to_beyond(out_outer)
     partner_0 = to_partner(in_inner)
-    q_out_inner_0, q_in_outer_0, screen, phase, refl, out_outer_again = call(
+    q_out_inner_0, q_in_outer_0, screen, phase, refl = call(
         setup_kernel,
         [HBM] * 4 + [SMEM] * 2 + [VMEM] * 2,
-        [VMEM] * 6,
-        [plane] * 2 + [screens, turns, pair, plane],
+        [VMEM] * 5,
+        [plane] * 2 + [screens, turns, pair],
         [
             pltpu.VMEM((2, *plane.shape), BF16),
             pltpu.VMEM((2, rows_x, rows_y), jnp.int32),
             work(2 * fronts),
-            dma((7,)),
+            dma((6,)),
         ],
     )(*kept_in_hbm(down_state, up_state, reflect, screen_class), screen_values, freq_index, hx, hy)
-    arrived_late = to_beyond(out_outer_again, perm=late_pairs)
     fixed = (screen, refl, phase, hx, hy)
     in_inner_1, q_out_inner_1 = call(ahead_kernel, [VMEM] * 7, [VMEM] * 2, [plane] * 2, buffers(2) + [work(fronts)])(
         partner_0, q_in_outer_0, *fixed
     )
     partner_1 = to_partner(in_inner_1)
-    out_outer_1, q_arrived = call(edge_kernel, [VMEM] * 9, [VMEM] * 2, [plane] * 2, [work(fronts)])(
-        arrived_early, arrived_late, source, q_out_inner_0, *fixed
+    out_outer_1, q_arrived = call(edge_kernel, [VMEM] * 8, [VMEM] * 2, [plane] * 2, [work(fronts)])(
+        arrived_0, source, q_out_inner_0, *fixed
     )
     arrived_1 = to_beyond(out_outer_1)
     in_inner_2, out_inner_2 = call(

time: 49.9 us -> 49.1 us (0.984)
  starting transfers between devices: 15.2 us -> 14.3 us
    ppermute x1, waiting for transfers between devices: 6.82 us -> 8.38 us  [per_device(): arrived_1 = to_beyond(out_outer_1)]
    ppermute x2 -> x1, waiting for transfers between devices: 6.69 us -> 5.84 us  [per_device(): arrived_0 = to_beyond(out_outer)]
    ppermute x1, waiting for transfers between devices: 0.8 us -> 0.01 us  [per_device(): last_far = to_beyond(last_far)]
    ppermute x2 -> x1, starting transfers between devices: 2.61 us -> 1.92 us  [per_device(): arrived_0 = to_beyond(out_outer)]
  transfers between devices with their start and end apart: 10 -> 9, of which waited for: 5 -> 4; matrix products, arithmetic and copies ran while one was open for 0% -> 0% of each run, Pallas kernels for 32% -> 32%
where the time goes in v9:
time: 49.1 us; the launch traced here: 48.8 us
  Pallas kernels  17.7 us (36%)
  waiting for transfers between devices  15.8 us (32%)
  starting transfers between devices  14.3 us (29%)
  between operations  1 us (2%)
    ppermute x1, waiting for transfers between devices, per_device(): arrived_1 = to_beyond(out_outer_1)  8.38 us
    ppermute x1, waiting for transfers between devices, per_device(): arrived_0 = to_beyond(out_outer)  5.84 us
    pallas_call x1, Pallas kernels, per_device(): call(setup_kernel, [HBM] * 4 + [SMEM] * 2 + [VMEM] * 2, [VMEM] * 5, [plan...  4.65 us
    ppermute x1, starting transfers between devices, per_device(): last_near = to_beyond(last_near)  3.82 us
    pallas_call x1, Pallas kernels, per_device(): call(ahead_kernel, [VMEM] * 7, [VMEM] * 2, [plane] * 2, buffers(2) + [wor...  1.94 us
    ppermute x1, starting transfers between devices, per_device(): arrived_0 = to_beyond(out_outer)  1.92 us
    ppermute x1, starting transfers between devices, per_device(): arrived_1 = to_beyond(out_outer_1)  1.92 us
    ppermute x1, starting transfers between devices, per_device(): last_far = to_beyond(last_far)  1.92 us
  transfers between devices with their start and end apart: 9, of which 4 were waited for; matrix products, arithmetic and copies ran while one was open for 0% of the time, Pallas kernels for 32%

profile of v9, /device:TPU:4, one launch (start us, length us, event | category | flops | bytes accessed | tf_op | source)
XLA Modules:
  0.0 48.8 jit_solution(2395856123609267041)
XLA Ops:
  0.6 0.0 copy-start
  0.6 0.0 copy-start.3
  0.7 1.3 %shard_map.112 = (bf16[2,2,256,256]{3,2,1,0:T(8,128)(2,1)S(1)}, bf16[2,2,256,256]{3,2,1,0:T(8,128)(2,1)S(1)}) custom-call(bf16[2,2,2,256,256]{4,3,2,1,0:T(8,128)(2,1)} %down.3, bf16[2,2,2,256,256]{4,3,2,1,0:T(8,128)(2,1)} %up.3), custom_call_target="tpu_custom_call" | custom-call | tf_op jit(solution)/shard_map/pallas_call | solution.py:536
  2.0 0.1 collective-permute-start.2
  2.0 1.9 %collective-permute-start = (bf16[2,2,256,256]{3,2,1,0:T(8,128)(2,1)S(1)}, bf16[2,2,256,256]{3,2,1,0:T(8,128)(2,1)S(1)}, u32[]{:S(2)}, u32[]{:S(2)}) collective-permute-start(bf16[2,2,256,256]{3,2,1,0:T(8,128)(2,1)S(1)} %get-tuple-element.29), channel_id=1, source_target_pairs={{2,4},{6,8},{10,12},{14,16},{18,20},{22,24},{26,28},{4,2},{8,6},{1... | collective-permute-start | bytes 1572872 | tf_op jit(solution)/shard_map/ppermute | solution.py:539
  4.0 4.7 %shard_map.113 = (bf16[2,2,256,256]{3,2,1,0:T(8,128)(2,1)S(1)}, bf16[2,2,256,256]{3,2,1,0:T(8,128)(2,1)S(1)}, f32[2,2,2,256,256]{4,3,2,1,0:T(8,128)S(1)}, f32[2,...) custom-call(bf16[2,2,2,256,256]{4,3,2,1,0:T(8,128)(2,1)} %down.3, bf16[2,2,2,256,256]{4,3,2,1,0:T(8,128)(2,1)} %up.3, ...), custom_call_target="tpu_custom_call" | custom-call | tf_op jit(solution)/shard_map/pallas_call | solution.py:541
  8.6 0.0 collective-permute-done.2.partner
  8.7 0.0 copy-start.1
  8.7 1.9 %shard_map.115 = (bf16[2,2,256,256]{3,2,1,0:T(8,128)(2,1)S(1)}, bf16[2,2,256,256]{3,2,1,0:T(8,128)(2,1)S(1)}) custom-call(bf16[2,2,256,256]{3,2,1,0:T(8,128)(2,1)S(1)} %collective-permute-done.2.partner, bf16[2,2,256,256]{3,2,1,0:T(8,128)(2,1)S(1)} %get-tuple-element.36.q_in_outer, f32[2,2,2,256,256]{4,3,2,1,0:T(8,128)S(1)} %get-tuple-element.31.screen, ...), custom_call_target="tpu_custom_call" | custom-call | tf_op jit(solution)/shard_map/pallas_call | solution.py:554
  10.6 1.7 %collective-permute-start.3 = (bf16[2,2,256,256]{3,2,1,0:T(8,128)(2,1)S(1)}, bf16[2,2,256,256]{3,2,1,0:T(8,128)(2,1)S(1)}, u32[]{:S(2)}, u32[]{:S(2)}) collective-permute-start(bf16[2,2,256,256]{3,2,1,0:T(8,128)(2,1)S(1)} %get-tuple-element.39), channel_id=1, source_target_pairs={{0,2},{2,0},{4,6},{6,4},{8,10},{10,8},{12,14},{14,12},{16,18},{18,... | collective-permute-start | bytes 1572872 | tf_op jit(solution)/shard_map/ppermute | solution.py:557
  12.3 5.8 %collective-permute-done.arrived = bf16[2,2,256,256]{3,2,1,0:T(8,128)(2,1)S(1)} collective-permute-done((bf16[2,2,256,256]{3,2,1,0:T(8,128)(2,1)S(1)}, bf16[2,2,256,256]{3,2,1,0:T(8,128)(2,1)S(1)}, u32[]{:S(2)}, u32[]{:S(2)}) %collective-permute-start) | collective-permute-done | bytes 524320 | tf_op jit(solution)/shard_map/ppermute | solution.py:539
  18.2 1.1 %shard_map.114 = (bf16[2,2,256,256]{3,2,1,0:T(8,128)(2,1)S(1)}, bf16[2,2,256,256]{3,2,1,0:T(8,128)(2,1)S(1)}) custom-call(bf16[2,2,256,256]{3,2,1,0:T(8,128)(2,1)S(1)} %collective-permute-done.arrived, bf16[2,2,256,256]{3,2,1,0:T(8,128)(2,1)S(1)} %copy-done.1, bf16[2,2,256,256]{3,2,1,0:T(8,128)(2,1)S(1)} %get-tuple-element.30.q_out_inner, ...), custom_call_target="tpu_custom_call" | custom-call | tf_op jit(solution)/shard_map/pallas_call | solution.py:558
  19.2 1.9 %collective-permute-start.1 = (bf16[2,2,256,256]{3,2,1,0:T(8,128)(2,1)S(1)}, bf16[2,2,256,256]{3,2,1,0:T(8,128)(2,1)S(1)}, u32[]{:S(2)}, u32[]{:S(2)}) collective-permute-start(bf16[2,2,256,256]{3,2,1,0:T(8,128)(2,1)S(1)} %get-tuple-element.34), channel_id=1, source_target_pairs={{2,4},{6,8},{10,12},{14,16},{18,20},{22,24},{26,28},{4,2},{8,6},{1... | collective-permute-start | bytes 1572872 | tf_op jit(solution)/shard_map/ppermute | solution.py:561
  21.1 0.0 collective-permute-done.3.partner
  21.1 1.8 %shard_map.116 = (bf16[2,2,256,256]{3,2,1,0:T(8,128)(2,1)S(1)}, bf16[2,2,256,256]{3,2,1,0:T(8,128)(2,1)S(1)}) custom-call(bf16[2,2,256,256]{3,2,1,0:T(8,128)(2,1)S(1)} %get-tuple-element.38.q_arrived, bf16[2,2,256,256]{3,2,1,0:T(8,128)(2,1)S(1)} %get-tuple-element.30.q_out_inner, bf16[2,2,256,256]{3,2,1,0:T(8,128)(2,1)S(1)} %collective-permute-done.3.partner, ...), custom_call_target="tpu_custom_call" | custom-call | tf_op jit(solution)/shard_map/pallas_call | solution.py:562
  22.9 0.1 collective-permute-start.5
  23.0 0.9 %shard_map.117.after.q_out_inner = bf16[2,2,256,256]{3,2,1,0:T(8,128)(2,1)S(1)} custom-call(bf16[2,2,256,256]{3,2,1,0:T(8,128)(2,1)S(1)} %get-tuple-element.40.fields, f32[2,2,256,256]{3,2,1,0:T(8,128)S(1)} %get-tuple-element.33.phase, bf16[256,256]{1,0:T(8,128)(2,1)S(1)} %copy-done, bf16[256,256]{1,0:T(8,128)(2,1)S(1)} %copy-done), custom_call_target="tpu_custom_call" | custom-call | tf_op jit(solution)/shard_map/pallas_call | solution.py:566
  23.9 8.4 %collective-permute-done.1.arrived = bf16[2,2,256,256]{3,2,1,0:T(8,128)(2,1)S(1)} collective-permute-done((bf16[2,2,256,256]{3,2,1,0:T(8,128)(2,1)S(1)}, bf16[2,2,256,256]{3,2,1,0:T(8,128)(2,1)S(1)}, u32[]{:S(2)}, u32[]{:S(2)}) %collective-permute-start.1) | collective-permute-done | bytes 524320 | tf_op jit(solution)/shard_map/ppermute | solution.py:561
  32.3 1.8 %shard_map.118 = (bf16[2,2,256,256]{3,2,1,0:T(8,128)(2,1)S(1)}, bf16[2,2,128,256]{3,2,1,0:T(8,128)(2,1)S(1)}, bf16[2,2,128,256]{3,2,1,0:T(8,128)(2,1)S(1)}) custom-call(bf16[2,2,256,256]{3,2,1,0:T(8,128)(2,1)S(1)} %collective-permute-done.1.arrived, bf16[2,2,256,256]{3,2,1,0:T(8,128)(2,1)S(1)} %copy-done.1, ...), custom_call_target="tpu_custom_call" | custom-call | tf_op jit(solution)/shard_map/pallas_call | solution.py:567
  34.1 1.9 %collective-permute-start.6 = (bf16[2,2,128,256]{3,2,1,0:T(8,128)(2,1)S(1)}, bf16[2,2,128,256]{3,2,1,0:T(8,128)(2,1)S(1)}, u32[]{:S(2)}, u32[]{:S(2)}) collective-permute-start(bf16[2,2,128,256]{3,2,1,0:T(8,128)(2,1)S(1)} %get-tuple-element.46), channel_id=1, source_target_pairs={{2,4},{6,8},{10,12},{14,16},{18,20},{22,24},{26,28},{4,2},{8,6},{1... | collective-permute-start | bytes 786440 | tf_op jit(solution)/shard_map/ppermute | solution.py:574
  36.0 3.8 %collective-permute-start.4 = (bf16[2,2,128,256]{3,2,1,0:T(8,128)(2,1)S(1)}, bf16[2,2,128,256]{3,2,1,0:T(8,128)(2,1)S(1)}, u32[]{:S(2)}, u32[]{:S(2)}) collective-permute-start(bf16[2,2,128,256]{3,2,1,0:T(8,128)(2,1)S(1)} %get-tuple-element.41), channel_id=1, source_target_pairs={{2,4},{6,8},{10,12},{14,16},{18,20},{22,24},{26,28},{4,2},{8,6},{1... | collective-permute-start | bytes 786440 | tf_op jit(solution)/shard_map/ppermute | solution.py:575
  39.9 0.0 collective-permute-done.5.partner
  39.9 1.8 %shard_map.119 = (bf16[2,2,256,256]{3,2,1,0:T(8,128)(2,1)S(1)}, bf16[2,2,256,256]{3,2,1,0:T(8,128)(2,1)S(1)}, f32[256,256]{1,0:T(8,128)S(1)}, bf16[128,256]{1,0:T(8,128)(2,1)S(1)}) custom-call(bf16[2,2,256,256]{3,2,1,0:T(8,128)(2,1)S(1)} %get-tuple-element.42.q_arrived, bf16[2,2,256,256]{3,2,1,0:T(8,128)(2,1)S(1)} %get-tuple-element.37.q_out_inner, ...), custom_call_target="tpu_custom_call" | custom-call | tf_op jit(solution)/shard_map/pallas_call | solution.py:577
  41.7 1.5 %collective-permute-start.8 = (bf16[128,256]{1,0:T(8,128)(2,1)S(1)}, bf16[128,256]{1,0:T(8,128)(2,1)S(1)}, u32[]{:S(2)}, u32[]{:S(2)}) collective-permute-start(bf16[128,256]{1,0:T(8,128)(2,1)S(1)} %get-tuple-element.54), channel_id=1, source_target_pairs={{0,1},{1,0},{2,3},{3,2},{4,5},{5,4},{6,7},{7,6},{8,9},{9,8},{10,11... | collective-permute-start | bytes 196616 | tf_op jit(solution)/shard_map/ppermute | solution.py:584
  43.2 0.0 collective-permute-done.6.last
  43.2 0.3 shard_map.120
  43.6 1.4 %collective-permute-start.7 = (bf16[128,256]{1,0:T(8,128)(2,1)S(1)}, bf16[128,256]{1,0:T(8,128)(2,1)S(1)}, u32[]{:S(2)}, u32[]{:S(2)}) collective-permute-start(bf16[128,256]{1,0:T(8,128)(2,1)S(1)} %get-tuple-element.53), channel_id=1, source_target_pairs={{0,1},{1,0},{2,3},{3,2},{4,5},{5,4},{6,7},{7,6},{8,9},{9,8},{10,11... | collective-permute-start | bytes 196616 | tf_op jit(solution)/shard_map/ppermute | solution.py:591
  45.0 0.9 %collective-permute-done.4.last = bf16[2,2,128,256]{3,2,1,0:T(8,128)(2,1)S(1)} collective-permute-done((bf16[2,2,128,256]{3,2,1,0:T(8,128)(2,1)S(1)}, bf16[2,2,128,256]{3,2,1,0:T(8,128)(2,1)S(1)}, u32[]{:S(2)}, u32[]{:S(2)}) %collective-permute-start.4) | collective-permute-done | bytes 262176 | tf_op jit(solution)/shard_map/ppermute | solution.py:575
  45.9 1.4 %shard_map.121 = (bf16[2,2,2,256,256]{4,3,2,1,0:T(8,128)(2,1)}, bf16[2,2,2,256,256]{4,3,2,1,0:T(8,128)(2,1)}, f32[128,256]{1,0:T(8,128)S(1)}) custom-call(bf16[2,2,128,256]{3,2,1,0:T(8,128)(2,1)S(1)} %collective-permute-done.4.last, bf16[2,2,256,256]{3,2,1,0:T(8,128)(2,1)S(1)} %get-tuple-element.38.q_arrived, ...), custom_call_target="tpu_custom_call" | custom-call | tf_op jit(solution)/shard_map/pallas_call | solution.py:592
  47.2 0.0 collective-permute-done.8.inner_other
  47.2 0.7 %collective-permute-done.7.outer_other = bf16[128,256]{1,0:T(8,128)(2,1)S(1)} collective-permute-done((bf16[128,256]{1,0:T(8,128)(2,1)S(1)}, bf16[128,256]{1,0:T(8,128)(2,1)S(1)}, u32[]{:S(2)}, u32[]{:S(2)}) %collective-permute-start.7) | collective-permute-done | bytes 65568 | tf_op jit(solution)/shard_map/ppermute | solution.py:591
  47.9 0.7 %shard_map.122 = f32[2,128,256]{2,1,0:T(8,128)} custom-call(f32[128,256]{1,0:T(8,128)S(1)} %get-tuple-element.52.outer_terms, f32[256,256]{1,0:T(8,128)S(1)} %get-tuple-element.47.after.inner_terms, bf16[128,256]{1,0:T(8,128)(2,1)S(1)} %collective-permute-done.7.outer_other, bf16[128,256]{1,0:T(8,128)(2,1)S(1)} %collective-permute-done.8.inner_other), custom_call_target="tpu_custom_call" | custom-call | tf_op jit(solution)/shard_map/pallas_call | solution.py:599
  (5 shorter events, 0.0 us)
Async XLA Ops:
  0.6 3.3 %copy-start = (bf16[256,256]{1,0:T(8,128)(2,1)S(1)}, bf16[256,256]{1,0:T(8,128)(2,1)}, u32[]{:S(2)}) copy-start(bf16[256,256]{1,0:T(8,128)(2,1)} %constant.2.clone.hx.hy) | copy-start | bytes 393220
  0.6 3.3 %copy-start.3 = (s32[2]{0:T(128)S(1)}, s32[2]{0:T(128)}, u32[]{:S(2)}) copy-start(s32[2]{0:T(128)} %freq.1) | copy-start | bytes 28
  0.7 3.3 %copy-start.2 = (f32[16]{0:T(128)S(1)}, f32[16]{0:T(128)}, u32[]{:S(2)}) copy-start(f32[16]{0:T(128)} %slowness.1) | copy-start | bytes 196
  2.0 6.7 %collective-permute-start.2 = (bf16[2,2,256,256]{3,2,1,0:T(8,128)(2,1)S(1)}, bf16[2,2,256,256]{3,2,1,0:T(8,128)(2,1)S(1)}, u32[]{:S(2)}, u32[]{:S(2)}) collective-permute-start(bf16[2,2,256,256]{3,2,1,0:T(8,128)(2,1)S(1)} %get-tuple-element.35), channel_id=1, source_target_pairs={{0,2},{2,0},{4,6},{6,4},{8,10},{10,8},{12,14},{14,12},{16,18},{18,... | collective-permute-start | bytes 1572872 | tf_op jit(solution)/shard_map/ppermute | solution.py:540
  2.0 16.1 %collective-permute-start = (bf16[2,2,256,256]{3,2,1,0:T(8,128)(2,1)S(1)}, bf16[2,2,256,256]{3,2,1,0:T(8,128)(2,1)S(1)}, u32[]{:S(2)}, u32[]{:S(2)}) collective-permute-start(bf16[2,2,256,256]{3,2,1,0:T(8,128)(2,1)S(1)} %get-tuple-element.29), channel_id=1, source_target_pairs={{2,4},{6,8},{10,12},{14,16},{18,20},{22,24},{26,28},{4,2},{8,6},{1... | collective-permute-start | bytes 1572872 | tf_op jit(solution)/shard_map/ppermute | solution.py:539
  8.7 9.5 %copy-start.1 = (bf16[2,2,256,256]{3,2,1,0:T(8,128)(2,1)S(1)}, bf16[2,2,256,256]{3,2,1,0:T(8,128)(2,1)}, u32[]{:S(2)}) copy-start(bf16[2,2,256,256]{3,2,1,0:T(8,128)(2,1)} %source.3) | copy-start | bytes 1572868
  10.6 10.5 %collective-permute-start.3 = (bf16[2,2,256,256]{3,2,1,0:T(8,128)(2,1)S(1)}, bf16[2,2,256,256]{3,2,1,0:T(8,128)(2,1)S(1)}, u32[]{:S(2)}, u32[]{:S(2)}) collective-permute-start(bf16[2,2,256,256]{3,2,1,0:T(8,128)(2,1)S(1)} %get-tuple-element.39), channel_id=1, source_target_pairs={{0,2},{2,0},{4,6},{6,4},{8,10},{10,8},{12,14},{14,12},{16,18},{18,... | collective-permute-start | bytes 1572872 | tf_op jit(solution)/shard_map/ppermute | solution.py:557
  19.2 13.1 %collective-permute-start.1 = (bf16[2,2,256,256]{3,2,1,0:T(8,128)(2,1)S(1)}, bf16[2,2,256,256]{3,2,1,0:T(8,128)(2,1)S(1)}, u32[]{:S(2)}, u32[]{:S(2)}) collective-permute-start(bf16[2,2,256,256]{3,2,1,0:T(8,128)(2,1)S(1)} %get-tuple-element.34), channel_id=1, source_target_pairs={{2,4},{6,8},{10,12},{14,16},{18,20},{22,24},{26,28},{4,2},{8,6},{1... | collective-permute-start | bytes 1572872 | tf_op jit(solution)/shard_map/ppermute | solution.py:561
  22.9 16.9 %collective-permute-start.5 = (bf16[2,2,256,256]{3,2,1,0:T(8,128)(2,1)S(1)}, bf16[2,2,256,256]{3,2,1,0:T(8,128)(2,1)S(1)}, u32[]{:S(2)}, u32[]{:S(2)}) collective-permute-start(bf16[2,2,256,256]{3,2,1,0:T(8,128)(2,1)S(1)} %get-tuple-element.43), channel_id=1, source_target_pairs={{0,2},{2,0},{4,6},{6,4},{8,10},{10,8},{12,14},{14,12},{16,18},{18,... | collective-permute-start | bytes 1572872 | tf_op jit(solution)/shard_map/ppermute | solution.py:565
  34.1 9.1 %collective-permute-start.6 = (bf16[2,2,128,256]{3,2,1,0:T(8,128)(2,1)S(1)}, bf16[2,2,128,256]{3,2,1,0:T(8,128)(2,1)S(1)}, u32[]{:S(2)}, u32[]{:S(2)}) collective-permute-start(bf16[2,2,128,256]{3,2,1,0:T(8,128)(2,1)S(1)} %get-tuple-element.46), channel_id=1, source_target_pairs={{2,4},{6,8},{10,12},{14,16},{18,20},{22,24},{26,28},{4,2},{8,6},{1... | collective-permute-start | bytes 786440 | tf_op jit(solution)/shard_map/ppermute | solution.py:574
  36.0 9.8 %collective-permute-start.4 = (bf16[2,2,128,256]{3,2,1,0:T(8,128)(2,1)S(1)}, bf16[2,2,128,256]{3,2,1,0:T(8,128)(2,1)S(1)}, u32[]{:S(2)}, u32[]{:S(2)}) collective-permute-start(bf16[2,2,128,256]{3,2,1,0:T(8,128)(2,1)S(1)} %get-tuple-element.41), channel_id=1, source_target_pairs={{2,4},{6,8},{10,12},{14,16},{18,20},{22,24},{26,28},{4,2},{8,6},{1... | collective-permute-start | bytes 786440 | tf_op jit(solution)/shard_map/ppermute | solution.py:575
  41.7 5.5 %collective-permute-start.8 = (bf16[128,256]{1,0:T(8,128)(2,1)S(1)}, bf16[128,256]{1,0:T(8,128)(2,1)S(1)}, u32[]{:S(2)}, u32[]{:S(2)}) collective-permute-start(bf16[128,256]{1,0:T(8,128)(2,1)S(1)} %get-tuple-element.54), channel_id=1, source_target_pairs={{0,1},{1,0},{2,3},{3,2},{4,5},{5,4},{6,7},{7,6},{8,9},{9,8},{10,11... | collective-permute-start | bytes 196616 | tf_op jit(solution)/shard_map/ppermute | solution.py:584
  43.6 4.3 %collective-permute-start.7 = (bf16[128,256]{1,0:T(8,128)(2,1)S(1)}, bf16[128,256]{1,0:T(8,128)(2,1)S(1)}, u32[]{:S(2)}, u32[]{:S(2)}) collective-permute-start(bf16[128,256]{1,0:T(8,128)(2,1)S(1)} %get-tuple-element.53), channel_id=1, source_target_pairs={{0,1},{1,0},{2,3},{3,2},{4,5},{5,4},{6,7},{7,6},{8,9},{9,8},{10,11... | collective-permute-start | bytes 196616 | tf_op jit(solution)/shard_map/ppermute | solution.py:591

commit v10 on v9

--- a/solution.py
+++ b/solution.py
@@ -417,31 +417,38 @@
     far_terms[...] = terms[half_rows(1, far_terms.shape[0]), :].astype(BF16)
 
 
-def far_rows_kernel(last, q_arrived, q_out_inner, screen, refl, after, inward, outward, terms):
-    del after
-    _, total = outer_rows(1, last, q_arrived, q_out_inner, screen, refl, inward, outward)
-    terms[...] = total.astype(BF16)
-
-
-def outer_rows(of, last, q_arrived, q_out_inner, screen, refl, inward, outward):
-    fronts, _, half, _ = last.shape
+def incoming(last, q_arrived, front, rows):
     first = lax.axis_index("depth") == 0
-    rows = half_rows(of, half)
+    return [jnp.where(first, q_arrived[front, part, rows, :], last[front, part]).astype(F32) for part in range(2)]
+
+
+def row_terms(of, last, q_arrived, q_out_inner):
     total = None
-    for front in range(fronts):
-        a_re, a_im = (
-            jnp.where(first, q_arrived[front, part, rows, :], last[front, part]).astype(F32)
-            for part in range(2)
-        )
+    rows = half_rows(of, last.shape[2])
+    for front in range(last.shape[0]):
+        a_re, a_im = incoming(last, q_arrived, front, rows)
+        b_re, b_im = (q_out_inner[front, part, rows, :].astype(F32) for part in range(2))
+        term = a_re * b_re + a_im * b_im
+        total = term if total is None else total + term
+    return total
+
+
+def row_fields(of, last, q_arrived, q_out_inner, screen, refl, inward, outward):
+    rows = half_rows(of, last.shape[2])
+    for front in range(last.shape[0]):
+        a_re, a_im = incoming(last, q_arrived, front, rows)
         b_re, b_im = (q_out_inner[front, part, rows, :].astype(F32) for part in range(2))
         in_re, in_im, out_re, out_im = mixed(
             a_re, a_im, b_re, b_im, refl[0, rows, :], screen[0, front, 0, rows, :], screen[0, front, 1, rows, :]
         )
         put(inward.at[front], in_re, in_im)
         put(outward.at[front], out_re, out_im)
-        term = a_re * b_re + a_im * b_im
-        total = term if total is None else total + term
-    return rows, total
+    return rows
+
+
+def far_terms_kernel(last, q_arrived, q_out_inner, after, terms):
+    del after
+    terms[...] = row_terms(1, last, q_arrived, q_out_inner).astype(BF16)
 
 
 def send_home(level, rows, inward, outward, down_out, up_out, sems):
@@ -466,26 +473,29 @@
     return copies(0, down_out, up_out)
 
 
-def near_rows_kernel(
-    last, q_arrived, q_out_inner, screen, refl, inner_in, inner_out, far_in, far_out,
-    down_out, up_out, terms,
-    inward, outward, sems,
+def outer_fields_kernel(
+    scale, near, far, q_arrived, q_out_inner, screen, refl, inner_in, inner_out, inner_terms, inner_other,
+    down_out, up_out, gradient, terms,
+    near_in, near_out, far_in, far_out, inner_sum, sems,
 ):
-    rows_x, half = inner_in.shape[2], far_in.shape[2]
+    rows_x = inner_in.shape[2]
     waits = send_home(1, pl.ds(0, rows_x), inner_in, inner_out, down_out, up_out, sems.at[0])
-    waits += send_home(0, half_rows(1, half), far_in, far_out, down_out, up_out, sems.at[1])
-    rows, total = outer_rows(0, last, q_arrived, q_out_inner, screen, refl, inward, outward)
-    waits += send_home(0, rows, inward, outward, down_out, up_out, sems.at[2])
-    terms[...] = total
+    rows = row_fields(1, far, q_arrived, q_out_inner, screen, refl, far_in, far_out)
+    waits += send_home(0, rows, far_in, far_out, down_out, up_out, sems.at[1])
+    rows = row_fields(0, near, q_arrived, q_out_inner, screen, refl, near_in, near_out)
+    waits += send_home(0, rows, near_in, near_out, down_out, up_out, sems.at[2])
+    inner_sum[...] = scale * (inner_terms[rows, :] + inner_other[...].astype(F32))
+    waits.append(pltpu.make_async_copy(inner_sum, gradient.at[1 - odd_place()], sems.at[3, 0]))
+    waits[-1].start()
+    terms[...] = row_terms(0, near, q_arrived, q_out_inner)
     for copy in waits:
         copy.wait()
 
 
-def gradient_kernel(scale, outer_terms, inner_terms, outer_other, inner_other, gradient, sums, sems):
-    odd = odd_place()
-    sums[odd] = scale * (outer_terms[...] + outer_other[...].astype(F32))
-    sums[1 - odd] = scale * (inner_terms[half_rows(0, sums.shape[1]), :] + inner_other[...].astype(F32))
-    done = pltpu.make_async_copy(sums, gradient, sems.at[0])
+def outer_gradient_kernel(scale, terms, other, gradient_in, gradient, outer_sum, sems):
+    del gradient_in
+    outer_sum[...] = scale * (terms[...] + other[...].astype(F32))
+    done = pltpu.make_async_copy(outer_sum, gradient.at[odd_place()], sems.at[0])
     done.start()
     done.wait()
 
@@ -582,27 +592,29 @@
         buffers(3) + [work(2 * fronts)],
     )(q_arrived_1, q_out_inner_1, partner_2, *fixed)
     inner_other = across(inner_far) if shots == 2 else jnp.zeros_like(inner_far)
-    far_in, far_out, outer_far = call(
-        far_rows_kernel,
-        [VMEM] * 5 + [pl.BlockSpec(memory_space=pl.ANY)],
-        [VMEM] * 3,
-        [half_plane] * 2 + [half_sum],
-    )(last_far, q_arrived, q_out_inner_2, screen, refl, inner_terms)
+    outer_far = call(far_terms_kernel, [VMEM] * 3 + [pl.BlockSpec(memory_space=pl.ANY)], VMEM, half_sum)(
+        last_far, q_arrived, q_out_inner_2, inner_terms
+    )
     outer_other = across(outer_far) if shots == 2 else jnp.zeros_like(outer_far)
-    down, up, outer_near = call(
-        near_rows_kernel,
-        [VMEM] * 9,
-        [HBM] * 2 + [VMEM],
-        [state, state, jax.ShapeDtypeStruct((half, rows_y), F32)],
-        buffers(2, half_plane) + [dma((3, 2))],
-    )(last_near, q_arrived, q_out_inner_2, screen, refl, inner_in, inner_out, far_in, far_out)
+    half_total = jax.ShapeDtypeStruct((half, rows_y), F32)
+    share = jax.ShapeDtypeStruct((2, half, rows_y), F32)
+    down, up, gradient, outer_near = call(
+        functools.partial(outer_fields_kernel, scale),
+        [VMEM] * 10,
+        [HBM] * 3 + [VMEM],
+        [state, state, share, half_total],
+        buffers(4, half_plane) + buffers(1, half_total) + [dma((4, 2))],
+    )(
+        last_near, last_far, q_arrived, q_out_inner_2, screen, refl, inner_in, inner_out, inner_terms, inner_other
+    )
     gradient = call(
-        functools.partial(gradient_kernel, scale),
-        [VMEM] * 4,
+        functools.partial(outer_gradient_kernel, scale),
+        [VMEM] * 2 + [HBM],
         HBM,
-        jax.ShapeDtypeStruct((2, half, rows_y), F32),
-        [pltpu.VMEM((2, half, rows_y), F32), dma((1,))],
-    )(outer_near, inner_terms, outer_other, inner_other)
+        share,
+        buffers(1, half_total) + [dma((1,))],
+        input_output_aliases={2: 0},
+    )(outer_near, outer_other, gradient)
     if shots != 2:
         terms = scale * jnp.stack([outer_far, inner_far]).astype(F32)
         far = jnp.where(odd_place() == 0, terms, terms[::-1])

time: 49.1 us -> 48.9 us (level)
  transfers between devices with their start and end apart: 9 -> 9, of which waited for: 4 -> 5; matrix products, arithmetic and copies ran while one was open for 0% -> 0% of each run, Pallas kernels for 32% -> 32%
where the time goes in v10:
time: 48.9 us; the launch traced here: 48.5 us
  Pallas kernels  17.4 us (36%)
  waiting for transfers between devices  15.8 us (32%)
  starting transfers between devices  14.3 us (29%)
  between operations  0.99 us (2%)
    ppermute x1, waiting for transfers between devices, per_device(): arrived_1 = to_beyond(out_outer_1)  8.38 us
    ppermute x1, waiting for transfers between devices, per_device(): arrived_0 = to_beyond(out_outer)  5.82 us
    pallas_call x1, Pallas kernels, per_device(): call(setup_kernel, [HBM] * 4 + [SMEM] * 2 + [VMEM] * 2, [VMEM] * 5, [plan...  4.65 us
    ppermute x1, starting transfers between devices, per_device(): last_near = to_beyond(last_near)  3.82 us
    pallas_call x1, Pallas kernels, per_device(): call(ahead_kernel, [VMEM] * 7, [VMEM] * 2, [plane] * 2, buffers(2) + [wor...  1.96 us
    ppermute x1, starting transfers between devices, per_device(): arrived_0 = to_beyond(out_outer)  1.92 us
    ppermute x1, starting transfers between devices, per_device(): arrived_1 = to_beyond(out_outer_1)  1.92 us
    ppermute x1, starting transfers between devices, per_device(): last_far = to_beyond(last_far)  1.92 us
  transfers between devices with their start and end apart: 9, of which 5 were waited for; matrix products, arithmetic and copies ran while one was open for 0% of the time, Pallas kernels for 32%

profile of v10, /device:TPU:4, one launch (start us, length us, event | category | flops | bytes accessed | tf_op | source)
XLA Modules:
  0.0 48.5 jit_solution(16800895204333469766)
XLA Ops:
  0.6 0.0 copy-start
  0.6 0.0 copy-start.3
  0.7 1.3 %shard_map.112 = (bf16[2,2,256,256]{3,2,1,0:T(8,128)(2,1)S(1)}, bf16[2,2,256,256]{3,2,1,0:T(8,128)(2,1)S(1)}) custom-call(bf16[2,2,2,256,256]{4,3,2,1,0:T(8,128)(2,1)} %down.3, bf16[2,2,2,256,256]{4,3,2,1,0:T(8,128)(2,1)} %up.3), custom_call_target="tpu_custom_call" | custom-call | tf_op jit(solution)/shard_map/pallas_call | solution.py:546
  2.0 0.1 collective-permute-start.2
  2.0 1.9 %collective-permute-start = (bf16[2,2,256,256]{3,2,1,0:T(8,128)(2,1)S(1)}, bf16[2,2,256,256]{3,2,1,0:T(8,128)(2,1)S(1)}, u32[]{:S(2)}, u32[]{:S(2)}) collective-permute-start(bf16[2,2,256,256]{3,2,1,0:T(8,128)(2,1)S(1)} %get-tuple-element.27), channel_id=1, source_target_pairs={{2,4},{6,8},{10,12},{14,16},{18,20},{22,24},{26,28},{4,2},{8,6},{1... | collective-permute-start | bytes 1572872 | tf_op jit(solution)/shard_map/ppermute | solution.py:549
  4.0 4.7 %shard_map.113 = (bf16[2,2,256,256]{3,2,1,0:T(8,128)(2,1)S(1)}, bf16[2,2,256,256]{3,2,1,0:T(8,128)(2,1)S(1)}, f32[2,2,2,256,256]{4,3,2,1,0:T(8,128)S(1)}, f32[2,...) custom-call(bf16[2,2,2,256,256]{4,3,2,1,0:T(8,128)(2,1)} %down.3, bf16[2,2,2,256,256]{4,3,2,1,0:T(8,128)(2,1)} %up.3, ...), custom_call_target="tpu_custom_call" | custom-call | tf_op jit(solution)/shard_map/pallas_call | solution.py:551
  8.6 0.0 collective-permute-done.2.partner
  8.7 0.0 copy-start.1
  8.7 2.0 %shard_map.115 = (bf16[2,2,256,256]{3,2,1,0:T(8,128)(2,1)S(1)}, bf16[2,2,256,256]{3,2,1,0:T(8,128)(2,1)S(1)}) custom-call(bf16[2,2,256,256]{3,2,1,0:T(8,128)(2,1)S(1)} %collective-permute-done.2.partner, bf16[2,2,256,256]{3,2,1,0:T(8,128)(2,1)S(1)} %get-tuple-element.34.q_in_outer, f32[2,2,2,256,256]{4,3,2,1,0:T(8,128)S(1)} %get-tuple-element.29.screen, ...), custom_call_target="tpu_custom_call" | custom-call | tf_op jit(solution)/shard_map/pallas_call | solution.py:564
  10.6 1.7 %collective-permute-start.3 = (bf16[2,2,256,256]{3,2,1,0:T(8,128)(2,1)S(1)}, bf16[2,2,256,256]{3,2,1,0:T(8,128)(2,1)S(1)}, u32[]{:S(2)}, u32[]{:S(2)}) collective-permute-start(bf16[2,2,256,256]{3,2,1,0:T(8,128)(2,1)S(1)} %get-tuple-element.37), channel_id=1, source_target_pairs={{0,2},{2,0},{4,6},{6,4},{8,10},{10,8},{12,14},{14,12},{16,18},{18,... | collective-permute-start | bytes 1572872 | tf_op jit(solution)/shard_map/ppermute | solution.py:567
  12.3 5.8 %collective-permute-done.arrived = bf16[2,2,256,256]{3,2,1,0:T(8,128)(2,1)S(1)} collective-permute-done((bf16[2,2,256,256]{3,2,1,0:T(8,128)(2,1)S(1)}, bf16[2,2,256,256]{3,2,1,0:T(8,128)(2,1)S(1)}, u32[]{:S(2)}, u32[]{:S(2)}) %collective-permute-start) | collective-permute-done | bytes 524320 | tf_op jit(solution)/shard_map/ppermute | solution.py:549
  18.2 1.1 %shard_map.114 = (bf16[2,2,256,256]{3,2,1,0:T(8,128)(2,1)S(1)}, bf16[2,2,256,256]{3,2,1,0:T(8,128)(2,1)S(1)}) custom-call(bf16[2,2,256,256]{3,2,1,0:T(8,128)(2,1)S(1)} %collective-permute-done.arrived, bf16[2,2,256,256]{3,2,1,0:T(8,128)(2,1)S(1)} %copy-done.1, bf16[2,2,256,256]{3,2,1,0:T(8,128)(2,1)S(1)} %get-tuple-element.28.q_out_inner, ...), custom_call_target="tpu_custom_call" | custom-call | tf_op jit(solution)/shard_map/pallas_call | solution.py:568
  19.2 1.9 %collective-permute-start.1 = (bf16[2,2,256,256]{3,2,1,0:T(8,128)(2,1)S(1)}, bf16[2,2,256,256]{3,2,1,0:T(8,128)(2,1)S(1)}, u32[]{:S(2)}, u32[]{:S(2)}) collective-permute-start(bf16[2,2,256,256]{3,2,1,0:T(8,128)(2,1)S(1)} %get-tuple-element.32), channel_id=1, source_target_pairs={{2,4},{6,8},{10,12},{14,16},{18,20},{22,24},{26,28},{4,2},{8,6},{1... | collective-permute-start | bytes 1572872 | tf_op jit(solution)/shard_map/ppermute | solution.py:571
  21.1 0.0 collective-permute-done.3.partner
  21.1 1.8 %shard_map.116 = (bf16[2,2,256,256]{3,2,1,0:T(8,128)(2,1)S(1)}, bf16[2,2,256,256]{3,2,1,0:T(8,128)(2,1)S(1)}) custom-call(bf16[2,2,256,256]{3,2,1,0:T(8,128)(2,1)S(1)} %get-tuple-element.36.q_arrived, bf16[2,2,256,256]{3,2,1,0:T(8,128)(2,1)S(1)} %get-tuple-element.28.q_out_inner, bf16[2,2,256,256]{3,2,1,0:T(8,128)(2,1)S(1)} %collective-permute-done.3.partner, ...), custom_call_target="tpu_custom_call" | custom-call | tf_op jit(solution)/shard_map/pallas_call | solution.py:572
  22.9 0.1 collective-permute-start.6
  23.0 0.9 %shard_map.117.after.q_out_inner = bf16[2,2,256,256]{3,2,1,0:T(8,128)(2,1)S(1)} custom-call(bf16[2,2,256,256]{3,2,1,0:T(8,128)(2,1)S(1)} %get-tuple-element.38.fields, f32[2,2,256,256]{3,2,1,0:T(8,128)S(1)} %get-tuple-element.31.phase, bf16[256,256]{1,0:T(8,128)(2,1)S(1)} %copy-done, bf16[256,256]{1,0:T(8,128)(2,1)S(1)} %copy-done), custom_call_target="tpu_custom_call" | custom-call | tf_op jit(solution)/shard_map/pallas_call | solution.py:576
  23.9 8.4 %collective-permute-done.1.arrived = bf16[2,2,256,256]{3,2,1,0:T(8,128)(2,1)S(1)} collective-permute-done((bf16[2,2,256,256]{3,2,1,0:T(8,128)(2,1)S(1)}, bf16[2,2,256,256]{3,2,1,0:T(8,128)(2,1)S(1)}, u32[]{:S(2)}, u32[]{:S(2)}) %collective-permute-start.1) | collective-permute-done | bytes 524320 | tf_op jit(solution)/shard_map/ppermute | solution.py:571
  32.3 1.8 %shard_map.118 = (bf16[2,2,256,256]{3,2,1,0:T(8,128)(2,1)S(1)}, bf16[2,2,128,256]{3,2,1,0:T(8,128)(2,1)S(1)}, bf16[2,2,128,256]{3,2,1,0:T(8,128)(2,1)S(1)}) custom-call(bf16[2,2,256,256]{3,2,1,0:T(8,128)(2,1)S(1)} %collective-permute-done.1.arrived, bf16[2,2,256,256]{3,2,1,0:T(8,128)(2,1)S(1)} %copy-done.1, ...), custom_call_target="tpu_custom_call" | custom-call | tf_op jit(solution)/shard_map/pallas_call | solution.py:577
  34.1 1.9 %collective-permute-start.5 = (bf16[2,2,128,256]{3,2,1,0:T(8,128)(2,1)S(1)}, bf16[2,2,128,256]{3,2,1,0:T(8,128)(2,1)S(1)}, u32[]{:S(2)}, u32[]{:S(2)}) collective-permute-start(bf16[2,2,128,256]{3,2,1,0:T(8,128)(2,1)S(1)} %get-tuple-element.40), channel_id=1, source_target_pairs={{2,4},{6,8},{10,12},{14,16},{18,20},{22,24},{26,28},{4,2},{8,6},{1... | collective-permute-start | bytes 786440 | tf_op jit(solution)/shard_map/ppermute | solution.py:584
  36.0 3.8 %collective-permute-start.4 = (bf16[2,2,128,256]{3,2,1,0:T(8,128)(2,1)S(1)}, bf16[2,2,128,256]{3,2,1,0:T(8,128)(2,1)S(1)}, u32[]{:S(2)}, u32[]{:S(2)}) collective-permute-start(bf16[2,2,128,256]{3,2,1,0:T(8,128)(2,1)S(1)} %get-tuple-element.39), channel_id=1, source_target_pairs={{2,4},{6,8},{10,12},{14,16},{18,20},{22,24},{26,28},{4,2},{8,6},{1... | collective-permute-start | bytes 786440 | tf_op jit(solution)/shard_map/ppermute | solution.py:585
  39.9 0.0 collective-permute-done.6.partner
  39.9 1.8 %shard_map.119 = (bf16[2,2,256,256]{3,2,1,0:T(8,128)(2,1)S(1)}, bf16[2,2,256,256]{3,2,1,0:T(8,128)(2,1)S(1)}, f32[256,256]{1,0:T(8,128)S(1)}, bf16[128,256]{1,0:T(8,128)(2,1)S(1)}) custom-call(bf16[2,2,256,256]{3,2,1,0:T(8,128)(2,1)S(1)} %get-tuple-element.41.q_arrived, bf16[2,2,256,256]{3,2,1,0:T(8,128)(2,1)S(1)} %get-tuple-element.35.q_out_inner, ...), custom_call_target="tpu_custom_call" | custom-call | tf_op jit(solution)/shard_map/pallas_call | solution.py:587
  41.7 1.5 %collective-permute-start.7 = (bf16[128,256]{1,0:T(8,128)(2,1)S(1)}, bf16[128,256]{1,0:T(8,128)(2,1)S(1)}, u32[]{:S(2)}, u32[]{:S(2)}) collective-permute-start(bf16[128,256]{1,0:T(8,128)(2,1)S(1)} %get-tuple-element.46), channel_id=1, source_target_pairs={{0,1},{1,0},{2,3},{3,2},{4,5},{5,4},{6,7},{7,6},{8,9},{9,8},{10,11... | collective-permute-start | bytes 196616 | tf_op jit(solution)/shard_map/ppermute | solution.py:594
  43.2 0.0 collective-permute-done.5.far.last
  43.2 0.1 shard_map.121
  43.3 1.4 %collective-permute-start.8 = (bf16[128,256]{1,0:T(8,128)(2,1)S(1)}, bf16[128,256]{1,0:T(8,128)(2,1)S(1)}, u32[]{:S(2)}, u32[]{:S(2)}) collective-permute-start(bf16[128,256]{1,0:T(8,128)(2,1)S(1)} %shard_map.121), channel_id=1, source_target_pairs={{0,1},{1,0},{2,3},{3,2},{4,5},{5,4},{6,7},{7,6},{8,9},{9,8},{10,11... | collective-permute-start | bytes 196616 | tf_op jit(solution)/shard_map/ppermute | solution.py:598
  44.7 1.2 %collective-permute-done.4.near = bf16[2,2,128,256]{3,2,1,0:T(8,128)(2,1)S(1)} collective-permute-done((bf16[2,2,128,256]{3,2,1,0:T(8,128)(2,1)S(1)}, bf16[2,2,128,256]{3,2,1,0:T(8,128)(2,1)S(1)}, u32[]{:S(2)}, u32[]{:S(2)}) %collective-permute-start.4) | collective-permute-done | bytes 262176 | tf_op jit(solution)/shard_map/ppermute | solution.py:585
  45.9 0.2 collective-permute-done.7.inner_other
  46.0 1.4 %shard_map.120 = (bf16[2,2,2,256,256]{4,3,2,1,0:T(8,128)(2,1)}, bf16[2,2,2,256,256]{4,3,2,1,0:T(8,128)(2,1)}, f32[2,128,256]{2,1,0:T(8,128)}, f32[128,256]{1,0:T(8,128)S(1)}) custom-call(bf16[2,2,128,256]{3,2,1,0:T(8,128)(2,1)S(1)} %collective-permute-done.4.near, bf16[2,2,128,256]{3,2,1,0:T(8,128)(2,1)S(1)} %collective-permute-done.5.far.last, ...), custom_call_target="tpu_custom_call" | custom-call | tf_op jit(solution)/shard_map/pallas_call | solution.py:601
  47.5 0.2 collective-permute-done.8.other
  47.7 0.7 %shard_map.122 = f32[2,128,256]{2,1,0:T(8,128)} custom-call(f32[128,256]{1,0:T(8,128)S(1)} %get-tuple-element.49.terms, bf16[128,256]{1,0:T(8,128)(2,1)S(1)} %collective-permute-done.8.other, f32[2,128,256]{2,1,0:T(8,128)} %get-tuple-element.50.gradient_in), custom_call_target="tpu_custom_call", output_to_operand_aliasing={{}: (2, {})} | custom-call | tf_op jit(solution)/shard_map/pallas_call | solution.py:610
  (5 shorter events, 0.0 us)
Async XLA Ops:
  0.6 3.3 %copy-start = (bf16[256,256]{1,0:T(8,128)(2,1)S(1)}, bf16[256,256]{1,0:T(8,128)(2,1)}, u32[]{:S(2)}) copy-start(bf16[256,256]{1,0:T(8,128)(2,1)} %constant.2.clone.hx.hy) | copy-start | bytes 393220
  0.6 3.3 %copy-start.3 = (s32[2]{0:T(128)S(1)}, s32[2]{0:T(128)}, u32[]{:S(2)}) copy-start(s32[2]{0:T(128)} %freq.1) | copy-start | bytes 28
  0.7 3.3 %copy-start.2 = (f32[16]{0:T(128)S(1)}, f32[16]{0:T(128)}, u32[]{:S(2)}) copy-start(f32[16]{0:T(128)} %slowness.1) | copy-start | bytes 196
  2.0 6.7 %collective-permute-start.2 = (bf16[2,2,256,256]{3,2,1,0:T(8,128)(2,1)S(1)}, bf16[2,2,256,256]{3,2,1,0:T(8,128)(2,1)S(1)}, u32[]{:S(2)}, u32[]{:S(2)}) collective-permute-start(bf16[2,2,256,256]{3,2,1,0:T(8,128)(2,1)S(1)} %get-tuple-element.33), channel_id=1, source_target_pairs={{0,2},{2,0},{4,6},{6,4},{8,10},{10,8},{12,14},{14,12},{16,18},{18,... | collective-permute-start | bytes 1572872 | tf_op jit(solution)/shard_map/ppermute | solution.py:550
  2.0 16.1 %collective-permute-start = (bf16[2,2,256,256]{3,2,1,0:T(8,128)(2,1)S(1)}, bf16[2,2,256,256]{3,2,1,0:T(8,128)(2,1)S(1)}, u32[]{:S(2)}, u32[]{:S(2)}) collective-permute-start(bf16[2,2,256,256]{3,2,1,0:T(8,128)(2,1)S(1)} %get-tuple-element.27), channel_id=1, source_target_pairs={{2,4},{6,8},{10,12},{14,16},{18,20},{22,24},{26,28},{4,2},{8,6},{1... | collective-permute-start | bytes 1572872 | tf_op jit(solution)/shard_map/ppermute | solution.py:549
  8.7 9.5 %copy-start.1 = (bf16[2,2,256,256]{3,2,1,0:T(8,128)(2,1)S(1)}, bf16[2,2,256,256]{3,2,1,0:T(8,128)(2,1)}, u32[]{:S(2)}) copy-start(bf16[2,2,256,256]{3,2,1,0:T(8,128)(2,1)} %source.3) | copy-start | bytes 1572868
  10.6 10.5 %collective-permute-start.3 = (bf16[2,2,256,256]{3,2,1,0:T(8,128)(2,1)S(1)}, bf16[2,2,256,256]{3,2,1,0:T(8,128)(2,1)S(1)}, u32[]{:S(2)}, u32[]{:S(2)}) collective-permute-start(bf16[2,2,256,256]{3,2,1,0:T(8,128)(2,1)S(1)} %get-tuple-element.37), channel_id=1, source_target_pairs={{0,2},{2,0},{4,6},{6,4},{8,10},{10,8},{12,14},{14,12},{16,18},{18,... | collective-permute-start | bytes 1572872 | tf_op jit(solution)/shard_map/ppermute | solution.py:567
  19.2 13.1 %collective-permute-start.1 = (bf16[2,2,256,256]{3,2,1,0:T(8,128)(2,1)S(1)}, bf16[2,2,256,256]{3,2,1,0:T(8,128)(2,1)S(1)}, u32[]{:S(2)}, u32[]{:S(2)}) collective-permute-start(bf16[2,2,256,256]{3,2,1,0:T(8,128)(2,1)S(1)} %get-tuple-element.32), channel_id=1, source_target_pairs={{2,4},{6,8},{10,12},{14,16},{18,20},{22,24},{26,28},{4,2},{8,6},{1... | collective-permute-start | bytes 1572872 | tf_op jit(solution)/shard_map/ppermute | solution.py:571
  22.9 16.9 %collective-permute-start.6 = (bf16[2,2,256,256]{3,2,1,0:T(8,128)(2,1)S(1)}, bf16[2,2,256,256]{3,2,1,0:T(8,128)(2,1)S(1)}, u32[]{:S(2)}, u32[]{:S(2)}) collective-permute-start(bf16[2,2,256,256]{3,2,1,0:T(8,128)(2,1)S(1)} %get-tuple-element.42), channel_id=1, source_target_pairs={{0,2},{2,0},{4,6},{6,4},{8,10},{10,8},{12,14},{14,12},{16,18},{18,... | collective-permute-start | bytes 1572872 | tf_op jit(solution)/shard_map/ppermute | solution.py:575
  34.1 9.1 %collective-permute-start.5 = (bf16[2,2,128,256]{3,2,1,0:T(8,128)(2,1)S(1)}, bf16[2,2,128,256]{3,2,1,0:T(8,128)(2,1)S(1)}, u32[]{:S(2)}, u32[]{:S(2)}) collective-permute-start(bf16[2,2,128,256]{3,2,1,0:T(8,128)(2,1)S(1)} %get-tuple-element.40), channel_id=1, source_target_pairs={{2,4},{6,8},{10,12},{14,16},{18,20},{22,24},{26,28},{4,2},{8,6},{1... | collective-permute-start | bytes 786440 | tf_op jit(solution)/shard_map/ppermute | solution.py:584
  36.0 9.8 %collective-permute-start.4 = (bf16[2,2,128,256]{3,2,1,0:T(8,128)(2,1)S(1)}, bf16[2,2,128,256]{3,2,1,0:T(8,128)(2,1)S(1)}, u32[]{:S(2)}, u32[]{:S(2)}) collective-permute-start(bf16[2,2,128,256]{3,2,1,0:T(8,128)(2,1)S(1)} %get-tuple-element.39), channel_id=1, source_target_pairs={{2,4},{6,8},{10,12},{14,16},{18,20},{22,24},{26,28},{4,2},{8,6},{1... | collective-permute-start | bytes 786440 | tf_op jit(solution)/shard_map/ppermute | solution.py:585
  41.7 4.3 %collective-permute-start.7 = (bf16[128,256]{1,0:T(8,128)(2,1)S(1)}, bf16[128,256]{1,0:T(8,128)(2,1)S(1)}, u32[]{:S(2)}, u32[]{:S(2)}) collective-permute-start(bf16[128,256]{1,0:T(8,128)(2,1)S(1)} %get-tuple-element.46), channel_id=1, source_target_pairs={{0,1},{1,0},{2,3},{3,2},{4,5},{5,4},{6,7},{7,6},{8,9},{9,8},{10,11... | collective-permute-start | bytes 196616 | tf_op jit(solution)/shard_map/ppermute | solution.py:594
  43.3 4.3 %collective-permute-start.8 = (bf16[128,256]{1,0:T(8,128)(2,1)S(1)}, bf16[128,256]{1,0:T(8,128)(2,1)S(1)}, u32[]{:S(2)}, u32[]{:S(2)}) collective-permute-start(bf16[128,256]{1,0:T(8,128)(2,1)S(1)} %shard_map.121), channel_id=1, source_target_pairs={{0,1},{1,0},{2,3},{3,2},{4,5},{5,4},{6,7},{7,6},{8,9},{9,8},{10,11... | collective-permute-start | bytes 196616 | tf_op jit(solution)/shard_map/ppermute | solution.py:598

commit v11 on v10

--- a/solution.py
+++ b/solution.py
@@ -201,6 +201,16 @@
     return pl.ds(pl.multiple_of((shot if of == 0 else 1 - shot) * half, half), half)
 
 
+def late_pair():
+    return lax.rem(lax.div(lax.axis_index("depth") + 1, 2), 2) == 1
+
+
+def by_turn(early, late):
+    is_late = late_pair()
+    pl.when(jnp.logical_not(is_late))(early)
+    pl.when(is_late)(late)
+
+
 def edges_kernel(down, up, outward_outer, inward_inner, sems):
     levels = down.shape[0]
     odd = odd_place()
@@ -345,10 +355,18 @@
         )
 
 
-def edge_kernel(arrived, source, q_out_inner, screen, refl, phase, hx, hy, outward, q_arrived, work):
+def edge_kernel(arrived, source, q_out_inner, screen, refl, phase, hx, hy, sent, q_arrived, field, work):
     everyone = range(arrived.shape[0])
     spread([(entering(arrived, source, front), front, q_arrived.at[front]) for front in everyone], work, hx, hy, phase)
-    outer_step(q_arrived, q_out_inner, screen, refl, "outward", outward)
+
+    def early():
+        outer_step(q_arrived, q_out_inner, screen, refl, "outward", sent)
+
+    def late():
+        outer_step(q_arrived, q_out_inner, screen, refl, "outward", field)
+        spread([(field.at[front], front, sent.at[front]) for front in everyone], work, hx, hy, phase)
+
+    by_turn(early, late)
 
 
 def last_edge_kernel(
@@ -359,7 +377,15 @@
     del after
     everyone = range(arrived.shape[0])
     half = arrived.shape[2] // 2
-    spread([(entering(arrived, source, front), front, q_arrived.at[front]) for front in everyone], work, hx, hy, phase)
+
+    def early():
+        jobs = [(entering(arrived, source, front), front, q_arrived.at[front]) for front in everyone]
+        spread(jobs, work, hx, hy, phase)
+
+    def late():
+        q_arrived[...] = arrived[...]
+
+    by_turn(early, late)
     outer_step(q_arrived, q_out_inner, screen, refl, "outward", outward)
     jobs = [
         (outward.at[front], front, [(half_rows(1, half), last_far.at[front]), (half_rows(0, half), last_near.at[front])])
@@ -565,7 +591,7 @@
         partner_0, q_in_outer_0, *fixed
     )
     partner_1 = to_partner(in_inner_1)
-    out_outer_1, q_arrived = call(edge_kernel, [VMEM] * 8, [VMEM] * 2, [plane] * 2, [work(fronts)])(
+    out_outer_1, q_arrived = call(edge_kernel, [VMEM] * 8, [VMEM] * 2, [plane] * 2, buffers(1) + [work(fronts)])(
         arrived_0, source, q_out_inner_0, *fixed
     )
     arrived_1 = to_beyond(out_outer_1)

time: 48.9 us -> 49 us (level)
    pallas_call x1, Pallas kernels: 1.05 us -> 1.87 us  [per_device(): call(edge_kernel, [VMEM] * 8, [VMEM] * 2, [plane] * 2, buffers(1) + [work...]
    ppermute x1, waiting for transfers between devices: 0.01 us -> 0.79 us  [per_device(): last_far = to_beyond(last_far)]
    ppermute x1, waiting for transfers between devices: 8.38 us -> 7.7 us  [per_device(): arrived_1 = to_beyond(out_outer_1)]
    pallas_call x1, Pallas kernels: 1.82 us -> 1.13 us  [per_device(): call(last_edge_kernel, [VMEM] * 8 + [pl.BlockSpec(memory_space=pl.ANY)],...]
where the time goes in v11:
time: 49 us; the launch traced here: 48.7 us
  Pallas kernels  17.5 us (36%)
  waiting for transfers between devices  15.7 us (32%)
  starting transfers between devices  14.5 us (30%)
  between operations  0.99 us (2%)
    ppermute x1, waiting for transfers between devices, per_device(): arrived_1 = to_beyond(out_outer_1)  7.7 us
    ppermute x1, waiting for transfers between devices, per_device(): arrived_0 = to_beyond(out_outer)  5.82 us
    pallas_call x1, Pallas kernels, per_device(): call(setup_kernel, [HBM] * 4 + [SMEM] * 2 + [VMEM] * 2, [VMEM] * 5, [plan...  4.65 us
    ppermute x1, starting transfers between devices, per_device(): last_near = to_beyond(last_near)  3.82 us
    pallas_call x1, Pallas kernels, per_device(): call(ahead_kernel, [VMEM] * 7, [VMEM] * 2, [plane] * 2, buffers(2) + [wor...  1.96 us
    ppermute x1, starting transfers between devices, per_device(): arrived_0 = to_beyond(out_outer)  1.92 us
    ppermute x1, starting transfers between devices, per_device(): arrived_1 = to_beyond(out_outer_1)  1.92 us
    ppermute x1, starting transfers between devices, per_device(): last_far = to_beyond(last_far)  1.92 us
  transfers between devices with their start and end apart: 9, of which 5 were waited for; matrix products, arithmetic and copies ran while one was open for 0% of the time, Pallas kernels for 32%

profile of v11, /device:TPU:4, one launch (start us, length us, event | category | flops | bytes accessed | tf_op | source)
XLA Modules:
  0.0 48.7 jit_solution(2687760663919282923)
XLA Ops:
  0.6 0.0 copy-start
  0.6 0.0 copy-start.3
  0.7 1.3 %shard_map.112 = (bf16[2,2,256,256]{3,2,1,0:T(8,128)(2,1)S(1)}, bf16[2,2,256,256]{3,2,1,0:T(8,128)(2,1)S(1)}) custom-call(bf16[2,2,2,256,256]{4,3,2,1,0:T(8,128)(2,1)} %down.3, bf16[2,2,2,256,256]{4,3,2,1,0:T(8,128)(2,1)} %up.3), custom_call_target="tpu_custom_call" | custom-call | tf_op jit(solution)/shard_map/pallas_call | solution.py:572
  2.0 0.1 collective-permute-start.2
  2.0 1.9 %collective-permute-start = (bf16[2,2,256,256]{3,2,1,0:T(8,128)(2,1)S(1)}, bf16[2,2,256,256]{3,2,1,0:T(8,128)(2,1)S(1)}, u32[]{:S(2)}, u32[]{:S(2)}) collective-permute-start(bf16[2,2,256,256]{3,2,1,0:T(8,128)(2,1)S(1)} %get-tuple-element.27), channel_id=1, source_target_pairs={{2,4},{6,8},{10,12},{14,16},{18,20},{22,24},{26,28},{4,2},{8,6},{1... | collective-permute-start | bytes 1572872 | tf_op jit(solution)/shard_map/ppermute | solution.py:575
  4.0 4.7 %shard_map.113 = (bf16[2,2,256,256]{3,2,1,0:T(8,128)(2,1)S(1)}, bf16[2,2,256,256]{3,2,1,0:T(8,128)(2,1)S(1)}, f32[2,2,2,256,256]{4,3,2,1,0:T(8,128)S(1)}, f32[2,...) custom-call(bf16[2,2,2,256,256]{4,3,2,1,0:T(8,128)(2,1)} %down.3, bf16[2,2,2,256,256]{4,3,2,1,0:T(8,128)(2,1)} %up.3, ...), custom_call_target="tpu_custom_call" | custom-call | tf_op jit(solution)/shard_map/pallas_call | solution.py:577
  8.6 0.0 collective-permute-done.2.partner
  8.7 0.0 copy-start.1
  8.7 2.0 %shard_map.115 = (bf16[2,2,256,256]{3,2,1,0:T(8,128)(2,1)S(1)}, bf16[2,2,256,256]{3,2,1,0:T(8,128)(2,1)S(1)}) custom-call(bf16[2,2,256,256]{3,2,1,0:T(8,128)(2,1)S(1)} %collective-permute-done.2.partner, bf16[2,2,256,256]{3,2,1,0:T(8,128)(2,1)S(1)} %get-tuple-element.34.q_in_outer, f32[2,2,2,256,256]{4,3,2,1,0:T(8,128)S(1)} %get-tuple-element.29.screen, ...), custom_call_target="tpu_custom_call" | custom-call | tf_op jit(solution)/shard_map/pallas_call | solution.py:590
  10.6 1.7 %collective-permute-start.3 = (bf16[2,2,256,256]{3,2,1,0:T(8,128)(2,1)S(1)}, bf16[2,2,256,256]{3,2,1,0:T(8,128)(2,1)S(1)}, u32[]{:S(2)}, u32[]{:S(2)}) collective-permute-start(bf16[2,2,256,256]{3,2,1,0:T(8,128)(2,1)S(1)} %get-tuple-element.37), channel_id=1, source_target_pairs={{0,2},{2,0},{4,6},{6,4},{8,10},{10,8},{12,14},{14,12},{16,18},{18,... | collective-permute-start | bytes 1572872 | tf_op jit(solution)/shard_map/ppermute | solution.py:593
  12.3 5.8 %collective-permute-done.arrived = bf16[2,2,256,256]{3,2,1,0:T(8,128)(2,1)S(1)} collective-permute-done((bf16[2,2,256,256]{3,2,1,0:T(8,128)(2,1)S(1)}, bf16[2,2,256,256]{3,2,1,0:T(8,128)(2,1)S(1)}, u32[]{:S(2)}, u32[]{:S(2)}) %collective-permute-start) | collective-permute-done | bytes 524320 | tf_op jit(solution)/shard_map/ppermute | solution.py:575
  18.2 1.9 %shard_map.114 = (bf16[2,2,256,256]{3,2,1,0:T(8,128)(2,1)S(1)}, bf16[2,2,256,256]{3,2,1,0:T(8,128)(2,1)S(1)}) custom-call(bf16[2,2,256,256]{3,2,1,0:T(8,128)(2,1)S(1)} %collective-permute-done.arrived, bf16[2,2,256,256]{3,2,1,0:T(8,128)(2,1)S(1)} %copy-done.1, bf16[2,2,256,256]{3,2,1,0:T(8,128)(2,1)S(1)} %get-tuple-element.28.q_out_inner, ...), custom_call_target="tpu_custom_call" | custom-call | tf_op jit(solution)/shard_map/pallas_call | solution.py:594
  20.0 1.9 %collective-permute-start.1 = (bf16[2,2,256,256]{3,2,1,0:T(8,128)(2,1)S(1)}, bf16[2,2,256,256]{3,2,1,0:T(8,128)(2,1)S(1)}, u32[]{:S(2)}, u32[]{:S(2)}) collective-permute-start(bf16[2,2,256,256]{3,2,1,0:T(8,128)(2,1)S(1)} %get-tuple-element.32), channel_id=1, source_target_pairs={{2,4},{6,8},{10,12},{14,16},{18,20},{22,24},{26,28},{4,2},{8,6},{1... | collective-permute-start | bytes 1572872 | tf_op jit(solution)/shard_map/ppermute | solution.py:597
  22.0 0.0 collective-permute-done.3.partner
  22.0 1.8 %shard_map.116 = (bf16[2,2,256,256]{3,2,1,0:T(8,128)(2,1)S(1)}, bf16[2,2,256,256]{3,2,1,0:T(8,128)(2,1)S(1)}) custom-call(bf16[2,2,256,256]{3,2,1,0:T(8,128)(2,1)S(1)} %get-tuple-element.36.q_arrived, bf16[2,2,256,256]{3,2,1,0:T(8,128)(2,1)S(1)} %get-tuple-element.28.q_out_inner, bf16[2,2,256,256]{3,2,1,0:T(8,128)(2,1)S(1)} %collective-permute-done.3.partner, ...), custom_call_target="tpu_custom_call" | custom-call | tf_op jit(solution)/shard_map/pallas_call | solution.py:598
  23.8 0.1 collective-permute-start.6
  23.8 0.9 %shard_map.117.after.q_out_inner = bf16[2,2,256,256]{3,2,1,0:T(8,128)(2,1)S(1)} custom-call(bf16[2,2,256,256]{3,2,1,0:T(8,128)(2,1)S(1)} %get-tuple-element.38.fields, f32[2,2,256,256]{3,2,1,0:T(8,128)S(1)} %get-tuple-element.31.phase, bf16[256,256]{1,0:T(8,128)(2,1)S(1)} %copy-done, bf16[256,256]{1,0:T(8,128)(2,1)S(1)} %copy-done), custom_call_target="tpu_custom_call" | custom-call | tf_op jit(solution)/shard_map/pallas_call | solution.py:602
  24.7 7.7 %collective-permute-done.1.arrived = bf16[2,2,256,256]{3,2,1,0:T(8,128)(2,1)S(1)} collective-permute-done((bf16[2,2,256,256]{3,2,1,0:T(8,128)(2,1)S(1)}, bf16[2,2,256,256]{3,2,1,0:T(8,128)(2,1)S(1)}, u32[]{:S(2)}, u32[]{:S(2)}) %collective-permute-start.1) | collective-permute-done | bytes 524320 | tf_op jit(solution)/shard_map/ppermute | solution.py:597
  32.4 1.1 %shard_map.118 = (bf16[2,2,256,256]{3,2,1,0:T(8,128)(2,1)S(1)}, bf16[2,2,128,256]{3,2,1,0:T(8,128)(2,1)S(1)}, bf16[2,2,128,256]{3,2,1,0:T(8,128)(2,1)S(1)}) custom-call(bf16[2,2,256,256]{3,2,1,0:T(8,128)(2,1)S(1)} %collective-permute-done.1.arrived, bf16[2,2,256,256]{3,2,1,0:T(8,128)(2,1)S(1)} %copy-done.1, ...), custom_call_target="tpu_custom_call" | custom-call | tf_op jit(solution)/shard_map/pallas_call | solution.py:603
  33.5 1.9 %collective-permute-start.5 = (bf16[2,2,128,256]{3,2,1,0:T(8,128)(2,1)S(1)}, bf16[2,2,128,256]{3,2,1,0:T(8,128)(2,1)S(1)}, u32[]{:S(2)}, u32[]{:S(2)}) collective-permute-start(bf16[2,2,128,256]{3,2,1,0:T(8,128)(2,1)S(1)} %get-tuple-element.40), channel_id=1, source_target_pairs={{2,4},{6,8},{10,12},{14,16},{18,20},{22,24},{26,28},{4,2},{8,6},{1... | collective-permute-start | bytes 786440 | tf_op jit(solution)/shard_map/ppermute | solution.py:610
  35.5 3.8 %collective-permute-start.4 = (bf16[2,2,128,256]{3,2,1,0:T(8,128)(2,1)S(1)}, bf16[2,2,128,256]{3,2,1,0:T(8,128)(2,1)S(1)}, u32[]{:S(2)}, u32[]{:S(2)}) collective-permute-start(bf16[2,2,128,256]{3,2,1,0:T(8,128)(2,1)S(1)} %get-tuple-element.39), channel_id=1, source_target_pairs={{2,4},{6,8},{10,12},{14,16},{18,20},{22,24},{26,28},{4,2},{8,6},{1... | collective-permute-start | bytes 786440 | tf_op jit(solution)/shard_map/ppermute | solution.py:611
  39.3 0.0 collective-permute-done.6.partner
  39.3 1.8 %shard_map.119 = (bf16[2,2,256,256]{3,2,1,0:T(8,128)(2,1)S(1)}, bf16[2,2,256,256]{3,2,1,0:T(8,128)(2,1)S(1)}, f32[256,256]{1,0:T(8,128)S(1)}, bf16[128,256]{1,0:T(8,128)(2,1)S(1)}) custom-call(bf16[2,2,256,256]{3,2,1,0:T(8,128)(2,1)S(1)} %get-tuple-element.41.q_arrived, bf16[2,2,256,256]{3,2,1,0:T(8,128)(2,1)S(1)} %get-tuple-element.35.q_out_inner, ...), custom_call_target="tpu_custom_call" | custom-call | tf_op jit(solution)/shard_map/pallas_call | solution.py:613
  41.1 1.5 %collective-permute-start.7 = (bf16[128,256]{1,0:T(8,128)(2,1)S(1)}, bf16[128,256]{1,0:T(8,128)(2,1)S(1)}, u32[]{:S(2)}, u32[]{:S(2)}) collective-permute-start(bf16[128,256]{1,0:T(8,128)(2,1)S(1)} %get-tuple-element.46), channel_id=1, source_target_pairs={{0,1},{1,0},{2,3},{3,2},{4,5},{5,4},{6,7},{7,6},{8,9},{9,8},{10,11... | collective-permute-start | bytes 196616 | tf_op jit(solution)/shard_map/ppermute | solution.py:620
  42.7 0.8 %collective-permute-done.5.far.last = bf16[2,2,128,256]{3,2,1,0:T(8,128)(2,1)S(1)} collective-permute-done((bf16[2,2,128,256]{3,2,1,0:T(8,128)(2,1)S(1)}, bf16[2,2,128,256]{3,2,1,0:T(8,128)(2,1)S(1)}, u32[]{:S(2)}, u32[]{:S(2)}) %collective-permute-start.5) | collective-permute-done | bytes 262176 | tf_op jit(solution)/shard_map/ppermute | solution.py:610
  43.5 0.1 shard_map.121
  43.6 1.6 %collective-permute-start.8 = (bf16[128,256]{1,0:T(8,128)(2,1)S(1)}, bf16[128,256]{1,0:T(8,128)(2,1)S(1)}, u32[]{:S(2)}, u32[]{:S(2)}) collective-permute-start(bf16[128,256]{1,0:T(8,128)(2,1)S(1)} %shard_map.121), channel_id=1, source_target_pairs={{0,1},{1,0},{2,3},{3,2},{4,5},{5,4},{6,7},{7,6},{8,9},{9,8},{10,11... | collective-permute-start | bytes 196616 | tf_op jit(solution)/shard_map/ppermute | solution.py:624
  45.1 1.2 %collective-permute-done.4.near = bf16[2,2,128,256]{3,2,1,0:T(8,128)(2,1)S(1)} collective-permute-done((bf16[2,2,128,256]{3,2,1,0:T(8,128)(2,1)S(1)}, bf16[2,2,128,256]{3,2,1,0:T(8,128)(2,1)S(1)}, u32[]{:S(2)}, u32[]{:S(2)}) %collective-permute-start.4) | collective-permute-done | bytes 262176 | tf_op jit(solution)/shard_map/ppermute | solution.py:611
  46.3 0.0 collective-permute-done.7.inner_other
  46.3 1.4 %shard_map.120 = (bf16[2,2,2,256,256]{4,3,2,1,0:T(8,128)(2,1)}, bf16[2,2,2,256,256]{4,3,2,1,0:T(8,128)(2,1)}, f32[2,128,256]{2,1,0:T(8,128)}, f32[128,256]{1,0:T(8,128)S(1)}) custom-call(bf16[2,2,128,256]{3,2,1,0:T(8,128)(2,1)S(1)} %collective-permute-done.4.near, bf16[2,2,128,256]{3,2,1,0:T(8,128)(2,1)S(1)} %collective-permute-done.5.far.last, ...), custom_call_target="tpu_custom_call" | custom-call | tf_op jit(solution)/shard_map/pallas_call | solution.py:627
  47.7 0.2 collective-permute-done.8.other
  47.9 0.7 %shard_map.122 = f32[2,128,256]{2,1,0:T(8,128)} custom-call(f32[128,256]{1,0:T(8,128)S(1)} %get-tuple-element.49.terms, bf16[128,256]{1,0:T(8,128)(2,1)S(1)} %collective-permute-done.8.other, f32[2,128,256]{2,1,0:T(8,128)} %get-tuple-element.50.gradient_in), custom_call_target="tpu_custom_call", output_to_operand_aliasing={{}: (2, {})} | custom-call | tf_op jit(solution)/shard_map/pallas_call | solution.py:636
  (5 shorter events, 0.0 us)
Async XLA Ops:
  0.6 3.3 %copy-start = (bf16[256,256]{1,0:T(8,128)(2,1)S(1)}, bf16[256,256]{1,0:T(8,128)(2,1)}, u32[]{:S(2)}) copy-start(bf16[256,256]{1,0:T(8,128)(2,1)} %constant.2.clone.hx.hy) | copy-start | bytes 393220
  0.6 3.3 %copy-start.3 = (s32[2]{0:T(128)S(1)}, s32[2]{0:T(128)}, u32[]{:S(2)}) copy-start(s32[2]{0:T(128)} %freq.1) | copy-start | bytes 28
  0.7 3.3 %copy-start.2 = (f32[16]{0:T(128)S(1)}, f32[16]{0:T(128)}, u32[]{:S(2)}) copy-start(f32[16]{0:T(128)} %slowness.1) | copy-start | bytes 196
  2.0 6.7 %collective-permute-start.2 = (bf16[2,2,256,256]{3,2,1,0:T(8,128)(2,1)S(1)}, bf16[2,2,256,256]{3,2,1,0:T(8,128)(2,1)S(1)}, u32[]{:S(2)}, u32[]{:S(2)}) collective-permute-start(bf16[2,2,256,256]{3,2,1,0:T(8,128)(2,1)S(1)} %get-tuple-element.33), channel_id=1, source_target_pairs={{0,2},{2,0},{4,6},{6,4},{8,10},{10,8},{12,14},{14,12},{16,18},{18,... | collective-permute-start | bytes 1572872 | tf_op jit(solution)/shard_map/ppermute | solution.py:576
  2.0 16.1 %collective-permute-start = (bf16[2,2,256,256]{3,2,1,0:T(8,128)(2,1)S(1)}, bf16[2,2,256,256]{3,2,1,0:T(8,128)(2,1)S(1)}, u32[]{:S(2)}, u32[]{:S(2)}) collective-permute-start(bf16[2,2,256,256]{3,2,1,0:T(8,128)(2,1)S(1)} %get-tuple-element.27), channel_id=1, source_target_pairs={{2,4},{6,8},{10,12},{14,16},{18,20},{22,24},{26,28},{4,2},{8,6},{1... | collective-permute-start | bytes 1572872 | tf_op jit(solution)/shard_map/ppermute | solution.py:575
  8.7 9.5 %copy-start.1 = (bf16[2,2,256,256]{3,2,1,0:T(8,128)(2,1)S(1)}, bf16[2,2,256,256]{3,2,1,0:T(8,128)(2,1)}, u32[]{:S(2)}) copy-start(bf16[2,2,256,256]{3,2,1,0:T(8,128)(2,1)} %source.3) | copy-start | bytes 1572868
  10.6 11.3 %collective-permute-start.3 = (bf16[2,2,256,256]{3,2,1,0:T(8,128)(2,1)S(1)}, bf16[2,2,256,256]{3,2,1,0:T(8,128)(2,1)S(1)}, u32[]{:S(2)}, u32[]{:S(2)}) collective-permute-start(bf16[2,2,256,256]{3,2,1,0:T(8,128)(2,1)S(1)} %get-tuple-element.37), channel_id=1, source_target_pairs={{0,2},{2,0},{4,6},{6,4},{8,10},{10,8},{12,14},{14,12},{16,18},{18,... | collective-permute-start | bytes 1572872 | tf_op jit(solution)/shard_map/ppermute | solution.py:593
  20.0 12.4 %collective-permute-start.1 = (bf16[2,2,256,256]{3,2,1,0:T(8,128)(2,1)S(1)}, bf16[2,2,256,256]{3,2,1,0:T(8,128)(2,1)S(1)}, u32[]{:S(2)}, u32[]{:S(2)}) collective-permute-start(bf16[2,2,256,256]{3,2,1,0:T(8,128)(2,1)S(1)} %get-tuple-element.32), channel_id=1, source_target_pairs={{2,4},{6,8},{10,12},{14,16},{18,20},{22,24},{26,28},{4,2},{8,6},{1... | collective-permute-start | bytes 1572872 | tf_op jit(solution)/shard_map/ppermute | solution.py:597
  23.8 15.5 %collective-permute-start.6 = (bf16[2,2,256,256]{3,2,1,0:T(8,128)(2,1)S(1)}, bf16[2,2,256,256]{3,2,1,0:T(8,128)(2,1)S(1)}, u32[]{:S(2)}, u32[]{:S(2)}) collective-permute-start(bf16[2,2,256,256]{3,2,1,0:T(8,128)(2,1)S(1)} %get-tuple-element.42), channel_id=1, source_target_pairs={{0,2},{2,0},{4,6},{6,4},{8,10},{10,8},{12,14},{14,12},{16,18},{18,... | collective-permute-start | bytes 1572872 | tf_op jit(solution)/shard_map/ppermute | solution.py:601
  33.5 9.9 %collective-permute-start.5 = (bf16[2,2,128,256]{3,2,1,0:T(8,128)(2,1)S(1)}, bf16[2,2,128,256]{3,2,1,0:T(8,128)(2,1)S(1)}, u32[]{:S(2)}, u32[]{:S(2)}) collective-permute-start(bf16[2,2,128,256]{3,2,1,0:T(8,128)(2,1)S(1)} %get-tuple-element.40), channel_id=1, source_target_pairs={{2,4},{6,8},{10,12},{14,16},{18,20},{22,24},{26,28},{4,2},{8,6},{1... | collective-permute-start | bytes 786440 | tf_op jit(solution)/shard_map/ppermute | solution.py:610
  35.5 10.8 %collective-permute-start.4 = (bf16[2,2,128,256]{3,2,1,0:T(8,128)(2,1)S(1)}, bf16[2,2,128,256]{3,2,1,0:T(8,128)(2,1)S(1)}, u32[]{:S(2)}, u32[]{:S(2)}) collective-permute-start(bf16[2,2,128,256]{3,2,1,0:T(8,128)(2,1)S(1)} %get-tuple-element.39), channel_id=1, source_target_pairs={{2,4},{6,8},{10,12},{14,16},{18,20},{22,24},{26,28},{4,2},{8,6},{1... | collective-permute-start | bytes 786440 | tf_op jit(solution)/shard_map/ppermute | solution.py:611
  41.1 5.1 %collective-permute-start.7 = (bf16[128,256]{1,0:T(8,128)(2,1)S(1)}, bf16[128,256]{1,0:T(8,128)(2,1)S(1)}, u32[]{:S(2)}, u32[]{:S(2)}) collective-permute-start(bf16[128,256]{1,0:T(8,128)(2,1)S(1)} %get-tuple-element.46), channel_id=1, source_target_pairs={{0,1},{1,0},{2,3},{3,2},{4,5},{5,4},{6,7},{7,6},{8,9},{9,8},{10,11... | collective-permute-start | bytes 196616 | tf_op jit(solution)/shard_map/ppermute | solution.py:620
  43.6 4.3 %collective-permute-start.8 = (bf16[128,256]{1,0:T(8,128)(2,1)S(1)}, bf16[128,256]{1,0:T(8,128)(2,1)S(1)}, u32[]{:S(2)}, u32[]{:S(2)}) collective-permute-start(bf16[128,256]{1,0:T(8,128)(2,1)S(1)} %shard_map.121), channel_id=1, source_target_pairs={{0,1},{1,0},{2,3},{3,2},{4,5},{5,4},{6,7},{7,6},{8,9},{9,8},{10,11... | collective-permute-start | bytes 196616 | tf_op jit(solution)/shard_map/ppermute | solution.py:624

commit v12 on v11

--- a/solution.py
+++ b/solution.py
@@ -357,13 +357,17 @@
 
 def edge_kernel(arrived, source, q_out_inner, screen, refl, phase, hx, hy, sent, q_arrived, field, work):
     everyone = range(arrived.shape[0])
-    spread([(entering(arrived, source, front), front, q_arrived.at[front]) for front in everyone], work, hx, hy, phase)
+
+    def step(target):
+        jobs = [(entering(arrived, source, front), front, q_arrived.at[front]) for front in everyone]
+        spread(jobs, work, hx, hy, phase)
+        outer_step(q_arrived, q_out_inner, screen, refl, "outward", target)
 
     def early():
-        outer_step(q_arrived, q_out_inner, screen, refl, "outward", sent)
+        step(sent)
 
     def late():
-        outer_step(q_arrived, q_out_inner, screen, refl, "outward", field)
+        step(field)
         spread([(field.at[front], front, sent.at[front]) for front in everyone], work, hx, hy, phase)
 
     by_turn(early, late)
@@ -378,20 +382,24 @@
     everyone = range(arrived.shape[0])
     half = arrived.shape[2] // 2
 
+    def step():
+        outer_step(q_arrived, q_out_inner, screen, refl, "outward", outward)
+        jobs = [
+            (outward.at[front], front, [(half_rows(1, half), last_far.at[front]), (half_rows(0, half), last_near.at[front])])
+            for front in everyone
+        ]
+        spread(jobs, work, hx, hy, phase)
+
     def early():
         jobs = [(entering(arrived, source, front), front, q_arrived.at[front]) for front in everyone]
         spread(jobs, work, hx, hy, phase)
+        step()
 
     def late():
         q_arrived[...] = arrived[...]
+        step()
 
     by_turn(early, late)
-    outer_step(q_arrived, q_out_inner, screen, refl, "outward", outward)
-    jobs = [
-        (outward.at[front], front, [(half_rows(1, half), last_far.at[front]), (half_rows(0, half), last_near.at[front])])
-        for front in everyone
-    ]
-    spread(jobs, work, hx, hy, phase)
 
 
 def inner_kernel(
@@ -414,16 +422,24 @@
 
 
 def spread_kernel(fields, phase, hx, hy, q_fields, work):
-    everyone = range(fields.shape[0])
-    spread([(fields.at[front], front, q_fields.at[front]) for front in everyone], work, hx, hy, phase)
+    @pl.when(late_pair())
+    def _():
+        everyone = range(fields.shape[0])
+        spread([(fields.at[front], front, q_fields.at[front]) for front in everyone], work, hx, hy, phase)
 
 
 def last_inner_kernel(
-    q_arrived, q_out_inner, partner, screen, refl, phase, hx, hy,
-    inward, outward, terms, far_terms,
+    q_arrived, q_out_inner, partner, screen, refl, phase, hx, hy, out_inner, q_next_in,
+    inward, outward, terms, far_terms, q_next,
     field, q_inward, q_partner, work,
 ):
+    del q_next_in
     everyone = range(partner.shape[0])
+
+    @pl.when(jnp.logical_not(late_pair()))
+    def _():
+        spread([(out_inner.at[front], front, q_next.at[front]) for front in everyone], work, hx, hy, phase)
+
     outer_step(q_arrived, q_out_inner, screen, refl, "inward", field)
     jobs = [(partner.at[front], front, q_partner.at[front]) for front in everyone]
     jobs += [(field.at[front], front, q_inward.at[front]) for front in everyone]
@@ -610,13 +626,14 @@
     last_far = to_beyond(last_far)
     last_near = to_beyond(last_near)
     half_sum = jax.ShapeDtypeStruct((half, rows_y), BF16)
-    inner_in, inner_out, inner_terms, inner_far = call(
+    inner_in, inner_out, inner_terms, inner_far, q_out_inner_2 = call(
         last_inner_kernel,
-        [VMEM] * 8,
-        [VMEM] * 4,
-        [plane] * 2 + [jax.ShapeDtypeStruct((rows_x, rows_y), F32), half_sum],
+        [VMEM] * 10,
+        [VMEM] * 5,
+        [plane] * 2 + [jax.ShapeDtypeStruct((rows_x, rows_y), F32), half_sum, plane],
         buffers(3) + [work(2 * fronts)],
-    )(q_arrived_1, q_out_inner_1, partner_2, *fixed)
+        input_output_aliases={9: 4},
+    )(q_arrived_1, q_out_inner_1, partner_2, *fixed, out_inner_2, q_out_inner_2)
     inner_other = across(inner_far) if shots == 2 else jnp.zeros_like(inner_far)
     outer_far = call(far_terms_kernel, [VMEM] * 3 + [pl.BlockSpec(memory_space=pl.ANY)], VMEM, half_sum)(
         last_far, q_arrived, q_out_inner_2, inner_terms

time: 49 us -> 48.7 us (level)
  no operation moved by 1% of the time
where the time goes in v12:
time: 48.7 us; the launch traced here: 48.5 us
  Pallas kernels  17.4 us (36%)
  waiting for transfers between devices  15.7 us (32%)
  starting transfers between devices  14.3 us (29%)
  between operations  0.99 us (2%)
    ppermute x1, waiting for transfers between devices, per_device(): arrived_1 = to_beyond(out_outer_1)  7.67 us
    ppermute x1, waiting for transfers between devices, per_device(): arrived_0 = to_beyond(out_outer)  5.84 us
    pallas_call x1, Pallas kernels, per_device(): call(setup_kernel, [HBM] * 4 + [SMEM] * 2 + [VMEM] * 2, [VMEM] * 5, [plan...  4.65 us
    ppermute x1, starting transfers between devices, per_device(): last_near = to_beyond(last_near)  3.64 us
    pallas_call x1, Pallas kernels, per_device(): call(ahead_kernel, [VMEM] * 7, [VMEM] * 2, [plane] * 2, buffers(2) + [wor...  1.94 us
    ppermute x1, starting transfers between devices, per_device(): arrived_1 = to_beyond(out_outer_1)  1.92 us
    ppermute x1, starting transfers between devices, per_device(): last_far = to_beyond(last_far)  1.92 us
    ppermute x1, starting transfers between devices, per_device(): arrived_0 = to_beyond(out_outer)  1.92 us
  transfers between devices with their start and end apart: 9, of which 5 were waited for; matrix products, arithmetic and copies ran while one was open for 0% of the time, Pallas kernels for 32%

profile of v12, /device:TPU:4, one launch (start us, length us, event | category | flops | bytes accessed | tf_op | source)
XLA Modules:
  0.0 48.5 jit_solution(9406727449641841396)
XLA Ops:
  0.6 0.0 copy-start
  0.6 0.0 copy-start.3
  0.7 1.3 %shard_map.112 = (bf16[2,2,256,256]{3,2,1,0:T(8,128)(2,1)S(1)}, bf16[2,2,256,256]{3,2,1,0:T(8,128)(2,1)S(1)}) custom-call(bf16[2,2,2,256,256]{4,3,2,1,0:T(8,128)(2,1)} %down.3, bf16[2,2,2,256,256]{4,3,2,1,0:T(8,128)(2,1)} %up.3), custom_call_target="tpu_custom_call" | custom-call | tf_op jit(solution)/shard_map/pallas_call | solution.py:588
  2.0 0.1 collective-permute-start.2
  2.0 1.9 %collective-permute-start = (bf16[2,2,256,256]{3,2,1,0:T(8,128)(2,1)S(1)}, bf16[2,2,256,256]{3,2,1,0:T(8,128)(2,1)S(1)}, u32[]{:S(2)}, u32[]{:S(2)}) collective-permute-start(bf16[2,2,256,256]{3,2,1,0:T(8,128)(2,1)S(1)} %get-tuple-element.28), channel_id=1, source_target_pairs={{2,4},{6,8},{10,12},{14,16},{18,20},{22,24},{26,28},{4,2},{8,6},{1... | collective-permute-start | bytes 1572872 | tf_op jit(solution)/shard_map/ppermute | solution.py:591
  4.0 4.7 %shard_map.113 = (bf16[2,2,256,256]{3,2,1,0:T(8,128)(2,1)S(1)}, bf16[2,2,256,256]{3,2,1,0:T(8,128)(2,1)S(1)}, f32[2,2,2,256,256]{4,3,2,1,0:T(8,128)S(1)}, f32[2,...) custom-call(bf16[2,2,2,256,256]{4,3,2,1,0:T(8,128)(2,1)} %down.3, bf16[2,2,2,256,256]{4,3,2,1,0:T(8,128)(2,1)} %up.3, ...), custom_call_target="tpu_custom_call" | custom-call | tf_op jit(solution)/shard_map/pallas_call | solution.py:593
  8.6 0.0 collective-permute-done.2.partner
  8.7 0.0 copy-start.1
  8.7 1.9 %shard_map.115 = (bf16[2,2,256,256]{3,2,1,0:T(8,128)(2,1)S(1)}, bf16[2,2,256,256]{3,2,1,0:T(8,128)(2,1)S(1)}) custom-call(bf16[2,2,256,256]{3,2,1,0:T(8,128)(2,1)S(1)} %collective-permute-done.2.partner, bf16[2,2,256,256]{3,2,1,0:T(8,128)(2,1)S(1)} %get-tuple-element.35.q_in_outer, f32[2,2,2,256,256]{4,3,2,1,0:T(8,128)S(1)} %get-tuple-element.30.screen, ...), custom_call_target="tpu_custom_call" | custom-call | tf_op jit(solution)/shard_map/pallas_call | solution.py:606
  10.6 1.7 %collective-permute-start.3 = (bf16[2,2,256,256]{3,2,1,0:T(8,128)(2,1)S(1)}, bf16[2,2,256,256]{3,2,1,0:T(8,128)(2,1)S(1)}, u32[]{:S(2)}, u32[]{:S(2)}) collective-permute-start(bf16[2,2,256,256]{3,2,1,0:T(8,128)(2,1)S(1)} %get-tuple-element.38), channel_id=1, source_target_pairs={{0,2},{2,0},{4,6},{6,4},{8,10},{10,8},{12,14},{14,12},{16,18},{18,... | collective-permute-start | bytes 1572872 | tf_op jit(solution)/shard_map/ppermute | solution.py:609
  12.3 5.8 %collective-permute-done.arrived = bf16[2,2,256,256]{3,2,1,0:T(8,128)(2,1)S(1)} collective-permute-done((bf16[2,2,256,256]{3,2,1,0:T(8,128)(2,1)S(1)}, bf16[2,2,256,256]{3,2,1,0:T(8,128)(2,1)S(1)}, u32[]{:S(2)}, u32[]{:S(2)}) %collective-permute-start) | collective-permute-done | bytes 524320 | tf_op jit(solution)/shard_map/ppermute | solution.py:591
  18.2 1.8 %shard_map.114 = (bf16[2,2,256,256]{3,2,1,0:T(8,128)(2,1)S(1)}, bf16[2,2,256,256]{3,2,1,0:T(8,128)(2,1)S(1)}) custom-call(bf16[2,2,256,256]{3,2,1,0:T(8,128)(2,1)S(1)} %collective-permute-done.arrived, bf16[2,2,256,256]{3,2,1,0:T(8,128)(2,1)S(1)} %copy-done.1, bf16[2,2,256,256]{3,2,1,0:T(8,128)(2,1)S(1)} %get-tuple-element.29.q_out_inner, ...), custom_call_target="tpu_custom_call" | custom-call | tf_op jit(solution)/shard_map/pallas_call | solution.py:610
  19.9 1.9 %collective-permute-start.1 = (bf16[2,2,256,256]{3,2,1,0:T(8,128)(2,1)S(1)}, bf16[2,2,256,256]{3,2,1,0:T(8,128)(2,1)S(1)}, u32[]{:S(2)}, u32[]{:S(2)}) collective-permute-start(bf16[2,2,256,256]{3,2,1,0:T(8,128)(2,1)S(1)} %get-tuple-element.33), channel_id=1, source_target_pairs={{2,4},{6,8},{10,12},{14,16},{18,20},{22,24},{26,28},{4,2},{8,6},{1... | collective-permute-start | bytes 1572872 | tf_op jit(solution)/shard_map/ppermute | solution.py:613
  21.9 0.0 collective-permute-done.3.partner
  21.9 1.8 %shard_map.116 = (bf16[2,2,256,256]{3,2,1,0:T(8,128)(2,1)S(1)}, bf16[2,2,256,256]{3,2,1,0:T(8,128)(2,1)S(1)}) custom-call(bf16[2,2,256,256]{3,2,1,0:T(8,128)(2,1)S(1)} %get-tuple-element.37.q_arrived, bf16[2,2,256,256]{3,2,1,0:T(8,128)(2,1)S(1)} %get-tuple-element.29.q_out_inner, bf16[2,2,256,256]{3,2,1,0:T(8,128)(2,1)S(1)} %collective-permute-done.3.partner, ...), custom_call_target="tpu_custom_call" | custom-call | tf_op jit(solution)/shard_map/pallas_call | solution.py:614
  23.7 0.1 collective-permute-start.6
  23.7 0.9 %shard_map.117.after.q_next_in = bf16[2,2,256,256]{3,2,1,0:T(8,128)(2,1)S(1)} custom-call(bf16[2,2,256,256]{3,2,1,0:T(8,128)(2,1)S(1)} %get-tuple-element.39.fields.out_inner, f32[2,2,256,256]{3,2,1,0:T(8,128)S(1)} %get-tuple-element.32.phase, bf16[256,256]{1,0:T(8,128)(2,1)S(1)} %copy-done, bf16[256,256]{1,0:T(8,128)(2,1)S(1)} %copy-done), custom_call_target="tpu_custom_call" | custom-call | tf_op jit(solution)/shard_map/pallas_call | solution.py:618
  24.6 7.7 %collective-permute-done.1.arrived = bf16[2,2,256,256]{3,2,1,0:T(8,128)(2,1)S(1)} collective-permute-done((bf16[2,2,256,256]{3,2,1,0:T(8,128)(2,1)S(1)}, bf16[2,2,256,256]{3,2,1,0:T(8,128)(2,1)S(1)}, u32[]{:S(2)}, u32[]{:S(2)}) %collective-permute-start.1) | collective-permute-done | bytes 524320 | tf_op jit(solution)/shard_map/ppermute | solution.py:613
  32.3 1.1 %shard_map.118 = (bf16[2,2,256,256]{3,2,1,0:T(8,128)(2,1)S(1)}, bf16[2,2,128,256]{3,2,1,0:T(8,128)(2,1)S(1)}, bf16[2,2,128,256]{3,2,1,0:T(8,128)(2,1)S(1)}) custom-call(bf16[2,2,256,256]{3,2,1,0:T(8,128)(2,1)S(1)} %collective-permute-done.1.arrived, bf16[2,2,256,256]{3,2,1,0:T(8,128)(2,1)S(1)} %copy-done.1, ...), custom_call_target="tpu_custom_call" | custom-call | tf_op jit(solution)/shard_map/pallas_call | solution.py:619
  33.4 1.9 %collective-permute-start.5 = (bf16[2,2,128,256]{3,2,1,0:T(8,128)(2,1)S(1)}, bf16[2,2,128,256]{3,2,1,0:T(8,128)(2,1)S(1)}, u32[]{:S(2)}, u32[]{:S(2)}) collective-permute-start(bf16[2,2,128,256]{3,2,1,0:T(8,128)(2,1)S(1)} %get-tuple-element.41), channel_id=1, source_target_pairs={{2,4},{6,8},{10,12},{14,16},{18,20},{22,24},{26,28},{4,2},{8,6},{1... | collective-permute-start | bytes 786440 | tf_op jit(solution)/shard_map/ppermute | solution.py:626
  35.3 3.6 %collective-permute-start.4 = (bf16[2,2,128,256]{3,2,1,0:T(8,128)(2,1)S(1)}, bf16[2,2,128,256]{3,2,1,0:T(8,128)(2,1)S(1)}, u32[]{:S(2)}, u32[]{:S(2)}) collective-permute-start(bf16[2,2,128,256]{3,2,1,0:T(8,128)(2,1)S(1)} %get-tuple-element.40), channel_id=1, source_target_pairs={{2,4},{6,8},{10,12},{14,16},{18,20},{22,24},{26,28},{4,2},{8,6},{1... | collective-permute-start | bytes 786440 | tf_op jit(solution)/shard_map/ppermute | solution.py:627
  39.0 0.0 collective-permute-done.6.partner
  39.0 1.8 %shard_map.119 = (bf16[2,2,256,256]{3,2,1,0:T(8,128)(2,1)S(1)}, bf16[2,2,256,256]{3,2,1,0:T(8,128)(2,1)S(1)}, f32[256,256]{1,0:T(8,128)S(1)}, bf16[128,256]{1,0:T(8,128)(2,1)S(1)}, bf16[2,2,256,256]{3,2,1,0:T(8,128)(2,1)S(1)}) custom-call(bf16[2,2,256,256]{3,2,1,0:T(8,128)(2,1)S(1)} %get-tuple-element.42.q_arrived, ...), custom_call_target="tpu_custom_call", output_to_operand_aliasing={{4}: (9, {})} | custom-call | tf_op jit(solution)/shard_map/pallas_call | solution.py:629
  40.8 1.5 %collective-permute-start.7 = (bf16[128,256]{1,0:T(8,128)(2,1)S(1)}, bf16[128,256]{1,0:T(8,128)(2,1)S(1)}, u32[]{:S(2)}, u32[]{:S(2)}) collective-permute-start(bf16[128,256]{1,0:T(8,128)(2,1)S(1)} %get-tuple-element.48), channel_id=1, source_target_pairs={{0,1},{1,0},{2,3},{3,2},{4,5},{5,4},{6,7},{7,6},{8,9},{9,8},{10,11... | collective-permute-start | bytes 196616 | tf_op jit(solution)/shard_map/ppermute | solution.py:637
  42.4 0.9 %collective-permute-done.5.far.last = bf16[2,2,128,256]{3,2,1,0:T(8,128)(2,1)S(1)} collective-permute-done((bf16[2,2,128,256]{3,2,1,0:T(8,128)(2,1)S(1)}, bf16[2,2,128,256]{3,2,1,0:T(8,128)(2,1)S(1)}, u32[]{:S(2)}, u32[]{:S(2)}) %collective-permute-start.5) | collective-permute-done | bytes 262176 | tf_op jit(solution)/shard_map/ppermute | solution.py:626
  43.2 0.1 shard_map.121
  43.3 1.6 %collective-permute-start.8 = (bf16[128,256]{1,0:T(8,128)(2,1)S(1)}, bf16[128,256]{1,0:T(8,128)(2,1)S(1)}, u32[]{:S(2)}, u32[]{:S(2)}) collective-permute-start(bf16[128,256]{1,0:T(8,128)(2,1)S(1)} %shard_map.121), channel_id=1, source_target_pairs={{0,1},{1,0},{2,3},{3,2},{4,5},{5,4},{6,7},{7,6},{8,9},{9,8},{10,11... | collective-permute-start | bytes 196616 | tf_op jit(solution)/shard_map/ppermute | solution.py:641
  44.9 1.2 %collective-permute-done.4.near = bf16[2,2,128,256]{3,2,1,0:T(8,128)(2,1)S(1)} collective-permute-done((bf16[2,2,128,256]{3,2,1,0:T(8,128)(2,1)S(1)}, bf16[2,2,128,256]{3,2,1,0:T(8,128)(2,1)S(1)}, u32[]{:S(2)}, u32[]{:S(2)}) %collective-permute-start.4) | collective-permute-done | bytes 262176 | tf_op jit(solution)/shard_map/ppermute | solution.py:627
  46.0 0.0 collective-permute-done.7.inner_other
  46.0 1.4 %shard_map.120 = (bf16[2,2,2,256,256]{4,3,2,1,0:T(8,128)(2,1)}, bf16[2,2,2,256,256]{4,3,2,1,0:T(8,128)(2,1)}, f32[2,128,256]{2,1,0:T(8,128)}, f32[128,256]{1,0:T(8,128)S(1)}) custom-call(bf16[2,2,128,256]{3,2,1,0:T(8,128)(2,1)S(1)} %collective-permute-done.4.near, bf16[2,2,128,256]{3,2,1,0:T(8,128)(2,1)S(1)} %collective-permute-done.5.far.last, ...), custom_call_target="tpu_custom_call" | custom-call | tf_op jit(solution)/shard_map/pallas_call | solution.py:644
  47.5 0.2 collective-permute-done.8.other
  47.7 0.7 %shard_map.122 = f32[2,128,256]{2,1,0:T(8,128)} custom-call(f32[128,256]{1,0:T(8,128)S(1)} %get-tuple-element.51.terms, bf16[128,256]{1,0:T(8,128)(2,1)S(1)} %collective-permute-done.8.other, f32[2,128,256]{2,1,0:T(8,128)} %get-tuple-element.52.gradient_in), custom_call_target="tpu_custom_call", output_to_operand_aliasing={{}: (2, {})} | custom-call | tf_op jit(solution)/shard_map/pallas_call | solution.py:653
  (5 shorter events, 0.0 us)
Async XLA Ops:
  0.6 3.3 %copy-start = (bf16[256,256]{1,0:T(8,128)(2,1)S(1)}, bf16[256,256]{1,0:T(8,128)(2,1)}, u32[]{:S(2)}) copy-start(bf16[256,256]{1,0:T(8,128)(2,1)} %constant.2.clone.hx.hy) | copy-start | bytes 393220
  0.6 3.3 %copy-start.3 = (s32[2]{0:T(128)S(1)}, s32[2]{0:T(128)}, u32[]{:S(2)}) copy-start(s32[2]{0:T(128)} %freq.1) | copy-start | bytes 28
  0.7 3.3 %copy-start.2 = (f32[16]{0:T(128)S(1)}, f32[16]{0:T(128)}, u32[]{:S(2)}) copy-start(f32[16]{0:T(128)} %slowness.1) | copy-start | bytes 196
  2.0 6.7 %collective-permute-start.2 = (bf16[2,2,256,256]{3,2,1,0:T(8,128)(2,1)S(1)}, bf16[2,2,256,256]{3,2,1,0:T(8,128)(2,1)S(1)}, u32[]{:S(2)}, u32[]{:S(2)}) collective-permute-start(bf16[2,2,256,256]{3,2,1,0:T(8,128)(2,1)S(1)} %get-tuple-element.34), channel_id=1, source_target_pairs={{0,2},{2,0},{4,6},{6,4},{8,10},{10,8},{12,14},{14,12},{16,18},{18,... | collective-permute-start | bytes 1572872 | tf_op jit(solution)/shard_map/ppermute | solution.py:592
  2.0 16.1 %collective-permute-start = (bf16[2,2,256,256]{3,2,1,0:T(8,128)(2,1)S(1)}, bf16[2,2,256,256]{3,2,1,0:T(8,128)(2,1)S(1)}, u32[]{:S(2)}, u32[]{:S(2)}) collective-permute-start(bf16[2,2,256,256]{3,2,1,0:T(8,128)(2,1)S(1)} %get-tuple-element.28), channel_id=1, source_target_pairs={{2,4},{6,8},{10,12},{14,16},{18,20},{22,24},{26,28},{4,2},{8,6},{1... | collective-permute-start | bytes 1572872 | tf_op jit(solution)/shard_map/ppermute | solution.py:591
  8.7 9.5 %copy-start.1 = (bf16[2,2,256,256]{3,2,1,0:T(8,128)(2,1)S(1)}, bf16[2,2,256,256]{3,2,1,0:T(8,128)(2,1)}, u32[]{:S(2)}) copy-start(bf16[2,2,256,256]{3,2,1,0:T(8,128)(2,1)} %source.3) | copy-start | bytes 1572868
  10.6 11.2 %collective-permute-start.3 = (bf16[2,2,256,256]{3,2,1,0:T(8,128)(2,1)S(1)}, bf16[2,2,256,256]{3,2,1,0:T(8,128)(2,1)S(1)}, u32[]{:S(2)}, u32[]{:S(2)}) collective-permute-start(bf16[2,2,256,256]{3,2,1,0:T(8,128)(2,1)S(1)} %get-tuple-element.38), channel_id=1, source_target_pairs={{0,2},{2,0},{4,6},{6,4},{8,10},{10,8},{12,14},{14,12},{16,18},{18,... | collective-permute-start | bytes 1572872 | tf_op jit(solution)/shard_map/ppermute | solution.py:609
  19.9 12.4 %collective-permute-start.1 = (bf16[2,2,256,256]{3,2,1,0:T(8,128)(2,1)S(1)}, bf16[2,2,256,256]{3,2,1,0:T(8,128)(2,1)S(1)}, u32[]{:S(2)}, u32[]{:S(2)}) collective-permute-start(bf16[2,2,256,256]{3,2,1,0:T(8,128)(2,1)S(1)} %get-tuple-element.33), channel_id=1, source_target_pairs={{2,4},{6,8},{10,12},{14,16},{18,20},{22,24},{26,28},{4,2},{8,6},{1... | collective-permute-start | bytes 1572872 | tf_op jit(solution)/shard_map/ppermute | solution.py:613
  23.7 15.3 %collective-permute-start.6 = (bf16[2,2,256,256]{3,2,1,0:T(8,128)(2,1)S(1)}, bf16[2,2,256,256]{3,2,1,0:T(8,128)(2,1)S(1)}, u32[]{:S(2)}, u32[]{:S(2)}) collective-permute-start(bf16[2,2,256,256]{3,2,1,0:T(8,128)(2,1)S(1)} %get-tuple-element.43), channel_id=1, source_target_pairs={{0,2},{2,0},{4,6},{6,4},{8,10},{10,8},{12,14},{14,12},{16,18},{18,... | collective-permute-start | bytes 1572872 | tf_op jit(solution)/shard_map/ppermute | solution.py:617
  33.4 9.8 %collective-permute-start.5 = (bf16[2,2,128,256]{3,2,1,0:T(8,128)(2,1)S(1)}, bf16[2,2,128,256]{3,2,1,0:T(8,128)(2,1)S(1)}, u32[]{:S(2)}, u32[]{:S(2)}) collective-permute-start(bf16[2,2,128,256]{3,2,1,0:T(8,128)(2,1)S(1)} %get-tuple-element.41), channel_id=1, source_target_pairs={{2,4},{6,8},{10,12},{14,16},{18,20},{22,24},{26,28},{4,2},{8,6},{1... | collective-permute-start | bytes 786440 | tf_op jit(solution)/shard_map/ppermute | solution.py:626
  35.3 10.7 %collective-permute-start.4 = (bf16[2,2,128,256]{3,2,1,0:T(8,128)(2,1)S(1)}, bf16[2,2,128,256]{3,2,1,0:T(8,128)(2,1)S(1)}, u32[]{:S(2)}, u32[]{:S(2)}) collective-permute-start(bf16[2,2,128,256]{3,2,1,0:T(8,128)(2,1)S(1)} %get-tuple-element.40), channel_id=1, source_target_pairs={{2,4},{6,8},{10,12},{14,16},{18,20},{22,24},{26,28},{4,2},{8,6},{1... | collective-permute-start | bytes 786440 | tf_op jit(solution)/shard_map/ppermute | solution.py:627
  40.8 5.2 %collective-permute-start.7 = (bf16[128,256]{1,0:T(8,128)(2,1)S(1)}, bf16[128,256]{1,0:T(8,128)(2,1)S(1)}, u32[]{:S(2)}, u32[]{:S(2)}) collective-permute-start(bf16[128,256]{1,0:T(8,128)(2,1)S(1)} %get-tuple-element.48), channel_id=1, source_target_pairs={{0,1},{1,0},{2,3},{3,2},{4,5},{5,4},{6,7},{7,6},{8,9},{9,8},{10,11... | collective-permute-start | bytes 196616 | tf_op jit(solution)/shard_map/ppermute | solution.py:637
  43.3 4.3 %collective-permute-start.8 = (bf16[128,256]{1,0:T(8,128)(2,1)S(1)}, bf16[128,256]{1,0:T(8,128)(2,1)S(1)}, u32[]{:S(2)}, u32[]{:S(2)}) collective-permute-start(bf16[128,256]{1,0:T(8,128)(2,1)S(1)} %shard_map.121), channel_id=1, source_target_pairs={{0,1},{1,0},{2,3},{3,2},{4,5},{5,4},{6,7},{7,6},{8,9},{9,8},{10,11... | collective-permute-start | bytes 196616 | tf_op jit(solution)/shard_map/ppermute | solution.py:641

commit v13 on v12

--- a/solution.py
+++ b/solution.py
@@ -153,23 +153,23 @@
     jobs = list(enumerate(jobs))
     for slot, (plane, _, _) in jobs:
         for part in range(2):
-            work[slot, part] = mm(plane(part) if callable(plane) else plane[part], hy[...]).astype(BF16)
+            work[slot, part] = mm(hx[...], plane(part) if callable(plane) else plane[part]).astype(BF16)
     for slot, (_, front, _) in jobs:
         turn_re, turn_im = phase[front, 0], phase[front, 1]
-        part_re = mm(hx[...], work[slot, 0])
-        part_im = mm(hx[...], work[slot, 1])
+        part_re = mm(work[slot, 0], hy[...])
+        part_im = mm(work[slot, 1], hy[...])
         work[slot, 0] = (part_re * turn_re - part_im * turn_im).astype(BF16)
         work[slot, 1] = (part_re * turn_im + part_im * turn_re).astype(BF16)
     for slot, _ in jobs:
         for part in range(2):
-            work[slot, part] = mm(hx[...], work[slot, part]).astype(BF16)
+            work[slot, part] = mm(work[slot, part], hy[...]).astype(BF16)
     for slot, (_, _, target) in jobs:
         for part in range(2):
             if isinstance(target, list):
                 for rows, piece in target:
-                    piece[part] = mm(work[slot, part, rows, :], hy[...]).astype(BF16)
+                    piece[part] = mm(hx[rows, :], work[slot, part]).astype(BF16)
             else:
-                target[part] = mm(work[slot, part], hy[...]).astype(BF16)
+                target[part] = mm(hx[...], work[slot, part]).astype(BF16)
 
 
 def screened(real_part, imag_part, screen_re, screen_im):

time: 48.7 us -> 48.3 us (level)
  no operation moved by 1% of the time
where the time goes in v13:
time: 48.3 us; the launch traced here: 48.1 us
  Pallas kernels  17.2 us (36%)
  waiting for transfers between devices  15.6 us (32%)
  starting transfers between devices  14.3 us (30%)
  between operations  0.99 us (2%)
    ppermute x1, waiting for transfers between devices, per_device(): arrived_1 = to_beyond(out_outer_1)  7.7 us
    ppermute x1, waiting for transfers between devices, per_device(): arrived_0 = to_beyond(out_outer)  5.93 us
    pallas_call x1, Pallas kernels, per_device(): call(setup_kernel, [HBM] * 4 + [SMEM] * 2 + [VMEM] * 2, [VMEM] * 5, [plan...  4.66 us
    ppermute x1, starting transfers between devices, per_device(): last_near = to_beyond(last_near)  3.64 us
    ppermute x1, starting transfers between devices, per_device(): arrived_0 = to_beyond(out_outer)  1.92 us
    ppermute x1, starting transfers between devices, per_device(): arrived_1 = to_beyond(out_outer_1)  1.92 us
    ppermute x1, starting transfers between devices, per_device(): last_far = to_beyond(last_far)  1.92 us
    pallas_call x1, Pallas kernels, per_device(): call(last_inner_kernel, [VMEM] * 10, [VMEM] * 5, [plane] * 2 + [jax.Shape...  1.88 us
  transfers between devices with their start and end apart: 9, of which 5 were waited for; matrix products, arithmetic and copies ran while one was open for 0% of the time, Pallas kernels for 32%

profile of v13, /device:TPU:4, one launch (start us, length us, event | category | flops | bytes accessed | tf_op | source)
XLA Modules:
  0.0 48.1 jit_solution(8133184525077588193)
XLA Ops:
  0.6 0.0 copy-start
  0.6 0.0 copy-start.3
  0.7 1.3 %shard_map.112 = (bf16[2,2,256,256]{3,2,1,0:T(8,128)(2,1)S(1)}, bf16[2,2,256,256]{3,2,1,0:T(8,128)(2,1)S(1)}) custom-call(bf16[2,2,2,256,256]{4,3,2,1,0:T(8,128)(2,1)} %down.3, bf16[2,2,2,256,256]{4,3,2,1,0:T(8,128)(2,1)} %up.3), custom_call_target="tpu_custom_call" | custom-call | tf_op jit(solution)/shard_map/pallas_call | solution.py:588
  2.0 0.1 collective-permute-start.2
  2.0 1.9 %collective-permute-start = (bf16[2,2,256,256]{3,2,1,0:T(8,128)(2,1)S(1)}, bf16[2,2,256,256]{3,2,1,0:T(8,128)(2,1)S(1)}, u32[]{:S(2)}, u32[]{:S(2)}) collective-permute-start(bf16[2,2,256,256]{3,2,1,0:T(8,128)(2,1)S(1)} %get-tuple-element.28), channel_id=1, source_target_pairs={{2,4},{6,8},{10,12},{14,16},{18,20},{22,24},{26,28},{4,2},{8,6},{1... | collective-permute-start | bytes 1572872 | tf_op jit(solution)/shard_map/ppermute | solution.py:591
  4.0 4.7 %shard_map.113 = (bf16[2,2,256,256]{3,2,1,0:T(8,128)(2,1)S(1)}, bf16[2,2,256,256]{3,2,1,0:T(8,128)(2,1)S(1)}, f32[2,2,2,256,256]{4,3,2,1,0:T(8,128)S(1)}, f32[2,...) custom-call(bf16[2,2,2,256,256]{4,3,2,1,0:T(8,128)(2,1)} %down.3, bf16[2,2,2,256,256]{4,3,2,1,0:T(8,128)(2,1)} %up.3, ...), custom_call_target="tpu_custom_call" | custom-call | tf_op jit(solution)/shard_map/pallas_call | solution.py:593
  8.7 0.0 collective-permute-done.2.partner
  8.7 0.0 copy-start.1
  8.7 1.8 %shard_map.115 = (bf16[2,2,256,256]{3,2,1,0:T(8,128)(2,1)S(1)}, bf16[2,2,256,256]{3,2,1,0:T(8,128)(2,1)S(1)}) custom-call(bf16[2,2,256,256]{3,2,1,0:T(8,128)(2,1)S(1)} %collective-permute-done.2.partner, bf16[2,2,256,256]{3,2,1,0:T(8,128)(2,1)S(1)} %get-tuple-element.35.q_in_outer, f32[2,2,2,256,256]{4,3,2,1,0:T(8,128)S(1)} %get-tuple-element.30.screen, ...), custom_call_target="tpu_custom_call" | custom-call | tf_op jit(solution)/shard_map/pallas_call | solution.py:606
  10.5 1.7 %collective-permute-start.3 = (bf16[2,2,256,256]{3,2,1,0:T(8,128)(2,1)S(1)}, bf16[2,2,256,256]{3,2,1,0:T(8,128)(2,1)S(1)}, u32[]{:S(2)}, u32[]{:S(2)}) collective-permute-start(bf16[2,2,256,256]{3,2,1,0:T(8,128)(2,1)S(1)} %get-tuple-element.38), channel_id=1, source_target_pairs={{0,2},{2,0},{4,6},{6,4},{8,10},{10,8},{12,14},{14,12},{16,18},{18,... | collective-permute-start | bytes 1572872 | tf_op jit(solution)/shard_map/ppermute | solution.py:609
  12.2 5.9 %collective-permute-done.arrived = bf16[2,2,256,256]{3,2,1,0:T(8,128)(2,1)S(1)} collective-permute-done((bf16[2,2,256,256]{3,2,1,0:T(8,128)(2,1)S(1)}, bf16[2,2,256,256]{3,2,1,0:T(8,128)(2,1)S(1)}, u32[]{:S(2)}, u32[]{:S(2)}) %collective-permute-start) | collective-permute-done | bytes 524320 | tf_op jit(solution)/shard_map/ppermute | solution.py:591
  18.2 1.7 %shard_map.114 = (bf16[2,2,256,256]{3,2,1,0:T(8,128)(2,1)S(1)}, bf16[2,2,256,256]{3,2,1,0:T(8,128)(2,1)S(1)}) custom-call(bf16[2,2,256,256]{3,2,1,0:T(8,128)(2,1)S(1)} %collective-permute-done.arrived, bf16[2,2,256,256]{3,2,1,0:T(8,128)(2,1)S(1)} %copy-done.1, bf16[2,2,256,256]{3,2,1,0:T(8,128)(2,1)S(1)} %get-tuple-element.29.q_out_inner, ...), custom_call_target="tpu_custom_call" | custom-call | tf_op jit(solution)/shard_map/pallas_call | solution.py:610
  19.9 1.9 %collective-permute-start.1 = (bf16[2,2,256,256]{3,2,1,0:T(8,128)(2,1)S(1)}, bf16[2,2,256,256]{3,2,1,0:T(8,128)(2,1)S(1)}, u32[]{:S(2)}, u32[]{:S(2)}) collective-permute-start(bf16[2,2,256,256]{3,2,1,0:T(8,128)(2,1)S(1)} %get-tuple-element.33), channel_id=1, source_target_pairs={{2,4},{6,8},{10,12},{14,16},{18,20},{22,24},{26,28},{4,2},{8,6},{1... | collective-permute-start | bytes 1572872 | tf_op jit(solution)/shard_map/ppermute | solution.py:613
  21.8 0.0 collective-permute-done.3.partner
  21.8 1.8 %shard_map.116 = (bf16[2,2,256,256]{3,2,1,0:T(8,128)(2,1)S(1)}, bf16[2,2,256,256]{3,2,1,0:T(8,128)(2,1)S(1)}) custom-call(bf16[2,2,256,256]{3,2,1,0:T(8,128)(2,1)S(1)} %get-tuple-element.37.q_arrived, bf16[2,2,256,256]{3,2,1,0:T(8,128)(2,1)S(1)} %get-tuple-element.29.q_out_inner, bf16[2,2,256,256]{3,2,1,0:T(8,128)(2,1)S(1)} %collective-permute-done.3.partner, ...), custom_call_target="tpu_custom_call" | custom-call | tf_op jit(solution)/shard_map/pallas_call | solution.py:614
  23.6 0.1 collective-permute-start.6
  23.7 0.8 %shard_map.117.after.q_next_in = bf16[2,2,256,256]{3,2,1,0:T(8,128)(2,1)S(1)} custom-call(bf16[2,2,256,256]{3,2,1,0:T(8,128)(2,1)S(1)} %get-tuple-element.39.fields.out_inner, f32[2,2,256,256]{3,2,1,0:T(8,128)S(1)} %get-tuple-element.32.phase, bf16[256,256]{1,0:T(8,128)(2,1)S(1)} %copy-done, bf16[256,256]{1,0:T(8,128)(2,1)S(1)} %copy-done), custom_call_target="tpu_custom_call" | custom-call | tf_op jit(solution)/shard_map/pallas_call | solution.py:618
  24.5 7.7 %collective-permute-done.1.arrived = bf16[2,2,256,256]{3,2,1,0:T(8,128)(2,1)S(1)} collective-permute-done((bf16[2,2,256,256]{3,2,1,0:T(8,128)(2,1)S(1)}, bf16[2,2,256,256]{3,2,1,0:T(8,128)(2,1)S(1)}, u32[]{:S(2)}, u32[]{:S(2)}) %collective-permute-start.1) | collective-permute-done | bytes 524320 | tf_op jit(solution)/shard_map/ppermute | solution.py:613
  32.2 1.0 %shard_map.118 = (bf16[2,2,256,256]{3,2,1,0:T(8,128)(2,1)S(1)}, bf16[2,2,128,256]{3,2,1,0:T(8,128)(2,1)S(1)}, bf16[2,2,128,256]{3,2,1,0:T(8,128)(2,1)S(1)}) custom-call(bf16[2,2,256,256]{3,2,1,0:T(8,128)(2,1)S(1)} %collective-permute-done.1.arrived, bf16[2,2,256,256]{3,2,1,0:T(8,128)(2,1)S(1)} %copy-done.1, ...), custom_call_target="tpu_custom_call" | custom-call | tf_op jit(solution)/shard_map/pallas_call | solution.py:619
  33.2 1.9 %collective-permute-start.5 = (bf16[2,2,128,256]{3,2,1,0:T(8,128)(2,1)S(1)}, bf16[2,2,128,256]{3,2,1,0:T(8,128)(2,1)S(1)}, u32[]{:S(2)}, u32[]{:S(2)}) collective-permute-start(bf16[2,2,128,256]{3,2,1,0:T(8,128)(2,1)S(1)} %get-tuple-element.41), channel_id=1, source_target_pairs={{2,4},{6,8},{10,12},{14,16},{18,20},{22,24},{26,28},{4,2},{8,6},{1... | collective-permute-start | bytes 786440 | tf_op jit(solution)/shard_map/ppermute | solution.py:626
  35.2 3.6 %collective-permute-start.4 = (bf16[2,2,128,256]{3,2,1,0:T(8,128)(2,1)S(1)}, bf16[2,2,128,256]{3,2,1,0:T(8,128)(2,1)S(1)}, u32[]{:S(2)}, u32[]{:S(2)}) collective-permute-start(bf16[2,2,128,256]{3,2,1,0:T(8,128)(2,1)S(1)} %get-tuple-element.40), channel_id=1, source_target_pairs={{2,4},{6,8},{10,12},{14,16},{18,20},{22,24},{26,28},{4,2},{8,6},{1... | collective-permute-start | bytes 786440 | tf_op jit(solution)/shard_map/ppermute | solution.py:627
  38.8 0.0 collective-permute-done.6.partner
  38.8 1.9 %shard_map.119 = (bf16[2,2,256,256]{3,2,1,0:T(8,128)(2,1)S(1)}, bf16[2,2,256,256]{3,2,1,0:T(8,128)(2,1)S(1)}, f32[256,256]{1,0:T(8,128)S(1)}, bf16[128,256]{1,0:T(8,128)(2,1)S(1)}, bf16[2,2,256,256]{3,2,1,0:T(8,128)(2,1)S(1)}) custom-call(bf16[2,2,256,256]{3,2,1,0:T(8,128)(2,1)S(1)} %get-tuple-element.42.q_arrived, ...), custom_call_target="tpu_custom_call", output_to_operand_aliasing={{4}: (9, {})} | custom-call | tf_op jit(solution)/shard_map/pallas_call | solution.py:629
  40.7 1.5 %collective-permute-start.7 = (bf16[128,256]{1,0:T(8,128)(2,1)S(1)}, bf16[128,256]{1,0:T(8,128)(2,1)S(1)}, u32[]{:S(2)}, u32[]{:S(2)}) collective-permute-start(bf16[128,256]{1,0:T(8,128)(2,1)S(1)} %get-tuple-element.48), channel_id=1, source_target_pairs={{0,1},{1,0},{2,3},{3,2},{4,5},{5,4},{6,7},{7,6},{8,9},{9,8},{10,11... | collective-permute-start | bytes 196616 | tf_op jit(solution)/shard_map/ppermute | solution.py:637
  42.2 0.6 %collective-permute-done.5.far.last = bf16[2,2,128,256]{3,2,1,0:T(8,128)(2,1)S(1)} collective-permute-done((bf16[2,2,128,256]{3,2,1,0:T(8,128)(2,1)S(1)}, bf16[2,2,128,256]{3,2,1,0:T(8,128)(2,1)S(1)}, u32[]{:S(2)}, u32[]{:S(2)}) %collective-permute-start.5) | collective-permute-done | bytes 262176 | tf_op jit(solution)/shard_map/ppermute | solution.py:626
  42.8 0.1 shard_map.121
  42.9 1.6 %collective-permute-start.8 = (bf16[128,256]{1,0:T(8,128)(2,1)S(1)}, bf16[128,256]{1,0:T(8,128)(2,1)S(1)}, u32[]{:S(2)}, u32[]{:S(2)}) collective-permute-start(bf16[128,256]{1,0:T(8,128)(2,1)S(1)} %shard_map.121), channel_id=1, source_target_pairs={{0,1},{1,0},{2,3},{3,2},{4,5},{5,4},{6,7},{7,6},{8,9},{9,8},{10,11... | collective-permute-start | bytes 196616 | tf_op jit(solution)/shard_map/ppermute | solution.py:641
  44.5 1.2 %collective-permute-done.4.near = bf16[2,2,128,256]{3,2,1,0:T(8,128)(2,1)S(1)} collective-permute-done((bf16[2,2,128,256]{3,2,1,0:T(8,128)(2,1)S(1)}, bf16[2,2,128,256]{3,2,1,0:T(8,128)(2,1)S(1)}, u32[]{:S(2)}, u32[]{:S(2)}) %collective-permute-start.4) | collective-permute-done | bytes 262176 | tf_op jit(solution)/shard_map/ppermute | solution.py:627
  45.6 0.0 collective-permute-done.7.inner_other
  45.6 1.4 %shard_map.120 = (bf16[2,2,2,256,256]{4,3,2,1,0:T(8,128)(2,1)}, bf16[2,2,2,256,256]{4,3,2,1,0:T(8,128)(2,1)}, f32[2,128,256]{2,1,0:T(8,128)}, f32[128,256]{1,0:T(8,128)S(1)}) custom-call(bf16[2,2,128,256]{3,2,1,0:T(8,128)(2,1)S(1)} %collective-permute-done.4.near, bf16[2,2,128,256]{3,2,1,0:T(8,128)(2,1)S(1)} %collective-permute-done.5.far.last, ...), custom_call_target="tpu_custom_call" | custom-call | tf_op jit(solution)/shard_map/pallas_call | solution.py:644
  47.1 0.2 collective-permute-done.8.other
  47.2 0.7 %shard_map.122 = f32[2,128,256]{2,1,0:T(8,128)} custom-call(f32[128,256]{1,0:T(8,128)S(1)} %get-tuple-element.51.terms, bf16[128,256]{1,0:T(8,128)(2,1)S(1)} %collective-permute-done.8.other, f32[2,128,256]{2,1,0:T(8,128)} %get-tuple-element.52.gradient_in), custom_call_target="tpu_custom_call", output_to_operand_aliasing={{}: (2, {})} | custom-call | tf_op jit(solution)/shard_map/pallas_call | solution.py:653
  (5 shorter events, 0.0 us)
Async XLA Ops:
  0.6 3.3 %copy-start = (bf16[256,256]{1,0:T(8,128)(2,1)S(1)}, bf16[256,256]{1,0:T(8,128)(2,1)}, u32[]{:S(2)}) copy-start(bf16[256,256]{1,0:T(8,128)(2,1)} %constant.2.clone.hx.hy) | copy-start | bytes 393220
  0.6 3.3 %copy-start.3 = (s32[2]{0:T(128)S(1)}, s32[2]{0:T(128)}, u32[]{:S(2)}) copy-start(s32[2]{0:T(128)} %freq.1) | copy-start | bytes 28
  0.7 3.3 %copy-start.2 = (f32[16]{0:T(128)S(1)}, f32[16]{0:T(128)}, u32[]{:S(2)}) copy-start(f32[16]{0:T(128)} %slowness.1) | copy-start | bytes 196
  2.0 6.7 %collective-permute-start.2 = (bf16[2,2,256,256]{3,2,1,0:T(8,128)(2,1)S(1)}, bf16[2,2,256,256]{3,2,1,0:T(8,128)(2,1)S(1)}, u32[]{:S(2)}, u32[]{:S(2)}) collective-permute-start(bf16[2,2,256,256]{3,2,1,0:T(8,128)(2,1)S(1)} %get-tuple-element.34), channel_id=1, source_target_pairs={{0,2},{2,0},{4,6},{6,4},{8,10},{10,8},{12,14},{14,12},{16,18},{18,... | collective-permute-start | bytes 1572872 | tf_op jit(solution)/shard_map/ppermute | solution.py:592
  2.0 16.1 %collective-permute-start = (bf16[2,2,256,256]{3,2,1,0:T(8,128)(2,1)S(1)}, bf16[2,2,256,256]{3,2,1,0:T(8,128)(2,1)S(1)}, u32[]{:S(2)}, u32[]{:S(2)}) collective-permute-start(bf16[2,2,256,256]{3,2,1,0:T(8,128)(2,1)S(1)} %get-tuple-element.28), channel_id=1, source_target_pairs={{2,4},{6,8},{10,12},{14,16},{18,20},{22,24},{26,28},{4,2},{8,6},{1... | collective-permute-start | bytes 1572872 | tf_op jit(solution)/shard_map/ppermute | solution.py:591
  8.7 9.5 %copy-start.1 = (bf16[2,2,256,256]{3,2,1,0:T(8,128)(2,1)S(1)}, bf16[2,2,256,256]{3,2,1,0:T(8,128)(2,1)}, u32[]{:S(2)}) copy-start(bf16[2,2,256,256]{3,2,1,0:T(8,128)(2,1)} %source.3) | copy-start | bytes 1572868
  10.5 11.3 %collective-permute-start.3 = (bf16[2,2,256,256]{3,2,1,0:T(8,128)(2,1)S(1)}, bf16[2,2,256,256]{3,2,1,0:T(8,128)(2,1)S(1)}, u32[]{:S(2)}, u32[]{:S(2)}) collective-permute-start(bf16[2,2,256,256]{3,2,1,0:T(8,128)(2,1)S(1)} %get-tuple-element.38), channel_id=1, source_target_pairs={{0,2},{2,0},{4,6},{6,4},{8,10},{10,8},{12,14},{14,12},{16,18},{18,... | collective-permute-start | bytes 1572872 | tf_op jit(solution)/shard_map/ppermute | solution.py:609
  19.9 12.4 %collective-permute-start.1 = (bf16[2,2,256,256]{3,2,1,0:T(8,128)(2,1)S(1)}, bf16[2,2,256,256]{3,2,1,0:T(8,128)(2,1)S(1)}, u32[]{:S(2)}, u32[]{:S(2)}) collective-permute-start(bf16[2,2,256,256]{3,2,1,0:T(8,128)(2,1)S(1)} %get-tuple-element.33), channel_id=1, source_target_pairs={{2,4},{6,8},{10,12},{14,16},{18,20},{22,24},{26,28},{4,2},{8,6},{1... | collective-permute-start | bytes 1572872 | tf_op jit(solution)/shard_map/ppermute | solution.py:613
  23.6 15.2 %collective-permute-start.6 = (bf16[2,2,256,256]{3,2,1,0:T(8,128)(2,1)S(1)}, bf16[2,2,256,256]{3,2,1,0:T(8,128)(2,1)S(1)}, u32[]{:S(2)}, u32[]{:S(2)}) collective-permute-start(bf16[2,2,256,256]{3,2,1,0:T(8,128)(2,1)S(1)} %get-tuple-element.43), channel_id=1, source_target_pairs={{0,2},{2,0},{4,6},{6,4},{8,10},{10,8},{12,14},{14,12},{16,18},{18,... | collective-permute-start | bytes 1572872 | tf_op jit(solution)/shard_map/ppermute | solution.py:617
  33.2 9.6 %collective-permute-start.5 = (bf16[2,2,128,256]{3,2,1,0:T(8,128)(2,1)S(1)}, bf16[2,2,128,256]{3,2,1,0:T(8,128)(2,1)S(1)}, u32[]{:S(2)}, u32[]{:S(2)}) collective-permute-start(bf16[2,2,128,256]{3,2,1,0:T(8,128)(2,1)S(1)} %get-tuple-element.41), channel_id=1, source_target_pairs={{2,4},{6,8},{10,12},{14,16},{18,20},{22,24},{26,28},{4,2},{8,6},{1... | collective-permute-start | bytes 786440 | tf_op jit(solution)/shard_map/ppermute | solution.py:626
  35.2 10.5 %collective-permute-start.4 = (bf16[2,2,128,256]{3,2,1,0:T(8,128)(2,1)S(1)}, bf16[2,2,128,256]{3,2,1,0:T(8,128)(2,1)S(1)}, u32[]{:S(2)}, u32[]{:S(2)}) collective-permute-start(bf16[2,2,128,256]{3,2,1,0:T(8,128)(2,1)S(1)} %get-tuple-element.40), channel_id=1, source_target_pairs={{2,4},{6,8},{10,12},{14,16},{18,20},{22,24},{26,28},{4,2},{8,6},{1... | collective-permute-start | bytes 786440 | tf_op jit(solution)/shard_map/ppermute | solution.py:627
  40.7 4.9 %collective-permute-start.7 = (bf16[128,256]{1,0:T(8,128)(2,1)S(1)}, bf16[128,256]{1,0:T(8,128)(2,1)S(1)}, u32[]{:S(2)}, u32[]{:S(2)}) collective-permute-start(bf16[128,256]{1,0:T(8,128)(2,1)S(1)} %get-tuple-element.48), channel_id=1, source_target_pairs={{0,1},{1,0},{2,3},{3,2},{4,5},{5,4},{6,7},{7,6},{8,9},{9,8},{10,11... | collective-permute-start | bytes 196616 | tf_op jit(solution)/shard_map/ppermute | solution.py:637
  42.9 4.3 %collective-permute-start.8 = (bf16[128,256]{1,0:T(8,128)(2,1)S(1)}, bf16[128,256]{1,0:T(8,128)(2,1)S(1)}, u32[]{:S(2)}, u32[]{:S(2)}) collective-permute-start(bf16[128,256]{1,0:T(8,128)(2,1)S(1)} %shard_map.121), channel_id=1, source_target_pairs={{0,1},{1,0},{2,3},{3,2},{4,5},{5,4},{6,7},{7,6},{8,9},{9,8},{10,11... | collective-permute-start | bytes 196616 | tf_op jit(solution)/shard_map/ppermute | solution.py:641

commit v14 on v13

--- a/solution.py
+++ b/solution.py
@@ -166,8 +166,11 @@
     for slot, (_, _, target) in jobs:
         for part in range(2):
             if isinstance(target, list):
-                for rows, piece in target:
-                    piece[part] = mm(hx[rows, :], work[slot, part]).astype(BF16)
+                rows = jnp.concatenate([hx[rows, :] for rows, _ in target], axis=0)
+                ends = np.cumsum([piece.shape[1] for _, piece in target])
+                done = mm(rows, work[slot, part]).astype(BF16)
+                for (_, piece), end in zip(target, ends, strict=True):
+                    piece[part] = done[end - piece.shape[1] : end]
             else:
                 target[part] = mm(hx[...], work[slot, part]).astype(BF16)
 
@@ -515,19 +518,26 @@
     return copies(0, down_out, up_out)
 
 
-def outer_fields_kernel(
-    scale, near, far, q_arrived, q_out_inner, screen, refl, inner_in, inner_out, inner_terms, inner_other,
-    down_out, up_out, gradient, terms,
-    near_in, near_out, far_in, far_out, inner_sum, sems,
+def home_kernel(
+    far, q_arrived, q_out_inner, screen, refl, inner_in, inner_out, down_out, up_out, far_in, far_out, sems
 ):
-    rows_x = inner_in.shape[2]
-    waits = send_home(1, pl.ds(0, rows_x), inner_in, inner_out, down_out, up_out, sems.at[0])
+    waits = send_home(1, pl.ds(0, inner_in.shape[2]), inner_in, inner_out, down_out, up_out, sems.at[0])
     rows = row_fields(1, far, q_arrived, q_out_inner, screen, refl, far_in, far_out)
     waits += send_home(0, rows, far_in, far_out, down_out, up_out, sems.at[1])
+    for copy in waits:
+        copy.wait()
+
+
+def near_kernel(
+    scale, near, q_arrived, q_out_inner, screen, refl, inner_terms, inner_other, down_in, up_in,
+    down_out, up_out, gradient, terms,
+    near_in, near_out, inner_sum, sems,
+):
+    del down_in, up_in
     rows = row_fields(0, near, q_arrived, q_out_inner, screen, refl, near_in, near_out)
-    waits += send_home(0, rows, near_in, near_out, down_out, up_out, sems.at[2])
+    waits = send_home(0, rows, near_in, near_out, down_out, up_out, sems.at[0])
     inner_sum[...] = scale * (inner_terms[rows, :] + inner_other[...].astype(F32))
-    waits.append(pltpu.make_async_copy(inner_sum, gradient.at[1 - odd_place()], sems.at[3, 0]))
+    waits.append(pltpu.make_async_copy(inner_sum, gradient.at[1 - odd_place()], sems.at[1, 0]))
     waits[-1].start()
     terms[...] = row_terms(0, near, q_arrived, q_out_inner)
     for copy in waits:
@@ -641,15 +651,17 @@
     outer_other = across(outer_far) if shots == 2 else jnp.zeros_like(outer_far)
     half_total = jax.ShapeDtypeStruct((half, rows_y), F32)
     share = jax.ShapeDtypeStruct((2, half, rows_y), F32)
+    down, up = call(
+        home_kernel, [VMEM] * 7, [HBM] * 2, [state] * 2, buffers(2, half_plane) + [dma((2, 2))]
+    )(last_far, q_arrived, q_out_inner_2, screen, refl, inner_in, inner_out)
     down, up, gradient, outer_near = call(
-        functools.partial(outer_fields_kernel, scale),
-        [VMEM] * 10,
+        functools.partial(near_kernel, scale),
+        [VMEM] * 7 + [HBM] * 2,
         [HBM] * 3 + [VMEM],
         [state, state, share, half_total],
-        buffers(4, half_plane) + buffers(1, half_total) + [dma((4, 2))],
-    )(
-        last_near, last_far, q_arrived, q_out_inner_2, screen, refl, inner_in, inner_out, inner_terms, inner_other
-    )
+        buffers(2, half_plane) + buffers(1, half_total) + [dma((2, 2))],
+        input_output_aliases={7: 0, 8: 1},
+    )(last_near, q_arrived, q_out_inner_2, screen, refl, inner_terms, inner_other, down, up)
     gradient = call(
         functools.partial(outer_gradient_kernel, scale),
         [VMEM] * 2 + [HBM],

time: 48.3 us -> 48.3 us (level)
  waiting for transfers between devices: 15.6 us -> 14.7 us
  Pallas kernels: 17.2 us -> 18 us
    ppermute x1, waiting for transfers between devices: 1.16 us -> 0.01 us  [per_device(): last_near = to_beyond(last_near)]
    pallas_call x1 -> x2, Pallas kernels: 1.41 us -> 2.23 us  [the longest x1 1.17 us: per_device(): call(home_kernel, [VMEM] * 7, [HBM] * 2, [state] * 2, buffers(2, half_pla...]
  transfers between devices with their start and end apart: 9 -> 9, of which waited for: 5 -> 4; matrix products, arithmetic and copies ran while one was open for 0% -> 0% of each run, Pallas kernels for 32% -> 33%
where the time goes in v14:
time: 48.3 us; the launch traced here: 48.1 us
  Pallas kernels  18 us (37%)
  waiting for transfers between devices  14.7 us (30%)
  starting transfers between devices  14.3 us (30%)
  between operations  1.01 us (2%)
    ppermute x1, waiting for transfers between devices, per_device(): arrived_1 = to_beyond(out_outer_1)  7.7 us
    ppermute x1, waiting for transfers between devices, per_device(): arrived_0 = to_beyond(out_outer)  5.93 us
    pallas_call x1, Pallas kernels, per_device(): call(setup_kernel, [HBM] * 4 + [SMEM] * 2 + [VMEM] * 2, [VMEM] * 5, [plan...  4.66 us
    ppermute x1, starting transfers between devices, per_device(): last_near = to_beyond(last_near)  3.64 us
    ppermute x1, starting transfers between devices, per_device(): arrived_0 = to_beyond(out_outer)  1.92 us
    ppermute x1, starting transfers between devices, per_device(): arrived_1 = to_beyond(out_outer_1)  1.92 us
    ppermute x1, starting transfers between devices, per_device(): last_far = to_beyond(last_far)  1.92 us
    pallas_call x1, Pallas kernels, per_device(): call(last_inner_kernel, [VMEM] * 10, [VMEM] * 5, [plane] * 2 + [jax.Shape...  1.88 us
  transfers between devices with their start and end apart: 9, of which 4 were waited for; matrix products, arithmetic and copies ran while one was open for 0% of the time, Pallas kernels for 33%

profile of v14, /device:TPU:4, one launch (start us, length us, event | category | flops | bytes accessed | tf_op | source)
XLA Modules:
  0.0 48.1 jit_solution(3594366375607334098)
XLA Ops:
  0.6 0.0 copy-start
  0.7 1.3 %shard_map.112 = (bf16[2,2,256,256]{3,2,1,0:T(8,128)(2,1)S(1)}, bf16[2,2,256,256]{3,2,1,0:T(8,128)(2,1)S(1)}) custom-call(bf16[2,2,2,256,256]{4,3,2,1,0:T(8,128)(2,1)} %down.3, bf16[2,2,2,256,256]{4,3,2,1,0:T(8,128)(2,1)} %up.3), custom_call_target="tpu_custom_call" | custom-call | tf_op jit(solution)/shard_map/pallas_call | solution.py:598
  2.0 0.1 collective-permute-start.2
  2.0 1.9 %collective-permute-start = (bf16[2,2,256,256]{3,2,1,0:T(8,128)(2,1)S(1)}, bf16[2,2,256,256]{3,2,1,0:T(8,128)(2,1)S(1)}, u32[]{:S(2)}, u32[]{:S(2)}) collective-permute-start(bf16[2,2,256,256]{3,2,1,0:T(8,128)(2,1)S(1)} %get-tuple-element.30), channel_id=1, source_target_pairs={{2,4},{6,8},{10,12},{14,16},{18,20},{22,24},{26,28},{4,2},{8,6},{1... | collective-permute-start | bytes 1572872 | tf_op jit(solution)/shard_map/ppermute | solution.py:601
  4.0 4.7 %shard_map.113 = (bf16[2,2,256,256]{3,2,1,0:T(8,128)(2,1)S(1)}, bf16[2,2,256,256]{3,2,1,0:T(8,128)(2,1)S(1)}, f32[2,2,2,256,256]{4,3,2,1,0:T(8,128)S(1)}, f32[2,...) custom-call(bf16[2,2,2,256,256]{4,3,2,1,0:T(8,128)(2,1)} %down.3, bf16[2,2,2,256,256]{4,3,2,1,0:T(8,128)(2,1)} %up.3, ...), custom_call_target="tpu_custom_call" | custom-call | tf_op jit(solution)/shard_map/pallas_call | solution.py:603
  8.7 0.0 collective-permute-done.2.partner
  8.7 0.0 copy-start.1
  8.7 1.8 %shard_map.115 = (bf16[2,2,256,256]{3,2,1,0:T(8,128)(2,1)S(1)}, bf16[2,2,256,256]{3,2,1,0:T(8,128)(2,1)S(1)}) custom-call(bf16[2,2,256,256]{3,2,1,0:T(8,128)(2,1)S(1)} %collective-permute-done.2.partner, bf16[2,2,256,256]{3,2,1,0:T(8,128)(2,1)S(1)} %get-tuple-element.37.q_in_outer, f32[2,2,2,256,256]{4,3,2,1,0:T(8,128)S(1)} %get-tuple-element.32.screen, ...), custom_call_target="tpu_custom_call" | custom-call | tf_op jit(solution)/shard_map/pallas_call | solution.py:616
  10.5 1.7 %collective-permute-start.3 = (bf16[2,2,256,256]{3,2,1,0:T(8,128)(2,1)S(1)}, bf16[2,2,256,256]{3,2,1,0:T(8,128)(2,1)S(1)}, u32[]{:S(2)}, u32[]{:S(2)}) collective-permute-start(bf16[2,2,256,256]{3,2,1,0:T(8,128)(2,1)S(1)} %get-tuple-element.40), channel_id=1, source_target_pairs={{0,2},{2,0},{4,6},{6,4},{8,10},{10,8},{12,14},{14,12},{16,18},{18,... | collective-permute-start | bytes 1572872 | tf_op jit(solution)/shard_map/ppermute | solution.py:619
  12.2 5.9 %collective-permute-done.arrived = bf16[2,2,256,256]{3,2,1,0:T(8,128)(2,1)S(1)} collective-permute-done((bf16[2,2,256,256]{3,2,1,0:T(8,128)(2,1)S(1)}, bf16[2,2,256,256]{3,2,1,0:T(8,128)(2,1)S(1)}, u32[]{:S(2)}, u32[]{:S(2)}) %collective-permute-start) | collective-permute-done | bytes 524320 | tf_op jit(solution)/shard_map/ppermute | solution.py:601
  18.2 1.7 %shard_map.114 = (bf16[2,2,256,256]{3,2,1,0:T(8,128)(2,1)S(1)}, bf16[2,2,256,256]{3,2,1,0:T(8,128)(2,1)S(1)}) custom-call(bf16[2,2,256,256]{3,2,1,0:T(8,128)(2,1)S(1)} %collective-permute-done.arrived, bf16[2,2,256,256]{3,2,1,0:T(8,128)(2,1)S(1)} %copy-done.1, bf16[2,2,256,256]{3,2,1,0:T(8,128)(2,1)S(1)} %get-tuple-element.31.q_out_inner, ...), custom_call_target="tpu_custom_call" | custom-call | tf_op jit(solution)/shard_map/pallas_call | solution.py:620
  19.9 1.9 %collective-permute-start.1 = (bf16[2,2,256,256]{3,2,1,0:T(8,128)(2,1)S(1)}, bf16[2,2,256,256]{3,2,1,0:T(8,128)(2,1)S(1)}, u32[]{:S(2)}, u32[]{:S(2)}) collective-permute-start(bf16[2,2,256,256]{3,2,1,0:T(8,128)(2,1)S(1)} %get-tuple-element.35), channel_id=1, source_target_pairs={{2,4},{6,8},{10,12},{14,16},{18,20},{22,24},{26,28},{4,2},{8,6},{1... | collective-permute-start | bytes 1572872 | tf_op jit(solution)/shard_map/ppermute | solution.py:623
  21.8 0.0 collective-permute-done.3.partner
  21.8 1.8 %shard_map.116 = (bf16[2,2,256,256]{3,2,1,0:T(8,128)(2,1)S(1)}, bf16[2,2,256,256]{3,2,1,0:T(8,128)(2,1)S(1)}) custom-call(bf16[2,2,256,256]{3,2,1,0:T(8,128)(2,1)S(1)} %get-tuple-element.39.q_arrived, bf16[2,2,256,256]{3,2,1,0:T(8,128)(2,1)S(1)} %get-tuple-element.31.q_out_inner, bf16[2,2,256,256]{3,2,1,0:T(8,128)(2,1)S(1)} %collective-permute-done.3.partner, ...), custom_call_target="tpu_custom_call" | custom-call | tf_op jit(solution)/shard_map/pallas_call | solution.py:624
  23.6 0.1 collective-permute-start.5
  23.7 0.8 %shard_map.117.after.q_next_in = bf16[2,2,256,256]{3,2,1,0:T(8,128)(2,1)S(1)} custom-call(bf16[2,2,256,256]{3,2,1,0:T(8,128)(2,1)S(1)} %get-tuple-element.41.fields.out_inner, f32[2,2,256,256]{3,2,1,0:T(8,128)S(1)} %get-tuple-element.34.phase, bf16[256,256]{1,0:T(8,128)(2,1)S(1)} %copy-done, bf16[256,256]{1,0:T(8,128)(2,1)S(1)} %copy-done), custom_call_target="tpu_custom_call" | custom-call | tf_op jit(solution)/shard_map/pallas_call | solution.py:628
  24.5 7.7 %collective-permute-done.1.arrived = bf16[2,2,256,256]{3,2,1,0:T(8,128)(2,1)S(1)} collective-permute-done((bf16[2,2,256,256]{3,2,1,0:T(8,128)(2,1)S(1)}, bf16[2,2,256,256]{3,2,1,0:T(8,128)(2,1)S(1)}, u32[]{:S(2)}, u32[]{:S(2)}) %collective-permute-start.1) | collective-permute-done | bytes 524320 | tf_op jit(solution)/shard_map/ppermute | solution.py:623
  32.2 1.0 %shard_map.118 = (bf16[2,2,256,256]{3,2,1,0:T(8,128)(2,1)S(1)}, bf16[2,2,128,256]{3,2,1,0:T(8,128)(2,1)S(1)}, bf16[2,2,128,256]{3,2,1,0:T(8,128)(2,1)S(1)}) custom-call(bf16[2,2,256,256]{3,2,1,0:T(8,128)(2,1)S(1)} %collective-permute-done.1.arrived, bf16[2,2,256,256]{3,2,1,0:T(8,128)(2,1)S(1)} %copy-done.1, ...), custom_call_target="tpu_custom_call" | custom-call | tf_op jit(solution)/shard_map/pallas_call | solution.py:629
  33.2 1.9 %collective-permute-start.7 = (bf16[2,2,128,256]{3,2,1,0:T(8,128)(2,1)S(1)}, bf16[2,2,128,256]{3,2,1,0:T(8,128)(2,1)S(1)}, u32[]{:S(2)}, u32[]{:S(2)}) collective-permute-start(bf16[2,2,128,256]{3,2,1,0:T(8,128)(2,1)S(1)} %get-tuple-element.48), channel_id=1, source_target_pairs={{2,4},{6,8},{10,12},{14,16},{18,20},{22,24},{26,28},{4,2},{8,6},{1... | collective-permute-start | bytes 786440 | tf_op jit(solution)/shard_map/ppermute | solution.py:636
  35.2 3.6 %collective-permute-start.4 = (bf16[2,2,128,256]{3,2,1,0:T(8,128)(2,1)S(1)}, bf16[2,2,128,256]{3,2,1,0:T(8,128)(2,1)S(1)}, u32[]{:S(2)}, u32[]{:S(2)}) collective-permute-start(bf16[2,2,128,256]{3,2,1,0:T(8,128)(2,1)S(1)} %get-tuple-element.42), channel_id=1, source_target_pairs={{2,4},{6,8},{10,12},{14,16},{18,20},{22,24},{26,28},{4,2},{8,6},{1... | collective-permute-start | bytes 786440 | tf_op jit(solution)/shard_map/ppermute | solution.py:637
  38.8 0.0 collective-permute-done.5.partner
  38.8 1.9 %shard_map.119 = (bf16[2,2,256,256]{3,2,1,0:T(8,128)(2,1)S(1)}, bf16[2,2,256,256]{3,2,1,0:T(8,128)(2,1)S(1)}, f32[256,256]{1,0:T(8,128)S(1)}, bf16[128,256]{1,0:T(8,128)(2,1)S(1)}, bf16[2,2,256,256]{3,2,1,0:T(8,128)(2,1)S(1)}) custom-call(bf16[2,2,256,256]{3,2,1,0:T(8,128)(2,1)S(1)} %get-tuple-element.43.q_arrived, ...), custom_call_target="tpu_custom_call", output_to_operand_aliasing={{4}: (9, {})} | custom-call | tf_op jit(solution)/shard_map/pallas_call | solution.py:639
  40.7 1.5 %collective-permute-start.6 = (bf16[128,256]{1,0:T(8,128)(2,1)S(1)}, bf16[128,256]{1,0:T(8,128)(2,1)S(1)}, u32[]{:S(2)}, u32[]{:S(2)}) collective-permute-start(bf16[128,256]{1,0:T(8,128)(2,1)S(1)} %get-tuple-element.47), channel_id=1, source_target_pairs={{0,1},{1,0},{2,3},{3,2},{4,5},{5,4},{6,7},{7,6},{8,9},{9,8},{10,11... | collective-permute-start | bytes 196616 | tf_op jit(solution)/shard_map/ppermute | solution.py:647
  42.2 0.6 %collective-permute-done.7.far.last = bf16[2,2,128,256]{3,2,1,0:T(8,128)(2,1)S(1)} collective-permute-done((bf16[2,2,128,256]{3,2,1,0:T(8,128)(2,1)S(1)}, bf16[2,2,128,256]{3,2,1,0:T(8,128)(2,1)S(1)}, u32[]{:S(2)}, u32[]{:S(2)}) %collective-permute-start.7) | collective-permute-done | bytes 262176 | tf_op jit(solution)/shard_map/ppermute | solution.py:636
  42.8 0.1 shard_map.122
  42.9 1.6 %collective-permute-start.8 = (bf16[128,256]{1,0:T(8,128)(2,1)S(1)}, bf16[128,256]{1,0:T(8,128)(2,1)S(1)}, u32[]{:S(2)}, u32[]{:S(2)}) collective-permute-start(bf16[128,256]{1,0:T(8,128)(2,1)S(1)} %shard_map.122), channel_id=1, source_target_pairs={{0,1},{1,0},{2,3},{3,2},{4,5},{5,4},{6,7},{7,6},{8,9},{9,8},{10,11... | collective-permute-start | bytes 196616 | tf_op jit(solution)/shard_map/ppermute | solution.py:651
  44.5 1.2 %shard_map.120 = (bf16[2,2,2,256,256]{4,3,2,1,0:T(8,128)(2,1)}, bf16[2,2,2,256,256]{4,3,2,1,0:T(8,128)(2,1)}) custom-call(bf16[2,2,128,256]{3,2,1,0:T(8,128)(2,1)S(1)} %collective-permute-done.7.far.last, bf16[2,2,256,256]{3,2,1,0:T(8,128)(2,1)S(1)} %get-tuple-element.39.q_arrived, bf16[2,2,256,256]{3,2,1,0:T(8,128)(2,1)S(1)} %get-tuple-element.45.q_out_inner, ...), custom_call_target="tpu_custom_call" | custom-call | tf_op jit(solution)/shard_map/pallas_call | solution.py:654
  45.6 0.0 collective-permute-done.4.near
  45.7 0.0 collective-permute-done.6.inner_other
  45.7 1.1 %shard_map.121 = (bf16[2,2,2,256,256]{4,3,2,1,0:T(8,128)(2,1)}, bf16[2,2,2,256,256]{4,3,2,1,0:T(8,128)(2,1)}, f32[2,128,256]{2,1,0:T(8,128)}, f32[128,256]{1,0:T(8,128)S(1)}) custom-call(bf16[2,2,128,256]{3,2,1,0:T(8,128)(2,1)S(1)} %collective-permute-done.4.near, ...), custom_call_target="tpu_custom_call", output_to_operand_aliasing={{0}: (7, {}), {1}: (8, {})} | custom-call | tf_op jit(solution)/shard_map/pallas_call | solution.py:657
  46.7 0.5 %collective-permute-done.8.other = bf16[128,256]{1,0:T(8,128)(2,1)S(1)} collective-permute-done((bf16[128,256]{1,0:T(8,128)(2,1)S(1)}, bf16[128,256]{1,0:T(8,128)(2,1)S(1)}, u32[]{:S(2)}, u32[]{:S(2)}) %collective-permute-start.8) | collective-permute-done | bytes 65568 | tf_op jit(solution)/shard_map/ppermute | solution.py:651
  47.2 0.7 %shard_map.123 = f32[2,128,256]{2,1,0:T(8,128)} custom-call(f32[128,256]{1,0:T(8,128)S(1)} %get-tuple-element.55.terms, bf16[128,256]{1,0:T(8,128)(2,1)S(1)} %collective-permute-done.8.other, f32[2,128,256]{2,1,0:T(8,128)} %get-tuple-element.56.gradient_in), custom_call_target="tpu_custom_call", output_to_operand_aliasing={{}: (2, {})} | custom-call | tf_op jit(solution)/shard_map/pallas_call | solution.py:665
  (6 shorter events, 0.0 us)
Async XLA Ops:
  0.6 3.3 %copy-start = (bf16[256,256]{1,0:T(8,128)(2,1)S(1)}, bf16[256,256]{1,0:T(8,128)(2,1)}, u32[]{:S(2)}) copy-start(bf16[256,256]{1,0:T(8,128)(2,1)} %constant.2.clone.hx.hy) | copy-start | bytes 393220
  0.6 3.3 %copy-start.3 = (s32[2]{0:T(128)S(1)}, s32[2]{0:T(128)}, u32[]{:S(2)}) copy-start(s32[2]{0:T(128)} %freq.1) | copy-start | bytes 28
  0.7 3.3 %copy-start.2 = (f32[16]{0:T(128)S(1)}, f32[16]{0:T(128)}, u32[]{:S(2)}) copy-start(f32[16]{0:T(128)} %slowness.1) | copy-start | bytes 196
  2.0 6.7 %collective-permute-start.2 = (bf16[2,2,256,256]{3,2,1,0:T(8,128)(2,1)S(1)}, bf16[2,2,256,256]{3,2,1,0:T(8,128)(2,1)S(1)}, u32[]{:S(2)}, u32[]{:S(2)}) collective-permute-start(bf16[2,2,256,256]{3,2,1,0:T(8,128)(2,1)S(1)} %get-tuple-element.36), channel_id=1, source_target_pairs={{0,2},{2,0},{4,6},{6,4},{8,10},{10,8},{12,14},{14,12},{16,18},{18,... | collective-permute-start | bytes 1572872 | tf_op jit(solution)/shard_map/ppermute | solution.py:602
  2.0 16.1 %collective-permute-start = (bf16[2,2,256,256]{3,2,1,0:T(8,128)(2,1)S(1)}, bf16[2,2,256,256]{3,2,1,0:T(8,128)(2,1)S(1)}, u32[]{:S(2)}, u32[]{:S(2)}) collective-permute-start(bf16[2,2,256,256]{3,2,1,0:T(8,128)(2,1)S(1)} %get-tuple-element.30), channel_id=1, source_target_pairs={{2,4},{6,8},{10,12},{14,16},{18,20},{22,24},{26,28},{4,2},{8,6},{1... | collective-permute-start | bytes 1572872 | tf_op jit(solution)/shard_map/ppermute | solution.py:601
  8.7 9.5 %copy-start.1 = (bf16[2,2,256,256]{3,2,1,0:T(8,128)(2,1)S(1)}, bf16[2,2,256,256]{3,2,1,0:T(8,128)(2,1)}, u32[]{:S(2)}) copy-start(bf16[2,2,256,256]{3,2,1,0:T(8,128)(2,1)} %source.3) | copy-start | bytes 1572868
  10.5 11.3 %collective-permute-start.3 = (bf16[2,2,256,256]{3,2,1,0:T(8,128)(2,1)S(1)}, bf16[2,2,256,256]{3,2,1,0:T(8,128)(2,1)S(1)}, u32[]{:S(2)}, u32[]{:S(2)}) collective-permute-start(bf16[2,2,256,256]{3,2,1,0:T(8,128)(2,1)S(1)} %get-tuple-element.40), channel_id=1, source_target_pairs={{0,2},{2,0},{4,6},{6,4},{8,10},{10,8},{12,14},{14,12},{16,18},{18,... | collective-permute-start | bytes 1572872 | tf_op jit(solution)/shard_map/ppermute | solution.py:619
  19.9 12.4 %collective-permute-start.1 = (bf16[2,2,256,256]{3,2,1,0:T(8,128)(2,1)S(1)}, bf16[2,2,256,256]{3,2,1,0:T(8,128)(2,1)S(1)}, u32[]{:S(2)}, u32[]{:S(2)}) collective-permute-start(bf16[2,2,256,256]{3,2,1,0:T(8,128)(2,1)S(1)} %get-tuple-element.35), channel_id=1, source_target_pairs={{2,4},{6,8},{10,12},{14,16},{18,20},{22,24},{26,28},{4,2},{8,6},{1... | collective-permute-start | bytes 1572872 | tf_op jit(solution)/shard_map/ppermute | solution.py:623
  23.6 15.2 %collective-permute-start.5 = (bf16[2,2,256,256]{3,2,1,0:T(8,128)(2,1)S(1)}, bf16[2,2,256,256]{3,2,1,0:T(8,128)(2,1)S(1)}, u32[]{:S(2)}, u32[]{:S(2)}) collective-permute-start(bf16[2,2,256,256]{3,2,1,0:T(8,128)(2,1)S(1)} %get-tuple-element.44), channel_id=1, source_target_pairs={{0,2},{2,0},{4,6},{6,4},{8,10},{10,8},{12,14},{14,12},{16,18},{18,... | collective-permute-start | bytes 1572872 | tf_op jit(solution)/shard_map/ppermute | solution.py:627
  33.2 9.6 %collective-permute-start.7 = (bf16[2,2,128,256]{3,2,1,0:T(8,128)(2,1)S(1)}, bf16[2,2,128,256]{3,2,1,0:T(8,128)(2,1)S(1)}, u32[]{:S(2)}, u32[]{:S(2)}) collective-permute-start(bf16[2,2,128,256]{3,2,1,0:T(8,128)(2,1)S(1)} %get-tuple-element.48), channel_id=1, source_target_pairs={{2,4},{6,8},{10,12},{14,16},{18,20},{22,24},{26,28},{4,2},{8,6},{1... | collective-permute-start | bytes 786440 | tf_op jit(solution)/shard_map/ppermute | solution.py:636
  35.2 10.5 %collective-permute-start.4 = (bf16[2,2,128,256]{3,2,1,0:T(8,128)(2,1)S(1)}, bf16[2,2,128,256]{3,2,1,0:T(8,128)(2,1)S(1)}, u32[]{:S(2)}, u32[]{:S(2)}) collective-permute-start(bf16[2,2,128,256]{3,2,1,0:T(8,128)(2,1)S(1)} %get-tuple-element.42), channel_id=1, source_target_pairs={{2,4},{6,8},{10,12},{14,16},{18,20},{22,24},{26,28},{4,2},{8,6},{1... | collective-permute-start | bytes 786440 | tf_op jit(solution)/shard_map/ppermute | solution.py:637
  40.7 5.0 %collective-permute-start.6 = (bf16[128,256]{1,0:T(8,128)(2,1)S(1)}, bf16[128,256]{1,0:T(8,128)(2,1)S(1)}, u32[]{:S(2)}, u32[]{:S(2)}) collective-permute-start(bf16[128,256]{1,0:T(8,128)(2,1)S(1)} %get-tuple-element.47), channel_id=1, source_target_pairs={{0,1},{1,0},{2,3},{3,2},{4,5},{5,4},{6,7},{7,6},{8,9},{9,8},{10,11... | collective-permute-start | bytes 196616 | tf_op jit(solution)/shard_map/ppermute | solution.py:647
  42.9 4.3 %collective-permute-start.8 = (bf16[128,256]{1,0:T(8,128)(2,1)S(1)}, bf16[128,256]{1,0:T(8,128)(2,1)S(1)}, u32[]{:S(2)}, u32[]{:S(2)}) collective-permute-start(bf16[128,256]{1,0:T(8,128)(2,1)S(1)} %shard_map.122), channel_id=1, source_target_pairs={{0,1},{1,0},{2,3},{3,2},{4,5},{5,4},{6,7},{7,6},{8,9},{9,8},{10,11... | collective-permute-start | bytes 196616 | tf_op jit(solution)/shard_map/ppermute | solution.py:651

commit v15 on v14

--- a/solution.py
+++ b/solution.py
@@ -431,22 +431,15 @@
         spread([(fields.at[front], front, q_fields.at[front]) for front in everyone], work, hx, hy, phase)
 
 
-def last_inner_kernel(
-    q_arrived, q_out_inner, partner, screen, refl, phase, hx, hy, out_inner, q_next_in,
-    inward, outward, terms, far_terms, q_next,
-    field, q_inward, q_partner, work,
-):
-    del q_next_in
+def last_inner_step(
+    extra, q_arrived, q_out_inner, partner, screen, refl, phase, hx, hy,
+    inward, outward, terms, far_terms, field, q_inward, q_partner, work,
+):
     everyone = range(partner.shape[0])
-
-    @pl.when(jnp.logical_not(late_pair()))
-    def _():
-        spread([(out_inner.at[front], front, q_next.at[front]) for front in everyone], work, hx, hy, phase)
-
     outer_step(q_arrived, q_out_inner, screen, refl, "inward", field)
     jobs = [(partner.at[front], front, q_partner.at[front]) for front in everyone]
     jobs += [(field.at[front], front, q_inward.at[front]) for front in everyone]
-    spread(jobs, work, hx, hy, phase)
+    spread(jobs + extra, work, hx, hy, phase)
     total = None
     for front in everyone:
         a_re, a_im = (q_inward[front, part].astype(F32) for part in range(2))
@@ -460,6 +453,38 @@
         total = term if total is None else total + term
     terms[...] = total
     far_terms[...] = terms[half_rows(1, far_terms.shape[0]), :].astype(BF16)
+
+
+def late_inner_kernel(
+    q_arrived, q_out_inner, partner, screen, refl, phase, hx, hy, held_in,
+    inward, outward, terms, far_terms, held_out,
+    field, q_inward, q_partner, work,
+):
+    del held_in, held_out
+
+    @pl.when(late_pair())
+    def _():
+        last_inner_step(
+            [], q_arrived, q_out_inner, partner, screen, refl, phase, hx, hy,
+            inward, outward, terms, far_terms, field, q_inward, q_partner, work,
+        )
+
+
+def early_inner_kernel(
+    q_arrived, q_out_inner, partner, screen, refl, phase, hx, hy, out_inner, inward_in, outward_in, terms_in,
+    far_terms_in, q_next_in,
+    inward, outward, terms, far_terms, q_next,
+    field, q_inward, q_partner, work,
+):
+    del inward_in, outward_in, terms_in, far_terms_in, q_next_in
+
+    @pl.when(jnp.logical_not(late_pair()))
+    def _():
+        extra = [(out_inner.at[front], front, q_next.at[front]) for front in range(partner.shape[0])]
+        last_inner_step(
+            extra, q_arrived, q_out_inner, partner, screen, refl, phase, hx, hy,
+            inward, outward, terms, far_terms, field, q_inward, q_partner, work,
+        )
 
 
 def incoming(last, q_arrived, front, rows):
@@ -634,16 +659,25 @@
         buffers(1) + [work(fronts)],
     )(arrived_1, source, q_out_inner_1, *fixed, q_out_inner_2)
     last_far = to_beyond(last_far)
+    half_sum = jax.ShapeDtypeStruct((half, rows_y), BF16)
+    inner_parts = [plane] * 2 + [jax.ShapeDtypeStruct((rows_x, rows_y), F32), half_sum]
+    *inner, last_near = call(
+        late_inner_kernel,
+        [VMEM] * 9,
+        [VMEM] * 5,
+        inner_parts + [half_plane],
+        buffers(3) + [work(2 * fronts)],
+        input_output_aliases={8: 4},
+    )(q_arrived_1, q_out_inner_1, partner_2, *fixed, last_near)
     last_near = to_beyond(last_near)
-    half_sum = jax.ShapeDtypeStruct((half, rows_y), BF16)
     inner_in, inner_out, inner_terms, inner_far, q_out_inner_2 = call(
-        last_inner_kernel,
-        [VMEM] * 10,
+        early_inner_kernel,
+        [VMEM] * 14,
         [VMEM] * 5,
-        [plane] * 2 + [jax.ShapeDtypeStruct((rows_x, rows_y), F32), half_sum, plane],
-        buffers(3) + [work(2 * fronts)],
-        input_output_aliases={9: 4},
-    )(q_arrived_1, q_out_inner_1, partner_2, *fixed, out_inner_2, q_out_inner_2)
+        inner_parts + [plane],
+        buffers(3) + [work(3 * fronts)],
+        input_output_aliases={9 + index: index for index in range(5)},
+    )(q_arrived_1, q_out_inner_1, partner_2, *fixed, out_inner_2, *inner, q_out_inner_2)
     inner_other = across(inner_far) if shots == 2 else jnp.zeros_like(inner_far)
     outer_far = call(far_terms_kernel, [VMEM] * 3 + [pl.BlockSpec(memory_space=pl.ANY)], VMEM, half_sum)(
         last_far, q_arrived, q_out_inner_2, inner_terms

time: 48.3 us -> 49.6 us (1.027)
  the two profiles are of different devices: /device:TPU:4 before, /device:TPU:1 now
where the time goes in v15:
time: 49.6 us; the launch traced here: 49.3 us
  Pallas kernels  18.1 us (36%)
  starting transfers between devices  18 us (36%)
  waiting for transfers between devices  12.2 us (25%)
  between operations  1.02 us (2%)
    ppermute x1, waiting for transfers between devices, per_device(): arrived_1 = to_beyond(out_outer_1)  5.25 us
    ppermute x1, waiting for transfers between devices, per_device(): arrived_0 = to_beyond(out_outer)  5.06 us
    pallas_call x1, Pallas kernels, per_device(): call(setup_kernel, [HBM] * 4 + [SMEM] * 2 + [VMEM] * 2, [VMEM] * 5, [plan...  4.66 us
    ppermute x1, starting transfers between devices, per_device(): arrived_0 = to_beyond(out_outer)  4.49 us
    ppermute x1, starting transfers between devices, per_device(): arrived_1 = to_beyond(out_outer_1)  4.39 us
    ppermute x1, starting transfers between devices, per_device(): last_far = to_beyond(last_far)  4.39 us
    ppermute x1, starting transfers between devices, per_device(): last_near = to_beyond(last_near)  1.92 us
    pallas_call x1, Pallas kernels, per_device(): call(late_inner_kernel, [VMEM] * 9, [VMEM] * 5, inner_parts + [half_plane...  1.87 us
  transfers between devices with their start and end apart: 9, of which 4 were waited for; matrix products, arithmetic and copies ran while one was open for 0% of the time, Pallas kernels for 33%

profile of v15, /device:TPU:1, one launch (start us, length us, event | category | flops | bytes accessed | tf_op | source)
XLA Modules:
  0.0 49.3 jit_solution(13600212355907367148)
XLA Ops:
  0.6 0.0 copy-start
  0.7 1.3 %shard_map.112 = (bf16[2,2,256,256]{3,2,1,0:T(8,128)(2,1)S(1)}, bf16[2,2,256,256]{3,2,1,0:T(8,128)(2,1)S(1)}) custom-call(bf16[2,2,2,256,256]{4,3,2,1,0:T(8,128)(2,1)} %down.3, bf16[2,2,2,256,256]{4,3,2,1,0:T(8,128)(2,1)} %up.3), custom_call_target="tpu_custom_call" | custom-call | tf_op jit(solution)/shard_map/pallas_call | solution.py:623
  2.0 0.1 collective-permute-start.2
  2.1 4.5 %collective-permute-start = (bf16[2,2,256,256]{3,2,1,0:T(8,128)(2,1)S(1)}, bf16[2,2,256,256]{3,2,1,0:T(8,128)(2,1)S(1)}, u32[]{:S(2)}, u32[]{:S(2)}) collective-permute-start(bf16[2,2,256,256]{3,2,1,0:T(8,128)(2,1)S(1)} %get-tuple-element.35), channel_id=1, source_target_pairs={{2,4},{6,8},{10,12},{14,16},{18,20},{22,24},{26,28},{4,2},{8,6},{1... | collective-permute-start | bytes 1572872 | tf_op jit(solution)/shard_map/ppermute | solution.py:626
  6.6 4.7 %shard_map.113 = (bf16[2,2,256,256]{3,2,1,0:T(8,128)(2,1)S(1)}, bf16[2,2,256,256]{3,2,1,0:T(8,128)(2,1)S(1)}, f32[2,2,2,256,256]{4,3,2,1,0:T(8,128)S(1)}, f32[2,...) custom-call(bf16[2,2,2,256,256]{4,3,2,1,0:T(8,128)(2,1)} %down.3, bf16[2,2,2,256,256]{4,3,2,1,0:T(8,128)(2,1)} %up.3, ...), custom_call_target="tpu_custom_call" | custom-call | tf_op jit(solution)/shard_map/pallas_call | solution.py:628
  11.3 0.0 collective-permute-done.2.partner
  11.3 0.0 copy-start.1
  11.3 1.9 %shard_map.115 = (bf16[2,2,256,256]{3,2,1,0:T(8,128)(2,1)S(1)}, bf16[2,2,256,256]{3,2,1,0:T(8,128)(2,1)S(1)}) custom-call(bf16[2,2,256,256]{3,2,1,0:T(8,128)(2,1)S(1)} %collective-permute-done.2.partner, bf16[2,2,256,256]{3,2,1,0:T(8,128)(2,1)S(1)} %get-tuple-element.42.q_in_outer, f32[2,2,2,256,256]{4,3,2,1,0:T(8,128)S(1)} %get-tuple-element.37.screen, ...), custom_call_target="tpu_custom_call" | custom-call | tf_op jit(solution)/shard_map/pallas_call | solution.py:641
  13.2 0.1 collective-permute-start.3
  13.2 5.1 %collective-permute-done.arrived = bf16[2,2,256,256]{3,2,1,0:T(8,128)(2,1)S(1)} collective-permute-done((bf16[2,2,256,256]{3,2,1,0:T(8,128)(2,1)S(1)}, bf16[2,2,256,256]{3,2,1,0:T(8,128)(2,1)S(1)}, u32[]{:S(2)}, u32[]{:S(2)}) %collective-permute-start) | collective-permute-done | bytes 524320 | tf_op jit(solution)/shard_map/ppermute | solution.py:626
  18.3 1.7 %shard_map.114 = (bf16[2,2,256,256]{3,2,1,0:T(8,128)(2,1)S(1)}, bf16[2,2,256,256]{3,2,1,0:T(8,128)(2,1)S(1)}) custom-call(bf16[2,2,256,256]{3,2,1,0:T(8,128)(2,1)S(1)} %collective-permute-done.arrived, bf16[2,2,256,256]{3,2,1,0:T(8,128)(2,1)S(1)} %copy-done.1, bf16[2,2,256,256]{3,2,1,0:T(8,128)(2,1)S(1)} %get-tuple-element.36.q_out_inner, ...), custom_call_target="tpu_custom_call" | custom-call | tf_op jit(solution)/shard_map/pallas_call | solution.py:645
  20.0 4.4 %collective-permute-start.1 = (bf16[2,2,256,256]{3,2,1,0:T(8,128)(2,1)S(1)}, bf16[2,2,256,256]{3,2,1,0:T(8,128)(2,1)S(1)}, u32[]{:S(2)}, u32[]{:S(2)}) collective-permute-start(bf16[2,2,256,256]{3,2,1,0:T(8,128)(2,1)S(1)} %get-tuple-element.40), channel_id=1, source_target_pairs={{2,4},{6,8},{10,12},{14,16},{18,20},{22,24},{26,28},{4,2},{8,6},{1... | collective-permute-start | bytes 1572872 | tf_op jit(solution)/shard_map/ppermute | solution.py:648
  24.4 0.0 collective-permute-done.3.partner
  24.4 1.8 %shard_map.116 = (bf16[2,2,256,256]{3,2,1,0:T(8,128)(2,1)S(1)}, bf16[2,2,256,256]{3,2,1,0:T(8,128)(2,1)S(1)}) custom-call(bf16[2,2,256,256]{3,2,1,0:T(8,128)(2,1)S(1)} %get-tuple-element.44.q_arrived, bf16[2,2,256,256]{3,2,1,0:T(8,128)(2,1)S(1)} %get-tuple-element.36.q_out_inner, bf16[2,2,256,256]{3,2,1,0:T(8,128)(2,1)S(1)} %collective-permute-done.3.partner, ...), custom_call_target="tpu_custom_call" | custom-call | tf_op jit(solution)/shard_map/pallas_call | solution.py:649
  26.2 0.1 collective-permute-start.4
  26.3 0.8 %shard_map.117.after.q_next_in = bf16[2,2,256,256]{3,2,1,0:T(8,128)(2,1)S(1)} custom-call(bf16[2,2,256,256]{3,2,1,0:T(8,128)(2,1)S(1)} %get-tuple-element.46.fields.out_inner, f32[2,2,256,256]{3,2,1,0:T(8,128)S(1)} %get-tuple-element.39.phase, bf16[256,256]{1,0:T(8,128)(2,1)S(1)} %copy-done, bf16[256,256]{1,0:T(8,128)(2,1)S(1)} %copy-done), custom_call_target="tpu_custom_call" | custom-call | tf_op jit(solution)/shard_map/pallas_call | solution.py:653
  27.1 5.2 %collective-permute-done.1.arrived = bf16[2,2,256,256]{3,2,1,0:T(8,128)(2,1)S(1)} collective-permute-done((bf16[2,2,256,256]{3,2,1,0:T(8,128)(2,1)S(1)}, bf16[2,2,256,256]{3,2,1,0:T(8,128)(2,1)S(1)}, u32[]{:S(2)}, u32[]{:S(2)}) %collective-permute-start.1) | collective-permute-done | bytes 524320 | tf_op jit(solution)/shard_map/ppermute | solution.py:648
  32.4 1.0 %shard_map.118 = (bf16[2,2,256,256]{3,2,1,0:T(8,128)(2,1)S(1)}, bf16[2,2,128,256]{3,2,1,0:T(8,128)(2,1)S(1)}, bf16[2,2,128,256]{3,2,1,0:T(8,128)(2,1)S(1)}) custom-call(bf16[2,2,256,256]{3,2,1,0:T(8,128)(2,1)S(1)} %collective-permute-done.1.arrived, bf16[2,2,256,256]{3,2,1,0:T(8,128)(2,1)S(1)} %copy-done.1, ...), custom_call_target="tpu_custom_call" | custom-call | tf_op jit(solution)/shard_map/pallas_call | solution.py:654
  33.4 4.4 %collective-permute-start.7 = (bf16[2,2,128,256]{3,2,1,0:T(8,128)(2,1)S(1)}, bf16[2,2,128,256]{3,2,1,0:T(8,128)(2,1)S(1)}, u32[]{:S(2)}, u32[]{:S(2)}) collective-permute-start(bf16[2,2,128,256]{3,2,1,0:T(8,128)(2,1)S(1)} %get-tuple-element.58), channel_id=1, source_target_pairs={{2,4},{6,8},{10,12},{14,16},{18,20},{22,24},{26,28},{4,2},{8,6},{1... | collective-permute-start | bytes 786440 | tf_op jit(solution)/shard_map/ppermute | solution.py:661
  37.8 0.0 collective-permute-done.4.partner
  37.8 1.9 %shard_map.119 = (bf16[2,2,256,256]{3,2,1,0:T(8,128)(2,1)S(1)}, bf16[2,2,256,256]{3,2,1,0:T(8,128)(2,1)S(1)}, f32[256,256]{1,0:T(8,128)S(1)}, bf16[128,256]{1,0:T(8,128)(2,1)S(1)}, bf16[2,2,128,256]{3,2,1,0:T(8,128)(2,1)S(1)}) custom-call(bf16[2,2,256,256]{3,2,1,0:T(8,128)(2,1)S(1)} %get-tuple-element.47.q_arrived, ...), custom_call_target="tpu_custom_call", output_to_operand_aliasing={{4}: (8, {})} | custom-call | tf_op jit(solution)/shard_map/pallas_call | solution.py:664
  39.6 1.9 %collective-permute-start.5 = (bf16[2,2,128,256]{3,2,1,0:T(8,128)(2,1)S(1)}, bf16[2,2,128,256]{3,2,1,0:T(8,128)(2,1)S(1)}, u32[]{:S(2)}, u32[]{:S(2)}) collective-permute-start(bf16[2,2,128,256]{3,2,1,0:T(8,128)(2,1)S(1)} %get-tuple-element.50), channel_id=1, source_target_pairs={{2,4},{6,8},{10,12},{14,16},{18,20},{22,24},{26,28},{4,2},{8,6},{1... | collective-permute-start | bytes 786440 | tf_op jit(solution)/shard_map/ppermute | solution.py:672
  41.6 1.3 %collective-permute-start.6 = (bf16[128,256]{1,0:T(8,128)(2,1)S(1)}, bf16[128,256]{1,0:T(8,128)(2,1)S(1)}, u32[]{:S(2)}, u32[]{:S(2)}) collective-permute-start(bf16[128,256]{1,0:T(8,128)(2,1)S(1)} %get-tuple-element.57), channel_id=1, source_target_pairs={{0,1},{1,0},{2,3},{3,2},{4,5},{5,4},{6,7},{7,6},{8,9},{9,8},{10,11... | collective-permute-start | bytes 196616 | tf_op jit(solution)/shard_map/ppermute | solution.py:681
  42.9 0.1 collective-permute-done.7.far.last
  43.0 0.1 shard_map.123
  43.1 1.3 %collective-permute-start.8 = (bf16[128,256]{1,0:T(8,128)(2,1)S(1)}, bf16[128,256]{1,0:T(8,128)(2,1)S(1)}, u32[]{:S(2)}, u32[]{:S(2)}) collective-permute-start(bf16[128,256]{1,0:T(8,128)(2,1)S(1)} %shard_map.123), channel_id=1, source_target_pairs={{0,1},{1,0},{2,3},{3,2},{4,5},{5,4},{6,7},{7,6},{8,9},{9,8},{10,11... | collective-permute-start | bytes 196616 | tf_op jit(solution)/shard_map/ppermute | solution.py:685
  44.4 1.2 %shard_map.121 = (bf16[2,2,2,256,256]{4,3,2,1,0:T(8,128)(2,1)}, bf16[2,2,2,256,256]{4,3,2,1,0:T(8,128)(2,1)}) custom-call(bf16[2,2,128,256]{3,2,1,0:T(8,128)(2,1)S(1)} %collective-permute-done.7.far.last, bf16[2,2,256,256]{3,2,1,0:T(8,128)(2,1)S(1)} %get-tuple-element.44.q_arrived, bf16[2,2,256,256]{3,2,1,0:T(8,128)(2,1)S(1)} %get-tuple-element.55.q_out_inner, ...), custom_call_target="tpu_custom_call" | custom-call | tf_op jit(solution)/shard_map/pallas_call | solution.py:688
  45.5 0.0 collective-permute-done.6.inner_other
  45.5 1.8 %collective-permute-done.5.near = bf16[2,2,128,256]{3,2,1,0:T(8,128)(2,1)S(1)} collective-permute-done((bf16[2,2,128,256]{3,2,1,0:T(8,128)(2,1)S(1)}, bf16[2,2,128,256]{3,2,1,0:T(8,128)(2,1)S(1)}, u32[]{:S(2)}, u32[]{:S(2)}) %collective-permute-start.5) | collective-permute-done | bytes 262176 | tf_op jit(solution)/shard_map/ppermute | solution.py:672
  47.3 1.1 %shard_map.122 = (bf16[2,2,2,256,256]{4,3,2,1,0:T(8,128)(2,1)}, bf16[2,2,2,256,256]{4,3,2,1,0:T(8,128)(2,1)}, f32[2,128,256]{2,1,0:T(8,128)}, f32[128,256]{1,0:T(8,128)S(1)}) custom-call(bf16[2,2,128,256]{3,2,1,0:T(8,128)(2,1)S(1)} %collective-permute-done.5.near, ...), custom_call_target="tpu_custom_call", output_to_operand_aliasing={{0}: (7, {}), {1}: (8, {})} | custom-call | tf_op jit(solution)/shard_map/pallas_call | solution.py:691
  48.5 0.0 collective-permute-done.8.other
  48.5 0.7 %shard_map.124 = f32[2,128,256]{2,1,0:T(8,128)} custom-call(f32[128,256]{1,0:T(8,128)S(1)} %get-tuple-element.65.terms, bf16[128,256]{1,0:T(8,128)(2,1)S(1)} %collective-permute-done.8.other, f32[2,128,256]{2,1,0:T(8,128)} %get-tuple-element.66.gradient_in), custom_call_target="tpu_custom_call", output_to_operand_aliasing={{}: (2, {})} | custom-call | tf_op jit(solution)/shard_map/pallas_call | solution.py:699
  (7 shorter events, 0.0 us)
Async XLA Ops:
  0.6 5.9 %copy-start = (bf16[256,256]{1,0:T(8,128)(2,1)S(1)}, bf16[256,256]{1,0:T(8,128)(2,1)}, u32[]{:S(2)}) copy-start(bf16[256,256]{1,0:T(8,128)(2,1)} %constant.2.clone.hx.hy) | copy-start | bytes 393220
  0.6 5.9 %copy-start.3 = (s32[2]{0:T(128)S(1)}, s32[2]{0:T(128)}, u32[]{:S(2)}) copy-start(s32[2]{0:T(128)} %freq.1) | copy-start | bytes 28
  0.7 5.9 %copy-start.2 = (f32[16]{0:T(128)S(1)}, f32[16]{0:T(128)}, u32[]{:S(2)}) copy-start(f32[16]{0:T(128)} %slowness.1) | copy-start | bytes 196
  2.0 9.3 %collective-permute-start.2 = (bf16[2,2,256,256]{3,2,1,0:T(8,128)(2,1)S(1)}, bf16[2,2,256,256]{3,2,1,0:T(8,128)(2,1)S(1)}, u32[]{:S(2)}, u32[]{:S(2)}) collective-permute-start(bf16[2,2,256,256]{3,2,1,0:T(8,128)(2,1)S(1)} %get-tuple-element.41), channel_id=1, source_target_pairs={{0,2},{2,0},{4,6},{6,4},{8,10},{10,8},{12,14},{14,12},{16,18},{18,... | collective-permute-start | bytes 1572872 | tf_op jit(solution)/shard_map/ppermute | solution.py:627
  2.1 16.2 %collective-permute-start = (bf16[2,2,256,256]{3,2,1,0:T(8,128)(2,1)S(1)}, bf16[2,2,256,256]{3,2,1,0:T(8,128)(2,1)S(1)}, u32[]{:S(2)}, u32[]{:S(2)}) collective-permute-start(bf16[2,2,256,256]{3,2,1,0:T(8,128)(2,1)S(1)} %get-tuple-element.35), channel_id=1, source_target_pairs={{2,4},{6,8},{10,12},{14,16},{18,20},{22,24},{26,28},{4,2},{8,6},{1... | collective-permute-start | bytes 1572872 | tf_op jit(solution)/shard_map/ppermute | solution.py:626
  11.3 7.0 %copy-start.1 = (bf16[2,2,256,256]{3,2,1,0:T(8,128)(2,1)S(1)}, bf16[2,2,256,256]{3,2,1,0:T(8,128)(2,1)}, u32[]{:S(2)}) copy-start(bf16[2,2,256,256]{3,2,1,0:T(8,128)(2,1)} %source.3) | copy-start | bytes 1572868
  13.2 11.2 %collective-permute-start.3 = (bf16[2,2,256,256]{3,2,1,0:T(8,128)(2,1)S(1)}, bf16[2,2,256,256]{3,2,1,0:T(8,128)(2,1)S(1)}, u32[]{:S(2)}, u32[]{:S(2)}) collective-permute-start(bf16[2,2,256,256]{3,2,1,0:T(8,128)(2,1)S(1)} %get-tuple-element.45), channel_id=1, source_target_pairs={{0,2},{2,0},{4,6},{6,4},{8,10},{10,8},{12,14},{14,12},{16,18},{18,... | collective-permute-start | bytes 1572872 | tf_op jit(solution)/shard_map/ppermute | solution.py:644
  20.0 12.4 %collective-permute-start.1 = (bf16[2,2,256,256]{3,2,1,0:T(8,128)(2,1)S(1)}, bf16[2,2,256,256]{3,2,1,0:T(8,128)(2,1)S(1)}, u32[]{:S(2)}, u32[]{:S(2)}) collective-permute-start(bf16[2,2,256,256]{3,2,1,0:T(8,128)(2,1)S(1)} %get-tuple-element.40), channel_id=1, source_target_pairs={{2,4},{6,8},{10,12},{14,16},{18,20},{22,24},{26,28},{4,2},{8,6},{1... | collective-permute-start | bytes 1572872 | tf_op jit(solution)/shard_map/ppermute | solution.py:648
  26.2 11.5 %collective-permute-start.4 = (bf16[2,2,256,256]{3,2,1,0:T(8,128)(2,1)S(1)}, bf16[2,2,256,256]{3,2,1,0:T(8,128)(2,1)S(1)}, u32[]{:S(2)}, u32[]{:S(2)}) collective-permute-start(bf16[2,2,256,256]{3,2,1,0:T(8,128)(2,1)S(1)} %get-tuple-element.48), channel_id=1, source_target_pairs={{0,2},{2,0},{4,6},{6,4},{8,10},{10,8},{12,14},{14,12},{16,18},{18,... | collective-permute-start | bytes 1572872 | tf_op jit(solution)/shard_map/ppermute | solution.py:652
  33.4 9.6 %collective-permute-start.7 = (bf16[2,2,128,256]{3,2,1,0:T(8,128)(2,1)S(1)}, bf16[2,2,128,256]{3,2,1,0:T(8,128)(2,1)S(1)}, u32[]{:S(2)}, u32[]{:S(2)}) collective-permute-start(bf16[2,2,128,256]{3,2,1,0:T(8,128)(2,1)S(1)} %get-tuple-element.58), channel_id=1, source_target_pairs={{2,4},{6,8},{10,12},{14,16},{18,20},{22,24},{26,28},{4,2},{8,6},{1... | collective-permute-start | bytes 786440 | tf_op jit(solution)/shard_map/ppermute | solution.py:661
  39.6 7.7 %collective-permute-start.5 = (bf16[2,2,128,256]{3,2,1,0:T(8,128)(2,1)S(1)}, bf16[2,2,128,256]{3,2,1,0:T(8,128)(2,1)S(1)}, u32[]{:S(2)}, u32[]{:S(2)}) collective-permute-start(bf16[2,2,128,256]{3,2,1,0:T(8,128)(2,1)S(1)} %get-tuple-element.50), channel_id=1, source_target_pairs={{2,4},{6,8},{10,12},{14,16},{18,20},{22,24},{26,28},{4,2},{8,6},{1... | collective-permute-start | bytes 786440 | tf_op jit(solution)/shard_map/ppermute | solution.py:672
  41.6 3.9 %collective-permute-start.6 = (bf16[128,256]{1,0:T(8,128)(2,1)S(1)}, bf16[128,256]{1,0:T(8,128)(2,1)S(1)}, u32[]{:S(2)}, u32[]{:S(2)}) collective-permute-start(bf16[128,256]{1,0:T(8,128)(2,1)S(1)} %get-tuple-element.57), channel_id=1, source_target_pairs={{0,1},{1,0},{2,3},{3,2},{4,5},{5,4},{6,7},{7,6},{8,9},{9,8},{10,11... | collective-permute-start | bytes 196616 | tf_op jit(solution)/shard_map/ppermute | solution.py:681
  43.1 5.4 %collective-permute-start.8 = (bf16[128,256]{1,0:T(8,128)(2,1)S(1)}, bf16[128,256]{1,0:T(8,128)(2,1)S(1)}, u32[]{:S(2)}, u32[]{:S(2)}) collective-permute-start(bf16[128,256]{1,0:T(8,128)(2,1)S(1)} %shard_map.123), channel_id=1, source_target_pairs={{0,1},{1,0},{2,3},{3,2},{4,5},{5,4},{6,7},{7,6},{8,9},{9,8},{10,11... | collective-permute-start | bytes 196616 | tf_op jit(solution)/shard_map/ppermute | solution.py:685

commit v16 on v14

--- a/solution.py
+++ b/solution.py
@@ -267,7 +267,7 @@
 
 def setup_kernel(
     down, up, reflect, classes_in, slowness, freq, hx, hy,
-    q_out_inner, q_in_outer, screen, phase, refl,
+    q_out_inner, q_in_outer, screen, phase, refl, back, base,
     fields, klass, work, sems,
 ):
     fronts = q_out_inner.shape[0]
@@ -323,11 +323,35 @@
     jobs = [(fields.at[1, front], front, q_out_inner.at[front]) for front in range(fronts)]
     jobs += [(fields.at[0, front], front, q_in_outer.at[front]) for front in range(fronts)]
     spread(jobs, work, hx, hy, phase)
+    for front in range(fronts):
+        for part in range(2):
+            back[front, part] = refl[0] * screen[0, front, part]
+    outward_base(q_out_inner, screen, refl, base)
+
+
+def outward_base(q_out_inner, screen, refl, base):
+    kept = 1.0 - refl[0]
+    for front in range(base.shape[0]):
+        b_re, b_im = (q_out_inner[front, part].astype(F32) for part in range(2))
+        b_re, b_im = screened(b_re, b_im, screen[0, front, 0], screen[0, front, 1])
+        base[front, 0] = kept * b_re
+        base[front, 1] = kept * b_im
+
+
+def outward_step(q_arrived, back, base, field):
+    for front in range(field.shape[0]):
+        a_re, a_im = (q_arrived[front, part].astype(F32) for part in range(2))
+        back_re, back_im = back[front, 0], back[front, 1]
+        put(
+            field.at[front],
+            base[front, 0] + (back_re * a_re - back_im * a_im),
+            base[front, 1] + (back_re * a_im + back_im * a_re),
+        )
 
 
 def ahead_kernel(
     partner, q_in_outer, screen, refl, phase, hx, hy,
-    inward_inner, q_out_inner,
+    inward_inner, q_out_inner, base,
     q_field, field, work,
 ):
     everyone = range(partner.shape[0])
@@ -340,6 +364,7 @@
         put(inward_inner.at[front], in_re, in_im)
         put(field.at[front], out_re, out_im)
     spread([(field.at[front], front, q_out_inner.at[front]) for front in everyone], work, hx, hy, phase)
+    outward_base(q_out_inner, screen, refl, base)
 
 
 def entering(arrived, source, front):
@@ -358,13 +383,13 @@
         )
 
 
-def edge_kernel(arrived, source, q_out_inner, screen, refl, phase, hx, hy, sent, q_arrived, field, work):
+def edge_kernel(arrived, source, back, base, phase, hx, hy, sent, q_arrived, field, work):
     everyone = range(arrived.shape[0])
 
     def step(target):
         jobs = [(entering(arrived, source, front), front, q_arrived.at[front]) for front in everyone]
         spread(jobs, work, hx, hy, phase)
-        outer_step(q_arrived, q_out_inner, screen, refl, "outward", target)
+        outward_step(q_arrived, back, base, target)
 
     def early():
         step(sent)
@@ -377,7 +402,7 @@
 
 
 def last_edge_kernel(
-    arrived, source, q_out_inner, screen, refl, phase, hx, hy, after,
+    arrived, source, back, base, phase, hx, hy, after,
     q_arrived, last_far, last_near,
     outward, work,
 ):
@@ -385,8 +410,8 @@
     everyone = range(arrived.shape[0])
     half = arrived.shape[2] // 2
 
-    def step():
-        outer_step(q_arrived, q_out_inner, screen, refl, "outward", outward)
+    def step(q_entered):
+        outward_step(q_entered, back, base, outward)
         jobs = [
             (outward.at[front], front, [(half_rows(1, half), last_far.at[front]), (half_rows(0, half), last_near.at[front])])
             for front in everyone
@@ -396,11 +421,10 @@
     def early():
         jobs = [(entering(arrived, source, front), front, q_arrived.at[front]) for front in everyone]
         spread(jobs, work, hx, hy, phase)
-        step()
+        step(q_arrived)
 
     def late():
-        q_arrived[...] = arrived[...]
-        step()
+        step(arrived)
 
     by_turn(early, late)
 
@@ -432,18 +456,21 @@
 
 
 def last_inner_kernel(
-    q_arrived, q_out_inner, partner, screen, refl, phase, hx, hy, out_inner, q_next_in,
+    q_arrived, arrived, q_out_inner, partner, screen, refl, phase, hx, hy, out_inner, q_next_in,
     inward, outward, terms, far_terms, q_next,
     field, q_inward, q_partner, work,
 ):
     del q_next_in
     everyone = range(partner.shape[0])
 
-    @pl.when(jnp.logical_not(late_pair()))
-    def _():
+    def early():
+        outer_step(q_arrived, q_out_inner, screen, refl, "inward", field)
         spread([(out_inner.at[front], front, q_next.at[front]) for front in everyone], work, hx, hy, phase)
 
-    outer_step(q_arrived, q_out_inner, screen, refl, "inward", field)
+    def late():
+        outer_step(arrived, q_out_inner, screen, refl, "inward", field)
+
+    by_turn(early, late)
     jobs = [(partner.at[front], front, q_partner.at[front]) for front in everyone]
     jobs += [(field.at[front], front, q_inward.at[front]) for front in everyone]
     spread(jobs, work, hx, hy, phase)
@@ -600,11 +627,11 @@
     )
     arrived_0 = to_beyond(out_outer)
     partner_0 = to_partner(in_inner)
-    q_out_inner_0, q_in_outer_0, screen, phase, refl = call(
+    q_out_inner_0, q_in_outer_0, screen, phase, refl, back, base_0 = call(
         setup_kernel,
         [HBM] * 4 + [SMEM] * 2 + [VMEM] * 2,
-        [VMEM] * 5,
-        [plane] * 2 + [screens, turns, pair],
+        [VMEM] * 7,
+        [plane] * 2 + [screens, turns, pair, turns, turns],
         [
             pltpu.VMEM((2, *plane.shape), BF16),
             pltpu.VMEM((2, rows_x, rows_y), jnp.int32),
@@ -613,12 +640,14 @@
         ],
     )(*kept_in_hbm(down_state, up_state, reflect, screen_class), screen_values, freq_index, hx, hy)
     fixed = (screen, refl, phase, hx, hy)
-    in_inner_1, q_out_inner_1 = call(ahead_kernel, [VMEM] * 7, [VMEM] * 2, [plane] * 2, buffers(2) + [work(fronts)])(
+    in_inner_1, q_out_inner_1, base_1 = call(
+        ahead_kernel, [VMEM] * 7, [VMEM] * 3, [plane] * 2 + [turns], buffers(2) + [work(fronts)]
+    )(
         partner_0, q_in_outer_0, *fixed
     )
     partner_1 = to_partner(in_inner_1)
-    out_outer_1, q_arrived = call(edge_kernel, [VMEM] * 8, [VMEM] * 2, [plane] * 2, buffers(1) + [work(fronts)])(
-        arrived_0, source, q_out_inner_0, *fixed
+    out_outer_1, q_arrived = call(edge_kernel, [VMEM] * 7, [VMEM] * 2, [plane] * 2, buffers(1) + [work(fronts)])(
+        arrived_0, source, back, base_0, phase, hx, hy
     )
     arrived_1 = to_beyond(out_outer_1)
     in_inner_2, out_inner_2 = call(
@@ -628,22 +657,22 @@
     q_out_inner_2 = call(spread_kernel, [VMEM] * 4, VMEM, plane, [work(fronts)])(out_inner_2, phase, hx, hy)
     q_arrived_1, last_far, last_near = call(
         last_edge_kernel,
-        [VMEM] * 8 + [pl.BlockSpec(memory_space=pl.ANY)],
+        [VMEM] * 7 + [pl.BlockSpec(memory_space=pl.ANY)],
         [VMEM] * 3,
         [plane] + [half_plane] * 2,
         buffers(1) + [work(fronts)],
-    )(arrived_1, source, q_out_inner_1, *fixed, q_out_inner_2)
+    )(arrived_1, source, back, base_1, phase, hx, hy, q_out_inner_2)
     last_far = to_beyond(last_far)
     last_near = to_beyond(last_near)
     half_sum = jax.ShapeDtypeStruct((half, rows_y), BF16)
     inner_in, inner_out, inner_terms, inner_far, q_out_inner_2 = call(
         last_inner_kernel,
-        [VMEM] * 10,
+        [VMEM] * 11,
         [VMEM] * 5,
         [plane] * 2 + [jax.ShapeDtypeStruct((rows_x, rows_y), F32), half_sum, plane],
         buffers(3) + [work(2 * fronts)],
-        input_output_aliases={9: 4},
-    )(q_arrived_1, q_out_inner_1, partner_2, *fixed, out_inner_2, q_out_inner_2)
+        input_output_aliases={10: 4},
+    )(q_arrived_1, arrived_1, q_out_inner_1, partner_2, *fixed, out_inner_2, q_out_inner_2)
     inner_other = across(inner_far) if shots == 2 else jnp.zeros_like(inner_far)
     outer_far = call(far_terms_kernel, [VMEM] * 3 + [pl.BlockSpec(memory_space=pl.ANY)], VMEM, half_sum)(
         last_far, q_arrived, q_out_inner_2, inner_terms

time: 48.3 us -> 48.1 us (level)
  transfers between devices with their start and end apart: 9 -> 9, of which waited for: 4 -> 4; matrix products, arithmetic and copies ran while one was open for 0% -> 0% of each run, Pallas kernels for 33% -> 34%
where the time goes in v16:
time: 48.1 us; the launch traced here: 47.9 us
  Pallas kernels  18.1 us (38%)
  waiting for transfers between devices  14.4 us (30%)
  starting transfers between devices  14.3 us (30%)
  between operations  1.01 us (2%)
    ppermute x1, waiting for transfers between devices, per_device(): arrived_1 = to_beyond(out_outer_1)  7.69 us
    ppermute x1, waiting for transfers between devices, per_device(): arrived_0 = to_beyond(out_outer)  5.74 us
    pallas_call x1, Pallas kernels, per_device(): call(setup_kernel, [HBM] * 4 + [SMEM] * 2 + [VMEM] * 2, [VMEM] * 7, [plan...  4.78 us
    ppermute x1, starting transfers between devices, per_device(): last_near = to_beyond(last_near)  3.64 us
    pallas_call x1, Pallas kernels, per_device(): call(last_inner_kernel, [VMEM] * 11, [VMEM] * 5, [plane] * 2 + [jax.Shape...  2.01 us
    ppermute x1, starting transfers between devices, per_device(): arrived_0 = to_beyond(out_outer)  1.92 us
    ppermute x1, starting transfers between devices, per_device(): arrived_1 = to_beyond(out_outer_1)  1.92 us
    ppermute x1, starting transfers between devices, per_device(): last_far = to_beyond(last_far)  1.92 us
  transfers between devices with their start and end apart: 9, of which 4 were waited for; matrix products, arithmetic and copies ran while one was open for 0% of the time, Pallas kernels for 34%

profile of v16, /device:TPU:4, one launch (start us, length us, event | category | flops | bytes accessed | tf_op | source)
XLA Modules:
  0.0 47.9 jit_solution(681263629196982746)
XLA Ops:
  0.6 0.0 copy-start
  0.7 1.3 %shard_map.112 = (bf16[2,2,256,256]{3,2,1,0:T(8,128)(2,1)S(1)}, bf16[2,2,256,256]{3,2,1,0:T(8,128)(2,1)S(1)}) custom-call(bf16[2,2,2,256,256]{4,3,2,1,0:T(8,128)(2,1)} %down.3, bf16[2,2,2,256,256]{4,3,2,1,0:T(8,128)(2,1)} %up.3), custom_call_target="tpu_custom_call" | custom-call | tf_op jit(solution)/shard_map/pallas_call | solution.py:625
  2.0 0.1 collective-permute-start.2
  2.0 1.9 %collective-permute-start = (bf16[2,2,256,256]{3,2,1,0:T(8,128)(2,1)S(1)}, bf16[2,2,256,256]{3,2,1,0:T(8,128)(2,1)S(1)}, u32[]{:S(2)}, u32[]{:S(2)}) collective-permute-start(bf16[2,2,256,256]{3,2,1,0:T(8,128)(2,1)S(1)} %get-tuple-element.33), channel_id=1, source_target_pairs={{2,4},{6,8},{10,12},{14,16},{18,20},{22,24},{26,28},{4,2},{8,6},{1... | collective-permute-start | bytes 1572872 | tf_op jit(solution)/shard_map/ppermute | solution.py:628
  4.0 4.8 %shard_map.113 = (bf16[2,2,256,256]{3,2,1,0:T(8,128)(2,1)S(1)}, bf16[2,2,256,256]{3,2,1,0:T(8,128)(2,1)S(1)}, f32[2,2,2,256,256]{4,3,2,1,0:T(8,128)S(1)}, f32[2,...) custom-call(bf16[2,2,2,256,256]{4,3,2,1,0:T(8,128)(2,1)} %down.3, ...), custom_call_target="tpu_custom_call" | custom-call | tf_op jit(solution)/shard_map/pallas_call | solution.py:630
  8.8 0.0 collective-permute-done.2.partner
  8.8 0.0 copy-start.1
  8.8 1.9 %shard_map.115 = (bf16[2,2,256,256]{3,2,1,0:T(8,128)(2,1)S(1)}, bf16[2,2,256,256]{3,2,1,0:T(8,128)(2,1)S(1)}, f32[2,2,256,256]{3,2,1,0:T(8,128)S(1)}) custom-call(bf16[2,2,256,256]{3,2,1,0:T(8,128)(2,1)S(1)} %collective-permute-done.2.partner, bf16[2,2,256,256]{3,2,1,0:T(8,128)(2,1)S(1)} %get-tuple-element.39.q_in_outer, ...), custom_call_target="tpu_custom_call" | custom-call | tf_op jit(solution)/shard_map/pallas_call | solution.py:643
  10.7 1.7 %collective-permute-start.3 = (bf16[2,2,256,256]{3,2,1,0:T(8,128)(2,1)S(1)}, bf16[2,2,256,256]{3,2,1,0:T(8,128)(2,1)S(1)}, u32[]{:S(2)}, u32[]{:S(2)}) collective-permute-start(bf16[2,2,256,256]{3,2,1,0:T(8,128)(2,1)S(1)} %get-tuple-element.45), channel_id=1, source_target_pairs={{0,2},{2,0},{4,6},{6,4},{8,10},{10,8},{12,14},{14,12},{16,18},{18,... | collective-permute-start | bytes 1572872 | tf_op jit(solution)/shard_map/ppermute | solution.py:648
  12.4 5.7 %collective-permute-done.arrived = bf16[2,2,256,256]{3,2,1,0:T(8,128)(2,1)S(1)} collective-permute-done((bf16[2,2,256,256]{3,2,1,0:T(8,128)(2,1)S(1)}, bf16[2,2,256,256]{3,2,1,0:T(8,128)(2,1)S(1)}, u32[]{:S(2)}, u32[]{:S(2)}) %collective-permute-start) | collective-permute-done | bytes 524320 | tf_op jit(solution)/shard_map/ppermute | solution.py:628
  18.2 1.6 %shard_map.114 = (bf16[2,2,256,256]{3,2,1,0:T(8,128)(2,1)S(1)}, bf16[2,2,256,256]{3,2,1,0:T(8,128)(2,1)S(1)}) custom-call(bf16[2,2,256,256]{3,2,1,0:T(8,128)(2,1)S(1)} %collective-permute-done.arrived, bf16[2,2,256,256]{3,2,1,0:T(8,128)(2,1)S(1)} %copy-done.1, f32[2,2,256,256]{3,2,1,0:T(8,128)S(1)} %get-tuple-element.34.back, ...), custom_call_target="tpu_custom_call" | custom-call | tf_op jit(solution)/shard_map/pallas_call | solution.py:649
  19.7 1.9 %collective-permute-start.1 = (bf16[2,2,256,256]{3,2,1,0:T(8,128)(2,1)S(1)}, bf16[2,2,256,256]{3,2,1,0:T(8,128)(2,1)S(1)}, u32[]{:S(2)}, u32[]{:S(2)}) collective-permute-start(bf16[2,2,256,256]{3,2,1,0:T(8,128)(2,1)S(1)} %get-tuple-element.37), channel_id=1, source_target_pairs={{2,4},{6,8},{10,12},{14,16},{18,20},{22,24},{26,28},{4,2},{8,6},{1... | collective-permute-start | bytes 1572872 | tf_op jit(solution)/shard_map/ppermute | solution.py:652
  21.7 0.0 collective-permute-done.3.partner
  21.7 1.8 %shard_map.116 = (bf16[2,2,256,256]{3,2,1,0:T(8,128)(2,1)S(1)}, bf16[2,2,256,256]{3,2,1,0:T(8,128)(2,1)S(1)}) custom-call(bf16[2,2,256,256]{3,2,1,0:T(8,128)(2,1)S(1)} %get-tuple-element.43.q_arrived, bf16[2,2,256,256]{3,2,1,0:T(8,128)(2,1)S(1)} %get-tuple-element.44.q_out_inner, bf16[2,2,256,256]{3,2,1,0:T(8,128)(2,1)S(1)} %collective-permute-done.3.partner, ...), custom_call_target="tpu_custom_call" | custom-call | tf_op jit(solution)/shard_map/pallas_call | solution.py:653
  23.5 0.1 collective-permute-start.5
  23.6 0.8 %shard_map.117.after.q_next_in = bf16[2,2,256,256]{3,2,1,0:T(8,128)(2,1)S(1)} custom-call(bf16[2,2,256,256]{3,2,1,0:T(8,128)(2,1)S(1)} %get-tuple-element.46.fields.out_inner, f32[2,2,256,256]{3,2,1,0:T(8,128)S(1)} %get-tuple-element.36.phase, bf16[256,256]{1,0:T(8,128)(2,1)S(1)} %copy-done, bf16[256,256]{1,0:T(8,128)(2,1)S(1)} %copy-done), custom_call_target="tpu_custom_call" | custom-call | tf_op jit(solution)/shard_map/pallas_call | solution.py:657
  24.4 7.7 %collective-permute-done.1.arrived = bf16[2,2,256,256]{3,2,1,0:T(8,128)(2,1)S(1)} collective-permute-done((bf16[2,2,256,256]{3,2,1,0:T(8,128)(2,1)S(1)}, bf16[2,2,256,256]{3,2,1,0:T(8,128)(2,1)S(1)}, u32[]{:S(2)}, u32[]{:S(2)}) %collective-permute-start.1) | collective-permute-done | bytes 524320 | tf_op jit(solution)/shard_map/ppermute | solution.py:652
  32.1 0.9 %shard_map.118 = (bf16[2,2,256,256]{3,2,1,0:T(8,128)(2,1)S(1)}, bf16[2,2,128,256]{3,2,1,0:T(8,128)(2,1)S(1)}, bf16[2,2,128,256]{3,2,1,0:T(8,128)(2,1)S(1)}) custom-call(bf16[2,2,256,256]{3,2,1,0:T(8,128)(2,1)S(1)} %collective-permute-done.1.arrived, bf16[2,2,256,256]{3,2,1,0:T(8,128)(2,1)S(1)} %copy-done.1, f32[2,2,256,256]{3,2,1,0:T(8,128)S(1)} %get-tuple-element.34.back, ...), custom_call_target="tpu_custom_call" | custom-call | tf_op jit(solution)/shard_map/pallas_call | solution.py:658
  33.0 1.9 %collective-permute-start.7 = (bf16[2,2,128,256]{3,2,1,0:T(8,128)(2,1)S(1)}, bf16[2,2,128,256]{3,2,1,0:T(8,128)(2,1)S(1)}, u32[]{:S(2)}, u32[]{:S(2)}) collective-permute-start(bf16[2,2,128,256]{3,2,1,0:T(8,128)(2,1)S(1)} %get-tuple-element.54), channel_id=1, source_target_pairs={{2,4},{6,8},{10,12},{14,16},{18,20},{22,24},{26,28},{4,2},{8,6},{1... | collective-permute-start | bytes 786440 | tf_op jit(solution)/shard_map/ppermute | solution.py:665
  35.0 3.6 %collective-permute-start.4 = (bf16[2,2,128,256]{3,2,1,0:T(8,128)(2,1)S(1)}, bf16[2,2,128,256]{3,2,1,0:T(8,128)(2,1)S(1)}, u32[]{:S(2)}, u32[]{:S(2)}) collective-permute-start(bf16[2,2,128,256]{3,2,1,0:T(8,128)(2,1)S(1)} %get-tuple-element.47), channel_id=1, source_target_pairs={{2,4},{6,8},{10,12},{14,16},{18,20},{22,24},{26,28},{4,2},{8,6},{1... | collective-permute-start | bytes 786440 | tf_op jit(solution)/shard_map/ppermute | solution.py:666
  38.6 0.0 collective-permute-done.5.partner
  38.6 2.0 %shard_map.119 = (bf16[2,2,256,256]{3,2,1,0:T(8,128)(2,1)S(1)}, bf16[2,2,256,256]{3,2,1,0:T(8,128)(2,1)S(1)}, f32[256,256]{1,0:T(8,128)S(1)}, bf16[128,256]{1,0:T(8,128)(2,1)S(1)}, bf16[2,2,256,256]{3,2,1,0:T(8,128)(2,1)S(1)}) custom-call(bf16[2,2,256,256]{3,2,1,0:T(8,128)(2,1)S(1)} %get-tuple-element.48.q_arrived, ...), custom_call_target="tpu_custom_call", output_to_operand_aliasing={{4}: (10, {})} | custom-call | tf_op jit(solution)/shard_map/pallas_call | solution.py:668
  40.6 1.5 %collective-permute-start.6 = (bf16[128,256]{1,0:T(8,128)(2,1)S(1)}, bf16[128,256]{1,0:T(8,128)(2,1)S(1)}, u32[]{:S(2)}, u32[]{:S(2)}) collective-permute-start(bf16[128,256]{1,0:T(8,128)(2,1)S(1)} %get-tuple-element.53), channel_id=1, source_target_pairs={{0,1},{1,0},{2,3},{3,2},{4,5},{5,4},{6,7},{7,6},{8,9},{9,8},{10,11... | collective-permute-start | bytes 196616 | tf_op jit(solution)/shard_map/ppermute | solution.py:676
  42.2 0.5 collective-permute-done.7.far.last
  42.6 0.1 shard_map.122
  42.7 1.5 %collective-permute-start.8 = (bf16[128,256]{1,0:T(8,128)(2,1)S(1)}, bf16[128,256]{1,0:T(8,128)(2,1)S(1)}, u32[]{:S(2)}, u32[]{:S(2)}) collective-permute-start(bf16[128,256]{1,0:T(8,128)(2,1)S(1)} %shard_map.122), channel_id=1, source_target_pairs={{0,1},{1,0},{2,3},{3,2},{4,5},{5,4},{6,7},{7,6},{8,9},{9,8},{10,11... | collective-permute-start | bytes 196616 | tf_op jit(solution)/shard_map/ppermute | solution.py:680
  44.3 1.2 %shard_map.120 = (bf16[2,2,2,256,256]{4,3,2,1,0:T(8,128)(2,1)}, bf16[2,2,2,256,256]{4,3,2,1,0:T(8,128)(2,1)}) custom-call(bf16[2,2,128,256]{3,2,1,0:T(8,128)(2,1)S(1)} %collective-permute-done.7.far.last, bf16[2,2,256,256]{3,2,1,0:T(8,128)(2,1)S(1)} %get-tuple-element.43.q_arrived, bf16[2,2,256,256]{3,2,1,0:T(8,128)(2,1)S(1)} %get-tuple-element.51.q_out_inner, ...), custom_call_target="tpu_custom_call" | custom-call | tf_op jit(solution)/shard_map/pallas_call | solution.py:683
  45.4 0.0 collective-permute-done.4.near
  45.4 0.0 collective-permute-done.6.inner_other
  45.5 1.1 %shard_map.121 = (bf16[2,2,2,256,256]{4,3,2,1,0:T(8,128)(2,1)}, bf16[2,2,2,256,256]{4,3,2,1,0:T(8,128)(2,1)}, f32[2,128,256]{2,1,0:T(8,128)}, f32[128,256]{1,0:T(8,128)S(1)}) custom-call(bf16[2,2,128,256]{3,2,1,0:T(8,128)(2,1)S(1)} %collective-permute-done.4.near, ...), custom_call_target="tpu_custom_call", output_to_operand_aliasing={{0}: (7, {}), {1}: (8, {})} | custom-call | tf_op jit(solution)/shard_map/pallas_call | solution.py:686
  46.5 0.5 %collective-permute-done.8.other = bf16[128,256]{1,0:T(8,128)(2,1)S(1)} collective-permute-done((bf16[128,256]{1,0:T(8,128)(2,1)S(1)}, bf16[128,256]{1,0:T(8,128)(2,1)S(1)}, u32[]{:S(2)}, u32[]{:S(2)}) %collective-permute-start.8) | collective-permute-done | bytes 65568 | tf_op jit(solution)/shard_map/ppermute | solution.py:680
  47.1 0.7 %shard_map.123 = f32[2,128,256]{2,1,0:T(8,128)} custom-call(f32[128,256]{1,0:T(8,128)S(1)} %get-tuple-element.61.terms, bf16[128,256]{1,0:T(8,128)(2,1)S(1)} %collective-permute-done.8.other, f32[2,128,256]{2,1,0:T(8,128)} %get-tuple-element.62.gradient_in), custom_call_target="tpu_custom_call", output_to_operand_aliasing={{}: (2, {})} | custom-call | tf_op jit(solution)/shard_map/pallas_call | solution.py:694
  (6 shorter events, 0.0 us)
Async XLA Ops:
  0.6 3.3 %copy-start = (bf16[256,256]{1,0:T(8,128)(2,1)S(1)}, bf16[256,256]{1,0:T(8,128)(2,1)}, u32[]{:S(2)}) copy-start(bf16[256,256]{1,0:T(8,128)(2,1)} %constant.2.clone.hx.hy) | copy-start | bytes 393220
  0.6 3.3 %copy-start.3 = (s32[2]{0:T(128)S(1)}, s32[2]{0:T(128)}, u32[]{:S(2)}) copy-start(s32[2]{0:T(128)} %freq.1) | copy-start | bytes 28
  0.7 3.3 %copy-start.2 = (f32[16]{0:T(128)S(1)}, f32[16]{0:T(128)}, u32[]{:S(2)}) copy-start(f32[16]{0:T(128)} %slowness.1) | copy-start | bytes 196
  2.0 6.8 %collective-permute-start.2 = (bf16[2,2,256,256]{3,2,1,0:T(8,128)(2,1)S(1)}, bf16[2,2,256,256]{3,2,1,0:T(8,128)(2,1)S(1)}, u32[]{:S(2)}, u32[]{:S(2)}) collective-permute-start(bf16[2,2,256,256]{3,2,1,0:T(8,128)(2,1)S(1)} %get-tuple-element.38), channel_id=1, source_target_pairs={{0,2},{2,0},{4,6},{6,4},{8,10},{10,8},{12,14},{14,12},{16,18},{18,... | collective-permute-start | bytes 1572872 | tf_op jit(solution)/shard_map/ppermute | solution.py:629
  2.0 16.1 %collective-permute-start = (bf16[2,2,256,256]{3,2,1,0:T(8,128)(2,1)S(1)}, bf16[2,2,256,256]{3,2,1,0:T(8,128)(2,1)S(1)}, u32[]{:S(2)}, u32[]{:S(2)}) collective-permute-start(bf16[2,2,256,256]{3,2,1,0:T(8,128)(2,1)S(1)} %get-tuple-element.33), channel_id=1, source_target_pairs={{2,4},{6,8},{10,12},{14,16},{18,20},{22,24},{26,28},{4,2},{8,6},{1... | collective-permute-start | bytes 1572872 | tf_op jit(solution)/shard_map/ppermute | solution.py:628
  8.8 9.4 %copy-start.1 = (bf16[2,2,256,256]{3,2,1,0:T(8,128)(2,1)S(1)}, bf16[2,2,256,256]{3,2,1,0:T(8,128)(2,1)}, u32[]{:S(2)}) copy-start(bf16[2,2,256,256]{3,2,1,0:T(8,128)(2,1)} %source.3) | copy-start | bytes 1572868
  10.7 11.0 %collective-permute-start.3 = (bf16[2,2,256,256]{3,2,1,0:T(8,128)(2,1)S(1)}, bf16[2,2,256,256]{3,2,1,0:T(8,128)(2,1)S(1)}, u32[]{:S(2)}, u32[]{:S(2)}) collective-permute-start(bf16[2,2,256,256]{3,2,1,0:T(8,128)(2,1)S(1)} %get-tuple-element.45), channel_id=1, source_target_pairs={{0,2},{2,0},{4,6},{6,4},{8,10},{10,8},{12,14},{14,12},{16,18},{18,... | collective-permute-start | bytes 1572872 | tf_op jit(solution)/shard_map/ppermute | solution.py:648
  19.7 12.4 %collective-permute-start.1 = (bf16[2,2,256,256]{3,2,1,0:T(8,128)(2,1)S(1)}, bf16[2,2,256,256]{3,2,1,0:T(8,128)(2,1)S(1)}, u32[]{:S(2)}, u32[]{:S(2)}) collective-permute-start(bf16[2,2,256,256]{3,2,1,0:T(8,128)(2,1)S(1)} %get-tuple-element.37), channel_id=1, source_target_pairs={{2,4},{6,8},{10,12},{14,16},{18,20},{22,24},{26,28},{4,2},{8,6},{1... | collective-permute-start | bytes 1572872 | tf_op jit(solution)/shard_map/ppermute | solution.py:652
  23.5 15.1 %collective-permute-start.5 = (bf16[2,2,256,256]{3,2,1,0:T(8,128)(2,1)S(1)}, bf16[2,2,256,256]{3,2,1,0:T(8,128)(2,1)S(1)}, u32[]{:S(2)}, u32[]{:S(2)}) collective-permute-start(bf16[2,2,256,256]{3,2,1,0:T(8,128)(2,1)S(1)} %get-tuple-element.50), channel_id=1, source_target_pairs={{0,2},{2,0},{4,6},{6,4},{8,10},{10,8},{12,14},{14,12},{16,18},{18,... | collective-permute-start | bytes 1572872 | tf_op jit(solution)/shard_map/ppermute | solution.py:656
  33.0 9.6 %collective-permute-start.7 = (bf16[2,2,128,256]{3,2,1,0:T(8,128)(2,1)S(1)}, bf16[2,2,128,256]{3,2,1,0:T(8,128)(2,1)S(1)}, u32[]{:S(2)}, u32[]{:S(2)}) collective-permute-start(bf16[2,2,128,256]{3,2,1,0:T(8,128)(2,1)S(1)} %get-tuple-element.54), channel_id=1, source_target_pairs={{2,4},{6,8},{10,12},{14,16},{18,20},{22,24},{26,28},{4,2},{8,6},{1... | collective-permute-start | bytes 786440 | tf_op jit(solution)/shard_map/ppermute | solution.py:665
  35.0 10.5 %collective-permute-start.4 = (bf16[2,2,128,256]{3,2,1,0:T(8,128)(2,1)S(1)}, bf16[2,2,128,256]{3,2,1,0:T(8,128)(2,1)S(1)}, u32[]{:S(2)}, u32[]{:S(2)}) collective-permute-start(bf16[2,2,128,256]{3,2,1,0:T(8,128)(2,1)S(1)} %get-tuple-element.47), channel_id=1, source_target_pairs={{2,4},{6,8},{10,12},{14,16},{18,20},{22,24},{26,28},{4,2},{8,6},{1... | collective-permute-start | bytes 786440 | tf_op jit(solution)/shard_map/ppermute | solution.py:666
  40.6 4.8 %collective-permute-start.6 = (bf16[128,256]{1,0:T(8,128)(2,1)S(1)}, bf16[128,256]{1,0:T(8,128)(2,1)S(1)}, u32[]{:S(2)}, u32[]{:S(2)}) collective-permute-start(bf16[128,256]{1,0:T(8,128)(2,1)S(1)} %get-tuple-element.53), channel_id=1, source_target_pairs={{0,1},{1,0},{2,3},{3,2},{4,5},{5,4},{6,7},{7,6},{8,9},{9,8},{10,11... | collective-permute-start | bytes 196616 | tf_op jit(solution)/shard_map/ppermute | solution.py:676
  42.7 4.3 %collective-permute-start.8 = (bf16[128,256]{1,0:T(8,128)(2,1)S(1)}, bf16[128,256]{1,0:T(8,128)(2,1)S(1)}, u32[]{:S(2)}, u32[]{:S(2)}) collective-permute-start(bf16[128,256]{1,0:T(8,128)(2,1)S(1)} %shard_map.122), channel_id=1, source_target_pairs={{0,1},{1,0},{2,3},{3,2},{4,5},{5,4},{6,7},{7,6},{8,9},{9,8},{10,11... | collective-permute-start | bytes 196616 | tf_op jit(solution)/shard_map/ppermute | solution.py:680

commit v17 on v16

--- a/solution.py
+++ b/solution.py
@@ -460,7 +460,6 @@
     inward, outward, terms, far_terms, q_next,
     field, q_inward, q_partner, work,
 ):
-    del q_next_in
     everyone = range(partner.shape[0])
 
     def early():
@@ -469,6 +468,7 @@
 
     def late():
         outer_step(arrived, q_out_inner, screen, refl, "inward", field)
+        q_next[...] = q_next_in[...]
 
     by_turn(early, late)
     jobs = [(partner.at[front], front, q_partner.at[front]) for front in everyone]

time: 48.1 us -> 48.1 us (level)
  no operation moved by 1% of the time
where the time goes in v17:
time: 48.1 us; the launch traced here: 47.9 us
  Pallas kernels  18.2 us (38%)
  starting transfers between devices  14.3 us (30%)
  waiting for transfers between devices  14.3 us (30%)
  between operations  1.01 us (2%)
    ppermute x1, waiting for transfers between devices, per_device(): arrived_1 = to_beyond(out_outer_1)  7.69 us
    ppermute x1, waiting for transfers between devices, per_device(): arrived_0 = to_beyond(out_outer)  5.74 us
    pallas_call x1, Pallas kernels, per_device(): call(setup_kernel, [HBM] * 4 + [SMEM] * 2 + [VMEM] * 2, [VMEM] * 7, [plan...  4.78 us
    ppermute x1, starting transfers between devices, per_device(): last_near = to_beyond(last_near)  3.64 us
    pallas_call x1, Pallas kernels, per_device(): call(last_inner_kernel, [VMEM] * 11, [VMEM] * 5, [plane] * 2 + [jax.Shape...  2.1 us
    ppermute x1, starting transfers between devices, per_device(): arrived_0 = to_beyond(out_outer)  1.92 us
    ppermute x1, starting transfers between devices, per_device(): arrived_1 = to_beyond(out_outer_1)  1.92 us
    ppermute x1, starting transfers between devices, per_device(): last_far = to_beyond(last_far)  1.92 us
  transfers between devices with their start and end apart: 9, of which 4 were waited for; matrix products, arithmetic and copies ran while one was open for 0% of the time, Pallas kernels for 34%

profile of v17, /device:TPU:4, one launch (start us, length us, event | category | flops | bytes accessed | tf_op | source)
XLA Modules:
  0.0 47.9 jit_solution(8721856923718282745)
XLA Ops:
  0.6 0.0 copy-start
  0.7 1.3 %shard_map.112 = (bf16[2,2,256,256]{3,2,1,0:T(8,128)(2,1)S(1)}, bf16[2,2,256,256]{3,2,1,0:T(8,128)(2,1)S(1)}) custom-call(bf16[2,2,2,256,256]{4,3,2,1,0:T(8,128)(2,1)} %down.3, bf16[2,2,2,256,256]{4,3,2,1,0:T(8,128)(2,1)} %up.3), custom_call_target="tpu_custom_call" | custom-call | tf_op jit(solution)/shard_map/pallas_call | solution.py:625
  2.0 0.1 collective-permute-start.2
  2.0 1.9 %collective-permute-start = (bf16[2,2,256,256]{3,2,1,0:T(8,128)(2,1)S(1)}, bf16[2,2,256,256]{3,2,1,0:T(8,128)(2,1)S(1)}, u32[]{:S(2)}, u32[]{:S(2)}) collective-permute-start(bf16[2,2,256,256]{3,2,1,0:T(8,128)(2,1)S(1)} %get-tuple-element.33), channel_id=1, source_target_pairs={{2,4},{6,8},{10,12},{14,16},{18,20},{22,24},{26,28},{4,2},{8,6},{1... | collective-permute-start | bytes 1572872 | tf_op jit(solution)/shard_map/ppermute | solution.py:628
  4.0 4.8 %shard_map.113 = (bf16[2,2,256,256]{3,2,1,0:T(8,128)(2,1)S(1)}, bf16[2,2,256,256]{3,2,1,0:T(8,128)(2,1)S(1)}, f32[2,2,2,256,256]{4,3,2,1,0:T(8,128)S(1)}, f32[2,...) custom-call(bf16[2,2,2,256,256]{4,3,2,1,0:T(8,128)(2,1)} %down.3, ...), custom_call_target="tpu_custom_call" | custom-call | tf_op jit(solution)/shard_map/pallas_call | solution.py:630
  8.8 0.0 collective-permute-done.2.partner
  8.8 0.0 copy-start.1
  8.8 1.9 %shard_map.115 = (bf16[2,2,256,256]{3,2,1,0:T(8,128)(2,1)S(1)}, bf16[2,2,256,256]{3,2,1,0:T(8,128)(2,1)S(1)}, f32[2,2,256,256]{3,2,1,0:T(8,128)S(1)}) custom-call(bf16[2,2,256,256]{3,2,1,0:T(8,128)(2,1)S(1)} %collective-permute-done.2.partner, bf16[2,2,256,256]{3,2,1,0:T(8,128)(2,1)S(1)} %get-tuple-element.39.q_in_outer, ...), custom_call_target="tpu_custom_call" | custom-call | tf_op jit(solution)/shard_map/pallas_call | solution.py:643
  10.7 1.7 %collective-permute-start.3 = (bf16[2,2,256,256]{3,2,1,0:T(8,128)(2,1)S(1)}, bf16[2,2,256,256]{3,2,1,0:T(8,128)(2,1)S(1)}, u32[]{:S(2)}, u32[]{:S(2)}) collective-permute-start(bf16[2,2,256,256]{3,2,1,0:T(8,128)(2,1)S(1)} %get-tuple-element.45), channel_id=1, source_target_pairs={{0,2},{2,0},{4,6},{6,4},{8,10},{10,8},{12,14},{14,12},{16,18},{18,... | collective-permute-start | bytes 1572872 | tf_op jit(solution)/shard_map/ppermute | solution.py:648
  12.4 5.7 %collective-permute-done.arrived = bf16[2,2,256,256]{3,2,1,0:T(8,128)(2,1)S(1)} collective-permute-done((bf16[2,2,256,256]{3,2,1,0:T(8,128)(2,1)S(1)}, bf16[2,2,256,256]{3,2,1,0:T(8,128)(2,1)S(1)}, u32[]{:S(2)}, u32[]{:S(2)}) %collective-permute-start) | collective-permute-done | bytes 524320 | tf_op jit(solution)/shard_map/ppermute | solution.py:628
  18.2 1.6 %shard_map.114 = (bf16[2,2,256,256]{3,2,1,0:T(8,128)(2,1)S(1)}, bf16[2,2,256,256]{3,2,1,0:T(8,128)(2,1)S(1)}) custom-call(bf16[2,2,256,256]{3,2,1,0:T(8,128)(2,1)S(1)} %collective-permute-done.arrived, bf16[2,2,256,256]{3,2,1,0:T(8,128)(2,1)S(1)} %copy-done.1, f32[2,2,256,256]{3,2,1,0:T(8,128)S(1)} %get-tuple-element.34.back, ...), custom_call_target="tpu_custom_call" | custom-call | tf_op jit(solution)/shard_map/pallas_call | solution.py:649
  19.7 1.9 %collective-permute-start.1 = (bf16[2,2,256,256]{3,2,1,0:T(8,128)(2,1)S(1)}, bf16[2,2,256,256]{3,2,1,0:T(8,128)(2,1)S(1)}, u32[]{:S(2)}, u32[]{:S(2)}) collective-permute-start(bf16[2,2,256,256]{3,2,1,0:T(8,128)(2,1)S(1)} %get-tuple-element.37), channel_id=1, source_target_pairs={{2,4},{6,8},{10,12},{14,16},{18,20},{22,24},{26,28},{4,2},{8,6},{1... | collective-permute-start | bytes 1572872 | tf_op jit(solution)/shard_map/ppermute | solution.py:652
  21.7 0.0 collective-permute-done.3.partner
  21.7 1.8 %shard_map.116 = (bf16[2,2,256,256]{3,2,1,0:T(8,128)(2,1)S(1)}, bf16[2,2,256,256]{3,2,1,0:T(8,128)(2,1)S(1)}) custom-call(bf16[2,2,256,256]{3,2,1,0:T(8,128)(2,1)S(1)} %get-tuple-element.43.q_arrived, bf16[2,2,256,256]{3,2,1,0:T(8,128)(2,1)S(1)} %get-tuple-element.44.q_out_inner, bf16[2,2,256,256]{3,2,1,0:T(8,128)(2,1)S(1)} %collective-permute-done.3.partner, ...), custom_call_target="tpu_custom_call" | custom-call | tf_op jit(solution)/shard_map/pallas_call | solution.py:653
  23.5 0.1 collective-permute-start.5
  23.6 0.8 %shard_map.117.after.q_next_in = bf16[2,2,256,256]{3,2,1,0:T(8,128)(2,1)S(1)} custom-call(bf16[2,2,256,256]{3,2,1,0:T(8,128)(2,1)S(1)} %get-tuple-element.46.fields.out_inner, f32[2,2,256,256]{3,2,1,0:T(8,128)S(1)} %get-tuple-element.36.phase, bf16[256,256]{1,0:T(8,128)(2,1)S(1)} %copy-done, bf16[256,256]{1,0:T(8,128)(2,1)S(1)} %copy-done), custom_call_target="tpu_custom_call" | custom-call | tf_op jit(solution)/shard_map/pallas_call | solution.py:657
  24.4 7.7 %collective-permute-done.1.arrived = bf16[2,2,256,256]{3,2,1,0:T(8,128)(2,1)S(1)} collective-permute-done((bf16[2,2,256,256]{3,2,1,0:T(8,128)(2,1)S(1)}, bf16[2,2,256,256]{3,2,1,0:T(8,128)(2,1)S(1)}, u32[]{:S(2)}, u32[]{:S(2)}) %collective-permute-start.1) | collective-permute-done | bytes 524320 | tf_op jit(solution)/shard_map/ppermute | solution.py:652
  32.1 0.9 %shard_map.118 = (bf16[2,2,256,256]{3,2,1,0:T(8,128)(2,1)S(1)}, bf16[2,2,128,256]{3,2,1,0:T(8,128)(2,1)S(1)}, bf16[2,2,128,256]{3,2,1,0:T(8,128)(2,1)S(1)}) custom-call(bf16[2,2,256,256]{3,2,1,0:T(8,128)(2,1)S(1)} %collective-permute-done.1.arrived, bf16[2,2,256,256]{3,2,1,0:T(8,128)(2,1)S(1)} %copy-done.1, f32[2,2,256,256]{3,2,1,0:T(8,128)S(1)} %get-tuple-element.34.back, ...), custom_call_target="tpu_custom_call" | custom-call | tf_op jit(solution)/shard_map/pallas_call | solution.py:658
  33.0 1.9 %collective-permute-start.7 = (bf16[2,2,128,256]{3,2,1,0:T(8,128)(2,1)S(1)}, bf16[2,2,128,256]{3,2,1,0:T(8,128)(2,1)S(1)}, u32[]{:S(2)}, u32[]{:S(2)}) collective-permute-start(bf16[2,2,128,256]{3,2,1,0:T(8,128)(2,1)S(1)} %get-tuple-element.54), channel_id=1, source_target_pairs={{2,4},{6,8},{10,12},{14,16},{18,20},{22,24},{26,28},{4,2},{8,6},{1... | collective-permute-start | bytes 786440 | tf_op jit(solution)/shard_map/ppermute | solution.py:665
  35.0 3.6 %collective-permute-start.4 = (bf16[2,2,128,256]{3,2,1,0:T(8,128)(2,1)S(1)}, bf16[2,2,128,256]{3,2,1,0:T(8,128)(2,1)S(1)}, u32[]{:S(2)}, u32[]{:S(2)}) collective-permute-start(bf16[2,2,128,256]{3,2,1,0:T(8,128)(2,1)S(1)} %get-tuple-element.47), channel_id=1, source_target_pairs={{2,4},{6,8},{10,12},{14,16},{18,20},{22,24},{26,28},{4,2},{8,6},{1... | collective-permute-start | bytes 786440 | tf_op jit(solution)/shard_map/ppermute | solution.py:666
  38.6 0.0 collective-permute-done.5.partner
  38.6 2.1 %shard_map.119 = (bf16[2,2,256,256]{3,2,1,0:T(8,128)(2,1)S(1)}, bf16[2,2,256,256]{3,2,1,0:T(8,128)(2,1)S(1)}, f32[256,256]{1,0:T(8,128)S(1)}, bf16[128,256]{1,0:T(8,128)(2,1)S(1)}, bf16[2,2,256,256]{3,2,1,0:T(8,128)(2,1)S(1)}) custom-call(bf16[2,2,256,256]{3,2,1,0:T(8,128)(2,1)S(1)} %get-tuple-element.48.q_arrived, ...), custom_call_target="tpu_custom_call", output_to_operand_aliasing={{4}: (10, {})} | custom-call | tf_op jit(solution)/shard_map/pallas_call | solution.py:668
  40.7 1.5 %collective-permute-start.6 = (bf16[128,256]{1,0:T(8,128)(2,1)S(1)}, bf16[128,256]{1,0:T(8,128)(2,1)S(1)}, u32[]{:S(2)}, u32[]{:S(2)}) collective-permute-start(bf16[128,256]{1,0:T(8,128)(2,1)S(1)} %get-tuple-element.53), channel_id=1, source_target_pairs={{0,1},{1,0},{2,3},{3,2},{4,5},{5,4},{6,7},{7,6},{8,9},{9,8},{10,11... | collective-permute-start | bytes 196616 | tf_op jit(solution)/shard_map/ppermute | solution.py:676
  42.3 0.4 collective-permute-done.7.far.last
  42.6 0.1 shard_map.122
  42.7 1.5 %collective-permute-start.8 = (bf16[128,256]{1,0:T(8,128)(2,1)S(1)}, bf16[128,256]{1,0:T(8,128)(2,1)S(1)}, u32[]{:S(2)}, u32[]{:S(2)}) collective-permute-start(bf16[128,256]{1,0:T(8,128)(2,1)S(1)} %shard_map.122), channel_id=1, source_target_pairs={{0,1},{1,0},{2,3},{3,2},{4,5},{5,4},{6,7},{7,6},{8,9},{9,8},{10,11... | collective-permute-start | bytes 196616 | tf_op jit(solution)/shard_map/ppermute | solution.py:680
  44.3 1.2 %shard_map.120 = (bf16[2,2,2,256,256]{4,3,2,1,0:T(8,128)(2,1)}, bf16[2,2,2,256,256]{4,3,2,1,0:T(8,128)(2,1)}) custom-call(bf16[2,2,128,256]{3,2,1,0:T(8,128)(2,1)S(1)} %collective-permute-done.7.far.last, bf16[2,2,256,256]{3,2,1,0:T(8,128)(2,1)S(1)} %get-tuple-element.43.q_arrived, bf16[2,2,256,256]{3,2,1,0:T(8,128)(2,1)S(1)} %get-tuple-element.51.q_out_inner, ...), custom_call_target="tpu_custom_call" | custom-call | tf_op jit(solution)/shard_map/pallas_call | solution.py:683
  45.4 0.0 collective-permute-done.4.near
  45.4 0.0 collective-permute-done.6.inner_other
  45.5 1.1 %shard_map.121 = (bf16[2,2,2,256,256]{4,3,2,1,0:T(8,128)(2,1)}, bf16[2,2,2,256,256]{4,3,2,1,0:T(8,128)(2,1)}, f32[2,128,256]{2,1,0:T(8,128)}, f32[128,256]{1,0:T(8,128)S(1)}) custom-call(bf16[2,2,128,256]{3,2,1,0:T(8,128)(2,1)S(1)} %collective-permute-done.4.near, ...), custom_call_target="tpu_custom_call", output_to_operand_aliasing={{0}: (7, {}), {1}: (8, {})} | custom-call | tf_op jit(solution)/shard_map/pallas_call | solution.py:686
  46.5 0.5 %collective-permute-done.8.other = bf16[128,256]{1,0:T(8,128)(2,1)S(1)} collective-permute-done((bf16[128,256]{1,0:T(8,128)(2,1)S(1)}, bf16[128,256]{1,0:T(8,128)(2,1)S(1)}, u32[]{:S(2)}, u32[]{:S(2)}) %collective-permute-start.8) | collective-permute-done | bytes 65568 | tf_op jit(solution)/shard_map/ppermute | solution.py:680
  47.1 0.7 %shard_map.123 = f32[2,128,256]{2,1,0:T(8,128)} custom-call(f32[128,256]{1,0:T(8,128)S(1)} %get-tuple-element.61.terms, bf16[128,256]{1,0:T(8,128)(2,1)S(1)} %collective-permute-done.8.other, f32[2,128,256]{2,1,0:T(8,128)} %get-tuple-element.62.gradient_in), custom_call_target="tpu_custom_call", output_to_operand_aliasing={{}: (2, {})} | custom-call | tf_op jit(solution)/shard_map/pallas_call | solution.py:694
  (6 shorter events, 0.0 us)
Async XLA Ops:
  0.6 3.3 %copy-start = (bf16[256,256]{1,0:T(8,128)(2,1)S(1)}, bf16[256,256]{1,0:T(8,128)(2,1)}, u32[]{:S(2)}) copy-start(bf16[256,256]{1,0:T(8,128)(2,1)} %constant.2.clone.hx.hy) | copy-start | bytes 393220
  0.6 3.3 %copy-start.3 = (s32[2]{0:T(128)S(1)}, s32[2]{0:T(128)}, u32[]{:S(2)}) copy-start(s32[2]{0:T(128)} %freq.1) | copy-start | bytes 28
  0.7 3.3 %copy-start.2 = (f32[16]{0:T(128)S(1)}, f32[16]{0:T(128)}, u32[]{:S(2)}) copy-start(f32[16]{0:T(128)} %slowness.1) | copy-start | bytes 196
  2.0 6.8 %collective-permute-start.2 = (bf16[2,2,256,256]{3,2,1,0:T(8,128)(2,1)S(1)}, bf16[2,2,256,256]{3,2,1,0:T(8,128)(2,1)S(1)}, u32[]{:S(2)}, u32[]{:S(2)}) collective-permute-start(bf16[2,2,256,256]{3,2,1,0:T(8,128)(2,1)S(1)} %get-tuple-element.38), channel_id=1, source_target_pairs={{0,2},{2,0},{4,6},{6,4},{8,10},{10,8},{12,14},{14,12},{16,18},{18,... | collective-permute-start | bytes 1572872 | tf_op jit(solution)/shard_map/ppermute | solution.py:629
  2.0 16.1 %collective-permute-start = (bf16[2,2,256,256]{3,2,1,0:T(8,128)(2,1)S(1)}, bf16[2,2,256,256]{3,2,1,0:T(8,128)(2,1)S(1)}, u32[]{:S(2)}, u32[]{:S(2)}) collective-permute-start(bf16[2,2,256,256]{3,2,1,0:T(8,128)(2,1)S(1)} %get-tuple-element.33), channel_id=1, source_target_pairs={{2,4},{6,8},{10,12},{14,16},{18,20},{22,24},{26,28},{4,2},{8,6},{1... | collective-permute-start | bytes 1572872 | tf_op jit(solution)/shard_map/ppermute | solution.py:628
  8.8 9.4 %copy-start.1 = (bf16[2,2,256,256]{3,2,1,0:T(8,128)(2,1)S(1)}, bf16[2,2,256,256]{3,2,1,0:T(8,128)(2,1)}, u32[]{:S(2)}) copy-start(bf16[2,2,256,256]{3,2,1,0:T(8,128)(2,1)} %source.3) | copy-start | bytes 1572868
  10.7 11.0 %collective-permute-start.3 = (bf16[2,2,256,256]{3,2,1,0:T(8,128)(2,1)S(1)}, bf16[2,2,256,256]{3,2,1,0:T(8,128)(2,1)S(1)}, u32[]{:S(2)}, u32[]{:S(2)}) collective-permute-start(bf16[2,2,256,256]{3,2,1,0:T(8,128)(2,1)S(1)} %get-tuple-element.45), channel_id=1, source_target_pairs={{0,2},{2,0},{4,6},{6,4},{8,10},{10,8},{12,14},{14,12},{16,18},{18,... | collective-permute-start | bytes 1572872 | tf_op jit(solution)/shard_map/ppermute | solution.py:648
  19.7 12.4 %collective-permute-start.1 = (bf16[2,2,256,256]{3,2,1,0:T(8,128)(2,1)S(1)}, bf16[2,2,256,256]{3,2,1,0:T(8,128)(2,1)S(1)}, u32[]{:S(2)}, u32[]{:S(2)}) collective-permute-start(bf16[2,2,256,256]{3,2,1,0:T(8,128)(2,1)S(1)} %get-tuple-element.37), channel_id=1, source_target_pairs={{2,4},{6,8},{10,12},{14,16},{18,20},{22,24},{26,28},{4,2},{8,6},{1... | collective-permute-start | bytes 1572872 | tf_op jit(solution)/shard_map/ppermute | solution.py:652
  23.5 15.1 %collective-permute-start.5 = (bf16[2,2,256,256]{3,2,1,0:T(8,128)(2,1)S(1)}, bf16[2,2,256,256]{3,2,1,0:T(8,128)(2,1)S(1)}, u32[]{:S(2)}, u32[]{:S(2)}) collective-permute-start(bf16[2,2,256,256]{3,2,1,0:T(8,128)(2,1)S(1)} %get-tuple-element.50), channel_id=1, source_target_pairs={{0,2},{2,0},{4,6},{6,4},{8,10},{10,8},{12,14},{14,12},{16,18},{18,... | collective-permute-start | bytes 1572872 | tf_op jit(solution)/shard_map/ppermute | solution.py:656
  33.0 9.6 %collective-permute-start.7 = (bf16[2,2,128,256]{3,2,1,0:T(8,128)(2,1)S(1)}, bf16[2,2,128,256]{3,2,1,0:T(8,128)(2,1)S(1)}, u32[]{:S(2)}, u32[]{:S(2)}) collective-permute-start(bf16[2,2,128,256]{3,2,1,0:T(8,128)(2,1)S(1)} %get-tuple-element.54), channel_id=1, source_target_pairs={{2,4},{6,8},{10,12},{14,16},{18,20},{22,24},{26,28},{4,2},{8,6},{1... | collective-permute-start | bytes 786440 | tf_op jit(solution)/shard_map/ppermute | solution.py:665
  35.0 10.5 %collective-permute-start.4 = (bf16[2,2,128,256]{3,2,1,0:T(8,128)(2,1)S(1)}, bf16[2,2,128,256]{3,2,1,0:T(8,128)(2,1)S(1)}, u32[]{:S(2)}, u32[]{:S(2)}) collective-permute-start(bf16[2,2,128,256]{3,2,1,0:T(8,128)(2,1)S(1)} %get-tuple-element.47), channel_id=1, source_target_pairs={{2,4},{6,8},{10,12},{14,16},{18,20},{22,24},{26,28},{4,2},{8,6},{1... | collective-permute-start | bytes 786440 | tf_op jit(solution)/shard_map/ppermute | solution.py:666
  40.7 4.7 %collective-permute-start.6 = (bf16[128,256]{1,0:T(8,128)(2,1)S(1)}, bf16[128,256]{1,0:T(8,128)(2,1)S(1)}, u32[]{:S(2)}, u32[]{:S(2)}) collective-permute-start(bf16[128,256]{1,0:T(8,128)(2,1)S(1)} %get-tuple-element.53), channel_id=1, source_target_pairs={{0,1},{1,0},{2,3},{3,2},{4,5},{5,4},{6,7},{7,6},{8,9},{9,8},{10,11... | collective-permute-start | bytes 196616 | tf_op jit(solution)/shard_map/ppermute | solution.py:676
  42.7 4.3 %collective-permute-start.8 = (bf16[128,256]{1,0:T(8,128)(2,1)S(1)}, bf16[128,256]{1,0:T(8,128)(2,1)S(1)}, u32[]{:S(2)}, u32[]{:S(2)}) collective-permute-start(bf16[128,256]{1,0:T(8,128)(2,1)S(1)} %shard_map.122), channel_id=1, source_target_pairs={{0,1},{1,0},{2,3},{3,2},{4,5},{5,4},{6,7},{7,6},{8,9},{9,8},{10,11... | collective-permute-start | bytes 196616 | tf_op jit(solution)/shard_map/ppermute | solution.py:680

commit v18 on v17

--- a/solution.py
+++ b/solution.py
@@ -152,8 +152,11 @@
 def spread(jobs, work, hx, hy, phase):
     jobs = list(enumerate(jobs))
     for slot, (plane, _, _) in jobs:
-        for part in range(2):
-            work[slot, part] = mm(hx[...], plane(part) if callable(plane) else plane[part]).astype(BF16)
+        parts = [plane(part) if callable(plane) else plane[part] for part in range(2)]
+        width = parts[0].shape[1]
+        both = mm(hx[...], jnp.concatenate(parts, axis=1)).astype(BF16)
+        work[slot, 0] = both[:, :width]
+        work[slot, 1] = both[:, width:]
     for slot, (_, front, _) in jobs:
         turn_re, turn_im = phase[front, 0], phase[front, 1]
         part_re = mm(work[slot, 0], hy[...])

time: 48.1 us -> 48.1 us (level)
  no operation moved by 1% of the time
where the time goes in v18:
time: 48.1 us; the launch traced here: 47.9 us
  Pallas kernels  18.2 us (38%)
  starting transfers between devices  14.3 us (30%)
  waiting for transfers between devices  14.3 us (30%)
  between operations  1.01 us (2%)
    ppermute x1, waiting for transfers between devices, per_device(): arrived_1 = to_beyond(out_outer_1)  7.69 us
    ppermute x1, waiting for transfers between devices, per_device(): arrived_0 = to_beyond(out_outer)  5.74 us
    pallas_call x1, Pallas kernels, per_device(): call(setup_kernel, [HBM] * 4 + [SMEM] * 2 + [VMEM] * 2, [VMEM] * 7, [plan...  4.78 us
    ppermute x1, starting transfers between devices, per_device(): last_near = to_beyond(last_near)  3.64 us
    pallas_call x1, Pallas kernels, per_device(): call(last_inner_kernel, [VMEM] * 11, [VMEM] * 5, [plane] * 2 + [jax.Shape...  2.1 us
    ppermute x1, starting transfers between devices, per_device(): arrived_0 = to_beyond(out_outer)  1.92 us
    ppermute x1, starting transfers between devices, per_device(): arrived_1 = to_beyond(out_outer_1)  1.92 us
    ppermute x1, starting transfers between devices, per_device(): last_far = to_beyond(last_far)  1.92 us
  transfers between devices with their start and end apart: 9, of which 4 were waited for; matrix products, arithmetic and copies ran while one was open for 0% of the time, Pallas kernels for 34%

profile of v18, /device:TPU:4, one launch (start us, length us, event | category | flops | bytes accessed | tf_op | source)
XLA Modules:
  0.0 47.9 jit_solution(170248824001629711)
XLA Ops:
  0.6 0.0 copy-start
  0.7 1.3 %shard_map.112 = (bf16[2,2,256,256]{3,2,1,0:T(8,128)(2,1)S(1)}, bf16[2,2,256,256]{3,2,1,0:T(8,128)(2,1)S(1)}) custom-call(bf16[2,2,2,256,256]{4,3,2,1,0:T(8,128)(2,1)} %down.3, bf16[2,2,2,256,256]{4,3,2,1,0:T(8,128)(2,1)} %up.3), custom_call_target="tpu_custom_call" | custom-call | tf_op jit(solution)/shard_map/pallas_call | solution.py:628
  2.0 0.1 collective-permute-start.2
  2.0 1.9 %collective-permute-start = (bf16[2,2,256,256]{3,2,1,0:T(8,128)(2,1)S(1)}, bf16[2,2,256,256]{3,2,1,0:T(8,128)(2,1)S(1)}, u32[]{:S(2)}, u32[]{:S(2)}) collective-permute-start(bf16[2,2,256,256]{3,2,1,0:T(8,128)(2,1)S(1)} %get-tuple-element.33), channel_id=1, source_target_pairs={{2,4},{6,8},{10,12},{14,16},{18,20},{22,24},{26,28},{4,2},{8,6},{1... | collective-permute-start | bytes 1572872 | tf_op jit(solution)/shard_map/ppermute | solution.py:631
  4.0 4.8 %shard_map.113 = (bf16[2,2,256,256]{3,2,1,0:T(8,128)(2,1)S(1)}, bf16[2,2,256,256]{3,2,1,0:T(8,128)(2,1)S(1)}, f32[2,2,2,256,256]{4,3,2,1,0:T(8,128)S(1)}, f32[2,...) custom-call(bf16[2,2,2,256,256]{4,3,2,1,0:T(8,128)(2,1)} %down.3, ...), custom_call_target="tpu_custom_call" | custom-call | tf_op jit(solution)/shard_map/pallas_call | solution.py:633
  8.8 0.0 collective-permute-done.2.partner
  8.8 0.0 copy-start.1
  8.8 1.9 %shard_map.115 = (bf16[2,2,256,256]{3,2,1,0:T(8,128)(2,1)S(1)}, bf16[2,2,256,256]{3,2,1,0:T(8,128)(2,1)S(1)}, f32[2,2,256,256]{3,2,1,0:T(8,128)S(1)}) custom-call(bf16[2,2,256,256]{3,2,1,0:T(8,128)(2,1)S(1)} %collective-permute-done.2.partner, bf16[2,2,256,256]{3,2,1,0:T(8,128)(2,1)S(1)} %get-tuple-element.39.q_in_outer, ...), custom_call_target="tpu_custom_call" | custom-call | tf_op jit(solution)/shard_map/pallas_call | solution.py:646
  10.7 1.7 %collective-permute-start.3 = (bf16[2,2,256,256]{3,2,1,0:T(8,128)(2,1)S(1)}, bf16[2,2,256,256]{3,2,1,0:T(8,128)(2,1)S(1)}, u32[]{:S(2)}, u32[]{:S(2)}) collective-permute-start(bf16[2,2,256,256]{3,2,1,0:T(8,128)(2,1)S(1)} %get-tuple-element.45), channel_id=1, source_target_pairs={{0,2},{2,0},{4,6},{6,4},{8,10},{10,8},{12,14},{14,12},{16,18},{18,... | collective-permute-start | bytes 1572872 | tf_op jit(solution)/shard_map/ppermute | solution.py:651
  12.4 5.7 %collective-permute-done.arrived = bf16[2,2,256,256]{3,2,1,0:T(8,128)(2,1)S(1)} collective-permute-done((bf16[2,2,256,256]{3,2,1,0:T(8,128)(2,1)S(1)}, bf16[2,2,256,256]{3,2,1,0:T(8,128)(2,1)S(1)}, u32[]{:S(2)}, u32[]{:S(2)}) %collective-permute-start) | collective-permute-done | bytes 524320 | tf_op jit(solution)/shard_map/ppermute | solution.py:631
  18.2 1.6 %shard_map.114 = (bf16[2,2,256,256]{3,2,1,0:T(8,128)(2,1)S(1)}, bf16[2,2,256,256]{3,2,1,0:T(8,128)(2,1)S(1)}) custom-call(bf16[2,2,256,256]{3,2,1,0:T(8,128)(2,1)S(1)} %collective-permute-done.arrived, bf16[2,2,256,256]{3,2,1,0:T(8,128)(2,1)S(1)} %copy-done.1, f32[2,2,256,256]{3,2,1,0:T(8,128)S(1)} %get-tuple-element.34.back, ...), custom_call_target="tpu_custom_call" | custom-call | tf_op jit(solution)/shard_map/pallas_call | solution.py:652
  19.7 1.9 %collective-permute-start.1 = (bf16[2,2,256,256]{3,2,1,0:T(8,128)(2,1)S(1)}, bf16[2,2,256,256]{3,2,1,0:T(8,128)(2,1)S(1)}, u32[]{:S(2)}, u32[]{:S(2)}) collective-permute-start(bf16[2,2,256,256]{3,2,1,0:T(8,128)(2,1)S(1)} %get-tuple-element.37), channel_id=1, source_target_pairs={{2,4},{6,8},{10,12},{14,16},{18,20},{22,24},{26,28},{4,2},{8,6},{1... | collective-permute-start | bytes 1572872 | tf_op jit(solution)/shard_map/ppermute | solution.py:655
  21.7 0.0 collective-permute-done.3.partner
  21.7 1.8 %shard_map.116 = (bf16[2,2,256,256]{3,2,1,0:T(8,128)(2,1)S(1)}, bf16[2,2,256,256]{3,2,1,0:T(8,128)(2,1)S(1)}) custom-call(bf16[2,2,256,256]{3,2,1,0:T(8,128)(2,1)S(1)} %get-tuple-element.43.q_arrived, bf16[2,2,256,256]{3,2,1,0:T(8,128)(2,1)S(1)} %get-tuple-element.44.q_out_inner, bf16[2,2,256,256]{3,2,1,0:T(8,128)(2,1)S(1)} %collective-permute-done.3.partner, ...), custom_call_target="tpu_custom_call" | custom-call | tf_op jit(solution)/shard_map/pallas_call | solution.py:656
  23.5 0.1 collective-permute-start.5
  23.6 0.8 %shard_map.117.after.q_next_in = bf16[2,2,256,256]{3,2,1,0:T(8,128)(2,1)S(1)} custom-call(bf16[2,2,256,256]{3,2,1,0:T(8,128)(2,1)S(1)} %get-tuple-element.46.fields.out_inner, f32[2,2,256,256]{3,2,1,0:T(8,128)S(1)} %get-tuple-element.36.phase, bf16[256,256]{1,0:T(8,128)(2,1)S(1)} %copy-done, bf16[256,256]{1,0:T(8,128)(2,1)S(1)} %copy-done), custom_call_target="tpu_custom_call" | custom-call | tf_op jit(solution)/shard_map/pallas_call | solution.py:660
  24.4 7.7 %collective-permute-done.1.arrived = bf16[2,2,256,256]{3,2,1,0:T(8,128)(2,1)S(1)} collective-permute-done((bf16[2,2,256,256]{3,2,1,0:T(8,128)(2,1)S(1)}, bf16[2,2,256,256]{3,2,1,0:T(8,128)(2,1)S(1)}, u32[]{:S(2)}, u32[]{:S(2)}) %collective-permute-start.1) | collective-permute-done | bytes 524320 | tf_op jit(solution)/shard_map/ppermute | solution.py:655
  32.1 0.9 %shard_map.118 = (bf16[2,2,256,256]{3,2,1,0:T(8,128)(2,1)S(1)}, bf16[2,2,128,256]{3,2,1,0:T(8,128)(2,1)S(1)}, bf16[2,2,128,256]{3,2,1,0:T(8,128)(2,1)S(1)}) custom-call(bf16[2,2,256,256]{3,2,1,0:T(8,128)(2,1)S(1)} %collective-permute-done.1.arrived, bf16[2,2,256,256]{3,2,1,0:T(8,128)(2,1)S(1)} %copy-done.1, f32[2,2,256,256]{3,2,1,0:T(8,128)S(1)} %get-tuple-element.34.back, ...), custom_call_target="tpu_custom_call" | custom-call | tf_op jit(solution)/shard_map/pallas_call | solution.py:661
  33.0 1.9 %collective-permute-start.7 = (bf16[2,2,128,256]{3,2,1,0:T(8,128)(2,1)S(1)}, bf16[2,2,128,256]{3,2,1,0:T(8,128)(2,1)S(1)}, u32[]{:S(2)}, u32[]{:S(2)}) collective-permute-start(bf16[2,2,128,256]{3,2,1,0:T(8,128)(2,1)S(1)} %get-tuple-element.54), channel_id=1, source_target_pairs={{2,4},{6,8},{10,12},{14,16},{18,20},{22,24},{26,28},{4,2},{8,6},{1... | collective-permute-start | bytes 786440 | tf_op jit(solution)/shard_map/ppermute | solution.py:668
  35.0 3.6 %collective-permute-start.4 = (bf16[2,2,128,256]{3,2,1,0:T(8,128)(2,1)S(1)}, bf16[2,2,128,256]{3,2,1,0:T(8,128)(2,1)S(1)}, u32[]{:S(2)}, u32[]{:S(2)}) collective-permute-start(bf16[2,2,128,256]{3,2,1,0:T(8,128)(2,1)S(1)} %get-tuple-element.47), channel_id=1, source_target_pairs={{2,4},{6,8},{10,12},{14,16},{18,20},{22,24},{26,28},{4,2},{8,6},{1... | collective-permute-start | bytes 786440 | tf_op jit(solution)/shard_map/ppermute | solution.py:669
  38.6 0.0 collective-permute-done.5.partner
  38.6 2.1 %shard_map.119 = (bf16[2,2,256,256]{3,2,1,0:T(8,128)(2,1)S(1)}, bf16[2,2,256,256]{3,2,1,0:T(8,128)(2,1)S(1)}, f32[256,256]{1,0:T(8,128)S(1)}, bf16[128,256]{1,0:T(8,128)(2,1)S(1)}, bf16[2,2,256,256]{3,2,1,0:T(8,128)(2,1)S(1)}) custom-call(bf16[2,2,256,256]{3,2,1,0:T(8,128)(2,1)S(1)} %get-tuple-element.48.q_arrived, ...), custom_call_target="tpu_custom_call", output_to_operand_aliasing={{4}: (10, {})} | custom-call | tf_op jit(solution)/shard_map/pallas_call | solution.py:671
  40.7 1.5 %collective-permute-start.6 = (bf16[128,256]{1,0:T(8,128)(2,1)S(1)}, bf16[128,256]{1,0:T(8,128)(2,1)S(1)}, u32[]{:S(2)}, u32[]{:S(2)}) collective-permute-start(bf16[128,256]{1,0:T(8,128)(2,1)S(1)} %get-tuple-element.53), channel_id=1, source_target_pairs={{0,1},{1,0},{2,3},{3,2},{4,5},{5,4},{6,7},{7,6},{8,9},{9,8},{10,11... | collective-permute-start | bytes 196616 | tf_op jit(solution)/shard_map/ppermute | solution.py:679
  42.3 0.4 collective-permute-done.7.far.last
  42.6 0.1 shard_map.122
  42.7 1.5 %collective-permute-start.8 = (bf16[128,256]{1,0:T(8,128)(2,1)S(1)}, bf16[128,256]{1,0:T(8,128)(2,1)S(1)}, u32[]{:S(2)}, u32[]{:S(2)}) collective-permute-start(bf16[128,256]{1,0:T(8,128)(2,1)S(1)} %shard_map.122), channel_id=1, source_target_pairs={{0,1},{1,0},{2,3},{3,2},{4,5},{5,4},{6,7},{7,6},{8,9},{9,8},{10,11... | collective-permute-start | bytes 196616 | tf_op jit(solution)/shard_map/ppermute | solution.py:683
  44.3 1.2 %shard_map.120 = (bf16[2,2,2,256,256]{4,3,2,1,0:T(8,128)(2,1)}, bf16[2,2,2,256,256]{4,3,2,1,0:T(8,128)(2,1)}) custom-call(bf16[2,2,128,256]{3,2,1,0:T(8,128)(2,1)S(1)} %collective-permute-done.7.far.last, bf16[2,2,256,256]{3,2,1,0:T(8,128)(2,1)S(1)} %get-tuple-element.43.q_arrived, bf16[2,2,256,256]{3,2,1,0:T(8,128)(2,1)S(1)} %get-tuple-element.51.q_out_inner, ...), custom_call_target="tpu_custom_call" | custom-call | tf_op jit(solution)/shard_map/pallas_call | solution.py:686
  45.4 0.0 collective-permute-done.4.near
  45.4 0.0 collective-permute-done.6.inner_other
  45.5 1.1 %shard_map.121 = (bf16[2,2,2,256,256]{4,3,2,1,0:T(8,128)(2,1)}, bf16[2,2,2,256,256]{4,3,2,1,0:T(8,128)(2,1)}, f32[2,128,256]{2,1,0:T(8,128)}, f32[128,256]{1,0:T(8,128)S(1)}) custom-call(bf16[2,2,128,256]{3,2,1,0:T(8,128)(2,1)S(1)} %collective-permute-done.4.near, ...), custom_call_target="tpu_custom_call", output_to_operand_aliasing={{0}: (7, {}), {1}: (8, {})} | custom-call | tf_op jit(solution)/shard_map/pallas_call | solution.py:689
  46.5 0.5 %collective-permute-done.8.other = bf16[128,256]{1,0:T(8,128)(2,1)S(1)} collective-permute-done((bf16[128,256]{1,0:T(8,128)(2,1)S(1)}, bf16[128,256]{1,0:T(8,128)(2,1)S(1)}, u32[]{:S(2)}, u32[]{:S(2)}) %collective-permute-start.8) | collective-permute-done | bytes 65568 | tf_op jit(solution)/shard_map/ppermute | solution.py:683
  47.1 0.7 %shard_map.123 = f32[2,128,256]{2,1,0:T(8,128)} custom-call(f32[128,256]{1,0:T(8,128)S(1)} %get-tuple-element.61.terms, bf16[128,256]{1,0:T(8,128)(2,1)S(1)} %collective-permute-done.8.other, f32[2,128,256]{2,1,0:T(8,128)} %get-tuple-element.62.gradient_in), custom_call_target="tpu_custom_call", output_to_operand_aliasing={{}: (2, {})} | custom-call | tf_op jit(solution)/shard_map/pallas_call | solution.py:697
  (6 shorter events, 0.0 us)
Async XLA Ops:
  0.6 3.3 %copy-start = (bf16[256,256]{1,0:T(8,128)(2,1)S(1)}, bf16[256,256]{1,0:T(8,128)(2,1)}, u32[]{:S(2)}) copy-start(bf16[256,256]{1,0:T(8,128)(2,1)} %constant.2.clone.hx.hy) | copy-start | bytes 393220
  0.6 3.3 %copy-start.3 = (s32[2]{0:T(128)S(1)}, s32[2]{0:T(128)}, u32[]{:S(2)}) copy-start(s32[2]{0:T(128)} %freq.1) | copy-start | bytes 28
  0.7 3.3 %copy-start.2 = (f32[16]{0:T(128)S(1)}, f32[16]{0:T(128)}, u32[]{:S(2)}) copy-start(f32[16]{0:T(128)} %slowness.1) | copy-start | bytes 196
  2.0 6.8 %collective-permute-start.2 = (bf16[2,2,256,256]{3,2,1,0:T(8,128)(2,1)S(1)}, bf16[2,2,256,256]{3,2,1,0:T(8,128)(2,1)S(1)}, u32[]{:S(2)}, u32[]{:S(2)}) collective-permute-start(bf16[2,2,256,256]{3,2,1,0:T(8,128)(2,1)S(1)} %get-tuple-element.38), channel_id=1, source_target_pairs={{0,2},{2,0},{4,6},{6,4},{8,10},{10,8},{12,14},{14,12},{16,18},{18,... | collective-permute-start | bytes 1572872 | tf_op jit(solution)/shard_map/ppermute | solution.py:632
  2.0 16.1 %collective-permute-start = (bf16[2,2,256,256]{3,2,1,0:T(8,128)(2,1)S(1)}, bf16[2,2,256,256]{3,2,1,0:T(8,128)(2,1)S(1)}, u32[]{:S(2)}, u32[]{:S(2)}) collective-permute-start(bf16[2,2,256,256]{3,2,1,0:T(8,128)(2,1)S(1)} %get-tuple-element.33), channel_id=1, source_target_pairs={{2,4},{6,8},{10,12},{14,16},{18,20},{22,24},{26,28},{4,2},{8,6},{1... | collective-permute-start | bytes 1572872 | tf_op jit(solution)/shard_map/ppermute | solution.py:631
  8.8 9.4 %copy-start.1 = (bf16[2,2,256,256]{3,2,1,0:T(8,128)(2,1)S(1)}, bf16[2,2,256,256]{3,2,1,0:T(8,128)(2,1)}, u32[]{:S(2)}) copy-start(bf16[2,2,256,256]{3,2,1,0:T(8,128)(2,1)} %source.3) | copy-start | bytes 1572868
  10.7 11.0 %collective-permute-start.3 = (bf16[2,2,256,256]{3,2,1,0:T(8,128)(2,1)S(1)}, bf16[2,2,256,256]{3,2,1,0:T(8,128)(2,1)S(1)}, u32[]{:S(2)}, u32[]{:S(2)}) collective-permute-start(bf16[2,2,256,256]{3,2,1,0:T(8,128)(2,1)S(1)} %get-tuple-element.45), channel_id=1, source_target_pairs={{0,2},{2,0},{4,6},{6,4},{8,10},{10,8},{12,14},{14,12},{16,18},{18,... | collective-permute-start | bytes 1572872 | tf_op jit(solution)/shard_map/ppermute | solution.py:651
  19.7 12.4 %collective-permute-start.1 = (bf16[2,2,256,256]{3,2,1,0:T(8,128)(2,1)S(1)}, bf16[2,2,256,256]{3,2,1,0:T(8,128)(2,1)S(1)}, u32[]{:S(2)}, u32[]{:S(2)}) collective-permute-start(bf16[2,2,256,256]{3,2,1,0:T(8,128)(2,1)S(1)} %get-tuple-element.37), channel_id=1, source_target_pairs={{2,4},{6,8},{10,12},{14,16},{18,20},{22,24},{26,28},{4,2},{8,6},{1... | collective-permute-start | bytes 1572872 | tf_op jit(solution)/shard_map/ppermute | solution.py:655
  23.5 15.1 %collective-permute-start.5 = (bf16[2,2,256,256]{3,2,1,0:T(8,128)(2,1)S(1)}, bf16[2,2,256,256]{3,2,1,0:T(8,128)(2,1)S(1)}, u32[]{:S(2)}, u32[]{:S(2)}) collective-permute-start(bf16[2,2,256,256]{3,2,1,0:T(8,128)(2,1)S(1)} %get-tuple-element.50), channel_id=1, source_target_pairs={{0,2},{2,0},{4,6},{6,4},{8,10},{10,8},{12,14},{14,12},{16,18},{18,... | collective-permute-start | bytes 1572872 | tf_op jit(solution)/shard_map/ppermute | solution.py:659
  33.0 9.6 %collective-permute-start.7 = (bf16[2,2,128,256]{3,2,1,0:T(8,128)(2,1)S(1)}, bf16[2,2,128,256]{3,2,1,0:T(8,128)(2,1)S(1)}, u32[]{:S(2)}, u32[]{:S(2)}) collective-permute-start(bf16[2,2,128,256]{3,2,1,0:T(8,128)(2,1)S(1)} %get-tuple-element.54), channel_id=1, source_target_pairs={{2,4},{6,8},{10,12},{14,16},{18,20},{22,24},{26,28},{4,2},{8,6},{1... | collective-permute-start | bytes 786440 | tf_op jit(solution)/shard_map/ppermute | solution.py:668
  35.0 10.5 %collective-permute-start.4 = (bf16[2,2,128,256]{3,2,1,0:T(8,128)(2,1)S(1)}, bf16[2,2,128,256]{3,2,1,0:T(8,128)(2,1)S(1)}, u32[]{:S(2)}, u32[]{:S(2)}) collective-permute-start(bf16[2,2,128,256]{3,2,1,0:T(8,128)(2,1)S(1)} %get-tuple-element.47), channel_id=1, source_target_pairs={{2,4},{6,8},{10,12},{14,16},{18,20},{22,24},{26,28},{4,2},{8,6},{1... | collective-permute-start | bytes 786440 | tf_op jit(solution)/shard_map/ppermute | solution.py:669
  40.7 4.7 %collective-permute-start.6 = (bf16[128,256]{1,0:T(8,128)(2,1)S(1)}, bf16[128,256]{1,0:T(8,128)(2,1)S(1)}, u32[]{:S(2)}, u32[]{:S(2)}) collective-permute-start(bf16[128,256]{1,0:T(8,128)(2,1)S(1)} %get-tuple-element.53), channel_id=1, source_target_pairs={{0,1},{1,0},{2,3},{3,2},{4,5},{5,4},{6,7},{7,6},{8,9},{9,8},{10,11... | collective-permute-start | bytes 196616 | tf_op jit(solution)/shard_map/ppermute | solution.py:679
  42.7 4.3 %collective-permute-start.8 = (bf16[128,256]{1,0:T(8,128)(2,1)S(1)}, bf16[128,256]{1,0:T(8,128)(2,1)S(1)}, u32[]{:S(2)}, u32[]{:S(2)}) collective-permute-start(bf16[128,256]{1,0:T(8,128)(2,1)S(1)} %shard_map.122), channel_id=1, source_target_pairs={{0,1},{1,0},{2,3},{3,2},{4,5},{5,4},{6,7},{7,6},{8,9},{9,8},{10,11... | collective-permute-start | bytes 196616 | tf_op jit(solution)/shard_map/ppermute | solution.py:683
